TPU v7x, 32 devices: a whole 2x2x4 slice. The times are simulated.
32 devices in a mesh: groups: 2 (over y), shard: 4 (over z), section: 2 (over x), halo: 2 (over core).
Axes of the slice: x: 2, y: 2, z: 4, core: 2. Of those that a mesh axis runs over, the one named last changes fastest.
Arguments:
- features: bfloat16 [4, 4, 16, 64, 320], P(('groups', 'section'), 'shard', 'halo'), parts along dimension 0, may hold values from -6 to 6
- timesteps: int32 [4, 2], P(('groups', 'section')), parts along dimension 0, may hold values from 0 to 999
- conv_first: bfloat16 [2, 3, 3, 320, 320], P('section'), may hold values from -0.109375 to 0.109375
- conv_second: bfloat16 [2, 3, 3, 320, 320], P('section'), may hold values from -0.109375 to 0.109375
- time_weight: bfloat16 [2, 320, 320], P('section'), may hold values from -0.3125 to 0.3125
- qkv_weight: bfloat16 [2, 320, 960], P('section'), may hold values from -7 to 7
- attn_out: bfloat16 [2, 320, 320], P('section'), may hold values from -0.3125 to 0.3125
- geglu_in: bfloat16 [2, 320, 2560], P('section'), may hold values from -0.3125 to 0.3125
- geglu_out: bfloat16 [2, 1280, 320], P('section'), may hold values from -0.15625 to 0.15625
Outputs:
- result: bfloat16 [4, 4, 16, 64, 320], P(('groups', 'section'), 'shard', 'halo'), parts along dimension 0
There are 2 independent parts, one for each index of `groups`. A program takes and returns all parts, laid end to end along the dimension named above; an argument that names none is the same for every part. Nothing has to cross between parts.
All inputs are finite; a program needn't handle non-finite values.
Results may differ from a plain program's by a relative error of at most 0.02.
Values may be sent and summed in bfloat16 or wider, within the bound.
No kernel may reach another device: no remote copies, remote signals or barrier semaphores. Data moves between devices by JAX's collectives and lax.ppermute only.
A program may use at most 64 MiB of HBM per device.

v0:
```python
import functools
import math

import jax
import jax.numpy as jnp
from jax import lax
from jax.experimental import pallas as pl
from jax.experimental.pallas import tpu as pltpu
from jax.sharding import PartitionSpec as P

HEAD_DIM = 64
GROUPS = 32
STEPS = 2
LANES = 128
WIDE = 256
F32 = jnp.float32
BF16 = jnp.bfloat16


def round_up(value, unit):
    return -(-value // unit) * unit


def group_scale(total, square, entries, group_width, channels):
    lanes = total.shape[1]
    left = lax.broadcasted_iota(jnp.int32, (lanes, lanes), 0)
    right = lax.broadcasted_iota(jnp.int32, (lanes, lanes), 1)
    group = [
        sum((side >= g * group_width).astype(jnp.int32) for g in range(1, channels // group_width))
        for side in (left[:, :1], right[:1, :])
    ]
    same = (group[0] == group[1]) & (left < channels) & (right < channels)
    both = jnp.concatenate([total, square, jnp.zeros((6, lanes), F32)], axis=0)
    summed = jnp.dot(
        both, same.astype(F32), preferred_element_type=F32, precision=lax.Precision.HIGHEST
    ) / entries
    average = summed[0:1]
    scale = lax.rsqrt(summed[1:2] - average * average + 1e-05)
    inside = lax.broadcasted_iota(jnp.int32, (1, lanes), 1) < channels
    scale = jnp.where(inside, scale, 0.0)
    return scale, -average * scale


def spatial_kernel(rows, half, columns, channels, group_width, step, pieces, shards, *refs):
    own_refs, other_refs = refs[:pieces], refs[pieces : 2 * pieces]
    weights = refs[2 * pieces : 2 * pieces + 4]
    embeds = refs[2 * pieces + 4]
    outs = refs[2 * pieces + 5 : 2 * pieces + 5 + shards]
    field, active, hidden, tails, main1, tail1, main2, tail2, arrived_sems = refs[
        2 * pieces + 5 + shards :
    ]
    loads = [
        pltpu.make_async_copy(source, target, arrived_sems.at[i])
        for i, (source, target) in enumerate(zip(weights, (main1, tail1, main2, tail2)))
    ]
    for load in loads:
        load.start()
    embed = embeds[step : step + 1, :]
    lanes = field.shape[1]
    own_rows = rows // half
    part = own_rows * columns // shards
    size = own_rows * columns // pieces
    here = lax.axis_index("halo")
    spot = lax.axis_index("shard")
    own_base = here * (own_rows * columns)
    other_base = (1 - here) * (own_rows * columns)

    field[:, lanes - LANES :] = jnp.zeros((rows * columns, LANES), F32)
    for base, arrived in ((own_base, own_refs), (other_base, other_refs)):
        for d in range(pieces):
            place = pl.multiple_of(base + lax.rem(spot + d, pieces) * size, size)
            field[pl.ds(place, size), :channels] = arrived[d][...].astype(F32)

    column = lax.broadcasted_iota(jnp.int32, (columns, 1), 0)

    def sums(source):
        def body(i, carry):
            total, square = carry
            chunk = source[pl.ds(pl.multiple_of(i * columns, columns), columns), :]
            chunk = chunk.reshape(columns // 8, 8, lanes)
            return total + jnp.sum(chunk, axis=0), square + jnp.sum(chunk * chunk, axis=0)

        zero = jnp.zeros((8, lanes), F32)
        total, square = lax.fori_loop(0, rows, body, (zero, zero))
        return jnp.sum(total, axis=0, keepdims=True), jnp.sum(square, axis=0, keepdims=True)

    def activate(source, scale, shift, first, count):
        def body(i, _):
            row = first - 1 + i
            inside = (row >= 0) & (row < rows)
            at = pl.multiple_of(jnp.clip(row, 0, rows - 1) * columns, columns)
            u = source[pl.ds(at, columns), :] * scale + shift
            g = u * (0.5 + 0.5 * jnp.tanh(0.5 * u))
            g = g * inside.astype(F32)
            before = jnp.where(column == 0, 0.0, pltpu.roll(g, 1, 0))
            after = jnp.where(column == columns - 1, 0.0, pltpu.roll(g, columns - 1, 0))
            to = pl.ds(pl.multiple_of(i * columns, columns), columns)
            active[to, 0:WIDE] = before[:, :WIDE].astype(BF16)
            active[to, WIDE : 2 * WIDE] = g[:, :WIDE].astype(BF16)
            active[to, 2 * WIDE : 3 * WIDE] = after[:, :WIDE].astype(BF16)
            mixed = before[:, WIDE:] + pltpu.roll(g[:, WIDE:], LANES // 2, 1)
            active[to, 3 * WIDE : 3 * WIDE + LANES] = mixed.astype(BF16)
            active[to, 3 * WIDE + LANES :] = after[:, WIDE:].astype(BF16)
            return 0

        lax.fori_loop(0, count + 2, body, 0)

    def convolve(main, tail, count):
        tokens = count * columns
        tails[0 : tokens + 2 * columns, :] = jnp.dot(
            active[0 : tokens + 2 * columns, :], tail[...], preferred_element_type=F32
        )
        wide = sum(
            jnp.dot(
                active[r * columns : r * columns + tokens, :], main[r], preferred_element_type=F32
            )
            for r in range(3)
        )
        narrow = (
            tails[0:tokens, :LANES]
            + pltpu.roll(tails[columns : columns + tokens, :LANES], LANES // 2, 1)
            + tails[2 * columns : 2 * columns + tokens, LANES:]
        )
        return wide, narrow

    entries = float(rows * columns * group_width)
    low = lax.broadcasted_iota(jnp.int32, (1, LANES), 1) < channels - WIDE
    activate(field, *group_scale(*sums(field), entries, group_width, channels), 0, rows)
    loads[0].wait()
    loads[1].wait()
    wide, narrow = convolve(main1, tail1, rows)
    hidden[:, :WIDE] = wide + embed[:, :WIDE]
    hidden[:, WIDE:] = jnp.where(low, narrow + embed[:, WIDE:], 0.0)
    activate(
        hidden,
        *group_scale(*sums(hidden), entries, group_width, channels),
        here * own_rows,
        own_rows,
    )
    loads[2].wait()
    loads[3].wait()
    wide, narrow = convolve(main2, tail2, own_rows)
    mine = pl.ds(pl.multiple_of(own_base, columns), own_rows * columns)
    hidden[mine, :WIDE] = wide + field[mine, :WIDE]
    hidden[mine, WIDE:] = narrow + field[mine, WIDE:]
    for d in range(shards):
        place = pl.multiple_of(own_base + lax.rem(spot + d, shards) * part, part)
        outs[d][...] = hidden[pl.ds(place, part), :channels].astype(BF16)


def spatial(own, other, weights, embeds, step, rows, columns, half, shards):
    pieces = len(own)
    channels = own[0].shape[1]
    lanes = round_up(channels, LANES)
    tokens = rows * columns
    depth = weights[0].shape[1]
    kernel = functools.partial(
        spatial_kernel, rows, half, columns, channels, channels // GROUPS, step, pieces, shards
    )
    flops = 2 * tokens * depth * 4 * WIDE * 3 // 2
    vmem = pl.BlockSpec(memory_space=pltpu.VMEM)
    hbm = pl.BlockSpec(memory_space=pltpu.HBM)
    return pl.pallas_call(
        kernel,
        out_shape=[jax.ShapeDtypeStruct((tokens // half // shards, channels), BF16)] * shards,
        in_specs=[vmem] * (2 * pieces) + [hbm] * 4 + [vmem],
        out_specs=[vmem] * shards,
        scratch_shapes=[
            pltpu.VMEM((tokens, lanes), F32),
            pltpu.VMEM((tokens + 2 * columns, depth), BF16),
            pltpu.VMEM((tokens, lanes), F32),
            pltpu.VMEM((tokens + 2 * columns, WIDE), F32),
            *[pltpu.VMEM(w.shape, BF16) for w in weights],
            pltpu.SemaphoreType.DMA((4,)),
        ],
        compiler_params=pltpu.CompilerParams(vmem_limit_bytes=40 * 1024 * 1024),
        cost_estimate=pl.CostEstimate(
            flops=flops, bytes_accessed=6000000, transcendentals=tokens * lanes
        ),
        name="spatial",
    )(*own, *other, *weights, embeds)


def prepare_kernel(channels, kernel1, kernel2, qkv, main1, tail1, main2, tail2, padded):
    spare = channels - WIDE
    depth = main1.shape[1]
    for kernel, main, tail in ((kernel1, main1, tail1), (kernel2, main2, tail2)):
        main[:, 3 * channels :, :] = jnp.zeros((3, depth - 3 * channels, WIDE), BF16)
        tail[3 * channels :, :] = jnp.zeros((depth - 3 * channels, WIDE), BF16)
        for s in range(3):
            for source, target in (
                (slice(0, WIDE), slice(s * WIDE, (s + 1) * WIDE)),
                (slice(WIDE, channels), slice(3 * WIDE + s * spare, 3 * WIDE + (s + 1) * spare)),
            ):
                for r in range(3):
                    main[r, target, :] = kernel[r, s, source, :WIDE]
                first, second, third = [kernel[r, s, source, WIDE:] for r in range(3)]
                tail[target, :LANES] = jnp.concatenate([first, second], axis=1)
                tail[target, LANES:] = jnp.concatenate([third, jnp.zeros_like(third)], axis=1)
    lanes = padded.shape[1] // 3
    padded[...] = jnp.zeros(padded.shape, BF16)
    for i in range(3):
        padded[:, i * lanes : i * lanes + channels] = qkv[:, i * channels : (i + 1) * channels]


def prepare(conv_first, conv_second, qkv):
    channels = qkv.shape[0]
    depth = round_up(3 * channels, WIDE)
    lanes = round_up(channels, LANES)
    vmem = pl.BlockSpec(memory_space=pltpu.VMEM)
    main = jax.ShapeDtypeStruct((3, depth, WIDE), BF16)
    tail = jax.ShapeDtypeStruct((depth, WIDE), BF16)
    outs = [main, tail, main, tail, jax.ShapeDtypeStruct((channels, 3 * lanes), BF16)]
    *packed, padded = pl.pallas_call(
        functools.partial(prepare_kernel, channels),
        out_shape=outs,
        in_specs=[vmem] * 3,
        out_specs=[vmem] * 5,
        compiler_params=pltpu.CompilerParams(vmem_limit_bytes=40 * 1024 * 1024),
        cost_estimate=pl.CostEstimate(flops=0, bytes_accessed=10000000, transcendentals=0),
        name="prepare",
    )(conv_first, conv_second, qkv)
    return packed, padded


def norm_rows(values):
    average = jnp.mean(values, axis=-1, keepdims=True)
    centred = values - average
    spread = jnp.mean(centred * centred, axis=-1, keepdims=True)
    return (centred * lax.rsqrt(spread + 1e-05)).astype(BF16)


def temporal_kernel(frames, heads, *refs):
    parts = refs[:frames]
    weights = refs[frames : frames + 4]
    outs = refs[frames + 4 : 2 * frames + 4]
    stream, projected, products, mixed, active = refs[2 * frames + 4 : 2 * frames + 9]
    qkv, attn_out, geglu_in, geglu_out, arrived_sems = refs[2 * frames + 9 :]
    loads = [
        pltpu.make_async_copy(source, target, arrived_sems.at[i])
        for i, (source, target) in enumerate(zip(weights, (qkv, attn_out, geglu_in, geglu_out)))
    ]
    for load in loads:
        load.start()
    pixels, channels = parts[0].shape
    lanes = projected.shape[1] // 3
    inner = geglu_out.shape[1]

    for f in range(frames):
        stream[f * pixels : (f + 1) * pixels, :] = parts[f][...]
    normed = norm_rows(stream[...].astype(F32))
    loads[0].wait()
    projected[...] = jnp.dot(normed, qkv[...], preferred_element_type=F32).astype(BF16)

    lane = lax.broadcasted_iota(jnp.int32, (2 * lanes, LANES), 0)
    head = lax.broadcasted_iota(jnp.int32, (2 * lanes, LANES), 1)
    lane = jnp.where(lane >= lanes, lane - lanes, lane)
    gather = ((lane >= head * HEAD_DIM) & (lane < (head + 1) * HEAD_DIM) & (head < heads)).astype(BF16)
    lane = lax.broadcasted_iota(jnp.int32, (LANES, lanes), 1)
    head = lax.broadcasted_iota(jnp.int32, (LANES, lanes), 0)
    spread = ((lane >= head * HEAD_DIM) & (lane < (head + 1) * HEAD_DIM) & (head < heads)).astype(BF16)

    for f in range(frames):
        query = projected[f * pixels : (f + 1) * pixels, 0:lanes].astype(F32)
        for g in range(frames):
            key = projected[g * pixels : (g + 1) * pixels, lanes : 2 * lanes].astype(F32)
            product = query * key
            high = product.astype(BF16)
            at = slice(g * pixels, (g + 1) * pixels)
            products[at, 0:lanes] = high
            products[at, lanes:] = (product - high.astype(F32)).astype(BF16)
        scores = jnp.dot(products[...], gather, preferred_element_type=F32) * HEAD_DIM ** (-0.5)
        scores = [scores[g * pixels : (g + 1) * pixels] for g in range(frames)]
        top = functools.reduce(jnp.maximum, scores)
        scores = [jnp.exp(score - top) for score in scores]
        total = 1.0 / sum(scores)
        weights = jnp.concatenate([score * total for score in scores], axis=0).astype(BF16)
        weights = jnp.dot(weights, spread, preferred_element_type=F32)
        mix = sum(
            weights[g * pixels : (g + 1) * pixels]
            * projected[g * pixels : (g + 1) * pixels, 2 * lanes :].astype(F32)
            for g in range(frames)
        )
        mixed[f * pixels : (f + 1) * pixels, :] = mix.astype(BF16)

    loads[1].wait()
    update = jnp.dot(mixed[:, :channels], attn_out[...], preferred_element_type=F32)
    stream[...] = (stream[...].astype(F32) + update).astype(BF16)
    normed = norm_rows(stream[...].astype(F32))
    loads[2].wait()
    for at in range(0, inner, WIDE):
        value = jnp.dot(normed, geglu_in[:, at : at + WIDE], preferred_element_type=F32)
        gate = jnp.dot(normed, geglu_in[:, inner + at : inner + at + WIDE], preferred_element_type=F32)
        act = value * (0.5 * gate) * (1.0 + lax.erf(gate * math.sqrt(0.5)))
        active[:, at : at + WIDE] = act.astype(BF16)
    loads[3].wait()
    update = lax.dot_general(
        active[...], geglu_out[...], (((1,), (1,)), ((), ())), preferred_element_type=F32
    )
    update = (stream[...].astype(F32) + update).astype(BF16)
    for f in range(frames):
        outs[f][...] = update[f * pixels : (f + 1) * pixels, :]


def temporal(parts, weights):
    frames = len(parts)
    pixels, channels = parts[0].shape
    lanes = round_up(channels, LANES)
    tokens = frames * pixels
    inner = weights[3].shape[1]
    vmem = pl.BlockSpec(memory_space=pltpu.VMEM)
    hbm = pl.BlockSpec(memory_space=pltpu.HBM)
    flops = 2 * tokens * channels * (3 * lanes + channels + 3 * inner)
    return pl.pallas_call(
        functools.partial(temporal_kernel, frames, channels // HEAD_DIM),
        out_shape=[jax.ShapeDtypeStruct((pixels, channels), BF16)] * frames,
        in_specs=[vmem] * frames + [hbm] * 4,
        out_specs=[vmem] * frames,
        scratch_shapes=[
            pltpu.VMEM((tokens, channels), BF16),
            pltpu.VMEM((tokens, 3 * lanes), BF16),
            pltpu.VMEM((tokens, 2 * lanes), BF16),
            pltpu.VMEM((tokens, lanes), BF16),
            pltpu.VMEM((tokens, inner), BF16),
            *[pltpu.VMEM(w.shape, BF16) for w in weights],
            pltpu.SemaphoreType.DMA((4,)),
        ],
        compiler_params=pltpu.CompilerParams(vmem_limit_bytes=40 * 1024 * 1024),
        cost_estimate=pl.CostEstimate(
            flops=flops, bytes_accessed=4000000, transcendentals=tokens * inner
        ),
        name="temporal",
    )(*parts, *weights)


def send(block, hops):
    axes = tuple(axis for axis, _ in hops)
    sizes = [lax.axis_size(axis) for axis in axes]
    route = []
    for source in range(math.prod(sizes)):
        rest, target, stride = source, 0, 1
        for size, (_, distance) in zip(reversed(sizes), reversed(hops)):
            target += (rest % size + distance) % size * stride
            rest, stride = rest // size, stride * size
        route.append((source, target))
    if all(a == b for a, b in route):
        return block
    return lax.ppermute(block, axes if len(axes) > 1 else axes[0], route)


def embed_time(stamps, time_weight):
    half_width = time_weight.shape[0] // 2
    frequency = jnp.exp(-math.log(10000.0) * jnp.arange(half_width, dtype=F32) / half_width)
    angles = stamps.astype(F32)[:, None] * frequency[None, :]
    sinusoid = jnp.concatenate([jnp.cos(angles), jnp.sin(angles)], axis=1)
    out = jnp.dot(jax.nn.silu(sinusoid).astype(BF16), time_weight, preferred_element_type=F32)
    return jnp.pad(out, ((0, 0), (0, round_up(out.shape[1], LANES) - out.shape[1])))


def per_device(
    features,
    timesteps,
    conv_first,
    conv_second,
    time_weight,
    qkv_weight,
    attn_out,
    geglu_in,
    geglu_out,
):
    _, _, own_rows, columns, channels = features.shape
    half = lax.axis_size("halo")
    rows = own_rows * half
    shards = lax.axis_size("shard")
    spot = lax.axis_index("shard")
    part = own_rows * columns // shards

    moved = send(features.reshape(own_rows * columns, channels), (("section", 1),))
    embeds = embed_time(timesteps[0], time_weight[0])
    spatial_weights, padded = prepare(conv_first[0], conv_second[0], qkv_weight[0])
    temporal_weights = (padded, attn_out[0], geglu_in[0], geglu_out[0].T)

    own, other = [moved], [send(moved, (("halo", 1),))]
    for denoise_step in range(STEPS):
        parts = spatial(
            own, other, spatial_weights, embeds, denoise_step, rows, columns, half, shards
        )
        parts = [send(parts[d], (("shard", d),)) for d in range(shards)]
        parts = temporal(parts, temporal_weights)
        if denoise_step < STEPS - 1:
            own = [send(parts[d], (("shard", -d), ("section", 1))) for d in range(shards)]
            other = [send(block, (("halo", 1),)) for block in own]
        else:
            own = [send(parts[d], (("shard", -d),)) for d in range(shards)]
    result = jnp.zeros((own_rows * columns, channels), BF16)
    for d in range(shards):
        result = lax.dynamic_update_slice_in_dim(
            result, own[d], lax.rem(spot + d, shards) * part, axis=0
        )
    return result.reshape(features.shape)


def solution(mesh):
    return jax.shard_map(
        per_device,
        mesh=mesh,
        in_specs=(
            P(("groups", "section"), "shard", "halo", None, None),
            P(("groups", "section"), None),
            P("section", None, None, None, None),
            P("section", None, None, None, None),
            P("section", None, None),
            P("section", None, None),
            P("section", None, None),
            P("section", None, None),
            P("section", None, None),
        ),
        out_specs=P(("groups", "section"), "shard", "halo", None, None),
        check_vma=False,
    )
```

profile of v0, /device:TPU:0, one launch (start us, length us, event | category | flops | bytes accessed | tf_op | source)
XLA Modules:
  0.0 112.4 jit_solution(3021563267231354398)
XLA Ops:
  0.0 2.9 %collective-permute-start = (bf16[512,320]{1,0:T(8,128)(2,1)}, bf16[512,320]{1,0:T(8,128)(2,1)S(1)}, u32[]{:S(2)}, u32[]{:S(2)}) collective-permute-start(bf16[512,320]{1,0:T(8,128)(2,1)} %bitcast.24), channel_id=1, source_target_pairs={{0,2},{2,0},{1,3},{3,1},{4,6},{6,4},{5,7},{7,5},{8,10},{10,8},{9,1... | collective-permute-start | bytes 983048 | tf_op jit(solution)/shard_map/ppermute | solution.py:348
  3.0 0.7 convert_bitcast_fusion
  3.6 8.6 %collective-permute-done.refs_0_ = bf16[512,320]{1,0:T(8,128)(2,1)S(1)} collective-permute-done((bf16[512,320]{1,0:T(8,128)(2,1)}, bf16[512,320]{1,0:T(8,128)(2,1)S(1)}, u32[]{:S(2)}, u32[]{:S(2)}) %collective-permute-start) | collective-permute-done | bytes 327712 | tf_op jit(solution)/shard_map/ppermute | solution.py:348
  12.3 0.1 multiply_cosine_fusion
  12.4 0.2 fusion
  12.6 0.0 copy-start.1
  12.6 1.6 %copy-done.1 = bf16[1,3,3,320,320]{4,3,2,1,0:T(8,128)(2,1)S(1)} copy-done((bf16[1,3,3,320,320]{4,3,2,1,0:T(8,128)(2,1)S(1)}, bf16[1,3,3,320,320]{4,3,2,1,0:T(8,128)(2,1)}, u32[]{:S(2)}) %copy-start.1) | copy-done | bytes 1843224
  14.3 1.6 %copy-done.2 = bf16[1,3,3,320,320]{4,3,2,1,0:T(8,128)(2,1)S(1)} copy-done((bf16[1,3,3,320,320]{4,3,2,1,0:T(8,128)(2,1)S(1)}, bf16[1,3,3,320,320]{4,3,2,1,0:T(8,128)(2,1)}, u32[]{:S(2)}) %copy-start.2) | copy-done | bytes 1843224
  15.9 1.1 copy-done.3
  17.0 0.5 prepare.1
  17.5 0.0 copy-start.4
  17.5 0.0 copy-start.5
  17.5 0.0 copy-start.6
  17.6 11.2 %spatial.2 = (bf16[128,320]{1,0:T(8,128)(2,1)S(1)}, bf16[128,320]{1,0:T(8,128)(2,1)S(1)}, bf16[128,320]{1,0:T(8,128)(2,1)S(1)}, bf16[128,320]{1,0:T(8,128)(2,1)S(1)}) custom-call(bf16[512,320]{1,0:T(8,128)(2,1)S(1)} %collective-permute-done.refs_0_, bf16[512,320]{1,0:T(8,128)(2,1)S(1)} %collective-permute-done.1.refs_1_, ...), custom_call_target="tpu_custom_call" | custom-call | flops 3221225472 | bytes 6000000 | tf_op jit(solution)/shard_map/spatial/pallas_call | solution.py:163
  28.8 1.9 %collective-permute-start.2 = (bf16[128,320]{1,0:T(8,128)(2,1)S(1)}, bf16[128,320]{1,0:T(8,128)(2,1)S(1)}, u32[]{:S(2)}, u32[]{:S(2)}) collective-permute-start(bf16[128,320]{1,0:T(8,128)(2,1)S(1)} %get-tuple-element.31), channel_id=1, source_target_pairs={{0,4},{4,8},{8,12},{12,0},{1,5},{5,9},{9,13},{13,1},{2,6},{6,10},{... | collective-permute-start | bytes 245768 | tf_op jit(solution)/shard_map/ppermute | solution.py:348
  30.6 2.6 %collective-permute-start.3 = (bf16[128,320]{1,0:T(8,128)(2,1)S(1)}, bf16[128,320]{1,0:T(8,128)(2,1)S(1)}, u32[]{:S(2)}, u32[]{:S(2)}) collective-permute-start(bf16[128,320]{1,0:T(8,128)(2,1)S(1)} %get-tuple-element.32), channel_id=1, source_target_pairs={{0,8},{4,12},{8,0},{12,4},{1,9},{5,13},{9,1},{13,5},{2,10},{6,14},... | collective-permute-start | bytes 245768 | tf_op jit(solution)/shard_map/ppermute | solution.py:348
  33.2 1.3 %collective-permute-start.4 = (bf16[128,320]{1,0:T(8,128)(2,1)S(1)}, bf16[128,320]{1,0:T(8,128)(2,1)S(1)}, u32[]{:S(2)}, u32[]{:S(2)}) collective-permute-start(bf16[128,320]{1,0:T(8,128)(2,1)S(1)} %get-tuple-element.33), channel_id=1, source_target_pairs={{0,12},{4,0},{8,4},{12,8},{1,13},{5,1},{9,5},{13,9},{2,14},{6,2},{... | collective-permute-start | bytes 245768 | tf_op jit(solution)/shard_map/ppermute | solution.py:348
  34.6 1.8 %collective-permute-done.2.refs_1_ = bf16[128,320]{1,0:T(8,128)(2,1)S(1)} collective-permute-done((bf16[128,320]{1,0:T(8,128)(2,1)S(1)}, bf16[128,320]{1,0:T(8,128)(2,1)S(1)}, u32[]{:S(2)}, u32[]{:S(2)}) %collective-permute-start.2) | collective-permute-done | bytes 81952 | tf_op jit(solution)/shard_map/ppermute | solution.py:348
  36.4 4.0 %collective-permute-done.3.refs_2_ = bf16[128,320]{1,0:T(8,128)(2,1)S(1)} collective-permute-done((bf16[128,320]{1,0:T(8,128)(2,1)S(1)}, bf16[128,320]{1,0:T(8,128)(2,1)S(1)}, u32[]{:S(2)}, u32[]{:S(2)}) %collective-permute-start.3) | collective-permute-done | bytes 81952 | tf_op jit(solution)/shard_map/ppermute | solution.py:348
  40.4 8.2 %temporal.2 = (bf16[128,320]{1,0:T(8,128)(2,1)S(1)}, bf16[128,320]{1,0:T(8,128)(2,1)S(1)}, bf16[128,320]{1,0:T(8,128)(2,1)S(1)}, bf16[128,320]{1,0:T(8,128)(2,1)S(1)}) custom-call(bf16[128,320]{1,0:T(8,128)(2,1)S(1)} %get-tuple-element.30.refs_0_, bf16[128,320]{1,0:T(8,128)(2,1)S(1)} %collective-permute-done.2.refs_1_, ...), custom_call_target="tpu_custom_call" | custom-call | flops 1740636160 | bytes 4000000 | tf_op jit(solution)/shard_map/temporal/pallas_call | solution.py:314
  48.7 4.7 %collective-permute-start.6 = (bf16[128,320]{1,0:T(8,128)(2,1)S(1)}, bf16[128,320]{1,0:T(8,128)(2,1)S(1)}, u32[]{:S(2)}, u32[]{:S(2)}) collective-permute-start(bf16[128,320]{1,0:T(8,128)(2,1)S(1)} %get-tuple-element.36), channel_id=1, source_target_pairs={{0,14},{2,12},{4,2},{6,0},{8,6},{10,4},{12,10},{14,8},{1,15},{3,13... | collective-permute-start | bytes 245768 | tf_op jit(solution)/shard_map/ppermute | solution.py:348
  53.3 0.4 collective-permute-start.7
  53.7 0.5 collective-permute-start.8
  54.2 1.3 %collective-permute-start.5 = (bf16[128,320]{1,0:T(8,128)(2,1)S(1)}, bf16[128,320]{1,0:T(8,128)(2,1)S(1)}, u32[]{:S(2)}, u32[]{:S(2)}) collective-permute-start(bf16[128,320]{1,0:T(8,128)(2,1)S(1)} %get-tuple-element.35), channel_id=1, source_target_pairs={{0,2},{2,0},{4,6},{6,4},{8,10},{10,8},{12,14},{14,12},{1,3},{3,1},... | collective-permute-start | bytes 245768 | tf_op jit(solution)/shard_map/ppermute | solution.py:348
  55.4 1.1 collective-permute-done.6.refs_1_
  56.6 6.2 %collective-permute-done.7.refs_2_ = bf16[128,320]{1,0:T(8,128)(2,1)S(1)} collective-permute-done((bf16[128,320]{1,0:T(8,128)(2,1)S(1)}, bf16[128,320]{1,0:T(8,128)(2,1)S(1)}, u32[]{:S(2)}, u32[]{:S(2)}) %collective-permute-start.7) | collective-permute-done | bytes 81952 | tf_op jit(solution)/shard_map/ppermute | solution.py:348
  62.8 0.5 collective-permute-start.12
  63.3 0.1 collective-permute-start.9
  63.4 0.7 collective-permute-done.11.refs_6_
  64.1 0.2 collective-permute-done.12.refs_7_
  64.2 0.4 collective-permute-done.9.refs_4_
  64.6 11.9 %spatial.3 = (bf16[128,320]{1,0:T(8,128)(2,1)S(1)}, bf16[128,320]{1,0:T(8,128)(2,1)}, bf16[128,320]{1,0:T(8,128)(2,1)}, bf16[128,320]{1,0:T(8,128)(2,1)S(1)}) custom-call(bf16[128,320]{1,0:T(8,128)(2,1)S(1)} %collective-permute-done.5.refs_0_, bf16[128,320]{1,0:T(8,128)(2,1)S(1)} %collective-permute-done.6.refs_1_, ...), custom_call_target="tpu_custom_call" | custom-call | flops 3221225472 | bytes 6000000 | tf_op jit(solution)/shard_map/spatial/pallas_call | solution.py:163
  76.5 0.6 copy-done.8
  77.1 0.2 collective-permute-start.13
  77.3 2.3 %collective-permute-start.14 = (bf16[128,320]{1,0:T(8,128)(2,1)}, bf16[128,320]{1,0:T(8,128)(2,1)}, u32[]{:S(2)}, u32[]{:S(2)}) collective-permute-start(bf16[128,320]{1,0:T(8,128)(2,1)} %get-tuple-element.41), channel_id=1, source_target_pairs={{0,8},{4,12},{8,0},{12,4},{1,9},{5,13},{9,1},{13,5},{2,10},{6,14},... | collective-permute-start | bytes 245768 | tf_op jit(solution)/shard_map/ppermute | solution.py:348
  79.6 1.6 %collective-permute-start.15 = (bf16[128,320]{1,0:T(8,128)(2,1)S(1)}, bf16[128,320]{1,0:T(8,128)(2,1)}, u32[]{:S(2)}, u32[]{:S(2)}) collective-permute-start(bf16[128,320]{1,0:T(8,128)(2,1)S(1)} %get-tuple-element.42), channel_id=1, source_target_pairs={{0,12},{4,0},{8,4},{12,8},{1,13},{5,1},{9,5},{13,9},{2,14},{6,2},{... | collective-permute-start | bytes 245768 | tf_op jit(solution)/shard_map/ppermute | solution.py:348
  81.2 3.7 %collective-permute-done.13.refs_1_ = bf16[128,320]{1,0:T(8,128)(2,1)} collective-permute-done((bf16[128,320]{1,0:T(8,128)(2,1)}, bf16[128,320]{1,0:T(8,128)(2,1)}, u32[]{:S(2)}, u32[]{:S(2)}) %collective-permute-start.13) | collective-permute-done | bytes 81952 | tf_op jit(solution)/shard_map/ppermute | solution.py:348
  85.0 3.4 %collective-permute-done.14.refs_2_ = bf16[128,320]{1,0:T(8,128)(2,1)} collective-permute-done((bf16[128,320]{1,0:T(8,128)(2,1)}, bf16[128,320]{1,0:T(8,128)(2,1)}, u32[]{:S(2)}, u32[]{:S(2)}) %collective-permute-start.14) | collective-permute-done | bytes 81952 | tf_op jit(solution)/shard_map/ppermute | solution.py:348
  88.4 0.9 copy-done.7
  89.3 0.9 copy-done.9
  90.2 9.2 %temporal.3 = (bf16[128,320]{1,0:T(8,128)(2,1)S(1)}, bf16[128,320]{1,0:T(8,128)(2,1)S(1)}, bf16[128,320]{1,0:T(8,128)(2,1)S(1)}, bf16[128,320]{1,0:T(8,128)(2,1)S(1)}) custom-call(bf16[128,320]{1,0:T(8,128)(2,1)S(1)} %copy-done.9, bf16[128,320]{1,0:T(8,128)(2,1)} %collective-permute-done.13.refs_1_, bf16[128,320]{1,0:T(8,128)(2,1)} %collective-permute-done.14.refs_2_, ...), custom_call_target="tpu_custom_call" | custom-call | flops 1740636160 | bytes 4000000 | tf_op jit(solution)/shard_map/temporal/pallas_call | solution.py:314
  99.4 2.6 %collective-permute-start.16 = (bf16[128,320]{1,0:T(8,128)(2,1)S(1)}, bf16[128,320]{1,0:T(8,128)(2,1)S(1)}, u32[]{:S(2)}, u32[]{:S(2)}) collective-permute-start(bf16[128,320]{1,0:T(8,128)(2,1)S(1)} %get-tuple-element.44), channel_id=1, source_target_pairs={{0,12},{4,0},{8,4},{12,8},{1,13},{5,1},{9,5},{13,9},{2,14},{6,2},{... | collective-permute-start | bytes 245768 | tf_op jit(solution)/shard_map/ppermute | solution.py:348
  102.0 0.6 collective-permute-start.17
  102.6 0.0 collective-permute-start.18
  102.7 2.5 %collective-permute-done.16 = bf16[128,320]{1,0:T(8,128)(2,1)S(1)} collective-permute-done((bf16[128,320]{1,0:T(8,128)(2,1)S(1)}, bf16[128,320]{1,0:T(8,128)(2,1)S(1)}, u32[]{:S(2)}, u32[]{:S(2)}) %collective-permute-start.16) | collective-permute-done | bytes 81952 | tf_op jit(solution)/shard_map/ppermute | solution.py:348
  105.3 6.3 %collective-permute-done.17 = bf16[128,320]{1,0:T(8,128)(2,1)S(1)} collective-permute-done((bf16[128,320]{1,0:T(8,128)(2,1)S(1)}, bf16[128,320]{1,0:T(8,128)(2,1)S(1)}, u32[]{:S(2)}, u32[]{:S(2)}) %collective-permute-start.17) | collective-permute-done | bytes 81952 | tf_op jit(solution)/shard_map/ppermute | solution.py:348
  111.6 0.0 copy-start.10
  111.6 0.7 copy-done.10
  (27 shorter events, 0.2 us)
Async XLA Ops:
  0.0 12.4 %copy-start = (bf16[1,320,320]{2,1,0:T(8,128)(2,1)S(1)}, bf16[1,320,320]{2,1,0:T(8,128)(2,1)}, u32[]{:S(2)}) copy-start(bf16[1,320,320]{2,1,0:T(8,128)(2,1)} %param.13) | copy-start | bytes 614404
  0.0 12.3 %collective-permute-start = (bf16[512,320]{1,0:T(8,128)(2,1)}, bf16[512,320]{1,0:T(8,128)(2,1)S(1)}, u32[]{:S(2)}, u32[]{:S(2)}) collective-permute-start(bf16[512,320]{1,0:T(8,128)(2,1)} %bitcast.24), channel_id=1, source_target_pairs={{0,2},{2,0},{1,3},{3,1},{4,6},{6,4},{5,7},{7,5},{8,10},{10,8},{9,1... | collective-permute-start | bytes 983048 | tf_op jit(solution)/shard_map/ppermute | solution.py:348
  12.3 5.3 %collective-permute-start.1 = (bf16[512,320]{1,0:T(8,128)(2,1)S(1)}, bf16[512,320]{1,0:T(8,128)(2,1)S(1)}, u32[]{:S(2)}, u32[]{:S(2)}) collective-permute-start(bf16[512,320]{1,0:T(8,128)(2,1)S(1)} %collective-permute-done.refs_0_), channel_id=1, source_target_pairs={{0,1},{1,0},{2,3},{3,2},{4,5},{5,4},{6,7},{7,6},{8,9},{9,8},{10,11... | collective-permute-start | bytes 983048 | tf_op jit(solution)/shard_map/ppermute | solution.py:348
  12.6 1.6 %copy-start.1 = (bf16[1,3,3,320,320]{4,3,2,1,0:T(8,128)(2,1)S(1)}, bf16[1,3,3,320,320]{4,3,2,1,0:T(8,128)(2,1)}, u32[]{:S(2)}) copy-start(bf16[1,3,3,320,320]{4,3,2,1,0:T(8,128)(2,1)} %param.11) | copy-start | bytes 5529604
  14.3 1.6 %copy-start.2 = (bf16[1,3,3,320,320]{4,3,2,1,0:T(8,128)(2,1)S(1)}, bf16[1,3,3,320,320]{4,3,2,1,0:T(8,128)(2,1)}, u32[]{:S(2)}) copy-start(bf16[1,3,3,320,320]{4,3,2,1,0:T(8,128)(2,1)} %param.12) | copy-start | bytes 5529604
  15.9 1.1 copy-start.3
  17.5 22.9 %copy-start.4 = (bf16[1,320,2560]{2,1,0:T(8,128)(2,1)S(1)}, bf16[1,320,2560]{2,1,0:T(8,128)(2,1)}, u32[]{:S(2)}) copy-start(bf16[1,320,2560]{2,1,0:T(8,128)(2,1)} %param.16) | copy-start | bytes 4915204
  17.5 22.9 %copy-start.5 = (bf16[1,1280,320]{1,2,0:T(8,128)(2,1)S(1)}, bf16[1,1280,320]{1,2,0:T(8,128)(2,1)}, u32[]{:S(2)}) copy-start(bf16[1,1280,320]{1,2,0:T(8,128)(2,1)} %param.17) | copy-start | bytes 2457604
  17.5 22.9 %copy-start.6 = (bf16[1,320,320]{2,1,0:T(8,128)(2,1)S(1)}, bf16[1,320,320]{2,1,0:T(8,128)(2,1)}, u32[]{:S(2)}) copy-start(bf16[1,320,320]{2,1,0:T(8,128)(2,1)} %param.15) | copy-start | bytes 614404
  28.8 7.7 %collective-permute-start.2 = (bf16[128,320]{1,0:T(8,128)(2,1)S(1)}, bf16[128,320]{1,0:T(8,128)(2,1)S(1)}, u32[]{:S(2)}, u32[]{:S(2)}) collective-permute-start(bf16[128,320]{1,0:T(8,128)(2,1)S(1)} %get-tuple-element.31), channel_id=1, source_target_pairs={{0,4},{4,8},{8,12},{12,0},{1,5},{5,9},{9,13},{13,1},{2,6},{6,10},{... | collective-permute-start | bytes 245768 | tf_op jit(solution)/shard_map/ppermute | solution.py:348
  30.6 9.8 %collective-permute-start.3 = (bf16[128,320]{1,0:T(8,128)(2,1)S(1)}, bf16[128,320]{1,0:T(8,128)(2,1)S(1)}, u32[]{:S(2)}, u32[]{:S(2)}) collective-permute-start(bf16[128,320]{1,0:T(8,128)(2,1)S(1)} %get-tuple-element.32), channel_id=1, source_target_pairs={{0,8},{4,12},{8,0},{12,4},{1,9},{5,13},{9,1},{13,5},{2,10},{6,14},... | collective-permute-start | bytes 245768 | tf_op jit(solution)/shard_map/ppermute | solution.py:348
  33.2 7.2 %collective-permute-start.4 = (bf16[128,320]{1,0:T(8,128)(2,1)S(1)}, bf16[128,320]{1,0:T(8,128)(2,1)S(1)}, u32[]{:S(2)}, u32[]{:S(2)}) collective-permute-start(bf16[128,320]{1,0:T(8,128)(2,1)S(1)} %get-tuple-element.33), channel_id=1, source_target_pairs={{0,12},{4,0},{8,4},{12,8},{1,13},{5,1},{9,5},{13,9},{2,14},{6,2},{... | collective-permute-start | bytes 245768 | tf_op jit(solution)/shard_map/ppermute | solution.py:348
  48.7 7.9 %collective-permute-start.6 = (bf16[128,320]{1,0:T(8,128)(2,1)S(1)}, bf16[128,320]{1,0:T(8,128)(2,1)S(1)}, u32[]{:S(2)}, u32[]{:S(2)}) collective-permute-start(bf16[128,320]{1,0:T(8,128)(2,1)S(1)} %get-tuple-element.36), channel_id=1, source_target_pairs={{0,14},{2,12},{4,2},{6,0},{8,6},{10,4},{12,10},{14,8},{1,15},{3,13... | collective-permute-start | bytes 245768 | tf_op jit(solution)/shard_map/ppermute | solution.py:348
  53.3 9.5 %collective-permute-start.7 = (bf16[128,320]{1,0:T(8,128)(2,1)S(1)}, bf16[128,320]{1,0:T(8,128)(2,1)S(1)}, u32[]{:S(2)}, u32[]{:S(2)}) collective-permute-start(bf16[128,320]{1,0:T(8,128)(2,1)S(1)} %get-tuple-element.37), channel_id=1, source_target_pairs={{0,10},{2,8},{4,14},{6,12},{8,2},{10,0},{12,6},{14,4},{1,11},{3,9}... | collective-permute-start | bytes 245768 | tf_op jit(solution)/shard_map/ppermute | solution.py:348
  53.7 9.1 %collective-permute-start.8 = (bf16[128,320]{1,0:T(8,128)(2,1)S(1)}, bf16[128,320]{1,0:T(8,128)(2,1)S(1)}, u32[]{:S(2)}, u32[]{:S(2)}) collective-permute-start(bf16[128,320]{1,0:T(8,128)(2,1)S(1)} %get-tuple-element.38), channel_id=1, source_target_pairs={{0,6},{2,4},{4,10},{6,8},{8,14},{10,12},{12,2},{14,0},{1,7},{3,5},... | collective-permute-start | bytes 245768 | tf_op jit(solution)/shard_map/ppermute | solution.py:348
  54.2 9.1 %collective-permute-start.5 = (bf16[128,320]{1,0:T(8,128)(2,1)S(1)}, bf16[128,320]{1,0:T(8,128)(2,1)S(1)}, u32[]{:S(2)}, u32[]{:S(2)}) collective-permute-start(bf16[128,320]{1,0:T(8,128)(2,1)S(1)} %get-tuple-element.35), channel_id=1, source_target_pairs={{0,2},{2,0},{4,6},{6,4},{8,10},{10,8},{12,14},{14,12},{1,3},{3,1},... | collective-permute-start | bytes 245768 | tf_op jit(solution)/shard_map/ppermute | solution.py:348
  56.6 6.8 %collective-permute-start.10 = (bf16[128,320]{1,0:T(8,128)(2,1)S(1)}, bf16[128,320]{1,0:T(8,128)(2,1)S(1)}, u32[]{:S(2)}, u32[]{:S(2)}) collective-permute-start(bf16[128,320]{1,0:T(8,128)(2,1)S(1)} %collective-permute-done.6.refs_1_), channel_id=1, source_target_pairs={{0,1},{1,0},{2,3},{3,2},{4,5},{5,4},{6,7},{7,6},{8,9},{9,8},{10,11... | collective-permute-start | bytes 245768 | tf_op jit(solution)/shard_map/ppermute | solution.py:348
  62.8 1.3 %collective-permute-start.11 = (bf16[128,320]{1,0:T(8,128)(2,1)S(1)}, bf16[128,320]{1,0:T(8,128)(2,1)S(1)}, u32[]{:S(2)}, u32[]{:S(2)}) collective-permute-start(bf16[128,320]{1,0:T(8,128)(2,1)S(1)} %collective-permute-done.7.refs_2_), channel_id=1, source_target_pairs={{0,1},{1,0},{2,3},{3,2},{4,5},{5,4},{6,7},{7,6},{8,9},{9,8},{10,11... | collective-permute-start | bytes 245768 | tf_op jit(solution)/shard_map/ppermute | solution.py:348
  62.8 1.5 %collective-permute-start.12 = (bf16[128,320]{1,0:T(8,128)(2,1)S(1)}, bf16[128,320]{1,0:T(8,128)(2,1)S(1)}, u32[]{:S(2)}, u32[]{:S(2)}) collective-permute-start(bf16[128,320]{1,0:T(8,128)(2,1)S(1)} %collective-permute-done.8.refs_3_), channel_id=1, source_target_pairs={{0,1},{1,0},{2,3},{3,2},{4,5},{5,4},{6,7},{7,6},{8,9},{9,8},{10,11... | collective-permute-start | bytes 245768 | tf_op jit(solution)/shard_map/ppermute | solution.py:348
  63.3 1.3 %collective-permute-start.9 = (bf16[128,320]{1,0:T(8,128)(2,1)S(1)}, bf16[128,320]{1,0:T(8,128)(2,1)S(1)}, u32[]{:S(2)}, u32[]{:S(2)}) collective-permute-start(bf16[128,320]{1,0:T(8,128)(2,1)S(1)} %collective-permute-done.5.refs_0_), channel_id=1, source_target_pairs={{0,1},{1,0},{2,3},{3,2},{4,5},{5,4},{6,7},{7,6},{8,9},{9,8},{10,11... | collective-permute-start | bytes 245768 | tf_op jit(solution)/shard_map/ppermute | solution.py:348
  76.5 0.6 copy-start.8
  77.1 7.9 %collective-permute-start.13 = (bf16[128,320]{1,0:T(8,128)(2,1)}, bf16[128,320]{1,0:T(8,128)(2,1)}, u32[]{:S(2)}, u32[]{:S(2)}) collective-permute-start(bf16[128,320]{1,0:T(8,128)(2,1)} %get-tuple-element.40), channel_id=1, source_target_pairs={{0,4},{4,8},{8,12},{12,0},{1,5},{5,9},{9,13},{13,1},{2,6},{6,10},{... | collective-permute-start | bytes 245768 | tf_op jit(solution)/shard_map/ppermute | solution.py:348
  77.3 11.1 %collective-permute-start.14 = (bf16[128,320]{1,0:T(8,128)(2,1)}, bf16[128,320]{1,0:T(8,128)(2,1)}, u32[]{:S(2)}, u32[]{:S(2)}) collective-permute-start(bf16[128,320]{1,0:T(8,128)(2,1)} %get-tuple-element.41), channel_id=1, source_target_pairs={{0,8},{4,12},{8,0},{12,4},{1,9},{5,13},{9,1},{13,5},{2,10},{6,14},... | collective-permute-start | bytes 245768 | tf_op jit(solution)/shard_map/ppermute | solution.py:348
  79.6 8.7 %collective-permute-start.15 = (bf16[128,320]{1,0:T(8,128)(2,1)S(1)}, bf16[128,320]{1,0:T(8,128)(2,1)}, u32[]{:S(2)}, u32[]{:S(2)}) collective-permute-start(bf16[128,320]{1,0:T(8,128)(2,1)S(1)} %get-tuple-element.42), channel_id=1, source_target_pairs={{0,12},{4,0},{8,4},{12,8},{1,13},{5,1},{9,5},{13,9},{2,14},{6,2},{... | collective-permute-start | bytes 245768 | tf_op jit(solution)/shard_map/ppermute | solution.py:348
  88.4 0.9 copy-start.7
  89.3 0.9 copy-start.9
  99.4 5.8 %collective-permute-start.16 = (bf16[128,320]{1,0:T(8,128)(2,1)S(1)}, bf16[128,320]{1,0:T(8,128)(2,1)S(1)}, u32[]{:S(2)}, u32[]{:S(2)}) collective-permute-start(bf16[128,320]{1,0:T(8,128)(2,1)S(1)} %get-tuple-element.44), channel_id=1, source_target_pairs={{0,12},{4,0},{8,4},{12,8},{1,13},{5,1},{9,5},{13,9},{2,14},{6,2},{... | collective-permute-start | bytes 245768 | tf_op jit(solution)/shard_map/ppermute | solution.py:348
  102.0 9.5 %collective-permute-start.17 = (bf16[128,320]{1,0:T(8,128)(2,1)S(1)}, bf16[128,320]{1,0:T(8,128)(2,1)S(1)}, u32[]{:S(2)}, u32[]{:S(2)}) collective-permute-start(bf16[128,320]{1,0:T(8,128)(2,1)S(1)} %get-tuple-element.45), channel_id=1, source_target_pairs={{0,8},{4,12},{8,0},{12,4},{1,9},{5,13},{9,1},{13,5},{2,10},{6,14},... | collective-permute-start | bytes 245768 | tf_op jit(solution)/shard_map/ppermute | solution.py:348
  102.6 8.9 %collective-permute-start.18 = (bf16[128,320]{1,0:T(8,128)(2,1)S(1)}, bf16[128,320]{1,0:T(8,128)(2,1)S(1)}, u32[]{:S(2)}, u32[]{:S(2)}) collective-permute-start(bf16[128,320]{1,0:T(8,128)(2,1)S(1)} %get-tuple-element.46), channel_id=1, source_target_pairs={{0,4},{4,8},{8,12},{12,0},{1,5},{5,9},{9,13},{13,1},{2,6},{6,10},{... | collective-permute-start | bytes 245768 | tf_op jit(solution)/shard_map/ppermute | solution.py:348
  111.6 0.7 copy-start.10
where the time goes:
time: 113 us; the launch traced here: 112 us
  Pallas kernels  41 us (36%)
  waiting for transfers between devices  39 us (35%)
  starting transfers between devices  23.5 us (21%)
  local copies, waits for them, and re-layouts  7.69 us (7%)
    ppermute x19, waiting for transfers between devices, send(): return lax.ppermute(block, axes if len(axes) > 1 else axes[0], route)  39 us
    ppermute x19, starting transfers between devices, send(): return lax.ppermute(block, axes if len(axes) > 1 else axes[0], route)  23.5 us
    pallas_call x2, Pallas kernels, spatial(): pl.pallas_call(kernel, out_shape=[jax.ShapeDtypeStruct((tokens // half //...  23.1 us
    pallas_call x2, Pallas kernels, temporal(): pl.pallas_call(functools.partial(temporal_kernel, frames, channels // HEA...  17.5 us
    unnamed x22, local copies, waits for them, and re-layouts  7.56 us
  transfers between devices with their start and end apart: 19, of which 12 were waited for; matrix products, arithmetic and copies ran while one was open for 1% of the time, Pallas kernels for 0%

commit v1 on v0

v1 whole, which is shorter than its diff:
```python
import functools
import math

import jax
import jax.numpy as jnp
from jax import lax
from jax.experimental import pallas as pl
from jax.experimental.pallas import tpu as pltpu
from jax.sharding import PartitionSpec as P

HEAD_DIM = 64
GROUPS = 32
STEPS = 2
LANES = 128
WIDE = 256
F32 = jnp.float32
BF16 = jnp.bfloat16


def round_up(value, unit):
    return -(-value // unit) * unit


def window_sum(values, width, direction):
    lanes = values.shape[1]
    done, result, power, size = 0, None, values, 1
    while True:
        if width & size:
            moved = power
            if done:
                moved = pltpu.roll(power, done if direction > 0 else lanes - done, 1)
            result = moved if result is None else result + moved
            done += size
        if done == width:
            return result
        power = power + pltpu.roll(power, size if direction > 0 else lanes - size, 1)
        size *= 2


def group_scale(total, square, entries, group_width, channels):
    lanes = total.shape[1]
    lane = lax.broadcasted_iota(jnp.int32, (1, lanes), 1)
    last = (lane % group_width == group_width - 1) & (lane < channels)

    def mean(sums):
        sums = window_sum(jnp.broadcast_to(jnp.sum(sums, axis=0, keepdims=True), (8, lanes)), group_width, 1)
        return window_sum(jnp.where(last, sums, 0.0), group_width, -1)[0:1] / entries

    average = mean(total)
    scale = lax.rsqrt(mean(square) - average * average + 1e-05)
    scale = jnp.where(lane < channels, 0.5 * scale, 0.0)
    return scale, -average * scale


def spatial_kernel(rows, half, columns, channels, group_width, step, pieces, shards, *refs):
    own_refs, other_refs = refs[:pieces], refs[pieces : 2 * pieces]
    sources = refs[2 * pieces : 2 * pieces + 2]
    embeds = refs[2 * pieces + 2]
    outs = refs[2 * pieces + 3 : 2 * pieces + 3 + shards]
    field, hidden, middle, edge, pair, kernel1, kernel2, arrived_sems = refs[
        2 * pieces + 3 + shards :
    ]
    loads = [
        pltpu.make_async_copy(source, target, arrived_sems.at[i])
        for i, (source, target) in enumerate(zip(sources, (kernel1, kernel2)))
    ]
    for load in loads:
        load.start()
    embed = embeds[step : step + 1, :]
    lanes = field.shape[1]
    own_rows = rows // half
    part = own_rows * columns // shards
    size = own_rows * columns // pieces
    here = lax.axis_index("halo")
    spot = lax.axis_index("shard")
    own_base = here * (own_rows * columns)
    other_base = (1 - here) * (own_rows * columns)
    zero = jnp.zeros((8, lanes), F32)

    field[:, lanes - LANES :] = jnp.zeros((rows * columns, LANES), F32)
    for base, arrived in ((own_base, own_refs), (other_base, other_refs)):
        for d in range(pieces):
            place = pl.multiple_of(base + lax.rem(spot + d, pieces) * size, size)
            field[pl.ds(place, size), :channels] = arrived[d][...].astype(F32)

    def sum_row(i, carry):
        total, square = carry
        chunk = field[pl.ds(pl.multiple_of(i * columns, columns), columns), :]
        chunk = chunk.reshape(columns // 8, 8, lanes)
        return total + jnp.sum(chunk, axis=0), square + jnp.sum(chunk * chunk, axis=0)

    field_sums = lax.fori_loop(0, rows, sum_row, (zero, zero), unroll=4)

    def activate(source, scale, shift, first, start, stop):
        def body(i, before):
            row = first - 1 + i
            inside = ((row >= 0) & (row < rows)).astype(F32)
            at = pl.multiple_of(jnp.clip(row, 0, rows - 1) * columns, columns)
            u = source[pl.ds(at, columns), :] * (scale * inside) + shift * inside
            g = u + u * jnp.tanh(u)
            to = pl.ds(pl.multiple_of(i * columns, columns), columns)
            rest = g[:, WIDE:]
            middle[to, :] = g[:, :WIDE].astype(BF16)
            edge[to, :] = rest.astype(BF16)
            pair[to, :] = (before + pltpu.roll(rest, LANES // 2, 1)).astype(BF16)
            return rest

        lax.fori_loop(start, stop, body, jnp.zeros((columns, LANES), F32), unroll=4)

    step_rows = min(WIDE, own_rows * columns)
    column = lax.broadcasted_iota(jnp.int32, (step_rows, 1), 0) % columns
    low = lax.broadcasted_iota(jnp.int32, (1, LANES), 1) < channels - WIDE

    def convolve(kernel, start):
        top, mid, bottom = [slice(start + r * columns, start + r * columns + step_rows) for r in range(3)]
        window = jnp.concatenate(
            [middle[top, :], middle[mid, :], middle[bottom, :], pair[mid, :], edge[bottom, :]], axis=1
        )
        y = jnp.dot(window, kernel[...], preferred_element_type=F32)

        def from_left(values):
            return jnp.where(column == 0, 0.0, pltpu.roll(values, 1, 0))

        def from_right(values):
            return jnp.where(column == columns - 1, 0.0, pltpu.roll(values, step_rows - 1, 0))

        wide = y[:, WIDE : 2 * WIDE] + from_left(y[:, :WIDE]) + from_right(y[:, 2 * WIDE : 3 * WIDE])
        tail = y[:, 3 * WIDE : 3 * WIDE + LANES]
        narrow = from_left(tail) + pltpu.roll(tail, LANES // 2, 1) + from_right(y[:, 3 * WIDE + LANES :])
        return wide, narrow

    entries = float(rows * columns * group_width)
    for pad in (0, (rows + 1) * columns):
        middle[pad : pad + columns, :] = jnp.zeros((columns, WIDE), BF16)
        edge[pad : pad + columns, :] = jnp.zeros((columns, LANES), BF16)
    activate(field, *group_scale(*field_sums, entries, group_width, channels), 0, 1, rows + 1)
    loads[0].wait()
    total, square = zero, zero
    for start in range(0, rows * columns, step_rows):
        wide, narrow = convolve(kernel1, start)
        chunk = jnp.concatenate(
            [wide + embed[:, :WIDE], jnp.where(low, narrow + embed[:, WIDE:], 0.0)], axis=1
        )
        hidden[start : start + step_rows, :] = chunk
        chunk = chunk.reshape(step_rows // 8, 8, lanes)
        total = total + jnp.sum(chunk, axis=0)
        square = square + jnp.sum(chunk * chunk, axis=0)
    activate(
        hidden,
        *group_scale(total, square, entries, group_width, channels),
        here * own_rows,
        0,
        own_rows + 2,
    )
    loads[1].wait()
    for start in range(0, own_rows * columns, step_rows):
        wide, narrow = convolve(kernel2, start)
        mine = pl.ds(pl.multiple_of(own_base + start, step_rows), step_rows)
        hidden[mine, :WIDE] = wide + field[mine, :WIDE]
        hidden[mine, WIDE:] = narrow + field[mine, WIDE:]
    for d in range(shards):
        place = pl.multiple_of(own_base + lax.rem(spot + d, shards) * part, part)
        outs[d][...] = hidden[pl.ds(place, part), :channels].astype(BF16)


def spatial(own, other, weights, embeds, step, rows, columns, half, shards):
    pieces = len(own)
    channels = own[0].shape[1]
    lanes = round_up(channels, LANES)
    tokens = rows * columns
    padded = tokens + 2 * columns
    depth = weights[0].shape[0]
    kernel = functools.partial(
        spatial_kernel, rows, half, columns, channels, channels // GROUPS, step, pieces, shards
    )
    vmem = pl.BlockSpec(memory_space=pltpu.VMEM)
    hbm = pl.BlockSpec(memory_space=pltpu.HBM)
    return pl.pallas_call(
        kernel,
        out_shape=[jax.ShapeDtypeStruct((tokens // half // shards, channels), BF16)] * shards,
        in_specs=[vmem] * (2 * pieces) + [hbm] * 2 + [vmem],
        out_specs=[vmem] * shards,
        scratch_shapes=[
            pltpu.VMEM((tokens, lanes), F32),
            pltpu.VMEM((tokens, lanes), F32),
            pltpu.VMEM((padded, WIDE), BF16),
            pltpu.VMEM((padded, LANES), BF16),
            pltpu.VMEM((padded, LANES), BF16),
            *[pltpu.VMEM(w.shape, BF16) for w in weights],
            pltpu.SemaphoreType.DMA((2,)),
        ],
        compiler_params=pltpu.CompilerParams(vmem_limit_bytes=40 * 1024 * 1024),
        cost_estimate=pl.CostEstimate(
            flops=3 * tokens * depth * depth,
            bytes_accessed=6000000,
            transcendentals=tokens * lanes,
        ),
        name="spatial",
    )(*own, *other, *weights, embeds)


def prepare_kernel(channels, *refs):
    sources, targets, buffers = refs[:3], refs[3:6], refs[6:12]
    arrived_sems, left_sems = refs[12:]
    loads = [
        pltpu.make_async_copy(source, buffer, arrived_sems.at[i])
        for i, (source, buffer) in enumerate(zip(sources, buffers[:3]))
    ]
    stores = [
        pltpu.make_async_copy(buffer, target, left_sems.at[i])
        for i, (buffer, target) in enumerate(zip(buffers[3:], targets))
    ]
    for load in loads:
        load.start()
    spare = channels - WIDE
    for i in range(2):
        kernel, packed = buffers[i], buffers[3 + i]
        depth = packed.shape[0]
        packed[3 * channels :, :] = jnp.zeros((depth - 3 * channels, depth), BF16)
        loads[i].wait()
        for r in range(3):
            for source, target in (
                (slice(0, WIDE), slice(r * WIDE, (r + 1) * WIDE)),
                (slice(WIDE, channels), slice(3 * WIDE + r * spare, 3 * WIDE + (r + 1) * spare)),
            ):
                for s in range(3):
                    packed[target, s * WIDE : (s + 1) * WIDE] = kernel[r, s, source, :WIDE]
                first, second, third = [kernel[r, s, source, WIDE:] for s in range(3)]
                packed[target, 3 * WIDE : 3 * WIDE + LANES] = jnp.concatenate([first, second], axis=1)
                packed[target, 3 * WIDE + LANES :] = jnp.concatenate(
                    [third, jnp.zeros_like(third)], axis=1
                )
        stores[i].start()
    qkv, padded = buffers[2], buffers[5]
    lanes = padded.shape[1] // 3
    padded[...] = jnp.zeros(padded.shape, BF16)
    loads[2].wait()
    for i in range(3):
        padded[:, i * lanes : i * lanes + channels] = qkv[:, i * channels : (i + 1) * channels]
    stores[2].start()
    for store in stores:
        store.wait()


def prepare(conv_first, conv_second, qkv):
    channels = qkv.shape[0]
    depth = round_up(3 * channels, WIDE)
    lanes = round_up(channels, LANES)
    hbm = pl.BlockSpec(memory_space=pltpu.HBM)
    sources = (conv_first, conv_second, qkv)
    shapes = [(depth, depth), (depth, depth), (channels, 3 * lanes)]
    *packed, padded = pl.pallas_call(
        functools.partial(prepare_kernel, channels),
        out_shape=[jax.ShapeDtypeStruct(shape, BF16) for shape in shapes],
        in_specs=[hbm] * 3,
        out_specs=[hbm] * 3,
        scratch_shapes=[
            *[pltpu.VMEM(source.shape, BF16) for source in sources],
            *[pltpu.VMEM(shape, BF16) for shape in shapes],
            pltpu.SemaphoreType.DMA((3,)),
            pltpu.SemaphoreType.DMA((3,)),
        ],
        compiler_params=pltpu.CompilerParams(vmem_limit_bytes=40 * 1024 * 1024),
        cost_estimate=pl.CostEstimate(flops=0, bytes_accessed=10000000, transcendentals=0),
        name="prepare",
    )(*sources)
    return packed, padded


def norm_rows(values):
    average = jnp.mean(values, axis=-1, keepdims=True)
    centred = values - average
    spread = jnp.mean(centred * centred, axis=-1, keepdims=True)
    return (centred * lax.rsqrt(spread + 1e-05)).astype(BF16)


def temporal_kernel(frames, *refs):
    parts = refs[:frames]
    weights = refs[frames : frames + 4]
    outs = refs[frames + 4 : 2 * frames + 4]
    stream, projected, mixed, active = refs[2 * frames + 4 : 2 * frames + 8]
    qkv, attn_out, geglu_in, geglu_out, arrived_sems = refs[2 * frames + 8 :]
    loads = [
        pltpu.make_async_copy(source, target, arrived_sems.at[i])
        for i, (source, target) in enumerate(zip(weights, (qkv, attn_out, geglu_in, geglu_out)))
    ]
    loads[0].start()
    pixels, channels = parts[0].shape
    lanes = projected.shape[1] // 3
    inner = geglu_out.shape[1]

    for f in range(frames):
        stream[f * pixels : (f + 1) * pixels, :] = parts[f][...]
    normed = norm_rows(stream[...].astype(F32))
    loads[0].wait()
    for load in loads[1:]:
        load.start()
    projected[...] = jnp.dot(normed, qkv[...], preferred_element_type=F32).astype(BF16)

    pack = min(pixels, WIDE // frames)
    tile = frames * pack
    same = (
        lax.broadcasted_iota(jnp.int32, (tile, tile), 0) % pack
        == lax.broadcasted_iota(jnp.int32, (tile, tile), 1) % pack
    )
    lane = lax.broadcasted_iota(jnp.int32, (1, LANES), 1)
    sharing = LANES // HEAD_DIM
    for first in range(0, pixels, pack):
        places = [slice(f * pixels + first, f * pixels + first + pack) for f in range(frames)]
        for at in range(0, channels, LANES):
            query, key, value = [
                jnp.concatenate([projected[p, i * lanes + at : i * lanes + at + LANES] for p in places])
                for i in range(3)
            ]
            mix = None
            for j in range(min(sharing, (channels - at) // HEAD_DIM)):
                chosen = (lane >= j * HEAD_DIM) & (lane < (j + 1) * HEAD_DIM)
                scores = lax.dot_general(
                    query * chosen.astype(BF16),
                    key,
                    (((1,), (1,)), ((), ())),
                    preferred_element_type=F32,
                )
                scores = jnp.where(same, scores, float(jnp.finfo(F32).min))
                top = jnp.max(scores, axis=1, keepdims=True)
                powers = jnp.exp((scores - top) * HEAD_DIM ** (-0.5))
                total = jnp.sum(powers, axis=1, keepdims=True)
                weights = (powers * (1.0 / total)).astype(BF16)
                head = jnp.dot(weights, value, preferred_element_type=F32)
                mix = head if mix is None else jnp.where(chosen, head, mix)
            mix = mix.astype(BF16)
            for f, p in enumerate(places):
                mixed[p, at : at + LANES] = mix[f * pack : (f + 1) * pack]

    loads[1].wait()
    update = jnp.dot(mixed[:, :channels], attn_out[...], preferred_element_type=F32)
    stream[...] = (stream[...].astype(F32) + update).astype(BF16)
    normed = norm_rows(stream[...].astype(F32))
    loads[2].wait()
    for at in range(0, inner, WIDE):
        value = jnp.dot(normed, geglu_in[:, at : at + WIDE], preferred_element_type=F32)
        gate = jnp.dot(normed, geglu_in[:, inner + at : inner + at + WIDE], preferred_element_type=F32)
        act = value * (0.5 * gate) * (1.0 + lax.erf(gate * math.sqrt(0.5)))
        active[:, at : at + WIDE] = act.astype(BF16)
    loads[3].wait()
    update = lax.dot_general(
        active[...], geglu_out[...], (((1,), (1,)), ((), ())), preferred_element_type=F32
    )
    update = (stream[...].astype(F32) + update).astype(BF16)
    for f in range(frames):
        outs[f][...] = update[f * pixels : (f + 1) * pixels, :]


def temporal(parts, weights):
    frames = len(parts)
    pixels, channels = parts[0].shape
    lanes = round_up(channels, LANES)
    tokens = frames * pixels
    inner = weights[3].shape[1]
    vmem = pl.BlockSpec(memory_space=pltpu.VMEM)
    hbm = pl.BlockSpec(memory_space=pltpu.HBM)
    flops = 2 * tokens * channels * (3 * lanes + channels + 3 * inner)
    return pl.pallas_call(
        functools.partial(temporal_kernel, frames),
        out_shape=[jax.ShapeDtypeStruct((pixels, channels), BF16)] * frames,
        in_specs=[vmem] * frames + [hbm] * 4,
        out_specs=[vmem] * frames,
        scratch_shapes=[
            pltpu.VMEM((tokens, channels), BF16),
            pltpu.VMEM((tokens, 3 * lanes), BF16),
            pltpu.VMEM((tokens, lanes), BF16),
            pltpu.VMEM((tokens, inner), BF16),
            *[pltpu.VMEM(w.shape, BF16) for w in weights],
            pltpu.SemaphoreType.DMA((4,)),
        ],
        compiler_params=pltpu.CompilerParams(vmem_limit_bytes=40 * 1024 * 1024),
        cost_estimate=pl.CostEstimate(
            flops=flops, bytes_accessed=4000000, transcendentals=tokens * inner
        ),
        name="temporal",
    )(*parts, *weights)


def send(block, hops):
    axes = tuple(axis for axis, _ in hops)
    sizes = [lax.axis_size(axis) for axis in axes]
    route = []
    for source in range(math.prod(sizes)):
        rest, target, stride = source, 0, 1
        for size, (_, distance) in zip(reversed(sizes), reversed(hops)):
            target += (rest % size + distance) % size * stride
            rest, stride = rest // size, stride * size
        route.append((source, target))
    if all(a == b for a, b in route):
        return block
    return lax.ppermute(block, axes if len(axes) > 1 else axes[0], route)


def embed_time(stamps, time_weight):
    half_width = time_weight.shape[0] // 2
    frequency = jnp.exp(-math.log(10000.0) * jnp.arange(half_width, dtype=F32) / half_width)
    angles = stamps.astype(F32)[:, None] * frequency[None, :]
    sinusoid = jnp.concatenate([jnp.cos(angles), jnp.sin(angles)], axis=1)
    out = jnp.dot(jax.nn.silu(sinusoid).astype(BF16), time_weight, preferred_element_type=F32)
    return jnp.pad(out, ((0, 0), (0, round_up(out.shape[1], LANES) - out.shape[1])))


def per_device(
    features,
    timesteps,
    conv_first,
    conv_second,
    time_weight,
    qkv_weight,
    attn_out,
    geglu_in,
    geglu_out,
):
    _, _, own_rows, columns, channels = features.shape
    half = lax.axis_size("halo")
    rows = own_rows * half
    shards = lax.axis_size("shard")
    spot = lax.axis_index("shard")
    part = own_rows * columns // shards

    moved = send(features.reshape(own_rows * columns, channels), (("section", 1),))
    embeds = embed_time(timesteps[0], time_weight[0])
    spatial_weights, padded = prepare(conv_first[0], conv_second[0], qkv_weight[0])

    moved, spatial_weights, padded = lax.optimization_barrier((moved, spatial_weights, padded))
    temporal_weights = (padded, attn_out[0], geglu_in[0], geglu_out[0].T)
    own, other = [moved], [send(moved, (("halo", 1),))]
    for denoise_step in range(STEPS):
        parts = spatial(
            own, other, spatial_weights, embeds, denoise_step, rows, columns, half, shards
        )
        parts = [send(parts[d], (("shard", d),)) for d in range(shards)]
        parts = temporal(parts, temporal_weights)
        if denoise_step < STEPS - 1:
            own = [send(parts[d], (("shard", -d), ("section", 1))) for d in range(shards)]
            other = [send(block, (("halo", 1),)) for block in own]
        else:
            own = [send(parts[d], (("shard", -d),)) for d in range(shards)]
    result = jnp.zeros((own_rows * columns, channels), BF16)
    for d in range(shards):
        result = lax.dynamic_update_slice_in_dim(
            result, own[d], lax.rem(spot + d, shards) * part, axis=0
        )
    return result.reshape(features.shape)


def solution(mesh):
    return jax.shard_map(
        per_device,
        mesh=mesh,
        in_specs=(
            P(("groups", "section"), "shard", "halo", None, None),
            P(("groups", "section"), None),
            P("section", None, None, None, None),
            P("section", None, None, None, None),
            P("section", None, None),
            P("section", None, None),
            P("section", None, None),
            P("section", None, None),
            P("section", None, None),
        ),
        out_specs=P(("groups", "section"), "shard", "halo", None, None),
        check_vma=False,
    )
```

time: 113 us -> 96.4 us (0.85)
  Pallas kernels: 41 us -> 30.6 us
  waiting for transfers between devices: 39 us -> 33.5 us
    pallas_call x2, Pallas kernels: 23.1 us -> 14 us  [spatial(): pl.pallas_call(kernel, out_shape=[jax.ShapeDtypeStruct((tokens // half //...]
    ppermute x19, waiting for transfers between devices: 39 us -> 33.5 us  [send(): return lax.ppermute(block, axes if len(axes) > 1 else axes[0], route)]
    pallas_call x3, Pallas kernels: 18 us -> 16.5 us  [the longest x2 14.1 us: temporal(): pl.pallas_call(functools.partial(temporal_kernel, frames), out_shape=[jax...]
    unnamed x22 -> x24, local copies, waits for them, and re-layouts: 7.56 us -> 7.57 us
  transfers between devices with their start and end apart: 19 -> 19, of which waited for: 12 -> 13; matrix products, arithmetic and copies ran while one was open for 1% -> 0% of each run, Pallas kernels for 0% -> 3%
where the time goes in v1:
time: 96.4 us; the launch traced here: 96.1 us
  waiting for transfers between devices  33.5 us (35%)
  Pallas kernels  30.6 us (32%)
  starting transfers between devices  23.7 us (25%)
  local copies, waits for them, and re-layouts  7.7 us (8%)
    ppermute x19, waiting for transfers between devices, send(): return lax.ppermute(block, axes if len(axes) > 1 else axes[0], route)  33.5 us
    ppermute x19, starting transfers between devices, send(): return lax.ppermute(block, axes if len(axes) > 1 else axes[0], route)  23.7 us
    pallas_call x2, Pallas kernels, temporal(): pl.pallas_call(functools.partial(temporal_kernel, frames), out_shape=[jax...  14.1 us
    pallas_call x2, Pallas kernels, spatial(): pl.pallas_call(kernel, out_shape=[jax.ShapeDtypeStruct((tokens // half //...  14 us
    unnamed x24, local copies, waits for them, and re-layouts  7.57 us
    pallas_call x1, Pallas kernels, prepare(): pl.pallas_call(functools.partial(prepare_kernel, channels), out_shape=[ja...  2.42 us
  transfers between devices with their start and end apart: 19, of which 13 were waited for; matrix products, arithmetic and copies ran while one was open for 0% of the time, Pallas kernels for 3%

profile of v1, /device:TPU:0, one launch (start us, length us, event | category | flops | bytes accessed | tf_op | source)
XLA Modules:
  0.0 96.1 jit_solution(8603208196195657676)
XLA Ops:
  0.0 2.9 %collective-permute-start = (bf16[512,320]{1,0:T(8,128)(2,1)}, bf16[512,320]{1,0:T(8,128)(2,1)S(1)}, u32[]{:S(2)}, u32[]{:S(2)}) collective-permute-start(bf16[512,320]{1,0:T(8,128)(2,1)} %bitcast.24), channel_id=1, source_target_pairs={{0,2},{2,0},{1,3},{3,1},{4,6},{6,4},{5,7},{7,5},{8,10},{10,8},{9,1... | collective-permute-start | bytes 983048 | tf_op jit(solution)/shard_map/ppermute | solution.py:396
  2.9 1.6 %copy-done.1 = bf16[1,3,3,320,320]{4,3,2,1,0:T(8,128)(2,1)S(1)} copy-done((bf16[1,3,3,320,320]{4,3,2,1,0:T(8,128)(2,1)S(1)}, bf16[1,3,3,320,320]{4,3,2,1,0:T(8,128)(2,1)}, u32[]{:S(2)}) %copy-start.1) | copy-done | bytes 1843224
  4.6 1.6 %copy-done.2 = bf16[1,3,3,320,320]{4,3,2,1,0:T(8,128)(2,1)S(1)} copy-done((bf16[1,3,3,320,320]{4,3,2,1,0:T(8,128)(2,1)S(1)}, bf16[1,3,3,320,320]{4,3,2,1,0:T(8,128)(2,1)}, u32[]{:S(2)}) %copy-start.2) | copy-done | bytes 1843224
  6.2 1.1 %copy-done.3 = bf16[1,320,960]{2,1,0:T(8,128)(2,1)S(1)} copy-done((bf16[1,320,960]{2,1,0:T(8,128)(2,1)S(1)}, bf16[1,320,960]{2,1,0:T(8,128)(2,1)}, u32[]{:S(2)}) %copy-start.3) | copy-done | bytes 614424
  7.3 2.4 %prepare.1 = (bf16[1024,1024]{1,0:T(8,128)(2,1)S(1)}, bf16[1024,1024]{1,0:T(8,128)(2,1)S(1)}, bf16[320,1152]{1,0:T(8,128)(2,1)S(1)}) custom-call(bf16[3,3,320,320]{3,2,1,0:T(8,128)(2,1)S(1)} %bitcast.15, bf16[3,3,320,320]{3,2,1,0:T(8,128)(2,1)S(1)} %bitcast.16, bf16[320,960]{1,0:T(8,128)(2,1)S(1)} %bitcast.17), custom_call_target="tpu_custom_call" | custom-call | bytes 10000000 | tf_op jit(solution)/shard_map/prepare/pallas_call | solution.py:252
  9.7 2.5 %collective-permute-done.refs_0_ = bf16[512,320]{1,0:T(8,128)(2,1)S(1)} collective-permute-done((bf16[512,320]{1,0:T(8,128)(2,1)}, bf16[512,320]{1,0:T(8,128)(2,1)S(1)}, u32[]{:S(2)}, u32[]{:S(2)}) %collective-permute-start) | collective-permute-done | bytes 327712 | tf_op jit(solution)/shard_map/ppermute | solution.py:396
  12.3 0.0 collective-permute-start.1
  12.3 0.1 multiply_cosine_fusion
  12.4 0.2 fusion
  12.6 0.0 copy-start.4
  12.6 0.0 copy-start.5
  12.6 0.0 copy-start.6
  12.7 1.3 %collective-permute-done.1.refs_1_ = bf16[512,320]{1,0:T(8,128)(2,1)S(1)} collective-permute-done((bf16[512,320]{1,0:T(8,128)(2,1)S(1)}, bf16[512,320]{1,0:T(8,128)(2,1)S(1)}, u32[]{:S(2)}, u32[]{:S(2)}) %collective-permute-start.1) | collective-permute-done | bytes 327712 | tf_op jit(solution)/shard_map/ppermute | solution.py:396
  14.0 6.7 %spatial.2 = (bf16[128,320]{1,0:T(8,128)(2,1)S(1)}, bf16[128,320]{1,0:T(8,128)(2,1)S(1)}, bf16[128,320]{1,0:T(8,128)(2,1)S(1)}, bf16[128,320]{1,0:T(8,128)(2,1)S(1)}) custom-call(bf16[512,320]{1,0:T(8,128)(2,1)S(1)} %collective-permute-done.refs_0_, bf16[512,320]{1,0:T(8,128)(2,1)S(1)} %collective-permute-done.1.refs_1_, ...), custom_call_target="tpu_custom_call" | custom-call | flops 3221225472 | bytes 6000000 | tf_op jit(solution)/shard_map/spatial/pallas_call | solution.py:178
  20.7 1.9 %collective-permute-start.2 = (bf16[128,320]{1,0:T(8,128)(2,1)S(1)}, bf16[128,320]{1,0:T(8,128)(2,1)S(1)}, u32[]{:S(2)}, u32[]{:S(2)}) collective-permute-start(bf16[128,320]{1,0:T(8,128)(2,1)S(1)} %get-tuple-element.35), channel_id=1, source_target_pairs={{0,4},{4,8},{8,12},{12,0},{1,5},{5,9},{9,13},{13,1},{2,6},{6,10},{... | collective-permute-start | bytes 245768 | tf_op jit(solution)/shard_map/ppermute | solution.py:396
  22.6 2.6 %collective-permute-start.3 = (bf16[128,320]{1,0:T(8,128)(2,1)S(1)}, bf16[128,320]{1,0:T(8,128)(2,1)S(1)}, u32[]{:S(2)}, u32[]{:S(2)}) collective-permute-start(bf16[128,320]{1,0:T(8,128)(2,1)S(1)} %get-tuple-element.36), channel_id=1, source_target_pairs={{0,8},{4,12},{8,0},{12,4},{1,9},{5,13},{9,1},{13,5},{2,10},{6,14},... | collective-permute-start | bytes 245768 | tf_op jit(solution)/shard_map/ppermute | solution.py:396
  25.2 1.3 %collective-permute-start.4 = (bf16[128,320]{1,0:T(8,128)(2,1)S(1)}, bf16[128,320]{1,0:T(8,128)(2,1)S(1)}, u32[]{:S(2)}, u32[]{:S(2)}) collective-permute-start(bf16[128,320]{1,0:T(8,128)(2,1)S(1)} %get-tuple-element.37), channel_id=1, source_target_pairs={{0,12},{4,0},{8,4},{12,8},{1,13},{5,1},{9,5},{13,9},{2,14},{6,2},{... | collective-permute-start | bytes 245768 | tf_op jit(solution)/shard_map/ppermute | solution.py:396
  26.5 1.8 %collective-permute-done.2.refs_1_ = bf16[128,320]{1,0:T(8,128)(2,1)S(1)} collective-permute-done((bf16[128,320]{1,0:T(8,128)(2,1)S(1)}, bf16[128,320]{1,0:T(8,128)(2,1)S(1)}, u32[]{:S(2)}, u32[]{:S(2)}) %collective-permute-start.2) | collective-permute-done | bytes 81952 | tf_op jit(solution)/shard_map/ppermute | solution.py:396
  28.3 3.7 %collective-permute-done.3.refs_2_ = bf16[128,320]{1,0:T(8,128)(2,1)S(1)} collective-permute-done((bf16[128,320]{1,0:T(8,128)(2,1)S(1)}, bf16[128,320]{1,0:T(8,128)(2,1)S(1)}, u32[]{:S(2)}, u32[]{:S(2)}) %collective-permute-start.3) | collective-permute-done | bytes 81952 | tf_op jit(solution)/shard_map/ppermute | solution.py:396
  32.0 6.6 %temporal.2 = (bf16[128,320]{1,0:T(8,128)(2,1)S(1)}, bf16[128,320]{1,0:T(8,128)(2,1)S(1)}, bf16[128,320]{1,0:T(8,128)(2,1)S(1)}, bf16[128,320]{1,0:T(8,128)(2,1)S(1)}) custom-call(bf16[128,320]{1,0:T(8,128)(2,1)S(1)} %get-tuple-element.34.refs_0_, bf16[128,320]{1,0:T(8,128)(2,1)S(1)} %collective-permute-done.2.refs_1_, ...), custom_call_target="tpu_custom_call" | custom-call | flops 1740636160 | bytes 4000000 | tf_op jit(solution)/shard_map/temporal/pallas_call | solution.py:363
  38.6 4.6 %collective-permute-start.6 = (bf16[128,320]{1,0:T(8,128)(2,1)S(1)}, bf16[128,320]{1,0:T(8,128)(2,1)S(1)}, u32[]{:S(2)}, u32[]{:S(2)}) collective-permute-start(bf16[128,320]{1,0:T(8,128)(2,1)S(1)} %get-tuple-element.40), channel_id=1, source_target_pairs={{0,14},{2,12},{4,2},{6,0},{8,6},{10,4},{12,10},{14,8},{1,15},{3,13... | collective-permute-start | bytes 245768 | tf_op jit(solution)/shard_map/ppermute | solution.py:396
  43.2 0.4 collective-permute-start.7
  43.6 0.5 collective-permute-start.8
  44.1 1.2 %collective-permute-start.5 = (bf16[128,320]{1,0:T(8,128)(2,1)S(1)}, bf16[128,320]{1,0:T(8,128)(2,1)S(1)}, u32[]{:S(2)}, u32[]{:S(2)}) collective-permute-start(bf16[128,320]{1,0:T(8,128)(2,1)S(1)} %get-tuple-element.39), channel_id=1, source_target_pairs={{0,2},{2,0},{4,6},{6,4},{8,10},{10,8},{12,14},{14,12},{1,3},{3,1},... | collective-permute-start | bytes 245768 | tf_op jit(solution)/shard_map/ppermute | solution.py:396
  45.3 1.1 %collective-permute-done.6.refs_1_ = bf16[128,320]{1,0:T(8,128)(2,1)S(1)} collective-permute-done((bf16[128,320]{1,0:T(8,128)(2,1)S(1)}, bf16[128,320]{1,0:T(8,128)(2,1)S(1)}, u32[]{:S(2)}, u32[]{:S(2)}) %collective-permute-start.6) | collective-permute-done | bytes 81952 | tf_op jit(solution)/shard_map/ppermute | solution.py:396
  46.5 6.2 %collective-permute-done.7.refs_2_ = bf16[128,320]{1,0:T(8,128)(2,1)S(1)} collective-permute-done((bf16[128,320]{1,0:T(8,128)(2,1)S(1)}, bf16[128,320]{1,0:T(8,128)(2,1)S(1)}, u32[]{:S(2)}, u32[]{:S(2)}) %collective-permute-start.7) | collective-permute-done | bytes 81952 | tf_op jit(solution)/shard_map/ppermute | solution.py:396
  52.7 0.5 collective-permute-start.12
  53.2 0.1 collective-permute-start.9
  53.2 0.7 collective-permute-done.11.refs_6_
  53.9 0.2 collective-permute-done.12.refs_7_
  54.1 0.4 collective-permute-done.9.refs_4_
  54.5 7.4 %spatial.3 = (bf16[128,320]{1,0:T(8,128)(2,1)S(1)}, bf16[128,320]{1,0:T(8,128)(2,1)}, bf16[128,320]{1,0:T(8,128)(2,1)}, bf16[128,320]{1,0:T(8,128)(2,1)S(1)}) custom-call(bf16[128,320]{1,0:T(8,128)(2,1)S(1)} %collective-permute-done.5.refs_0_, bf16[128,320]{1,0:T(8,128)(2,1)S(1)} %collective-permute-done.6.refs_1_, ...), custom_call_target="tpu_custom_call" | custom-call | flops 3221225472 | bytes 6000000 | tf_op jit(solution)/shard_map/spatial/pallas_call | solution.py:178
  61.8 0.6 copy-done.8
  62.5 0.0 collective-permute-start.13
  62.5 2.5 %collective-permute-start.14 = (bf16[128,320]{1,0:T(8,128)(2,1)}, bf16[128,320]{1,0:T(8,128)(2,1)}, u32[]{:S(2)}, u32[]{:S(2)}) collective-permute-start(bf16[128,320]{1,0:T(8,128)(2,1)} %get-tuple-element.45), channel_id=1, source_target_pairs={{0,8},{4,12},{8,0},{12,4},{1,9},{5,13},{9,1},{13,5},{2,10},{6,14},... | collective-permute-start | bytes 245768 | tf_op jit(solution)/shard_map/ppermute | solution.py:396
  65.1 1.6 %collective-permute-start.15 = (bf16[128,320]{1,0:T(8,128)(2,1)S(1)}, bf16[128,320]{1,0:T(8,128)(2,1)}, u32[]{:S(2)}, u32[]{:S(2)}) collective-permute-start(bf16[128,320]{1,0:T(8,128)(2,1)S(1)} %get-tuple-element.46), channel_id=1, source_target_pairs={{0,12},{4,0},{8,4},{12,8},{1,13},{5,1},{9,5},{13,9},{2,14},{6,2},{... | collective-permute-start | bytes 245768 | tf_op jit(solution)/shard_map/ppermute | solution.py:396
  66.7 3.6 %collective-permute-done.13.refs_1_ = bf16[128,320]{1,0:T(8,128)(2,1)} collective-permute-done((bf16[128,320]{1,0:T(8,128)(2,1)}, bf16[128,320]{1,0:T(8,128)(2,1)}, u32[]{:S(2)}, u32[]{:S(2)}) %collective-permute-start.13) | collective-permute-done | bytes 81952 | tf_op jit(solution)/shard_map/ppermute | solution.py:396
  70.3 3.3 %collective-permute-done.14.refs_2_ = bf16[128,320]{1,0:T(8,128)(2,1)} collective-permute-done((bf16[128,320]{1,0:T(8,128)(2,1)}, bf16[128,320]{1,0:T(8,128)(2,1)}, u32[]{:S(2)}, u32[]{:S(2)}) %collective-permute-start.14) | collective-permute-done | bytes 81952 | tf_op jit(solution)/shard_map/ppermute | solution.py:396
  73.6 0.9 copy-done.7
  74.5 0.9 copy-done.9
  75.4 7.5 %temporal.3 = (bf16[128,320]{1,0:T(8,128)(2,1)S(1)}, bf16[128,320]{1,0:T(8,128)(2,1)S(1)}, bf16[128,320]{1,0:T(8,128)(2,1)S(1)}, bf16[128,320]{1,0:T(8,128)(2,1)S(1)}) custom-call(bf16[128,320]{1,0:T(8,128)(2,1)S(1)} %copy-done.9, bf16[128,320]{1,0:T(8,128)(2,1)} %collective-permute-done.13.refs_1_, bf16[128,320]{1,0:T(8,128)(2,1)} %collective-permute-done.14.refs_2_, ...), custom_call_target="tpu_custom_call" | custom-call | flops 1740636160 | bytes 4000000 | tf_op jit(solution)/shard_map/temporal/pallas_call | solution.py:363
  83.0 2.8 %collective-permute-start.16 = (bf16[128,320]{1,0:T(8,128)(2,1)S(1)}, bf16[128,320]{1,0:T(8,128)(2,1)S(1)}, u32[]{:S(2)}, u32[]{:S(2)}) collective-permute-start(bf16[128,320]{1,0:T(8,128)(2,1)S(1)} %get-tuple-element.48), channel_id=1, source_target_pairs={{0,12},{4,0},{8,4},{12,8},{1,13},{5,1},{9,5},{13,9},{2,14},{6,2},{... | collective-permute-start | bytes 245768 | tf_op jit(solution)/shard_map/ppermute | solution.py:396
  85.8 0.6 collective-permute-start.17
  86.3 0.1 collective-permute-start.18
  86.5 2.5 %collective-permute-done.16 = bf16[128,320]{1,0:T(8,128)(2,1)S(1)} collective-permute-done((bf16[128,320]{1,0:T(8,128)(2,1)S(1)}, bf16[128,320]{1,0:T(8,128)(2,1)S(1)}, u32[]{:S(2)}, u32[]{:S(2)}) %collective-permute-start.16) | collective-permute-done | bytes 81952 | tf_op jit(solution)/shard_map/ppermute | solution.py:396
  89.0 6.3 %collective-permute-done.17 = bf16[128,320]{1,0:T(8,128)(2,1)S(1)} collective-permute-done((bf16[128,320]{1,0:T(8,128)(2,1)S(1)}, bf16[128,320]{1,0:T(8,128)(2,1)S(1)}, u32[]{:S(2)}, u32[]{:S(2)}) %collective-permute-start.17) | collective-permute-done | bytes 81952 | tf_op jit(solution)/shard_map/ppermute | solution.py:396
  95.3 0.0 copy-start.10
  95.3 0.7 copy-done.10
  (29 shorter events, 0.2 us)
Async XLA Ops:
  0.0 12.4 %copy-start = (bf16[1,320,320]{2,1,0:T(8,128)(2,1)S(1)}, bf16[1,320,320]{2,1,0:T(8,128)(2,1)}, u32[]{:S(2)}) copy-start(bf16[1,320,320]{2,1,0:T(8,128)(2,1)} %param.13) | copy-start | bytes 614404
  0.0 12.3 %collective-permute-start = (bf16[512,320]{1,0:T(8,128)(2,1)}, bf16[512,320]{1,0:T(8,128)(2,1)S(1)}, u32[]{:S(2)}, u32[]{:S(2)}) collective-permute-start(bf16[512,320]{1,0:T(8,128)(2,1)} %bitcast.24), channel_id=1, source_target_pairs={{0,2},{2,0},{1,3},{3,1},{4,6},{6,4},{5,7},{7,5},{8,10},{10,8},{9,1... | collective-permute-start | bytes 983048 | tf_op jit(solution)/shard_map/ppermute | solution.py:396
  2.9 1.6 %copy-start.1 = (bf16[1,3,3,320,320]{4,3,2,1,0:T(8,128)(2,1)S(1)}, bf16[1,3,3,320,320]{4,3,2,1,0:T(8,128)(2,1)}, u32[]{:S(2)}) copy-start(bf16[1,3,3,320,320]{4,3,2,1,0:T(8,128)(2,1)} %param.11) | copy-start | bytes 5529604
  4.6 1.6 %copy-start.2 = (bf16[1,3,3,320,320]{4,3,2,1,0:T(8,128)(2,1)S(1)}, bf16[1,3,3,320,320]{4,3,2,1,0:T(8,128)(2,1)}, u32[]{:S(2)}) copy-start(bf16[1,3,3,320,320]{4,3,2,1,0:T(8,128)(2,1)} %param.12) | copy-start | bytes 5529604
  6.2 1.1 %copy-start.3 = (bf16[1,320,960]{2,1,0:T(8,128)(2,1)S(1)}, bf16[1,320,960]{2,1,0:T(8,128)(2,1)}, u32[]{:S(2)}) copy-start(bf16[1,320,960]{2,1,0:T(8,128)(2,1)} %param.14) | copy-start | bytes 1843204
  7.3 2.4 %copy-start.11 = (s32[1,2]{1,0:T(1,128)S(1)}, s32[1,2]{1,0:T(1,128)}, u32[]{:S(2)}) copy-start(s32[1,2]{1,0:T(1,128)} %param.10) | copy-start | bytes 28
  12.3 1.7 %collective-permute-start.1 = (bf16[512,320]{1,0:T(8,128)(2,1)S(1)}, bf16[512,320]{1,0:T(8,128)(2,1)S(1)}, u32[]{:S(2)}, u32[]{:S(2)}) collective-permute-start(bf16[512,320]{1,0:T(8,128)(2,1)S(1)} %collective-permute-done.refs_0_), channel_id=1, source_target_pairs={{0,1},{1,0},{2,3},{3,2},{4,5},{5,4},{6,7},{7,6},{8,9},{9,8},{10,11... | collective-permute-start | bytes 983048 | tf_op jit(solution)/shard_map/ppermute | solution.py:396
  12.6 19.4 %copy-start.4 = (bf16[1,320,2560]{2,1,0:T(8,128)(2,1)S(1)}, bf16[1,320,2560]{2,1,0:T(8,128)(2,1)}, u32[]{:S(2)}) copy-start(bf16[1,320,2560]{2,1,0:T(8,128)(2,1)} %param.16) | copy-start | bytes 4915204
  12.6 19.4 %copy-start.5 = (bf16[1,1280,320]{1,2,0:T(8,128)(2,1)S(1)}, bf16[1,1280,320]{1,2,0:T(8,128)(2,1)}, u32[]{:S(2)}) copy-start(bf16[1,1280,320]{1,2,0:T(8,128)(2,1)} %param.17) | copy-start | bytes 2457604
  12.6 19.4 %copy-start.6 = (bf16[1,320,320]{2,1,0:T(8,128)(2,1)S(1)}, bf16[1,320,320]{2,1,0:T(8,128)(2,1)}, u32[]{:S(2)}) copy-start(bf16[1,320,320]{2,1,0:T(8,128)(2,1)} %param.15) | copy-start | bytes 614404
  20.7 7.6 %collective-permute-start.2 = (bf16[128,320]{1,0:T(8,128)(2,1)S(1)}, bf16[128,320]{1,0:T(8,128)(2,1)S(1)}, u32[]{:S(2)}, u32[]{:S(2)}) collective-permute-start(bf16[128,320]{1,0:T(8,128)(2,1)S(1)} %get-tuple-element.35), channel_id=1, source_target_pairs={{0,4},{4,8},{8,12},{12,0},{1,5},{5,9},{9,13},{13,1},{2,6},{6,10},{... | collective-permute-start | bytes 245768 | tf_op jit(solution)/shard_map/ppermute | solution.py:396
  22.6 9.4 %collective-permute-start.3 = (bf16[128,320]{1,0:T(8,128)(2,1)S(1)}, bf16[128,320]{1,0:T(8,128)(2,1)S(1)}, u32[]{:S(2)}, u32[]{:S(2)}) collective-permute-start(bf16[128,320]{1,0:T(8,128)(2,1)S(1)} %get-tuple-element.36), channel_id=1, source_target_pairs={{0,8},{4,12},{8,0},{12,4},{1,9},{5,13},{9,1},{13,5},{2,10},{6,14},... | collective-permute-start | bytes 245768 | tf_op jit(solution)/shard_map/ppermute | solution.py:396
  25.2 6.8 %collective-permute-start.4 = (bf16[128,320]{1,0:T(8,128)(2,1)S(1)}, bf16[128,320]{1,0:T(8,128)(2,1)S(1)}, u32[]{:S(2)}, u32[]{:S(2)}) collective-permute-start(bf16[128,320]{1,0:T(8,128)(2,1)S(1)} %get-tuple-element.37), channel_id=1, source_target_pairs={{0,12},{4,0},{8,4},{12,8},{1,13},{5,1},{9,5},{13,9},{2,14},{6,2},{... | collective-permute-start | bytes 245768 | tf_op jit(solution)/shard_map/ppermute | solution.py:396
  38.6 7.9 %collective-permute-start.6 = (bf16[128,320]{1,0:T(8,128)(2,1)S(1)}, bf16[128,320]{1,0:T(8,128)(2,1)S(1)}, u32[]{:S(2)}, u32[]{:S(2)}) collective-permute-start(bf16[128,320]{1,0:T(8,128)(2,1)S(1)} %get-tuple-element.40), channel_id=1, source_target_pairs={{0,14},{2,12},{4,2},{6,0},{8,6},{10,4},{12,10},{14,8},{1,15},{3,13... | collective-permute-start | bytes 245768 | tf_op jit(solution)/shard_map/ppermute | solution.py:396
  43.2 9.4 %collective-permute-start.7 = (bf16[128,320]{1,0:T(8,128)(2,1)S(1)}, bf16[128,320]{1,0:T(8,128)(2,1)S(1)}, u32[]{:S(2)}, u32[]{:S(2)}) collective-permute-start(bf16[128,320]{1,0:T(8,128)(2,1)S(1)} %get-tuple-element.41), channel_id=1, source_target_pairs={{0,10},{2,8},{4,14},{6,12},{8,2},{10,0},{12,6},{14,4},{1,11},{3,9}... | collective-permute-start | bytes 245768 | tf_op jit(solution)/shard_map/ppermute | solution.py:396
  43.6 9.1 %collective-permute-start.8 = (bf16[128,320]{1,0:T(8,128)(2,1)S(1)}, bf16[128,320]{1,0:T(8,128)(2,1)S(1)}, u32[]{:S(2)}, u32[]{:S(2)}) collective-permute-start(bf16[128,320]{1,0:T(8,128)(2,1)S(1)} %get-tuple-element.42), channel_id=1, source_target_pairs={{0,6},{2,4},{4,10},{6,8},{8,14},{10,12},{12,2},{14,0},{1,7},{3,5},... | collective-permute-start | bytes 245768 | tf_op jit(solution)/shard_map/ppermute | solution.py:396
  44.1 9.1 %collective-permute-start.5 = (bf16[128,320]{1,0:T(8,128)(2,1)S(1)}, bf16[128,320]{1,0:T(8,128)(2,1)S(1)}, u32[]{:S(2)}, u32[]{:S(2)}) collective-permute-start(bf16[128,320]{1,0:T(8,128)(2,1)S(1)} %get-tuple-element.39), channel_id=1, source_target_pairs={{0,2},{2,0},{4,6},{6,4},{8,10},{10,8},{12,14},{14,12},{1,3},{3,1},... | collective-permute-start | bytes 245768 | tf_op jit(solution)/shard_map/ppermute | solution.py:396
  46.5 6.8 %collective-permute-start.10 = (bf16[128,320]{1,0:T(8,128)(2,1)S(1)}, bf16[128,320]{1,0:T(8,128)(2,1)S(1)}, u32[]{:S(2)}, u32[]{:S(2)}) collective-permute-start(bf16[128,320]{1,0:T(8,128)(2,1)S(1)} %collective-permute-done.6.refs_1_), channel_id=1, source_target_pairs={{0,1},{1,0},{2,3},{3,2},{4,5},{5,4},{6,7},{7,6},{8,9},{9,8},{10,11... | collective-permute-start | bytes 245768 | tf_op jit(solution)/shard_map/ppermute | solution.py:396
  52.6 1.3 %collective-permute-start.11 = (bf16[128,320]{1,0:T(8,128)(2,1)S(1)}, bf16[128,320]{1,0:T(8,128)(2,1)S(1)}, u32[]{:S(2)}, u32[]{:S(2)}) collective-permute-start(bf16[128,320]{1,0:T(8,128)(2,1)S(1)} %collective-permute-done.7.refs_2_), channel_id=1, source_target_pairs={{0,1},{1,0},{2,3},{3,2},{4,5},{5,4},{6,7},{7,6},{8,9},{9,8},{10,11... | collective-permute-start | bytes 245768 | tf_op jit(solution)/shard_map/ppermute | solution.py:396
  52.7 1.5 %collective-permute-start.12 = (bf16[128,320]{1,0:T(8,128)(2,1)S(1)}, bf16[128,320]{1,0:T(8,128)(2,1)S(1)}, u32[]{:S(2)}, u32[]{:S(2)}) collective-permute-start(bf16[128,320]{1,0:T(8,128)(2,1)S(1)} %collective-permute-done.8.refs_3_), channel_id=1, source_target_pairs={{0,1},{1,0},{2,3},{3,2},{4,5},{5,4},{6,7},{7,6},{8,9},{9,8},{10,11... | collective-permute-start | bytes 245768 | tf_op jit(solution)/shard_map/ppermute | solution.py:396
  53.2 1.3 %collective-permute-start.9 = (bf16[128,320]{1,0:T(8,128)(2,1)S(1)}, bf16[128,320]{1,0:T(8,128)(2,1)S(1)}, u32[]{:S(2)}, u32[]{:S(2)}) collective-permute-start(bf16[128,320]{1,0:T(8,128)(2,1)S(1)} %collective-permute-done.5.refs_0_), channel_id=1, source_target_pairs={{0,1},{1,0},{2,3},{3,2},{4,5},{5,4},{6,7},{7,6},{8,9},{9,8},{10,11... | collective-permute-start | bytes 245768 | tf_op jit(solution)/shard_map/ppermute | solution.py:396
  61.8 0.6 copy-start.8
  62.5 7.9 %collective-permute-start.13 = (bf16[128,320]{1,0:T(8,128)(2,1)}, bf16[128,320]{1,0:T(8,128)(2,1)}, u32[]{:S(2)}, u32[]{:S(2)}) collective-permute-start(bf16[128,320]{1,0:T(8,128)(2,1)} %get-tuple-element.44), channel_id=1, source_target_pairs={{0,4},{4,8},{8,12},{12,0},{1,5},{5,9},{9,13},{13,1},{2,6},{6,10},{... | collective-permute-start | bytes 245768 | tf_op jit(solution)/shard_map/ppermute | solution.py:396
  62.5 11.1 %collective-permute-start.14 = (bf16[128,320]{1,0:T(8,128)(2,1)}, bf16[128,320]{1,0:T(8,128)(2,1)}, u32[]{:S(2)}, u32[]{:S(2)}) collective-permute-start(bf16[128,320]{1,0:T(8,128)(2,1)} %get-tuple-element.45), channel_id=1, source_target_pairs={{0,8},{4,12},{8,0},{12,4},{1,9},{5,13},{9,1},{13,5},{2,10},{6,14},... | collective-permute-start | bytes 245768 | tf_op jit(solution)/shard_map/ppermute | solution.py:396
  65.1 8.5 %collective-permute-start.15 = (bf16[128,320]{1,0:T(8,128)(2,1)S(1)}, bf16[128,320]{1,0:T(8,128)(2,1)}, u32[]{:S(2)}, u32[]{:S(2)}) collective-permute-start(bf16[128,320]{1,0:T(8,128)(2,1)S(1)} %get-tuple-element.46), channel_id=1, source_target_pairs={{0,12},{4,0},{8,4},{12,8},{1,13},{5,1},{9,5},{13,9},{2,14},{6,2},{... | collective-permute-start | bytes 245768 | tf_op jit(solution)/shard_map/ppermute | solution.py:396
  73.6 0.9 copy-start.7
  74.5 0.9 copy-start.9
  83.0 6.0 %collective-permute-start.16 = (bf16[128,320]{1,0:T(8,128)(2,1)S(1)}, bf16[128,320]{1,0:T(8,128)(2,1)S(1)}, u32[]{:S(2)}, u32[]{:S(2)}) collective-permute-start(bf16[128,320]{1,0:T(8,128)(2,1)S(1)} %get-tuple-element.48), channel_id=1, source_target_pairs={{0,12},{4,0},{8,4},{12,8},{1,13},{5,1},{9,5},{13,9},{2,14},{6,2},{... | collective-permute-start | bytes 245768 | tf_op jit(solution)/shard_map/ppermute | solution.py:396
  85.8 9.5 %collective-permute-start.17 = (bf16[128,320]{1,0:T(8,128)(2,1)S(1)}, bf16[128,320]{1,0:T(8,128)(2,1)S(1)}, u32[]{:S(2)}, u32[]{:S(2)}) collective-permute-start(bf16[128,320]{1,0:T(8,128)(2,1)S(1)} %get-tuple-element.49), channel_id=1, source_target_pairs={{0,8},{4,12},{8,0},{12,4},{1,9},{5,13},{9,1},{13,5},{2,10},{6,14},... | collective-permute-start | bytes 245768 | tf_op jit(solution)/shard_map/ppermute | solution.py:396
  86.3 8.9 %collective-permute-start.18 = (bf16[128,320]{1,0:T(8,128)(2,1)S(1)}, bf16[128,320]{1,0:T(8,128)(2,1)S(1)}, u32[]{:S(2)}, u32[]{:S(2)}) collective-permute-start(bf16[128,320]{1,0:T(8,128)(2,1)S(1)} %get-tuple-element.50), channel_id=1, source_target_pairs={{0,4},{4,8},{8,12},{12,0},{1,5},{5,9},{9,13},{13,1},{2,6},{6,10},{... | collective-permute-start | bytes 245768 | tf_op jit(solution)/shard_map/ppermute | solution.py:396
  95.3 0.7 copy-start.10

commit v2 on v1

v2 whole, which is shorter than its diff:
```python
import functools
import math

import jax
import jax.numpy as jnp
from jax import lax
from jax.experimental import pallas as pl
from jax.experimental.pallas import tpu as pltpu
from jax.sharding import PartitionSpec as P

HEAD_DIM = 64
GROUPS = 32
STEPS = 2
LANES = 128
WIDE = 256
F32 = jnp.float32
BF16 = jnp.bfloat16


def partner(spot, distance, count):
    if count & (count - 1):
        return (spot + distance) % count
    return spot ^ distance


def distances(count):
    order, low = [], count
    while low > 1:
        low = (low + 1) // 2
        order += [d for d in range(low, count) if d not in order]
    return order + [0]


def round_up(value, unit):
    return -(-value // unit) * unit


def dense_rows(pixels, channels):
    return pixels * channels // LANES


def pack_part(values, target, at, channels):
    pixels, full = values.shape[0], channels // LANES
    for i in range(full):
        block = values[:, i * LANES : (i + 1) * LANES].astype(BF16)
        target[at + i * pixels : at + (i + 1) * pixels, :] = block
    if channels % LANES:
        rest = values[:, full * LANES :]
        first, second = rest[: pixels // 2], rest[pixels // 2 :]
        lane = lax.broadcasted_iota(jnp.int32, (1, LANES), 1)
        both = jnp.where(lane < LANES // 2, first, pltpu.roll(second, LANES // 2, 1))
        target[at + full * pixels : at + full * pixels + pixels // 2, :] = both.astype(BF16)


def unpack_part(source, at, pixels, channels):
    full = channels // LANES
    blocks = [
        (i, 0, source[at + i * pixels : at + (i + 1) * pixels, :].astype(F32)) for i in range(full)
    ]
    if channels % LANES:
        both = source[at + full * pixels : at + full * pixels + pixels // 2, :].astype(F32)
        low = lax.broadcasted_iota(jnp.int32, (1, LANES), 1) < LANES // 2
        blocks.append((full, 0, jnp.where(low, both, 0.0)))
        blocks.append((full, pixels // 2, jnp.where(low, pltpu.roll(both, LANES // 2, 1), 0.0)))
    return blocks


def window_sum(values, width, direction):
    lanes = values.shape[1]
    done, result, power, size = 0, None, values, 1
    while True:
        if width & size:
            moved = power
            if done:
                moved = pltpu.roll(power, done if direction > 0 else lanes - done, 1)
            result = moved if result is None else result + moved
            done += size
        if done == width:
            return result
        power = power + pltpu.roll(power, size if direction > 0 else lanes - size, 1)
        size *= 2


def group_scale(total, square, entries, group_width, channels):
    lanes = total.shape[1]
    lane = lax.broadcasted_iota(jnp.int32, (1, lanes), 1)
    last = (lane % group_width == group_width - 1) & (lane < channels)

    def mean(sums):
        sums = window_sum(jnp.broadcast_to(jnp.sum(sums, axis=0, keepdims=True), (8, lanes)), group_width, 1)
        return window_sum(jnp.where(last, sums, 0.0), group_width, -1)[0:1] / entries

    average = mean(total)
    scale = lax.rsqrt(mean(square) - average * average + 1e-05)
    scale = jnp.where(lane < channels, 0.5 * scale, 0.0)
    return scale, -average * scale


def spatial_kernel(rows, half, columns, channels, group_width, step, ways, shards, *refs):
    own, other = refs[:ways], refs[ways : 2 * ways]
    kernels, embeds = refs[2 * ways : 2 * ways + 2]
    outs = refs[2 * ways + 2 : 2 * ways + 2 + shards]
    field, hidden, middle, edge, pair = refs[2 * ways + 2 + shards :]
    embed = embeds[step : step + 1, :]
    lanes = field.shape[1]
    own_rows = rows // half
    part = own_rows * columns // shards
    here = lax.axis_index("halo")
    spot = lax.axis_index("shard")
    own_base = here * (own_rows * columns)
    other_base = (1 - here) * (own_rows * columns)
    zero = jnp.zeros((8, lanes), F32)

    height = dense_rows(part, channels)
    for base, arrived in ((own_base, own), (other_base, other)):
        if ways == 1:
            place = pl.ds(pl.multiple_of(base, columns), own_rows * columns)
            field[place, lanes - LANES :] = jnp.zeros((own_rows * columns, LANES), F32)
            field[place, :channels] = arrived[0][...].astype(F32)
            continue
        held = [(block, at) for block in arrived for at in range(0, block.shape[0], height)]
        for (block, at), d in zip(held, distances(shards)):
            here_part = base + partner(spot, d, shards) * part
            for i, first, values in unpack_part(block, at, part, channels):
                place = pl.multiple_of(here_part + first, 8)
                field[pl.ds(place, values.shape[0]), i * LANES : (i + 1) * LANES] = values

    def sum_row(i, carry):
        total, square = carry
        chunk = field[pl.ds(pl.multiple_of(i * columns, columns), columns), :]
        chunk = chunk.reshape(columns // 8, 8, lanes)
        return total + jnp.sum(chunk, axis=0), square + jnp.sum(chunk * chunk, axis=0)

    field_sums = lax.fori_loop(0, rows, sum_row, (zero, zero), unroll=4)

    def activate(source, scale, shift, first, start, stop):
        def body(i, before):
            row = first - 1 + i
            inside = ((row >= 0) & (row < rows)).astype(F32)
            at = pl.multiple_of(jnp.clip(row, 0, rows - 1) * columns, columns)
            u = source[pl.ds(at, columns), :] * (scale * inside) + shift * inside
            g = u + u * jnp.tanh(u)
            to = pl.ds(pl.multiple_of(i * columns, columns), columns)
            rest = g[:, WIDE:]
            middle[to, :] = g[:, :WIDE].astype(BF16)
            edge[to, :] = rest.astype(BF16)
            pair[to, :] = (before + pltpu.roll(rest, LANES // 2, 1)).astype(BF16)
            return rest

        lax.fori_loop(start, stop, body, jnp.zeros((columns, LANES), F32), unroll=4)

    step_rows = min(WIDE, own_rows * columns)
    column = lax.broadcasted_iota(jnp.int32, (step_rows, 1), 0) % columns
    low = lax.broadcasted_iota(jnp.int32, (1, LANES), 1) < channels - WIDE

    def convolve(kernel, start):
        top, mid, bottom = [slice(start + r * columns, start + r * columns + step_rows) for r in range(3)]
        window = jnp.concatenate(
            [middle[top, :], middle[mid, :], middle[bottom, :], pair[mid, :], edge[bottom, :]], axis=1
        )
        y = jnp.dot(window, kernel[...], preferred_element_type=F32)

        def from_left(values):
            return jnp.where(column == 0, 0.0, pltpu.roll(values, 1, 0))

        def from_right(values):
            return jnp.where(column == columns - 1, 0.0, pltpu.roll(values, step_rows - 1, 0))

        wide = y[:, WIDE : 2 * WIDE] + from_left(y[:, :WIDE]) + from_right(y[:, 2 * WIDE : 3 * WIDE])
        tail = y[:, 3 * WIDE : 3 * WIDE + LANES]
        narrow = from_left(tail) + pltpu.roll(tail, LANES // 2, 1) + from_right(y[:, 3 * WIDE + LANES :])
        return wide, narrow

    entries = float(rows * columns * group_width)
    for pad in (0, (rows + 1) * columns):
        middle[pad : pad + columns, :] = jnp.zeros((columns, WIDE), BF16)
        edge[pad : pad + columns, :] = jnp.zeros((columns, LANES), BF16)
    activate(field, *group_scale(*field_sums, entries, group_width, channels), 0, 1, rows + 1)
    total, square = zero, zero
    for start in range(0, rows * columns, step_rows):
        wide, narrow = convolve(kernels.at[0], start)
        chunk = jnp.concatenate(
            [wide + embed[:, :WIDE], jnp.where(low, narrow + embed[:, WIDE:], 0.0)], axis=1
        )
        hidden[start : start + step_rows, :] = chunk
        chunk = chunk.reshape(step_rows // 8, 8, lanes)
        total = total + jnp.sum(chunk, axis=0)
        square = square + jnp.sum(chunk * chunk, axis=0)
    activate(
        hidden,
        *group_scale(total, square, entries, group_width, channels),
        here * own_rows,
        0,
        own_rows + 2,
    )
    for start in range(0, own_rows * columns, step_rows):
        wide, narrow = convolve(kernels.at[1], start)
        mine = pl.ds(pl.multiple_of(own_base + start, step_rows), step_rows)
        hidden[mine, :WIDE] = wide + field[mine, :WIDE]
        hidden[mine, WIDE:] = narrow + field[mine, WIDE:]
    for i, d in enumerate(distances(shards)):
        place = pl.multiple_of(own_base + partner(spot, d, shards) * part, part)
        pack_part(hidden[pl.ds(place, part), :], outs[i], 0, channels)


def spatial(own, other, weights, embeds, step, rows, columns, half, shards):
    tokens = rows * columns
    part = tokens // half // shards
    channels = sum(block.size for block in own) // (tokens // half)
    ways = len(own)
    lanes = round_up(channels, LANES)
    padded = tokens + 2 * columns
    depth = weights.shape[1]
    kernel = functools.partial(
        spatial_kernel,
        rows,
        half,
        columns,
        channels,
        channels // GROUPS,
        step,
        ways,
        shards,
    )
    vmem = pl.BlockSpec(memory_space=pltpu.VMEM)
    return pl.pallas_call(
        kernel,
        out_shape=[jax.ShapeDtypeStruct((dense_rows(part, channels), LANES), BF16)] * shards,
        in_specs=[vmem] * (2 * ways + 2),
        out_specs=[vmem] * shards,
        scratch_shapes=[
            pltpu.VMEM((tokens, lanes), F32),
            pltpu.VMEM((tokens, lanes), F32),
            pltpu.VMEM((padded, WIDE), BF16),
            pltpu.VMEM((padded, LANES), BF16),
            pltpu.VMEM((padded, LANES), BF16),
        ],
        compiler_params=pltpu.CompilerParams(vmem_limit_bytes=14 * 1024 * 1024),
        cost_estimate=pl.CostEstimate(
            flops=3 * tokens * depth * depth,
            bytes_accessed=6000000,
            transcendentals=tokens * lanes,
        ),
        name="spatial",
    )(*own, *other, weights, embeds)


def prepare_kernel(channels, kernel1, kernel2, qkv, kernels, padded):
    spare = channels - WIDE
    for kernel, packed in ((kernel1, kernels.at[0]), (kernel2, kernels.at[1])):
        depth = packed.shape[0]
        packed[3 * channels :, :] = jnp.zeros((depth - 3 * channels, depth), BF16)
        for r in range(3):
            for source, target in (
                (slice(0, WIDE), slice(r * WIDE, (r + 1) * WIDE)),
                (slice(WIDE, channels), slice(3 * WIDE + r * spare, 3 * WIDE + (r + 1) * spare)),
            ):
                for s in range(3):
                    packed[target, s * WIDE : (s + 1) * WIDE] = kernel[r, s, source, :WIDE]
                first, second, third = [kernel[r, s, source, WIDE:] for s in range(3)]
                packed[target, 3 * WIDE : 3 * WIDE + LANES] = jnp.concatenate([first, second], axis=1)
                packed[target, 3 * WIDE + LANES :] = jnp.concatenate(
                    [third, jnp.zeros_like(third)], axis=1
                )
    lanes = padded.shape[1] // 3
    padded[...] = jnp.zeros(padded.shape, BF16)
    for i in range(3):
        padded[:, i * lanes : i * lanes + channels] = qkv[:, i * channels : (i + 1) * channels]


def prepare(conv_first, conv_second, qkv):
    channels = qkv.shape[0]
    depth = round_up(3 * channels, WIDE)
    lanes = round_up(channels, LANES)
    vmem = pl.BlockSpec(memory_space=pltpu.VMEM)
    return pl.pallas_call(
        functools.partial(prepare_kernel, channels),
        out_shape=[
            jax.ShapeDtypeStruct((2, depth, depth), BF16),
            jax.ShapeDtypeStruct((channels, 3 * lanes), BF16),
        ],
        in_specs=[vmem] * 3,
        out_specs=[vmem] * 2,
        compiler_params=pltpu.CompilerParams(vmem_limit_bytes=14 * 1024 * 1024),
        cost_estimate=pl.CostEstimate(flops=0, bytes_accessed=10000000, transcendentals=0),
        name="prepare",
    )(conv_first, conv_second, qkv)


def norm_rows(values):
    average = jnp.mean(values, axis=-1, keepdims=True)
    centred = values - average
    spread = jnp.mean(centred * centred, axis=-1, keepdims=True)
    return (centred * lax.rsqrt(spread + 1e-05)).astype(BF16)


def feed_forward(stream, geglu_in, geglu_out, active):
    inner = geglu_out.shape[1]
    normed = norm_rows(stream.astype(F32))
    for at in range(0, inner, WIDE):
        value = jnp.dot(normed, geglu_in[:, at : at + WIDE], preferred_element_type=F32)
        gate = jnp.dot(normed, geglu_in[:, inner + at : inner + at + WIDE], preferred_element_type=F32)
        act = value * (0.5 * gate) * (1.0 + lax.erf(gate * math.sqrt(0.5)))
        active[:, at : at + WIDE] = act.astype(BF16)
    update = lax.dot_general(
        active[...], geglu_out[...], (((1,), (1,)), ((), ())), preferred_element_type=F32
    )
    return stream.astype(F32) + update


def leave(values, target):
    pixels, channels = values.shape
    if target.shape == values.shape:
        target[...] = values.astype(BF16)
        return
    spare = round_up(channels, LANES) - channels
    values = jnp.concatenate([values, jnp.zeros((pixels, spare), F32)], axis=1)
    pack_part(values, target, 0, channels)


def feed_kernel(count, *refs):
    rest, geglu_in, geglu_out = refs[:3]
    outs = refs[3 : 3 + count]
    (active,) = refs[3 + count :]
    done = feed_forward(rest[...], geglu_in, geglu_out, active)
    pixels = done.shape[0] // count
    for i in range(count):
        leave(done[i * pixels : (i + 1) * pixels, :], outs[i])


def temporal_kernel(frames, sooner, *refs):
    parts = refs[:frames]
    qkv, attn_out, geglu_in, geglu_out = refs[frames : frames + 4]
    outs = refs[frames + 4 : frames + 4 + sooner]
    rest = refs[frames + 4 + sooner]
    stream, projected, mixed, active = refs[frames + 5 + sooner :]
    channels = stream.shape[1]
    pixels = stream.shape[0] // frames
    lanes = projected.shape[1] // 3

    for f in range(frames):
        for i, first, values in unpack_part(parts[f], 0, pixels, channels):
            rows = slice(f * pixels + first, f * pixels + first + values.shape[0])
            width = min(LANES, channels - i * LANES)
            stream[rows, i * LANES : i * LANES + width] = values[:, :width].astype(BF16)
    normed = norm_rows(stream[...].astype(F32))
    projected[...] = jnp.dot(normed, qkv[...], preferred_element_type=F32).astype(BF16)

    pack = min(pixels, WIDE // frames)
    tile = frames * pack
    same = (
        lax.broadcasted_iota(jnp.int32, (tile, tile), 0) % pack
        == lax.broadcasted_iota(jnp.int32, (tile, tile), 1) % pack
    )
    lane = lax.broadcasted_iota(jnp.int32, (1, LANES), 1)
    sharing = LANES // HEAD_DIM
    for first in range(0, pixels, pack):
        places = [slice(f * pixels + first, f * pixels + first + pack) for f in range(frames)]
        for at in range(0, channels, LANES):
            query, key, value = [
                jnp.concatenate([projected[p, i * lanes + at : i * lanes + at + LANES] for p in places])
                for i in range(3)
            ]
            mix = None
            for j in range(min(sharing, (channels - at) // HEAD_DIM)):
                chosen = (lane >= j * HEAD_DIM) & (lane < (j + 1) * HEAD_DIM)
                scores = lax.dot_general(
                    query * chosen.astype(BF16),
                    key,
                    (((1,), (1,)), ((), ())),
                    preferred_element_type=F32,
                )
                scores = jnp.where(same, scores, float(jnp.finfo(F32).min))
                top = jnp.max(scores, axis=1, keepdims=True)
                powers = jnp.exp((scores - top) * HEAD_DIM ** (-0.5))
                total = jnp.sum(powers, axis=1, keepdims=True)
                weights = (powers * (1.0 / total)).astype(BF16)
                head = jnp.dot(weights, value, preferred_element_type=F32)
                mix = head if mix is None else jnp.where(chosen, head, mix)
            mix = mix.astype(BF16)
            for f, p in enumerate(places):
                mixed[p, at : at + LANES] = mix[f * pack : (f + 1) * pack]

    update = jnp.dot(mixed[:, :channels], attn_out[...], preferred_element_type=F32)
    after = (stream[...].astype(F32) + update).astype(BF16)
    rest[...] = after[sooner * pixels :, :]
    done = feed_forward(after[: sooner * pixels, :], geglu_in, geglu_out, active)
    for f in range(sooner):
        leave(done[f * pixels : (f + 1) * pixels, :], outs[f])


def temporal(parts, weights, dense):
    frames = len(parts)
    sooner = frames // 2
    later = frames - sooner
    channels = weights[0].shape[0]
    pixels = parts[0].size // channels
    lanes = round_up(channels, LANES)
    tokens = frames * pixels
    inner = weights[3].shape[1]
    vmem = pl.BlockSpec(memory_space=pltpu.VMEM)
    piece = jax.ShapeDtypeStruct(parts[0].shape if dense else (pixels, channels), BF16)
    feed_flops = 6 * pixels * channels * inner
    params = pltpu.CompilerParams(vmem_limit_bytes=14 * 1024 * 1024)
    *first, rest = pl.pallas_call(
        functools.partial(temporal_kernel, frames, sooner),
        out_shape=[piece] * sooner + [jax.ShapeDtypeStruct((later * pixels, channels), BF16)],
        in_specs=[vmem] * (frames + 4),
        out_specs=[vmem] * (sooner + 1),
        scratch_shapes=[
            pltpu.VMEM((tokens, channels), BF16),
            pltpu.VMEM((tokens, 3 * lanes), BF16),
            pltpu.VMEM((tokens, lanes), BF16),
            pltpu.VMEM((sooner * pixels, inner), BF16),
        ],
        compiler_params=params,
        cost_estimate=pl.CostEstimate(
            flops=8 * tokens * channels * lanes + sooner * feed_flops,
            bytes_accessed=4000000,
            transcendentals=sooner * pixels * inner,
        ),
        name="temporal",
    )(*parts, *weights)
    second = pl.pallas_call(
        functools.partial(feed_kernel, later),
        out_shape=[piece] * later,
        in_specs=[vmem] * 3,
        out_specs=[vmem] * later,
        scratch_shapes=[pltpu.VMEM((later * pixels, inner), BF16)],
        compiler_params=params,
        cost_estimate=pl.CostEstimate(
            flops=later * feed_flops,
            bytes_accessed=3000000,
            transcendentals=later * pixels * inner,
        ),
        name="feed",
    )(rest, weights[2], weights[3])
    return [*first, *second]


def send(block, axis, distance):
    count = lax.axis_size(axis)
    return lax.ppermute(block, axis, [(i, (i + distance) % count) for i in range(count)])


def exchange(parts, back=False, across=0):
    shards, sections = lax.axis_size("shard"), lax.axis_size("section")
    arrived = []
    for part, d in zip(parts, distances(shards)):
        target = [partner(z, d, shards) for z in range(shards)]
        if back:
            target = [target.index(z) for z in range(shards)]
        if across:
            route = [
                (z * sections + s, target[z] * sections + (s + across) % sections)
                for z in range(shards)
                for s in range(sections)
            ]
            part = lax.ppermute(part, ("shard", "section"), route)
        elif d:
            part = lax.ppermute(part, "shard", list(enumerate(target)))
        arrived.append(part)
    return arrived


def join_kernel(*refs):
    *parts, whole = refs
    height = parts[0].shape[0]
    for i, part in enumerate(parts):
        whole[i * height : (i + 1) * height, :] = part[...]


def join(parts):
    vmem = pl.BlockSpec(memory_space=pltpu.VMEM)
    height, lanes = parts[0].shape
    return pl.pallas_call(
        join_kernel,
        out_shape=jax.ShapeDtypeStruct((len(parts) * height, lanes), parts[0].dtype),
        in_specs=[vmem] * len(parts),
        out_specs=vmem,
        compiler_params=pltpu.CompilerParams(vmem_limit_bytes=4 * 1024 * 1024),
        name="join",
    )(*parts)


def assemble(parts):
    size, channels = parts[0].shape
    spot = lax.axis_index("shard")
    whole = jnp.zeros((len(parts) * size, channels), parts[0].dtype)
    for part, d in zip(parts, distances(len(parts))):
        place = partner(spot, d, len(parts)) * size
        whole = lax.dynamic_update_slice_in_dim(whole, part, place, axis=0)
    return whole


def embed_time(stamps, time_weight):
    half_width = time_weight.shape[0] // 2
    frequency = jnp.exp(-math.log(10000.0) * jnp.arange(half_width, dtype=F32) / half_width)
    angles = stamps.astype(F32)[:, None] * frequency[None, :]
    sinusoid = jnp.concatenate([jnp.cos(angles), jnp.sin(angles)], axis=1)
    out = jnp.dot(jax.nn.silu(sinusoid).astype(BF16), time_weight, preferred_element_type=F32)
    return jnp.pad(out, ((0, 0), (0, round_up(out.shape[1], LANES) - out.shape[1])))


def per_device(
    features,
    timesteps,
    conv_first,
    conv_second,
    time_weight,
    qkv_weight,
    attn_out,
    geglu_in,
    geglu_out,
):
    _, _, own_rows, columns, channels = features.shape
    half = lax.axis_size("halo")
    rows = own_rows * half
    shards = lax.axis_size("shard")

    moved = send(features.reshape(own_rows * columns, channels), "section", 1)
    embeds = embed_time(timesteps[0], time_weight[0])
    spatial_weights, padded = prepare(conv_first[0], conv_second[0], qkv_weight[0])

    moved, spatial_weights, padded = lax.optimization_barrier((moved, spatial_weights, padded))
    own = [moved]
    temporal_weights = (padded, attn_out[0], geglu_in[0], geglu_out[0].T)
    for denoise_step in range(STEPS):
        last = denoise_step == STEPS - 1
        parts = spatial(
            own,
            [send(block, "halo", 1) for block in own],
            spatial_weights,
            embeds,
            denoise_step,
            rows,
            columns,
            half,
            shards,
        )
        parts = temporal(exchange(parts), temporal_weights, dense=not last)
        parts = exchange(parts, back=True, across=0 if last else 1)
        own = [join(parts[: shards // 2]), *parts[shards // 2 :]]
    return assemble(parts).reshape(features.shape)


def solution(mesh):
    return jax.shard_map(
        per_device,
        mesh=mesh,
        in_specs=(
            P(("groups", "section"), "shard", "halo", None, None),
            P(("groups", "section"), None),
            P("section", None, None, None, None),
            P("section", None, None, None, None),
            P("section", None, None),
            P("section", None, None),
            P("section", None, None),
            P("section", None, None),
            P("section", None, None),
        ),
        out_specs=P(("groups", "section"), "shard", "halo", None, None),
        check_vma=False,
    )
```

time: 96.4 us -> 84.1 us (0.87)
  Pallas kernels: 30.6 us -> 25.1 us
  starting transfers between devices: 23.7 us -> 21.2 us
  local copies, waits for them, and re-layouts: 7.7 us -> 5.24 us
  waiting for transfers between devices: 33.5 us -> 31.8 us
    pallas_call x4 -> x7, Pallas kernels: 28.2 us -> 24.4 us  [the longest x2 13.1 us: spatial(): pl.pallas_call(kernel, out_shape=[jax.ShapeDtypeStruct((dense_rows(part,...]
    ppermute x19 -> x18, starting transfers between devices: 23.7 us -> 21.2 us  [the longest x9 11.7 us: exchange(): part = lax.ppermute(part, 'shard', list(enumerate(target)))]
    unnamed x24 -> x18, local copies, waits for them, and re-layouts: 7.57 us -> 5.1 us
    ppermute x19 -> x18, waiting for transfers between devices: 33.5 us -> 31.8 us  [the longest x9 19.3 us: exchange(): part = lax.ppermute(part, 'shard', list(enumerate(target)))]
    pallas_call x1, Pallas kernels: 2.42 us -> 0.72 us  [prepare(): pl.pallas_call(functools.partial(prepare_kernel, channels), out_shape=[ja...]
  transfers between devices with their start and end apart: 19 -> 18, of which waited for: 13 -> 15; matrix products, arithmetic and copies ran while one was open for 0% -> 1% of each run, Pallas kernels for 3% -> 4%
where the time goes in v2:
time: 84.1 us; the launch traced here: 83.9 us
  waiting for transfers between devices  31.8 us (38%)
  Pallas kernels  25.1 us (30%)
  starting transfers between devices  21.2 us (25%)
  local copies, waits for them, and re-layouts  5.24 us (6%)
    ppermute x9, waiting for transfers between devices, exchange(): part = lax.ppermute(part, 'shard', list(enumerate(target)))  19.3 us
    pallas_call x2, Pallas kernels, spatial(): pl.pallas_call(kernel, out_shape=[jax.ShapeDtypeStruct((dense_rows(part,...  13.1 us
    ppermute x9, starting transfers between devices, exchange(): part = lax.ppermute(part, 'shard', list(enumerate(target)))  11.7 us
    pallas_call x2, Pallas kernels, temporal(): pl.pallas_call(functools.partial(temporal_kernel, frames, sooner), out_sh...  8.46 us
    ppermute x5, waiting for transfers between devices, send(): lax.ppermute(block, axis, [(i, (i + distance) % count) for i in range(cou...  6.83 us
    ppermute x4, starting transfers between devices, exchange(): part = lax.ppermute(part, ('shard', 'section'), route)  6.47 us
    ppermute x4, waiting for transfers between devices, exchange(): part = lax.ppermute(part, ('shard', 'section'), route)  5.71 us
    unnamed x18, local copies, waits for them, and re-layouts  5.1 us
  transfers between devices with their start and end apart: 18, of which 15 were waited for; matrix products, arithmetic and copies ran while one was open for 1% of the time, Pallas kernels for 4%

profile of v2, /device:TPU:0, one launch (start us, length us, event | category | flops | bytes accessed | tf_op | source)
XLA Modules:
  0.0 83.9 jit_solution(3651641672597857937)
XLA Ops:
  0.0 2.9 %collective-permute-start = (bf16[512,320]{1,0:T(8,128)(2,1)}, bf16[512,320]{1,0:T(8,128)(2,1)S(1)}, u32[]{:S(2)}, u32[]{:S(2)}) collective-permute-start(bf16[512,320]{1,0:T(8,128)(2,1)} %bitcast.28), channel_id=1, source_target_pairs={{0,2},{2,0},{1,3},{3,1},{4,6},{6,4},{5,7},{7,5},{8,10},{10,8},{9,1... | collective-permute-start | bytes 983048 | tf_op jit(solution)/shard_map/ppermute | solution.py:443
  2.9 1.6 %copy-done.3 = bf16[1,3,3,320,320]{4,3,2,1,0:T(8,128)(2,1)S(1)} copy-done((bf16[1,3,3,320,320]{4,3,2,1,0:T(8,128)(2,1)S(1)}, bf16[1,3,3,320,320]{4,3,2,1,0:T(8,128)(2,1)}, u32[]{:S(2)}) %copy-start.3) | copy-done | bytes 1843224
  4.6 1.6 %copy-done.4 = bf16[1,3,3,320,320]{4,3,2,1,0:T(8,128)(2,1)S(1)} copy-done((bf16[1,3,3,320,320]{4,3,2,1,0:T(8,128)(2,1)S(1)}, bf16[1,3,3,320,320]{4,3,2,1,0:T(8,128)(2,1)}, u32[]{:S(2)}) %copy-start.4) | copy-done | bytes 1843224
  6.2 1.1 %copy-done.5 = bf16[1,320,960]{2,1,0:T(8,128)(2,1)S(1)} copy-done((bf16[1,320,960]{2,1,0:T(8,128)(2,1)S(1)}, bf16[1,320,960]{2,1,0:T(8,128)(2,1)}, u32[]{:S(2)}) %copy-start.5) | copy-done | bytes 614424
  7.3 0.7 prepare.1
  8.0 4.2 %collective-permute-done.refs_0_ = bf16[512,320]{1,0:T(8,128)(2,1)S(1)} collective-permute-done((bf16[512,320]{1,0:T(8,128)(2,1)}, bf16[512,320]{1,0:T(8,128)(2,1)S(1)}, u32[]{:S(2)}, u32[]{:S(2)}) %collective-permute-start) | collective-permute-done | bytes 327712 | tf_op jit(solution)/shard_map/ppermute | solution.py:443
  12.3 0.1 multiply_cosine_fusion
  12.4 0.2 fusion
  12.6 0.0 copy-start.1
  12.6 0.0 copy-start.2
  12.6 0.0 copy-start.6
  12.7 1.3 %collective-permute-done.1.refs_1_ = bf16[512,320]{1,0:T(8,128)(2,1)S(1)} collective-permute-done((bf16[512,320]{1,0:T(8,128)(2,1)S(1)}, bf16[512,320]{1,0:T(8,128)(2,1)S(1)}, u32[]{:S(2)}, u32[]{:S(2)}) %collective-permute-start.1) | collective-permute-done | bytes 327712 | tf_op jit(solution)/shard_map/ppermute | solution.py:443
  14.0 6.5 %spatial.2 = (bf16[320,128]{1,0:T(8,128)(2,1)S(1)}, bf16[320,128]{1,0:T(8,128)(2,1)S(1)}, bf16[320,128]{1,0:T(8,128)(2,1)S(1)}, bf16[320,128]{1,0:T(8,128)(2,1)S(1)}) custom-call(bf16[512,320]{1,0:T(8,128)(2,1)S(1)} %collective-permute-done.refs_0_, bf16[512,320]{1,0:T(8,128)(2,1)S(1)} %collective-permute-done.1.refs_1_, ...), custom_call_target="tpu_custom_call" | custom-call | flops 3221225472 | bytes 6000000 | tf_op jit(solution)/shard_map/spatial/pallas_call | solution.py:226
  20.5 2.9 %collective-permute-start.2 = (bf16[320,128]{1,0:T(8,128)(2,1)S(1)}, bf16[320,128]{1,0:T(8,128)(2,1)S(1)}, u32[]{:S(2)}, u32[]{:S(2)}) collective-permute-start(bf16[320,128]{1,0:T(8,128)(2,1)S(1)} %get-tuple-element.32), channel_id=1, source_target_pairs={{0,8},{4,12},{8,0},{12,4},{1,9},{5,13},{9,1},{13,5},{2,10},{6,14},... | collective-permute-start | bytes 245768 | tf_op jit(solution)/shard_map/ppermute | solution.py:461
  23.4 1.3 %collective-permute-start.3 = (bf16[320,128]{1,0:T(8,128)(2,1)S(1)}, bf16[320,128]{1,0:T(8,128)(2,1)S(1)}, u32[]{:S(2)}, u32[]{:S(2)}) collective-permute-start(bf16[320,128]{1,0:T(8,128)(2,1)S(1)} %get-tuple-element.33), channel_id=1, source_target_pairs={{0,12},{4,8},{8,4},{12,0},{1,13},{5,9},{9,5},{13,1},{2,14},{6,10},... | collective-permute-start | bytes 245768 | tf_op jit(solution)/shard_map/ppermute | solution.py:461
  24.7 0.2 collective-permute-start.4
  24.9 4.9 %collective-permute-done.2.refs_0_ = bf16[320,128]{1,0:T(8,128)(2,1)S(1)} collective-permute-done((bf16[320,128]{1,0:T(8,128)(2,1)S(1)}, bf16[320,128]{1,0:T(8,128)(2,1)S(1)}, u32[]{:S(2)}, u32[]{:S(2)}) %collective-permute-start.2) | collective-permute-done | bytes 81952 | tf_op jit(solution)/shard_map/ppermute | solution.py:461
  29.9 0.4 collective-permute-done.3.refs_1_
  30.3 0.7 collective-permute-done.4.refs_2_
  31.0 4.3 %temporal.2 = (bf16[320,128]{1,0:T(8,128)(2,1)S(1)}, bf16[320,128]{1,0:T(8,128)(2,1)S(1)}, bf16[256,320]{1,0:T(8,128)(2,1)S(1)}) custom-call(bf16[320,128]{1,0:T(8,128)(2,1)S(1)} %collective-permute-done.2.refs_0_, bf16[320,128]{1,0:T(8,128)(2,1)S(1)} %collective-permute-done.3.refs_1_, bf16[320,128]{1,0:T(8,128)(2,1)S(1)} %collective-permute-done.4.refs_2_, ...), custom_call_target="tpu_custom_call" | custom-call | flops 1132462080 | bytes 4000000 | tf_op jit(solution)/shard_map/temporal/pallas_call | solution.py:405
  35.3 4.1 %collective-permute-start.5 = (bf16[320,128]{1,0:T(8,128)(2,1)S(1)}, bf16[320,128]{1,0:T(8,128)(2,1)S(1)}, u32[]{:S(2)}, u32[]{:S(2)}) collective-permute-start(bf16[320,128]{1,0:T(8,128)(2,1)S(1)} %get-tuple-element.37), channel_id=1, source_target_pairs={{0,10},{2,8},{4,14},{6,12},{8,2},{10,0},{12,6},{14,4},{1,11},{3,9}... | collective-permute-start | bytes 245768 | tf_op jit(solution)/shard_map/ppermute | solution.py:459
  39.3 0.4 collective-permute-start.6
  39.7 1.4 %feed.2 = (bf16[320,128]{1,0:T(8,128)(2,1)S(1)}, bf16[320,128]{1,0:T(8,128)(2,1)S(1)}) custom-call(bf16[256,320]{1,0:T(8,128)(2,1)S(1)} %get-tuple-element.39.refs_0_, bf16[320,2560]{1,0:T(8,128)(2,1)S(1)} %bitcast.16, bf16[320,1280]{1,0:T(8,128)(2,1)S(1)} %bitcast.20), custom_call_target="tpu_custom_call" | custom-call | flops 629145600 | bytes 3000000 | tf_op jit(solution)/shard_map/feed/pallas_call | solution.py:424
  41.2 1.0 %collective-permute-start.7 = (bf16[320,128]{1,0:T(8,128)(2,1)S(1)}, bf16[320,128]{1,0:T(8,128)(2,1)S(1)}, u32[]{:S(2)}, u32[]{:S(2)}) collective-permute-start(bf16[320,128]{1,0:T(8,128)(2,1)S(1)} %get-tuple-element.40), channel_id=1, source_target_pairs={{0,6},{2,4},{4,2},{6,0},{8,14},{10,12},{12,10},{14,8},{1,7},{3,5},... | collective-permute-start | bytes 245768 | tf_op jit(solution)/shard_map/ppermute | solution.py:459
  42.2 1.0 %collective-permute-start.8 = (bf16[320,128]{1,0:T(8,128)(2,1)S(1)}, bf16[320,128]{1,0:T(8,128)(2,1)S(1)}, u32[]{:S(2)}, u32[]{:S(2)}) collective-permute-start(bf16[320,128]{1,0:T(8,128)(2,1)S(1)} %get-tuple-element.41), channel_id=1, source_target_pairs={{0,2},{2,0},{4,6},{6,4},{8,10},{10,8},{12,14},{14,12},{1,3},{3,1},... | collective-permute-start | bytes 245768 | tf_op jit(solution)/shard_map/ppermute | solution.py:459
  43.2 0.8 collective-permute-done.5.refs_0_
  44.0 3.2 %collective-permute-done.6.refs_1_ = bf16[320,128]{1,0:T(8,128)(2,1)S(1)} collective-permute-done((bf16[320,128]{1,0:T(8,128)(2,1)S(1)}, bf16[320,128]{1,0:T(8,128)(2,1)S(1)}, u32[]{:S(2)}, u32[]{:S(2)}) %collective-permute-start.6) | collective-permute-done | bytes 81952 | tf_op jit(solution)/shard_map/ppermute | solution.py:459
  47.1 0.1 collective-permute-start.9
  47.2 0.6 collective-permute-done.7.refs_1_
  47.8 1.2 %collective-permute-done.8.refs_2_ = bf16[320,128]{1,0:T(8,128)(2,1)S(1)} collective-permute-done((bf16[320,128]{1,0:T(8,128)(2,1)S(1)}, bf16[320,128]{1,0:T(8,128)(2,1)S(1)}, u32[]{:S(2)}, u32[]{:S(2)}) %collective-permute-start.8) | collective-permute-done | bytes 81952 | tf_op jit(solution)/shard_map/ppermute | solution.py:459
  49.0 0.0 collective-permute-start.11
  49.0 0.1 collective-permute-done.10.refs_4_
  49.1 1.2 %collective-permute-done.11.refs_5_ = bf16[320,128]{1,0:T(8,128)(2,1)S(1)} collective-permute-done((bf16[320,128]{1,0:T(8,128)(2,1)S(1)}, bf16[320,128]{1,0:T(8,128)(2,1)S(1)}, u32[]{:S(2)}, u32[]{:S(2)}) %collective-permute-start.11) | collective-permute-done | bytes 81952 | tf_op jit(solution)/shard_map/ppermute | solution.py:443
  50.3 6.7 %spatial.3 = (bf16[320,128]{1,0:T(8,128)(2,1)S(1)}, bf16[320,128]{1,0:T(8,128)(2,1)S(1)}, bf16[320,128]{1,0:T(8,128)(2,1)S(1)}, bf16[320,128]{1,0:T(8,128)(2,1)S(1)}) custom-call(bf16[640,128]{1,0:T(8,128)(2,1)S(1)} %join.1.refs_0_, bf16[320,128]{1,0:T(8,128)(2,1)S(1)} %collective-permute-done.7.refs_1_, ...), custom_call_target="tpu_custom_call" | custom-call | flops 3221225472 | bytes 6000000 | tf_op jit(solution)/shard_map/spatial/pallas_call | solution.py:226
  57.0 2.5 %collective-permute-start.12 = (bf16[320,128]{1,0:T(8,128)(2,1)S(1)}, bf16[320,128]{1,0:T(8,128)(2,1)S(1)}, u32[]{:S(2)}, u32[]{:S(2)}) collective-permute-start(bf16[320,128]{1,0:T(8,128)(2,1)S(1)} %get-tuple-element.42), channel_id=1, source_target_pairs={{0,8},{4,12},{8,0},{12,4},{1,9},{5,13},{9,1},{13,5},{2,10},{6,14},... | collective-permute-start | bytes 245768 | tf_op jit(solution)/shard_map/ppermute | solution.py:461
  59.5 0.8 collective-permute-start.13
  60.3 0.3 collective-permute-start.14
  60.5 5.9 %collective-permute-done.12.refs_0_ = bf16[320,128]{1,0:T(8,128)(2,1)S(1)} collective-permute-done((bf16[320,128]{1,0:T(8,128)(2,1)S(1)}, bf16[320,128]{1,0:T(8,128)(2,1)S(1)}, u32[]{:S(2)}, u32[]{:S(2)}) %collective-permute-start.12) | collective-permute-done | bytes 81952 | tf_op jit(solution)/shard_map/ppermute | solution.py:461
  66.4 0.9 %collective-permute-done.14.refs_2_ = bf16[320,128]{1,0:T(8,128)(2,1)S(1)} collective-permute-done((bf16[320,128]{1,0:T(8,128)(2,1)S(1)}, bf16[320,128]{1,0:T(8,128)(2,1)S(1)}, u32[]{:S(2)}, u32[]{:S(2)}) %collective-permute-start.14) | collective-permute-done | bytes 81952 | tf_op jit(solution)/shard_map/ppermute | solution.py:461
  67.3 4.2 %temporal.3 = (bf16[128,320]{1,0:T(8,128)(2,1)S(1)}, bf16[128,320]{1,0:T(8,128)(2,1)S(1)}, bf16[256,320]{1,0:T(8,128)(2,1)S(1)}) custom-call(bf16[320,128]{1,0:T(8,128)(2,1)S(1)} %collective-permute-done.12.refs_0_, bf16[320,128]{1,0:T(8,128)(2,1)S(1)} %collective-permute-done.13.refs_1_, bf16[320,128]{1,0:T(8,128)(2,1)S(1)} %collective-permute-done.14.refs_2_, ...), custom_call_target="tpu_custom_call" | custom-call | flops 1132462080 | bytes 4000000 | tf_op jit(solution)/shard_map/temporal/pallas_call | solution.py:405
  71.5 2.4 %collective-permute-start.15 = (bf16[128,320]{1,0:T(8,128)(2,1)S(1)}, bf16[128,320]{1,0:T(8,128)(2,1)S(1)}, u32[]{:S(2)}, u32[]{:S(2)}) collective-permute-start(bf16[128,320]{1,0:T(8,128)(2,1)S(1)} %get-tuple-element.46), channel_id=1, source_target_pairs={{0,8},{4,12},{8,0},{12,4},{1,9},{5,13},{9,1},{13,5},{2,10},{6,14},... | collective-permute-start | bytes 245768 | tf_op jit(solution)/shard_map/ppermute | solution.py:461
  73.9 1.0 %collective-permute-start.16 = (bf16[128,320]{1,0:T(8,128)(2,1)S(1)}, bf16[128,320]{1,0:T(8,128)(2,1)S(1)}, u32[]{:S(2)}, u32[]{:S(2)}) collective-permute-start(bf16[128,320]{1,0:T(8,128)(2,1)S(1)} %get-tuple-element.47), channel_id=1, source_target_pairs={{0,12},{4,8},{8,4},{12,0},{1,13},{5,9},{9,5},{13,1},{2,14},{6,10},... | collective-permute-start | bytes 245768 | tf_op jit(solution)/shard_map/ppermute | solution.py:461
  74.9 1.4 %feed.3 = (bf16[128,320]{1,0:T(8,128)(2,1)S(1)}, bf16[128,320]{1,0:T(8,128)(2,1)S(1)}) custom-call(bf16[256,320]{1,0:T(8,128)(2,1)S(1)} %get-tuple-element.48.refs_0_, bf16[320,2560]{1,0:T(8,128)(2,1)S(1)} %bitcast.18, bf16[320,1280]{1,0:T(8,128)(2,1)S(1)} %bitcast.22), custom_call_target="tpu_custom_call" | custom-call | flops 629145600 | bytes 3000000 | tf_op jit(solution)/shard_map/feed/pallas_call | solution.py:424
  76.3 0.2 collective-permute-start.17
  76.5 5.2 %collective-permute-done.15 = bf16[128,320]{1,0:T(8,128)(2,1)S(1)} collective-permute-done((bf16[128,320]{1,0:T(8,128)(2,1)S(1)}, bf16[128,320]{1,0:T(8,128)(2,1)S(1)}, u32[]{:S(2)}, u32[]{:S(2)}) %collective-permute-start.15) | collective-permute-done | bytes 81952 | tf_op jit(solution)/shard_map/ppermute | solution.py:461
  81.8 1.2 %collective-permute-done.17 = bf16[128,320]{1,0:T(8,128)(2,1)S(1)} collective-permute-done((bf16[128,320]{1,0:T(8,128)(2,1)S(1)}, bf16[128,320]{1,0:T(8,128)(2,1)S(1)}, u32[]{:S(2)}, u32[]{:S(2)}) %collective-permute-start.17) | collective-permute-done | bytes 81952 | tf_op jit(solution)/shard_map/ppermute | solution.py:461
  83.1 0.0 copy-start.7
  83.1 0.7 copy-done.7
  (24 shorter events, 0.2 us)
Async XLA Ops:
  0.0 12.4 %copy-start = (bf16[1,320,320]{2,1,0:T(8,128)(2,1)S(1)}, bf16[1,320,320]{2,1,0:T(8,128)(2,1)}, u32[]{:S(2)}) copy-start(bf16[1,320,320]{2,1,0:T(8,128)(2,1)} %param.13) | copy-start | bytes 614404
  0.0 12.3 %collective-permute-start = (bf16[512,320]{1,0:T(8,128)(2,1)}, bf16[512,320]{1,0:T(8,128)(2,1)S(1)}, u32[]{:S(2)}, u32[]{:S(2)}) collective-permute-start(bf16[512,320]{1,0:T(8,128)(2,1)} %bitcast.28), channel_id=1, source_target_pairs={{0,2},{2,0},{1,3},{3,1},{4,6},{6,4},{5,7},{7,5},{8,10},{10,8},{9,1... | collective-permute-start | bytes 983048 | tf_op jit(solution)/shard_map/ppermute | solution.py:443
  2.9 1.6 %copy-start.3 = (bf16[1,3,3,320,320]{4,3,2,1,0:T(8,128)(2,1)S(1)}, bf16[1,3,3,320,320]{4,3,2,1,0:T(8,128)(2,1)}, u32[]{:S(2)}) copy-start(bf16[1,3,3,320,320]{4,3,2,1,0:T(8,128)(2,1)} %param.11) | copy-start | bytes 5529604
  4.6 1.6 %copy-start.4 = (bf16[1,3,3,320,320]{4,3,2,1,0:T(8,128)(2,1)S(1)}, bf16[1,3,3,320,320]{4,3,2,1,0:T(8,128)(2,1)}, u32[]{:S(2)}) copy-start(bf16[1,3,3,320,320]{4,3,2,1,0:T(8,128)(2,1)} %param.12) | copy-start | bytes 5529604
  6.2 1.1 %copy-start.5 = (bf16[1,320,960]{2,1,0:T(8,128)(2,1)S(1)}, bf16[1,320,960]{2,1,0:T(8,128)(2,1)}, u32[]{:S(2)}) copy-start(bf16[1,320,960]{2,1,0:T(8,128)(2,1)} %param.14) | copy-start | bytes 1843204
  7.3 0.8 copy-start.8
  12.3 1.7 %collective-permute-start.1 = (bf16[512,320]{1,0:T(8,128)(2,1)S(1)}, bf16[512,320]{1,0:T(8,128)(2,1)S(1)}, u32[]{:S(2)}, u32[]{:S(2)}) collective-permute-start(bf16[512,320]{1,0:T(8,128)(2,1)S(1)} %collective-permute-done.refs_0_), channel_id=1, source_target_pairs={{0,1},{1,0},{2,3},{3,2},{4,5},{5,4},{6,7},{7,6},{8,9},{9,8},{10,11... | collective-permute-start | bytes 983048 | tf_op jit(solution)/shard_map/ppermute | solution.py:443
  12.6 18.4 %copy-start.1 = (bf16[1,320,2560]{2,1,0:T(8,128)(2,1)S(1)}, bf16[1,320,2560]{2,1,0:T(8,128)(2,1)}, u32[]{:S(2)}) copy-start(bf16[1,320,2560]{2,1,0:T(8,128)(2,1)} %param.16) | copy-start | bytes 4915204
  12.6 18.4 %copy-start.2 = (bf16[1,1280,320]{1,2,0:T(8,128)(2,1)S(1)}, bf16[1,1280,320]{1,2,0:T(8,128)(2,1)}, u32[]{:S(2)}) copy-start(bf16[1,1280,320]{1,2,0:T(8,128)(2,1)} %param.17) | copy-start | bytes 2457604
  12.6 18.4 %copy-start.6 = (bf16[1,320,320]{2,1,0:T(8,128)(2,1)S(1)}, bf16[1,320,320]{2,1,0:T(8,128)(2,1)}, u32[]{:S(2)}) copy-start(bf16[1,320,320]{2,1,0:T(8,128)(2,1)} %param.15) | copy-start | bytes 614404
  20.5 9.4 %collective-permute-start.2 = (bf16[320,128]{1,0:T(8,128)(2,1)S(1)}, bf16[320,128]{1,0:T(8,128)(2,1)S(1)}, u32[]{:S(2)}, u32[]{:S(2)}) collective-permute-start(bf16[320,128]{1,0:T(8,128)(2,1)S(1)} %get-tuple-element.32), channel_id=1, source_target_pairs={{0,8},{4,12},{8,0},{12,4},{1,9},{5,13},{9,1},{13,5},{2,10},{6,14},... | collective-permute-start | bytes 245768 | tf_op jit(solution)/shard_map/ppermute | solution.py:461
  23.4 6.9 %collective-permute-start.3 = (bf16[320,128]{1,0:T(8,128)(2,1)S(1)}, bf16[320,128]{1,0:T(8,128)(2,1)S(1)}, u32[]{:S(2)}, u32[]{:S(2)}) collective-permute-start(bf16[320,128]{1,0:T(8,128)(2,1)S(1)} %get-tuple-element.33), channel_id=1, source_target_pairs={{0,12},{4,8},{8,4},{12,0},{1,13},{5,9},{9,5},{13,1},{2,14},{6,10},... | collective-permute-start | bytes 245768 | tf_op jit(solution)/shard_map/ppermute | solution.py:461
  24.7 6.3 %collective-permute-start.4 = (bf16[320,128]{1,0:T(8,128)(2,1)S(1)}, bf16[320,128]{1,0:T(8,128)(2,1)S(1)}, u32[]{:S(2)}, u32[]{:S(2)}) collective-permute-start(bf16[320,128]{1,0:T(8,128)(2,1)S(1)} %get-tuple-element.34), channel_id=1, source_target_pairs={{0,4},{4,0},{8,12},{12,8},{1,5},{5,1},{9,13},{13,9},{2,6},{6,2},{1... | collective-permute-start | bytes 245768 | tf_op jit(solution)/shard_map/ppermute | solution.py:461
  35.3 8.7 %collective-permute-start.5 = (bf16[320,128]{1,0:T(8,128)(2,1)S(1)}, bf16[320,128]{1,0:T(8,128)(2,1)S(1)}, u32[]{:S(2)}, u32[]{:S(2)}) collective-permute-start(bf16[320,128]{1,0:T(8,128)(2,1)S(1)} %get-tuple-element.37), channel_id=1, source_target_pairs={{0,10},{2,8},{4,14},{6,12},{8,2},{10,0},{12,6},{14,4},{1,11},{3,9}... | collective-permute-start | bytes 245768 | tf_op jit(solution)/shard_map/ppermute | solution.py:459
  39.3 7.8 %collective-permute-start.6 = (bf16[320,128]{1,0:T(8,128)(2,1)S(1)}, bf16[320,128]{1,0:T(8,128)(2,1)S(1)}, u32[]{:S(2)}, u32[]{:S(2)}) collective-permute-start(bf16[320,128]{1,0:T(8,128)(2,1)S(1)} %get-tuple-element.38), channel_id=1, source_target_pairs={{0,14},{2,12},{4,10},{6,8},{8,6},{10,4},{12,2},{14,0},{1,15},{3,13... | collective-permute-start | bytes 245768 | tf_op jit(solution)/shard_map/ppermute | solution.py:459
  41.2 6.7 %collective-permute-start.7 = (bf16[320,128]{1,0:T(8,128)(2,1)S(1)}, bf16[320,128]{1,0:T(8,128)(2,1)S(1)}, u32[]{:S(2)}, u32[]{:S(2)}) collective-permute-start(bf16[320,128]{1,0:T(8,128)(2,1)S(1)} %get-tuple-element.40), channel_id=1, source_target_pairs={{0,6},{2,4},{4,2},{6,0},{8,14},{10,12},{12,10},{14,8},{1,7},{3,5},... | collective-permute-start | bytes 245768 | tf_op jit(solution)/shard_map/ppermute | solution.py:459
  42.2 6.8 %collective-permute-start.8 = (bf16[320,128]{1,0:T(8,128)(2,1)S(1)}, bf16[320,128]{1,0:T(8,128)(2,1)S(1)}, u32[]{:S(2)}, u32[]{:S(2)}) collective-permute-start(bf16[320,128]{1,0:T(8,128)(2,1)S(1)} %get-tuple-element.41), channel_id=1, source_target_pairs={{0,2},{2,0},{4,6},{6,4},{8,10},{10,8},{12,14},{14,12},{1,3},{3,1},... | collective-permute-start | bytes 245768 | tf_op jit(solution)/shard_map/ppermute | solution.py:459
  47.1 3.2 %collective-permute-start.9 = (bf16[640,128]{1,0:T(8,128)(2,1)S(1)}, bf16[640,128]{1,0:T(8,128)(2,1)S(1)}, u32[]{:S(2)}, u32[]{:S(2)}) collective-permute-start(bf16[640,128]{1,0:T(8,128)(2,1)S(1)} %join.1.refs_0_), channel_id=1, source_target_pairs={{0,1},{1,0},{2,3},{3,2},{4,5},{5,4},{6,7},{7,6},{8,9},{9,8},{10,11... | collective-permute-start | bytes 491528 | tf_op jit(solution)/shard_map/ppermute | solution.py:443
  47.8 1.3 %collective-permute-start.10 = (bf16[320,128]{1,0:T(8,128)(2,1)S(1)}, bf16[320,128]{1,0:T(8,128)(2,1)S(1)}, u32[]{:S(2)}, u32[]{:S(2)}) collective-permute-start(bf16[320,128]{1,0:T(8,128)(2,1)S(1)} %collective-permute-done.7.refs_1_), channel_id=1, source_target_pairs={{0,1},{1,0},{2,3},{3,2},{4,5},{5,4},{6,7},{7,6},{8,9},{9,8},{10,11... | collective-permute-start | bytes 245768 | tf_op jit(solution)/shard_map/ppermute | solution.py:443
  49.0 1.3 %collective-permute-start.11 = (bf16[320,128]{1,0:T(8,128)(2,1)S(1)}, bf16[320,128]{1,0:T(8,128)(2,1)S(1)}, u32[]{:S(2)}, u32[]{:S(2)}) collective-permute-start(bf16[320,128]{1,0:T(8,128)(2,1)S(1)} %collective-permute-done.8.refs_2_), channel_id=1, source_target_pairs={{0,1},{1,0},{2,3},{3,2},{4,5},{5,4},{6,7},{7,6},{8,9},{9,8},{10,11... | collective-permute-start | bytes 245768 | tf_op jit(solution)/shard_map/ppermute | solution.py:443
  57.0 9.4 %collective-permute-start.12 = (bf16[320,128]{1,0:T(8,128)(2,1)S(1)}, bf16[320,128]{1,0:T(8,128)(2,1)S(1)}, u32[]{:S(2)}, u32[]{:S(2)}) collective-permute-start(bf16[320,128]{1,0:T(8,128)(2,1)S(1)} %get-tuple-element.42), channel_id=1, source_target_pairs={{0,8},{4,12},{8,0},{12,4},{1,9},{5,13},{9,1},{13,5},{2,10},{6,14},... | collective-permute-start | bytes 245768 | tf_op jit(solution)/shard_map/ppermute | solution.py:461
  59.5 6.9 %collective-permute-start.13 = (bf16[320,128]{1,0:T(8,128)(2,1)S(1)}, bf16[320,128]{1,0:T(8,128)(2,1)S(1)}, u32[]{:S(2)}, u32[]{:S(2)}) collective-permute-start(bf16[320,128]{1,0:T(8,128)(2,1)S(1)} %get-tuple-element.43), channel_id=1, source_target_pairs={{0,12},{4,8},{8,4},{12,0},{1,13},{5,9},{9,5},{13,1},{2,14},{6,10},... | collective-permute-start | bytes 245768 | tf_op jit(solution)/shard_map/ppermute | solution.py:461
  60.3 7.0 %collective-permute-start.14 = (bf16[320,128]{1,0:T(8,128)(2,1)S(1)}, bf16[320,128]{1,0:T(8,128)(2,1)S(1)}, u32[]{:S(2)}, u32[]{:S(2)}) collective-permute-start(bf16[320,128]{1,0:T(8,128)(2,1)S(1)} %get-tuple-element.44), channel_id=1, source_target_pairs={{0,4},{4,0},{8,12},{12,8},{1,5},{5,1},{9,13},{13,9},{2,6},{6,2},{1... | collective-permute-start | bytes 245768 | tf_op jit(solution)/shard_map/ppermute | solution.py:461
  71.5 10.2 %collective-permute-start.15 = (bf16[128,320]{1,0:T(8,128)(2,1)S(1)}, bf16[128,320]{1,0:T(8,128)(2,1)S(1)}, u32[]{:S(2)}, u32[]{:S(2)}) collective-permute-start(bf16[128,320]{1,0:T(8,128)(2,1)S(1)} %get-tuple-element.46), channel_id=1, source_target_pairs={{0,8},{4,12},{8,0},{12,4},{1,9},{5,13},{9,1},{13,5},{2,10},{6,14},... | collective-permute-start | bytes 245768 | tf_op jit(solution)/shard_map/ppermute | solution.py:461
  73.9 7.9 %collective-permute-start.16 = (bf16[128,320]{1,0:T(8,128)(2,1)S(1)}, bf16[128,320]{1,0:T(8,128)(2,1)S(1)}, u32[]{:S(2)}, u32[]{:S(2)}) collective-permute-start(bf16[128,320]{1,0:T(8,128)(2,1)S(1)} %get-tuple-element.47), channel_id=1, source_target_pairs={{0,12},{4,8},{8,4},{12,0},{1,13},{5,9},{9,5},{13,1},{2,14},{6,10},... | collective-permute-start | bytes 245768 | tf_op jit(solution)/shard_map/ppermute | solution.py:461
  76.3 6.7 %collective-permute-start.17 = (bf16[128,320]{1,0:T(8,128)(2,1)S(1)}, bf16[128,320]{1,0:T(8,128)(2,1)S(1)}, u32[]{:S(2)}, u32[]{:S(2)}) collective-permute-start(bf16[128,320]{1,0:T(8,128)(2,1)S(1)} %get-tuple-element.49), channel_id=1, source_target_pairs={{0,4},{4,0},{8,12},{12,8},{1,5},{5,1},{9,13},{13,9},{2,6},{6,2},{1... | collective-permute-start | bytes 245768 | tf_op jit(solution)/shard_map/ppermute | solution.py:461
  83.1 0.7 copy-start.7

commit v3 on v2

--- a/solution.py
+++ b/solution.py
@@ -65,42 +65,89 @@
     return blocks
 
 
-def window_sum(values, width, direction):
-    lanes = values.shape[1]
-    done, result, power, size = 0, None, values, 1
-    while True:
-        if width & size:
-            moved = power
-            if done:
-                moved = pltpu.roll(power, done if direction > 0 else lanes - done, 1)
-            result = moved if result is None else result + moved
-            done += size
-        if done == width:
-            return result
-        power = power + pltpu.roll(power, size if direction > 0 else lanes - size, 1)
-        size *= 2
-
-
 def group_scale(total, square, entries, group_width, channels):
     lanes = total.shape[1]
     lane = lax.broadcasted_iota(jnp.int32, (1, lanes), 1)
-    last = (lane % group_width == group_width - 1) & (lane < channels)
-
-    def mean(sums):
-        sums = window_sum(jnp.broadcast_to(jnp.sum(sums, axis=0, keepdims=True), (8, lanes)), group_width, 1)
-        return window_sum(jnp.where(last, sums, 0.0), group_width, -1)[0:1] / entries
-
-    average = mean(total)
-    scale = lax.rsqrt(mean(square) - average * average + 1e-05)
+    spot = lane % group_width
+    row = lax.broadcasted_iota(jnp.int32, (8, 1), 0)
+    both = jnp.where(
+        row == 0, jnp.sum(total, axis=0, keepdims=True), jnp.sum(square, axis=0, keepdims=True)
+    )
+    group = both
+    for k in range(1, group_width):
+        group = group + jnp.where(spot + k < group_width, pltpu.roll(both, lanes - k, 1), 0.0)
+        group = group + jnp.where(spot >= k, pltpu.roll(both, k, 1), 0.0)
+    group = group / entries
+    average = group[0:1]
+    scale = lax.rsqrt(group[1:2] - average * average + 1e-05)
     scale = jnp.where(lane < channels, 0.5 * scale, 0.0)
     return scale, -average * scale
 
 
-def spatial_kernel(rows, half, columns, channels, group_width, step, ways, shards, *refs):
+def activate(source, targets, scale, shift, rows, columns, first, start, stop):
+    middle, edge, pair = targets
+
+    def body(i, before):
+        row = first - 1 + i
+        inside = ((row >= 0) & (row < rows)).astype(F32)
+        at = pl.multiple_of(jnp.clip(row, 0, rows - 1) * columns, columns)
+        u = source[pl.ds(at, columns), :] * (scale * inside) + shift * inside
+        g = u + u * jnp.tanh(u)
+        to = pl.ds(pl.multiple_of(i * columns, columns), columns)
+        rest = g[:, WIDE:]
+        middle[to, :] = g[:, :WIDE].astype(BF16)
+        edge[to, :] = rest.astype(BF16)
+        pair[to, :] = (before + pltpu.roll(rest, LANES // 2, 1)).astype(BF16)
+        return rest
+
+    lax.fori_loop(start, stop, body, jnp.zeros((columns, LANES), F32), unroll=stop - start)
+
+
+def convolve(targets, kernel, start, count, columns):
+    middle, edge, pair = targets
+    top, mid, bottom = [
+        pl.ds(pl.multiple_of(start + r * columns, columns), count) for r in range(3)
+    ]
+    window = jnp.concatenate(
+        [middle[top, :], middle[mid, :], middle[bottom, :], pair[mid, :], edge[bottom, :]], axis=1
+    )
+    y = jnp.dot(window, kernel[...], preferred_element_type=F32)
+    column = lax.broadcasted_iota(jnp.int32, (count, 1), 0) % columns
+
+    def from_left(values):
+        return jnp.where(column == 0, 0.0, pltpu.roll(values, 1, 0))
+
+    def from_right(values):
+        return jnp.where(column == columns - 1, 0.0, pltpu.roll(values, count - 1, 0))
+
+    wide = y[:, WIDE : 2 * WIDE] + from_left(y[:, :WIDE]) + from_right(y[:, 2 * WIDE : 3 * WIDE])
+    tail = y[:, 3 * WIDE : 3 * WIDE + LANES]
+    return wide, from_left(tail) + from_right(y[:, 3 * WIDE + LANES :]), tail
+
+
+def convolve_part(targets, kernel, start, columns, base, target):
+    pixels = base.shape[0]
+    wide, narrow, tail = convolve(targets, kernel, start, pixels, columns)
+    for i in range(WIDE // LANES):
+        lanes = slice(i * LANES, (i + 1) * LANES)
+        target[i * pixels : (i + 1) * pixels, :] = (wide[:, lanes] + base[:, lanes]).astype(BF16)
+    narrow = narrow + base[:, WIDE:]
+    low = lax.broadcasted_iota(jnp.int32, (1, LANES), 1) < LANES // 2
+    first, second = slice(0, pixels // 2), slice(pixels // 2, pixels)
+    both = jnp.where(
+        low,
+        narrow[first] + pltpu.roll(tail[first], LANES // 2, 1),
+        pltpu.roll(narrow[second], LANES // 2, 1) + tail[second],
+    )
+    target[WIDE // LANES * pixels :, :] = both.astype(BF16)
+
+
+def spatial_kernel(rows, half, columns, channels, group_width, step, ways, shards, sooner, *refs):
     own, other = refs[:ways], refs[ways : 2 * ways]
     kernels, embeds = refs[2 * ways : 2 * ways + 2]
-    outs = refs[2 * ways + 2 : 2 * ways + 2 + shards]
-    field, hidden, middle, edge, pair = refs[2 * ways + 2 + shards :]
+    outs = refs[2 * ways + 2 : 2 * ways + 2 + sooner]
+    keep, *targets = refs[2 * ways + 2 + sooner : 2 * ways + 6 + sooner]
+    field, hidden, *firsts = refs[2 * ways + 6 + sooner :]
     embed = embeds[step : step + 1, :]
     lanes = field.shape[1]
     own_rows = rows // half
@@ -131,76 +178,45 @@
         chunk = chunk.reshape(columns // 8, 8, lanes)
         return total + jnp.sum(chunk, axis=0), square + jnp.sum(chunk * chunk, axis=0)
 
-    field_sums = lax.fori_loop(0, rows, sum_row, (zero, zero), unroll=4)
-
-    def activate(source, scale, shift, first, start, stop):
-        def body(i, before):
-            row = first - 1 + i
-            inside = ((row >= 0) & (row < rows)).astype(F32)
-            at = pl.multiple_of(jnp.clip(row, 0, rows - 1) * columns, columns)
-            u = source[pl.ds(at, columns), :] * (scale * inside) + shift * inside
-            g = u + u * jnp.tanh(u)
-            to = pl.ds(pl.multiple_of(i * columns, columns), columns)
-            rest = g[:, WIDE:]
-            middle[to, :] = g[:, :WIDE].astype(BF16)
-            edge[to, :] = rest.astype(BF16)
-            pair[to, :] = (before + pltpu.roll(rest, LANES // 2, 1)).astype(BF16)
-            return rest
-
-        lax.fori_loop(start, stop, body, jnp.zeros((columns, LANES), F32), unroll=4)
-
-    step_rows = min(WIDE, own_rows * columns)
-    column = lax.broadcasted_iota(jnp.int32, (step_rows, 1), 0) % columns
-    low = lax.broadcasted_iota(jnp.int32, (1, LANES), 1) < channels - WIDE
-
-    def convolve(kernel, start):
-        top, mid, bottom = [slice(start + r * columns, start + r * columns + step_rows) for r in range(3)]
-        window = jnp.concatenate(
-            [middle[top, :], middle[mid, :], middle[bottom, :], pair[mid, :], edge[bottom, :]], axis=1
-        )
-        y = jnp.dot(window, kernel[...], preferred_element_type=F32)
-
-        def from_left(values):
-            return jnp.where(column == 0, 0.0, pltpu.roll(values, 1, 0))
-
-        def from_right(values):
-            return jnp.where(column == columns - 1, 0.0, pltpu.roll(values, step_rows - 1, 0))
-
-        wide = y[:, WIDE : 2 * WIDE] + from_left(y[:, :WIDE]) + from_right(y[:, 2 * WIDE : 3 * WIDE])
-        tail = y[:, 3 * WIDE : 3 * WIDE + LANES]
-        narrow = from_left(tail) + pltpu.roll(tail, LANES // 2, 1) + from_right(y[:, 3 * WIDE + LANES :])
-        return wide, narrow
-
+    total, square = lax.fori_loop(0, rows, sum_row, (zero, zero), unroll=4)
     entries = float(rows * columns * group_width)
+    middle, edge, _ = firsts
     for pad in (0, (rows + 1) * columns):
         middle[pad : pad + columns, :] = jnp.zeros((columns, WIDE), BF16)
         edge[pad : pad + columns, :] = jnp.zeros((columns, LANES), BF16)
-    activate(field, *group_scale(*field_sums, entries, group_width, channels), 0, 1, rows + 1)
+    scale, shift = group_scale(total, square, entries, group_width, channels)
+    activate(field, firsts, scale, shift, rows, columns, 0, 1, rows + 1)
+
+    low = lax.broadcasted_iota(jnp.int32, (1, LANES), 1) < channels - WIDE
     total, square = zero, zero
-    for start in range(0, rows * columns, step_rows):
-        wide, narrow = convolve(kernels.at[0], start)
-        chunk = jnp.concatenate(
-            [wide + embed[:, :WIDE], jnp.where(low, narrow + embed[:, WIDE:], 0.0)], axis=1
-        )
-        hidden[start : start + step_rows, :] = chunk
-        chunk = chunk.reshape(step_rows // 8, 8, lanes)
+    count = min(WIDE, own_rows * columns)
+    for start in range(0, rows * columns, count):
+        wide, narrow, tail = convolve(firsts, kernels.at[0], start, count, columns)
+        narrow = narrow + pltpu.roll(tail, LANES // 2, 1) + embed[:, WIDE:]
+        chunk = jnp.concatenate([wide + embed[:, :WIDE], jnp.where(low, narrow, 0.0)], axis=1)
+        hidden[start : start + count, :] = chunk
+        chunk = chunk.reshape(count // 8, 8, lanes)
         total = total + jnp.sum(chunk, axis=0)
         square = square + jnp.sum(chunk * chunk, axis=0)
-    activate(
-        hidden,
-        *group_scale(total, square, entries, group_width, channels),
-        here * own_rows,
-        0,
-        own_rows + 2,
-    )
-    for start in range(0, own_rows * columns, step_rows):
-        wide, narrow = convolve(kernels.at[1], start)
-        mine = pl.ds(pl.multiple_of(own_base + start, step_rows), step_rows)
-        hidden[mine, :WIDE] = wide + field[mine, :WIDE]
-        hidden[mine, WIDE:] = narrow + field[mine, WIDE:]
+    scale, shift = group_scale(total, square, entries, group_width, channels)
+    first_row = here * own_rows
+    activate(hidden, targets, scale, shift, rows, columns, first_row, 0, own_rows + 2)
     for i, d in enumerate(distances(shards)):
-        place = pl.multiple_of(own_base + partner(spot, d, shards) * part, part)
-        pack_part(hidden[pl.ds(place, part), :], outs[i], 0, channels)
+        start = partner(spot, d, shards) * part
+        base = field[pl.ds(pl.multiple_of(own_base + start, 8), part), :]
+        if i < sooner:
+            convolve_part(targets, kernels.at[1], start, columns, base, outs[i])
+        else:
+            keep[(i - sooner) * part : (i - sooner + 1) * part, :] = base
+
+
+def finish_kernel(columns, shards, sooner, keep, middle, edge, pair, kernels, *outs):
+    part = keep.shape[0] // (shards - sooner)
+    spot = lax.axis_index("shard")
+    for i, d in enumerate(distances(shards)[sooner:]):
+        start = partner(spot, d, shards) * part
+        base = keep[i * part : (i + 1) * part, :]
+        convolve_part((middle, edge, pair), kernels.at[1], start, columns, base, outs[i])
 
 
 def spatial(own, other, weights, embeds, step, rows, columns, half, shards):
@@ -208,34 +224,41 @@
     part = tokens // half // shards
     channels = sum(block.size for block in own) // (tokens // half)
     ways = len(own)
+    sooner = shards // 2
+    later = shards - sooner
     lanes = round_up(channels, LANES)
-    padded = tokens + 2 * columns
     depth = weights.shape[1]
-    kernel = functools.partial(
-        spatial_kernel,
-        rows,
-        half,
-        columns,
-        channels,
-        channels // GROUPS,
-        step,
-        ways,
-        shards,
-    )
+    piece = jax.ShapeDtypeStruct((dense_rows(part, channels), LANES), BF16)
     vmem = pl.BlockSpec(memory_space=pltpu.VMEM)
-    return pl.pallas_call(
-        kernel,
-        out_shape=[jax.ShapeDtypeStruct((dense_rows(part, channels), LANES), BF16)] * shards,
+    params = pltpu.CompilerParams(vmem_limit_bytes=14 * 1024 * 1024)
+
+    def active(rows_there):
+        return [((rows_there + 2) * columns, width) for width in (WIDE, LANES, LANES)]
+
+    *first, keep, middle, edge, pair = pl.pallas_call(
+        functools.partial(
+            spatial_kernel,
+            rows,
+            half,
+            columns,
+            channels,
+            channels // GROUPS,
+            step,
+            ways,
+            shards,
+            sooner,
+        ),
+        out_shape=[piece] * sooner
+        + [jax.ShapeDtypeStruct((later * part, lanes), F32)]
+        + [jax.ShapeDtypeStruct(shape, BF16) for shape in active(rows // half)],
         in_specs=[vmem] * (2 * ways + 2),
-        out_specs=[vmem] * shards,
+        out_specs=[vmem] * (sooner + 4),
         scratch_shapes=[
             pltpu.VMEM((tokens, lanes), F32),
             pltpu.VMEM((tokens, lanes), F32),
-            pltpu.VMEM((padded, WIDE), BF16),
-            pltpu.VMEM((padded, LANES), BF16),
-            pltpu.VMEM((padded, LANES), BF16),
+            *[pltpu.VMEM(shape, BF16) for shape in active(rows)],
         ],
-        compiler_params=pltpu.CompilerParams(vmem_limit_bytes=14 * 1024 * 1024),
+        compiler_params=params,
         cost_estimate=pl.CostEstimate(
             flops=3 * tokens * depth * depth,
             bytes_accessed=6000000,
@@ -243,6 +266,18 @@
         ),
         name="spatial",
     )(*own, *other, weights, embeds)
+    second = pl.pallas_call(
+        functools.partial(finish_kernel, columns, shards, sooner),
+        out_shape=[piece] * later,
+        in_specs=[vmem] * 5,
+        out_specs=[vmem] * later,
+        compiler_params=params,
+        cost_estimate=pl.CostEstimate(
+            flops=2 * later * part * depth * depth, bytes_accessed=3000000, transcendentals=0
+        ),
+        name="finish",
+    )(keep, middle, edge, pair, weights)
+    return [*first, *second]
 
 
 def prepare_kernel(channels, kernel1, kernel2, qkv, kernels, padded):
@@ -328,18 +363,20 @@
         leave(done[i * pixels : (i + 1) * pixels, :], outs[i])
 
 
-def temporal_kernel(frames, sooner, *refs):
-    parts = refs[:frames]
-    qkv, attn_out, geglu_in, geglu_out = refs[frames : frames + 4]
-    outs = refs[frames + 4 : frames + 4 + sooner]
-    rest = refs[frames + 4 + sooner]
-    stream, projected, mixed, active = refs[frames + 5 + sooner :]
+def temporal_kernel(frames, ways, sooner, *refs):
+    parts = refs[:ways]
+    qkv, attn_out, geglu_in, geglu_out = refs[ways : ways + 4]
+    outs = refs[ways + 4 : ways + 4 + sooner]
+    rest = refs[ways + 4 + sooner]
+    stream, projected, mixed, active = refs[ways + 5 + sooner :]
     channels = stream.shape[1]
     pixels = stream.shape[0] // frames
     lanes = projected.shape[1] // 3
 
-    for f in range(frames):
-        for i, first, values in unpack_part(parts[f], 0, pixels, channels):
+    height = dense_rows(pixels, channels)
+    held = [(block, at) for block in parts for at in range(0, block.shape[0], height)]
+    for f, (block, at) in enumerate(held):
+        for i, first, values in unpack_part(block, at, pixels, channels):
             rows = slice(f * pixels + first, f * pixels + first + values.shape[0])
             width = min(LANES, channels - i * LANES)
             stream[rows, i * LANES : i * LANES + width] = values[:, :width].astype(BF16)
@@ -390,22 +427,25 @@
 
 
 def temporal(parts, weights, dense):
-    frames = len(parts)
+    ways = len(parts)
+    frames = lax.axis_size("shard")
     sooner = frames // 2
     later = frames - sooner
     channels = weights[0].shape[0]
-    pixels = parts[0].size // channels
+    pixels = sum(part.size for part in parts) // channels // frames
     lanes = round_up(channels, LANES)
     tokens = frames * pixels
     inner = weights[3].shape[1]
     vmem = pl.BlockSpec(memory_space=pltpu.VMEM)
-    piece = jax.ShapeDtypeStruct(parts[0].shape if dense else (pixels, channels), BF16)
+    piece = jax.ShapeDtypeStruct(
+        (dense_rows(pixels, channels), LANES) if dense else (pixels, channels), BF16
+    )
     feed_flops = 6 * pixels * channels * inner
     params = pltpu.CompilerParams(vmem_limit_bytes=14 * 1024 * 1024)
     *first, rest = pl.pallas_call(
-        functools.partial(temporal_kernel, frames, sooner),
+        functools.partial(temporal_kernel, frames, ways, sooner),
         out_shape=[piece] * sooner + [jax.ShapeDtypeStruct((later * pixels, channels), BF16)],
-        in_specs=[vmem] * (frames + 4),
+        in_specs=[vmem] * (ways + 4),
         out_specs=[vmem] * (sooner + 1),
         scratch_shapes=[
             pltpu.VMEM((tokens, channels), BF16),
@@ -538,7 +578,9 @@
             half,
             shards,
         )
-        parts = temporal(exchange(parts), temporal_weights, dense=not last)
+        parts = exchange(parts)
+        parts = [join(parts[: shards // 2]), *parts[shards // 2 :]]
+        parts = temporal(parts, temporal_weights, dense=not last)
         parts = exchange(parts, back=True, across=0 if last else 1)
         own = [join(parts[: shards // 2]), *parts[shards // 2 :]]
     return assemble(parts).reshape(features.shape)

time: 84.1 us -> 80.8 us (0.961)
  Pallas kernels: 25.1 us -> 22 us
    pallas_call x4 -> x6, Pallas kernels: 21.6 us -> 18.4 us  [the longest x2 8.46 us: temporal(): pl.pallas_call(functools.partial(temporal_kernel, frames, ways, sooner),...]
  transfers between devices with their start and end apart: 18 -> 18, of which waited for: 15 -> 15; matrix products, arithmetic and copies ran while one was open for 1% -> 1% of each run, Pallas kernels for 4% -> 6%
where the time goes in v3:
time: 80.8 us; the launch traced here: 80.6 us
  waiting for transfers between devices  31.6 us (39%)
  Pallas kernels  22 us (27%)
  starting transfers between devices  21.2 us (26%)
  local copies, waits for them, and re-layouts  5.23 us (6%)
    ppermute x9, waiting for transfers between devices, exchange(): part = lax.ppermute(part, 'shard', list(enumerate(target)))  18.8 us
    ppermute x9, starting transfers between devices, exchange(): part = lax.ppermute(part, 'shard', list(enumerate(target)))  11.8 us
    pallas_call x2, Pallas kernels, temporal(): pl.pallas_call(functools.partial(temporal_kernel, frames, ways, sooner),...  8.46 us
    pallas_call x2, Pallas kernels, spatial(): pl.pallas_call(functools.partial(spatial_kernel, rows, half, columns, cha...  8.36 us
    ppermute x5, waiting for transfers between devices, send(): lax.ppermute(block, axis, [(i, (i + distance) % count) for i in range(cou...  6.86 us
    ppermute x4, starting transfers between devices, exchange(): part = lax.ppermute(part, ('shard', 'section'), route)  6.38 us
    ppermute x4, waiting for transfers between devices, exchange(): part = lax.ppermute(part, ('shard', 'section'), route)  5.96 us
    unnamed x18, local copies, waits for them, and re-layouts  5.09 us
  transfers between devices with their start and end apart: 18, of which 15 were waited for; matrix products, arithmetic and copies ran while one was open for 1% of the time, Pallas kernels for 6%

profile of v3, /device:TPU:0, one launch (start us, length us, event | category | flops | bytes accessed | tf_op | source)
XLA Modules:
  0.0 80.6 jit_solution(18403369128842318073)
XLA Ops:
  0.0 2.9 %collective-permute-start = (bf16[512,320]{1,0:T(8,128)(2,1)}, bf16[512,320]{1,0:T(8,128)(2,1)S(1)}, u32[]{:S(2)}, u32[]{:S(2)}) collective-permute-start(bf16[512,320]{1,0:T(8,128)(2,1)} %bitcast.28), channel_id=1, source_target_pairs={{0,2},{2,0},{1,3},{3,1},{4,6},{6,4},{5,7},{7,5},{8,10},{10,8},{9,1... | collective-permute-start | bytes 983048 | tf_op jit(solution)/shard_map/ppermute | solution.py:483
  2.9 1.6 %copy-done.3 = bf16[1,3,3,320,320]{4,3,2,1,0:T(8,128)(2,1)S(1)} copy-done((bf16[1,3,3,320,320]{4,3,2,1,0:T(8,128)(2,1)S(1)}, bf16[1,3,3,320,320]{4,3,2,1,0:T(8,128)(2,1)}, u32[]{:S(2)}) %copy-start.3) | copy-done | bytes 1843224
  4.6 1.6 %copy-done.4 = bf16[1,3,3,320,320]{4,3,2,1,0:T(8,128)(2,1)S(1)} copy-done((bf16[1,3,3,320,320]{4,3,2,1,0:T(8,128)(2,1)S(1)}, bf16[1,3,3,320,320]{4,3,2,1,0:T(8,128)(2,1)}, u32[]{:S(2)}) %copy-start.4) | copy-done | bytes 1843224
  6.2 1.1 %copy-done.5 = bf16[1,320,960]{2,1,0:T(8,128)(2,1)S(1)} copy-done((bf16[1,320,960]{2,1,0:T(8,128)(2,1)S(1)}, bf16[1,320,960]{2,1,0:T(8,128)(2,1)}, u32[]{:S(2)}) %copy-start.5) | copy-done | bytes 614424
  7.3 0.7 prepare.1
  8.0 4.2 %collective-permute-done.refs_0_ = bf16[512,320]{1,0:T(8,128)(2,1)S(1)} collective-permute-done((bf16[512,320]{1,0:T(8,128)(2,1)}, bf16[512,320]{1,0:T(8,128)(2,1)S(1)}, u32[]{:S(2)}, u32[]{:S(2)}) %collective-permute-start) | collective-permute-done | bytes 327712 | tf_op jit(solution)/shard_map/ppermute | solution.py:483
  12.3 0.0 collective-permute-start.1
  12.3 0.1 multiply_cosine_fusion
  12.4 0.2 fusion
  12.6 1.4 %collective-permute-done.1.refs_1_ = bf16[512,320]{1,0:T(8,128)(2,1)S(1)} collective-permute-done((bf16[512,320]{1,0:T(8,128)(2,1)S(1)}, bf16[512,320]{1,0:T(8,128)(2,1)S(1)}, u32[]{:S(2)}, u32[]{:S(2)}) %collective-permute-start.1) | collective-permute-done | bytes 327712 | tf_op jit(solution)/shard_map/ppermute | solution.py:483
  14.0 4.1 %spatial.2 = (bf16[320,128]{1,0:T(8,128)(2,1)S(1)}, bf16[320,128]{1,0:T(8,128)(2,1)S(1)}, f32[256,384]{1,0:T(8,128)S(1)}, bf16[640,256]{1,0:T(8,128)(2,1)S(1)}, ...) custom-call(bf16[512,320]{1,0:T(8,128)(2,1)S(1)} %collective-permute-done.refs_0_, ...), custom_call_target="tpu_custom_call" | custom-call | flops 3221225472 | bytes 6000000 | tf_op jit(solution)/shard_map/spatial/pallas_call | solution.py:238
  18.1 2.9 %collective-permute-start.2 = (bf16[320,128]{1,0:T(8,128)(2,1)S(1)}, bf16[320,128]{1,0:T(8,128)(2,1)S(1)}, u32[]{:S(2)}, u32[]{:S(2)}) collective-permute-start(bf16[320,128]{1,0:T(8,128)(2,1)S(1)} %get-tuple-element.40), channel_id=1, source_target_pairs={{0,8},{4,12},{8,0},{12,4},{1,9},{5,13},{9,1},{13,5},{2,10},{6,14},... | collective-permute-start | bytes 245768 | tf_op jit(solution)/shard_map/ppermute | solution.py:501
  21.0 1.3 %collective-permute-start.3 = (bf16[320,128]{1,0:T(8,128)(2,1)S(1)}, bf16[320,128]{1,0:T(8,128)(2,1)S(1)}, u32[]{:S(2)}, u32[]{:S(2)}) collective-permute-start(bf16[320,128]{1,0:T(8,128)(2,1)S(1)} %get-tuple-element.41), channel_id=1, source_target_pairs={{0,12},{4,8},{8,4},{12,0},{1,13},{5,9},{9,5},{13,1},{2,14},{6,10},... | collective-permute-start | bytes 245768 | tf_op jit(solution)/shard_map/ppermute | solution.py:501
  22.3 0.8 %finish.2 = (bf16[320,128]{1,0:T(8,128)(2,1)S(1)}, bf16[320,128]{1,0:T(8,128)(2,1)S(1)}) custom-call(f32[256,384]{1,0:T(8,128)S(1)} %get-tuple-element.42.keep, bf16[640,256]{1,0:T(8,128)(2,1)S(1)} %get-tuple-element.43.middle, bf16[640,128]{1,0:T(8,128)(2,1)S(1)} %get-tuple-element.44.edge, bf16[640,128]{1,0:T(8,128)(2,1)S(1)} %get-tuple-element.45.pair, ...), custom_call_target="tpu_custom_call" | custom-call | flops 536870912 | bytes 3000000 | tf_op jit(solution)/shard_map/finish/pallas_call | solution.py:269
  23.2 0.3 collective-permute-start.4
  23.5 4.2 %collective-permute-done.2.refs_0_ = bf16[320,128]{1,0:T(8,128)(2,1)S(1)} collective-permute-done((bf16[320,128]{1,0:T(8,128)(2,1)S(1)}, bf16[320,128]{1,0:T(8,128)(2,1)S(1)}, u32[]{:S(2)}, u32[]{:S(2)}) %collective-permute-start.2) | collective-permute-done | bytes 81952 | tf_op jit(solution)/shard_map/ppermute | solution.py:501
  27.7 0.2 collective-permute-done.3.refs_1_
  27.9 1.2 %collective-permute-done.4.refs_1_ = bf16[320,128]{1,0:T(8,128)(2,1)S(1)} collective-permute-done((bf16[320,128]{1,0:T(8,128)(2,1)S(1)}, bf16[320,128]{1,0:T(8,128)(2,1)S(1)}, u32[]{:S(2)}, u32[]{:S(2)}) %collective-permute-start.4) | collective-permute-done | bytes 81952 | tf_op jit(solution)/shard_map/ppermute | solution.py:501
  29.2 4.3 %temporal.2 = (bf16[320,128]{1,0:T(8,128)(2,1)S(1)}, bf16[320,128]{1,0:T(8,128)(2,1)S(1)}, bf16[256,320]{1,0:T(8,128)(2,1)S(1)}) custom-call(bf16[640,128]{1,0:T(8,128)(2,1)S(1)} %join.3.refs_0_, bf16[320,128]{1,0:T(8,128)(2,1)S(1)} %collective-permute-done.4.refs_1_, bf16[320,128]{1,0:T(8,128)(2,1)S(1)} %get-tuple-element.47.refs_2_, ...), custom_call_target="tpu_custom_call" | custom-call | flops 1132462080 | bytes 4000000 | tf_op jit(solution)/shard_map/temporal/pallas_call | solution.py:445
  33.4 3.5 %collective-permute-start.5 = (bf16[320,128]{1,0:T(8,128)(2,1)S(1)}, bf16[320,128]{1,0:T(8,128)(2,1)S(1)}, u32[]{:S(2)}, u32[]{:S(2)}) collective-permute-start(bf16[320,128]{1,0:T(8,128)(2,1)S(1)} %get-tuple-element.49), channel_id=1, source_target_pairs={{0,10},{2,8},{4,14},{6,12},{8,2},{10,0},{12,6},{14,4},{1,11},{3,9}... | collective-permute-start | bytes 245768 | tf_op jit(solution)/shard_map/ppermute | solution.py:499
  37.0 0.8 %collective-permute-start.6 = (bf16[320,128]{1,0:T(8,128)(2,1)S(1)}, bf16[320,128]{1,0:T(8,128)(2,1)S(1)}, u32[]{:S(2)}, u32[]{:S(2)}) collective-permute-start(bf16[320,128]{1,0:T(8,128)(2,1)S(1)} %get-tuple-element.50), channel_id=1, source_target_pairs={{0,14},{2,12},{4,10},{6,8},{8,6},{10,4},{12,2},{14,0},{1,15},{3,13... | collective-permute-start | bytes 245768 | tf_op jit(solution)/shard_map/ppermute | solution.py:499
  37.8 1.4 %feed.2 = (bf16[320,128]{1,0:T(8,128)(2,1)S(1)}, bf16[320,128]{1,0:T(8,128)(2,1)S(1)}) custom-call(bf16[256,320]{1,0:T(8,128)(2,1)S(1)} %get-tuple-element.51.refs_0_, bf16[320,2560]{1,0:T(8,128)(2,1)S(1)} %bitcast.16, bf16[320,1280]{1,0:T(8,128)(2,1)S(1)} %bitcast.20), custom_call_target="tpu_custom_call" | custom-call | flops 629145600 | bytes 3000000 | tf_op jit(solution)/shard_map/feed/pallas_call | solution.py:464
  39.2 1.1 %collective-permute-start.7 = (bf16[320,128]{1,0:T(8,128)(2,1)S(1)}, bf16[320,128]{1,0:T(8,128)(2,1)S(1)}, u32[]{:S(2)}, u32[]{:S(2)}) collective-permute-start(bf16[320,128]{1,0:T(8,128)(2,1)S(1)} %get-tuple-element.52), channel_id=1, source_target_pairs={{0,6},{2,4},{4,2},{6,0},{8,14},{10,12},{12,10},{14,8},{1,7},{3,5},... | collective-permute-start | bytes 245768 | tf_op jit(solution)/shard_map/ppermute | solution.py:499
  40.4 0.9 %collective-permute-start.8 = (bf16[320,128]{1,0:T(8,128)(2,1)S(1)}, bf16[320,128]{1,0:T(8,128)(2,1)S(1)}, u32[]{:S(2)}, u32[]{:S(2)}) collective-permute-start(bf16[320,128]{1,0:T(8,128)(2,1)S(1)} %get-tuple-element.53), channel_id=1, source_target_pairs={{0,2},{2,0},{4,6},{6,4},{8,10},{10,8},{12,14},{14,12},{1,3},{3,1},... | collective-permute-start | bytes 245768 | tf_op jit(solution)/shard_map/ppermute | solution.py:499
  41.3 0.6 collective-permute-done.5.refs_0_
  41.8 2.9 %collective-permute-done.6.refs_1_ = bf16[320,128]{1,0:T(8,128)(2,1)S(1)} collective-permute-done((bf16[320,128]{1,0:T(8,128)(2,1)S(1)}, bf16[320,128]{1,0:T(8,128)(2,1)S(1)}, u32[]{:S(2)}, u32[]{:S(2)}) %collective-permute-start.6) | collective-permute-done | bytes 81952 | tf_op jit(solution)/shard_map/ppermute | solution.py:499
  44.8 0.1 collective-permute-start.9
  44.8 0.9 %collective-permute-done.7.refs_1_ = bf16[320,128]{1,0:T(8,128)(2,1)S(1)} collective-permute-done((bf16[320,128]{1,0:T(8,128)(2,1)S(1)}, bf16[320,128]{1,0:T(8,128)(2,1)S(1)}, u32[]{:S(2)}, u32[]{:S(2)}) %collective-permute-start.7) | collective-permute-done | bytes 81952 | tf_op jit(solution)/shard_map/ppermute | solution.py:499
  45.8 1.6 %collective-permute-done.8.refs_2_ = bf16[320,128]{1,0:T(8,128)(2,1)S(1)} collective-permute-done((bf16[320,128]{1,0:T(8,128)(2,1)S(1)}, bf16[320,128]{1,0:T(8,128)(2,1)S(1)}, u32[]{:S(2)}, u32[]{:S(2)}) %collective-permute-start.8) | collective-permute-done | bytes 81952 | tf_op jit(solution)/shard_map/ppermute | solution.py:499
  47.3 0.0 collective-permute-start.11
  47.3 1.3 %collective-permute-done.11.refs_5_ = bf16[320,128]{1,0:T(8,128)(2,1)S(1)} collective-permute-done((bf16[320,128]{1,0:T(8,128)(2,1)S(1)}, bf16[320,128]{1,0:T(8,128)(2,1)S(1)}, u32[]{:S(2)}, u32[]{:S(2)}) %collective-permute-start.11) | collective-permute-done | bytes 81952 | tf_op jit(solution)/shard_map/ppermute | solution.py:483
  48.6 4.3 %spatial.3 = (bf16[320,128]{1,0:T(8,128)(2,1)S(1)}, bf16[320,128]{1,0:T(8,128)(2,1)S(1)}, f32[256,384]{1,0:T(8,128)S(1)}, bf16[640,256]{1,0:T(8,128)(2,1)S(1)}, ...) custom-call(bf16[640,128]{1,0:T(8,128)(2,1)S(1)} %join.4.refs_0_, ...), custom_call_target="tpu_custom_call" | custom-call | flops 3221225472 | bytes 6000000 | tf_op jit(solution)/shard_map/spatial/pallas_call | solution.py:238
  52.9 2.6 %collective-permute-start.12 = (bf16[320,128]{1,0:T(8,128)(2,1)S(1)}, bf16[320,128]{1,0:T(8,128)(2,1)S(1)}, u32[]{:S(2)}, u32[]{:S(2)}) collective-permute-start(bf16[320,128]{1,0:T(8,128)(2,1)S(1)} %get-tuple-element.54), channel_id=1, source_target_pairs={{0,8},{4,12},{8,0},{12,4},{1,9},{5,13},{9,1},{13,5},{2,10},{6,14},... | collective-permute-start | bytes 245768 | tf_op jit(solution)/shard_map/ppermute | solution.py:501
  55.5 0.2 collective-permute-start.13
  55.7 0.8 %finish.3 = (bf16[320,128]{1,0:T(8,128)(2,1)S(1)}, bf16[320,128]{1,0:T(8,128)(2,1)S(1)}) custom-call(f32[256,384]{1,0:T(8,128)S(1)} %get-tuple-element.56.keep, bf16[640,256]{1,0:T(8,128)(2,1)S(1)} %get-tuple-element.57.middle, bf16[640,128]{1,0:T(8,128)(2,1)S(1)} %get-tuple-element.58.edge, bf16[640,128]{1,0:T(8,128)(2,1)S(1)} %get-tuple-element.59.pair, ...), custom_call_target="tpu_custom_call" | custom-call | flops 536870912 | bytes 3000000 | tf_op jit(solution)/shard_map/finish/pallas_call | solution.py:269
  56.5 0.8 %collective-permute-start.14 = (bf16[320,128]{1,0:T(8,128)(2,1)S(1)}, bf16[320,128]{1,0:T(8,128)(2,1)S(1)}, u32[]{:S(2)}, u32[]{:S(2)}) collective-permute-start(bf16[320,128]{1,0:T(8,128)(2,1)S(1)} %get-tuple-element.60), channel_id=1, source_target_pairs={{0,4},{4,0},{8,12},{12,8},{1,5},{5,1},{9,13},{13,9},{2,6},{6,2},{1... | collective-permute-start | bytes 245768 | tf_op jit(solution)/shard_map/ppermute | solution.py:501
  57.3 3.9 %collective-permute-done.12.refs_0_ = bf16[320,128]{1,0:T(8,128)(2,1)S(1)} collective-permute-done((bf16[320,128]{1,0:T(8,128)(2,1)S(1)}, bf16[320,128]{1,0:T(8,128)(2,1)S(1)}, u32[]{:S(2)}, u32[]{:S(2)}) %collective-permute-start.12) | collective-permute-done | bytes 81952 | tf_op jit(solution)/shard_map/ppermute | solution.py:501
  61.2 1.2 %collective-permute-done.13.refs_1_ = bf16[320,128]{1,0:T(8,128)(2,1)S(1)} collective-permute-done((bf16[320,128]{1,0:T(8,128)(2,1)S(1)}, bf16[320,128]{1,0:T(8,128)(2,1)S(1)}, u32[]{:S(2)}, u32[]{:S(2)}) %collective-permute-start.13) | collective-permute-done | bytes 81952 | tf_op jit(solution)/shard_map/ppermute | solution.py:501
  62.5 1.1 %collective-permute-done.14.refs_1_ = bf16[320,128]{1,0:T(8,128)(2,1)S(1)} collective-permute-done((bf16[320,128]{1,0:T(8,128)(2,1)S(1)}, bf16[320,128]{1,0:T(8,128)(2,1)S(1)}, u32[]{:S(2)}, u32[]{:S(2)}) %collective-permute-start.14) | collective-permute-done | bytes 81952 | tf_op jit(solution)/shard_map/ppermute | solution.py:501
  63.6 4.2 %temporal.3 = (bf16[128,320]{1,0:T(8,128)(2,1)S(1)}, bf16[128,320]{1,0:T(8,128)(2,1)S(1)}, bf16[256,320]{1,0:T(8,128)(2,1)S(1)}) custom-call(bf16[640,128]{1,0:T(8,128)(2,1)S(1)} %join.5.refs_0_, bf16[320,128]{1,0:T(8,128)(2,1)S(1)} %collective-permute-done.14.refs_1_, bf16[320,128]{1,0:T(8,128)(2,1)S(1)} %get-tuple-element.61.refs_2_, ...), custom_call_target="tpu_custom_call" | custom-call | flops 1132462080 | bytes 4000000 | tf_op jit(solution)/shard_map/temporal/pallas_call | solution.py:445
  67.8 1.8 %collective-permute-start.15 = (bf16[128,320]{1,0:T(8,128)(2,1)S(1)}, bf16[128,320]{1,0:T(8,128)(2,1)S(1)}, u32[]{:S(2)}, u32[]{:S(2)}) collective-permute-start(bf16[128,320]{1,0:T(8,128)(2,1)S(1)} %get-tuple-element.62), channel_id=1, source_target_pairs={{0,8},{4,12},{8,0},{12,4},{1,9},{5,13},{9,1},{13,5},{2,10},{6,14},... | collective-permute-start | bytes 245768 | tf_op jit(solution)/shard_map/ppermute | solution.py:501
  69.6 1.2 %collective-permute-start.16 = (bf16[128,320]{1,0:T(8,128)(2,1)S(1)}, bf16[128,320]{1,0:T(8,128)(2,1)S(1)}, u32[]{:S(2)}, u32[]{:S(2)}) collective-permute-start(bf16[128,320]{1,0:T(8,128)(2,1)S(1)} %get-tuple-element.63), channel_id=1, source_target_pairs={{0,12},{4,8},{8,4},{12,0},{1,13},{5,9},{9,5},{13,1},{2,14},{6,10},... | collective-permute-start | bytes 245768 | tf_op jit(solution)/shard_map/ppermute | solution.py:501
  70.8 1.4 %feed.3 = (bf16[128,320]{1,0:T(8,128)(2,1)S(1)}, bf16[128,320]{1,0:T(8,128)(2,1)S(1)}) custom-call(bf16[256,320]{1,0:T(8,128)(2,1)S(1)} %get-tuple-element.64.refs_0_, bf16[320,2560]{1,0:T(8,128)(2,1)S(1)} %bitcast.18, bf16[320,1280]{1,0:T(8,128)(2,1)S(1)} %bitcast.22), custom_call_target="tpu_custom_call" | custom-call | flops 629145600 | bytes 3000000 | tf_op jit(solution)/shard_map/feed/pallas_call | solution.py:464
  72.2 0.6 collective-permute-start.17
  72.8 5.1 %collective-permute-done.15 = bf16[128,320]{1,0:T(8,128)(2,1)S(1)} collective-permute-done((bf16[128,320]{1,0:T(8,128)(2,1)S(1)}, bf16[128,320]{1,0:T(8,128)(2,1)S(1)}, u32[]{:S(2)}, u32[]{:S(2)}) %collective-permute-start.15) | collective-permute-done | bytes 81952 | tf_op jit(solution)/shard_map/ppermute | solution.py:501
  78.0 1.8 %collective-permute-done.17 = bf16[128,320]{1,0:T(8,128)(2,1)S(1)} collective-permute-done((bf16[128,320]{1,0:T(8,128)(2,1)S(1)}, bf16[128,320]{1,0:T(8,128)(2,1)S(1)}, u32[]{:S(2)}, u32[]{:S(2)}) %collective-permute-start.17) | collective-permute-done | bytes 81952 | tf_op jit(solution)/shard_map/ppermute | solution.py:501
  79.8 0.0 copy-start.7
  79.8 0.7 copy-done.7
  (28 shorter events, 0.2 us)
Async XLA Ops:
  0.0 12.4 %copy-start = (bf16[1,320,320]{2,1,0:T(8,128)(2,1)S(1)}, bf16[1,320,320]{2,1,0:T(8,128)(2,1)}, u32[]{:S(2)}) copy-start(bf16[1,320,320]{2,1,0:T(8,128)(2,1)} %param.13) | copy-start | bytes 614404
  0.0 12.3 %collective-permute-start = (bf16[512,320]{1,0:T(8,128)(2,1)}, bf16[512,320]{1,0:T(8,128)(2,1)S(1)}, u32[]{:S(2)}, u32[]{:S(2)}) collective-permute-start(bf16[512,320]{1,0:T(8,128)(2,1)} %bitcast.28), channel_id=1, source_target_pairs={{0,2},{2,0},{1,3},{3,1},{4,6},{6,4},{5,7},{7,5},{8,10},{10,8},{9,1... | collective-permute-start | bytes 983048 | tf_op jit(solution)/shard_map/ppermute | solution.py:483
  2.9 1.6 %copy-start.3 = (bf16[1,3,3,320,320]{4,3,2,1,0:T(8,128)(2,1)S(1)}, bf16[1,3,3,320,320]{4,3,2,1,0:T(8,128)(2,1)}, u32[]{:S(2)}) copy-start(bf16[1,3,3,320,320]{4,3,2,1,0:T(8,128)(2,1)} %param.11) | copy-start | bytes 5529604
  4.6 1.6 %copy-start.4 = (bf16[1,3,3,320,320]{4,3,2,1,0:T(8,128)(2,1)S(1)}, bf16[1,3,3,320,320]{4,3,2,1,0:T(8,128)(2,1)}, u32[]{:S(2)}) copy-start(bf16[1,3,3,320,320]{4,3,2,1,0:T(8,128)(2,1)} %param.12) | copy-start | bytes 5529604
  6.2 1.1 %copy-start.5 = (bf16[1,320,960]{2,1,0:T(8,128)(2,1)S(1)}, bf16[1,320,960]{2,1,0:T(8,128)(2,1)}, u32[]{:S(2)}) copy-start(bf16[1,320,960]{2,1,0:T(8,128)(2,1)} %param.14) | copy-start | bytes 1843204
  7.3 0.8 copy-start.8
  12.3 1.7 %collective-permute-start.1 = (bf16[512,320]{1,0:T(8,128)(2,1)S(1)}, bf16[512,320]{1,0:T(8,128)(2,1)S(1)}, u32[]{:S(2)}, u32[]{:S(2)}) collective-permute-start(bf16[512,320]{1,0:T(8,128)(2,1)S(1)} %collective-permute-done.refs_0_), channel_id=1, source_target_pairs={{0,1},{1,0},{2,3},{3,2},{4,5},{5,4},{6,7},{7,6},{8,9},{9,8},{10,11... | collective-permute-start | bytes 983048 | tf_op jit(solution)/shard_map/ppermute | solution.py:483
  18.1 9.6 %collective-permute-start.2 = (bf16[320,128]{1,0:T(8,128)(2,1)S(1)}, bf16[320,128]{1,0:T(8,128)(2,1)S(1)}, u32[]{:S(2)}, u32[]{:S(2)}) collective-permute-start(bf16[320,128]{1,0:T(8,128)(2,1)S(1)} %get-tuple-element.40), channel_id=1, source_target_pairs={{0,8},{4,12},{8,0},{12,4},{1,9},{5,13},{9,1},{13,5},{2,10},{6,14},... | collective-permute-start | bytes 245768 | tf_op jit(solution)/shard_map/ppermute | solution.py:501
  21.0 6.9 %collective-permute-start.3 = (bf16[320,128]{1,0:T(8,128)(2,1)S(1)}, bf16[320,128]{1,0:T(8,128)(2,1)S(1)}, u32[]{:S(2)}, u32[]{:S(2)}) collective-permute-start(bf16[320,128]{1,0:T(8,128)(2,1)S(1)} %get-tuple-element.41), channel_id=1, source_target_pairs={{0,12},{4,8},{8,4},{12,0},{1,13},{5,9},{9,5},{13,1},{2,14},{6,10},... | collective-permute-start | bytes 245768 | tf_op jit(solution)/shard_map/ppermute | solution.py:501
  22.3 6.8 %copy-start.1 = (bf16[1,320,2560]{2,1,0:T(8,128)(2,1)S(1)}, bf16[1,320,2560]{2,1,0:T(8,128)(2,1)}, u32[]{:S(2)}) copy-start(bf16[1,320,2560]{2,1,0:T(8,128)(2,1)} %param.16) | copy-start | bytes 4915204
  22.3 6.8 %copy-start.2 = (bf16[1,1280,320]{1,2,0:T(8,128)(2,1)S(1)}, bf16[1,1280,320]{1,2,0:T(8,128)(2,1)}, u32[]{:S(2)}) copy-start(bf16[1,1280,320]{1,2,0:T(8,128)(2,1)} %param.17) | copy-start | bytes 2457604
  22.3 6.8 %copy-start.6 = (bf16[1,320,320]{2,1,0:T(8,128)(2,1)S(1)}, bf16[1,320,320]{2,1,0:T(8,128)(2,1)}, u32[]{:S(2)}) copy-start(bf16[1,320,320]{2,1,0:T(8,128)(2,1)} %param.15) | copy-start | bytes 614404
  23.2 6.0 %collective-permute-start.4 = (bf16[320,128]{1,0:T(8,128)(2,1)S(1)}, bf16[320,128]{1,0:T(8,128)(2,1)S(1)}, u32[]{:S(2)}, u32[]{:S(2)}) collective-permute-start(bf16[320,128]{1,0:T(8,128)(2,1)S(1)} %get-tuple-element.46), channel_id=1, source_target_pairs={{0,4},{4,0},{8,12},{12,8},{1,5},{5,1},{9,13},{13,9},{2,6},{6,2},{1... | collective-permute-start | bytes 245768 | tf_op jit(solution)/shard_map/ppermute | solution.py:501
  33.4 8.4 %collective-permute-start.5 = (bf16[320,128]{1,0:T(8,128)(2,1)S(1)}, bf16[320,128]{1,0:T(8,128)(2,1)S(1)}, u32[]{:S(2)}, u32[]{:S(2)}) collective-permute-start(bf16[320,128]{1,0:T(8,128)(2,1)S(1)} %get-tuple-element.49), channel_id=1, source_target_pairs={{0,10},{2,8},{4,14},{6,12},{8,2},{10,0},{12,6},{14,4},{1,11},{3,9}... | collective-permute-start | bytes 245768 | tf_op jit(solution)/shard_map/ppermute | solution.py:499
  37.0 7.8 %collective-permute-start.6 = (bf16[320,128]{1,0:T(8,128)(2,1)S(1)}, bf16[320,128]{1,0:T(8,128)(2,1)S(1)}, u32[]{:S(2)}, u32[]{:S(2)}) collective-permute-start(bf16[320,128]{1,0:T(8,128)(2,1)S(1)} %get-tuple-element.50), channel_id=1, source_target_pairs={{0,14},{2,12},{4,10},{6,8},{8,6},{10,4},{12,2},{14,0},{1,15},{3,13... | collective-permute-start | bytes 245768 | tf_op jit(solution)/shard_map/ppermute | solution.py:499
  39.2 6.5 %collective-permute-start.7 = (bf16[320,128]{1,0:T(8,128)(2,1)S(1)}, bf16[320,128]{1,0:T(8,128)(2,1)S(1)}, u32[]{:S(2)}, u32[]{:S(2)}) collective-permute-start(bf16[320,128]{1,0:T(8,128)(2,1)S(1)} %get-tuple-element.52), channel_id=1, source_target_pairs={{0,6},{2,4},{4,2},{6,0},{8,14},{10,12},{12,10},{14,8},{1,7},{3,5},... | collective-permute-start | bytes 245768 | tf_op jit(solution)/shard_map/ppermute | solution.py:499
  40.4 6.9 %collective-permute-start.8 = (bf16[320,128]{1,0:T(8,128)(2,1)S(1)}, bf16[320,128]{1,0:T(8,128)(2,1)S(1)}, u32[]{:S(2)}, u32[]{:S(2)}) collective-permute-start(bf16[320,128]{1,0:T(8,128)(2,1)S(1)} %get-tuple-element.53), channel_id=1, source_target_pairs={{0,2},{2,0},{4,6},{6,4},{8,10},{10,8},{12,14},{14,12},{1,3},{3,1},... | collective-permute-start | bytes 245768 | tf_op jit(solution)/shard_map/ppermute | solution.py:499
  44.8 3.8 %collective-permute-start.9 = (bf16[640,128]{1,0:T(8,128)(2,1)S(1)}, bf16[640,128]{1,0:T(8,128)(2,1)S(1)}, u32[]{:S(2)}, u32[]{:S(2)}) collective-permute-start(bf16[640,128]{1,0:T(8,128)(2,1)S(1)} %join.4.refs_0_), channel_id=1, source_target_pairs={{0,1},{1,0},{2,3},{3,2},{4,5},{5,4},{6,7},{7,6},{8,9},{9,8},{10,11... | collective-permute-start | bytes 491528 | tf_op jit(solution)/shard_map/ppermute | solution.py:483
  45.8 1.6 %collective-permute-start.10 = (bf16[320,128]{1,0:T(8,128)(2,1)S(1)}, bf16[320,128]{1,0:T(8,128)(2,1)S(1)}, u32[]{:S(2)}, u32[]{:S(2)}) collective-permute-start(bf16[320,128]{1,0:T(8,128)(2,1)S(1)} %collective-permute-done.7.refs_1_), channel_id=1, source_target_pairs={{0,1},{1,0},{2,3},{3,2},{4,5},{5,4},{6,7},{7,6},{8,9},{9,8},{10,11... | collective-permute-start | bytes 245768 | tf_op jit(solution)/shard_map/ppermute | solution.py:483
  47.3 1.3 %collective-permute-start.11 = (bf16[320,128]{1,0:T(8,128)(2,1)S(1)}, bf16[320,128]{1,0:T(8,128)(2,1)S(1)}, u32[]{:S(2)}, u32[]{:S(2)}) collective-permute-start(bf16[320,128]{1,0:T(8,128)(2,1)S(1)} %collective-permute-done.8.refs_2_), channel_id=1, source_target_pairs={{0,1},{1,0},{2,3},{3,2},{4,5},{5,4},{6,7},{7,6},{8,9},{9,8},{10,11... | collective-permute-start | bytes 245768 | tf_op jit(solution)/shard_map/ppermute | solution.py:483
  52.9 8.3 %collective-permute-start.12 = (bf16[320,128]{1,0:T(8,128)(2,1)S(1)}, bf16[320,128]{1,0:T(8,128)(2,1)S(1)}, u32[]{:S(2)}, u32[]{:S(2)}) collective-permute-start(bf16[320,128]{1,0:T(8,128)(2,1)S(1)} %get-tuple-element.54), channel_id=1, source_target_pairs={{0,8},{4,12},{8,0},{12,4},{1,9},{5,13},{9,1},{13,5},{2,10},{6,14},... | collective-permute-start | bytes 245768 | tf_op jit(solution)/shard_map/ppermute | solution.py:501
  55.5 6.9 %collective-permute-start.13 = (bf16[320,128]{1,0:T(8,128)(2,1)S(1)}, bf16[320,128]{1,0:T(8,128)(2,1)S(1)}, u32[]{:S(2)}, u32[]{:S(2)}) collective-permute-start(bf16[320,128]{1,0:T(8,128)(2,1)S(1)} %get-tuple-element.55), channel_id=1, source_target_pairs={{0,12},{4,8},{8,4},{12,0},{1,13},{5,9},{9,5},{13,1},{2,14},{6,10},... | collective-permute-start | bytes 245768 | tf_op jit(solution)/shard_map/ppermute | solution.py:501
  56.5 7.1 %collective-permute-start.14 = (bf16[320,128]{1,0:T(8,128)(2,1)S(1)}, bf16[320,128]{1,0:T(8,128)(2,1)S(1)}, u32[]{:S(2)}, u32[]{:S(2)}) collective-permute-start(bf16[320,128]{1,0:T(8,128)(2,1)S(1)} %get-tuple-element.60), channel_id=1, source_target_pairs={{0,4},{4,0},{8,12},{12,8},{1,5},{5,1},{9,13},{13,9},{2,6},{6,2},{1... | collective-permute-start | bytes 245768 | tf_op jit(solution)/shard_map/ppermute | solution.py:501
  67.8 10.1 %collective-permute-start.15 = (bf16[128,320]{1,0:T(8,128)(2,1)S(1)}, bf16[128,320]{1,0:T(8,128)(2,1)S(1)}, u32[]{:S(2)}, u32[]{:S(2)}) collective-permute-start(bf16[128,320]{1,0:T(8,128)(2,1)S(1)} %get-tuple-element.62), channel_id=1, source_target_pairs={{0,8},{4,12},{8,0},{12,4},{1,9},{5,13},{9,1},{13,5},{2,10},{6,14},... | collective-permute-start | bytes 245768 | tf_op jit(solution)/shard_map/ppermute | solution.py:501
  69.6 8.4 %collective-permute-start.16 = (bf16[128,320]{1,0:T(8,128)(2,1)S(1)}, bf16[128,320]{1,0:T(8,128)(2,1)S(1)}, u32[]{:S(2)}, u32[]{:S(2)}) collective-permute-start(bf16[128,320]{1,0:T(8,128)(2,1)S(1)} %get-tuple-element.63), channel_id=1, source_target_pairs={{0,12},{4,8},{8,4},{12,0},{1,13},{5,9},{9,5},{13,1},{2,14},{6,10},... | collective-permute-start | bytes 245768 | tf_op jit(solution)/shard_map/ppermute | solution.py:501
  72.2 7.6 %collective-permute-start.17 = (bf16[128,320]{1,0:T(8,128)(2,1)S(1)}, bf16[128,320]{1,0:T(8,128)(2,1)S(1)}, u32[]{:S(2)}, u32[]{:S(2)}) collective-permute-start(bf16[128,320]{1,0:T(8,128)(2,1)S(1)} %get-tuple-element.65), channel_id=1, source_target_pairs={{0,4},{4,0},{8,12},{12,8},{1,5},{5,1},{9,13},{13,9},{2,6},{6,2},{1... | collective-permute-start | bytes 245768 | tf_op jit(solution)/shard_map/ppermute | solution.py:501
  79.8 0.7 copy-start.7

commit v4 on v3

--- a/solution.py
+++ b/solution.py
@@ -17,18 +17,17 @@
 BF16 = jnp.bfloat16
 
 
-def partner(spot, distance, count):
-    if count & (count - 1):
-        return (spot + distance) % count
-    return spot ^ distance
-
-
-def distances(count):
-    order, low = [], count
+def orders(count):
+    far, near, low = list(range(count // 2, count)), [], count // 2
     while low > 1:
-        low = (low + 1) // 2
-        order += [d for d in range(low, count) if d not in order]
-    return order + [0]
+        near += range(low // 2, low)
+        low //= 2
+    return far + near + [0], near + far + [0]
+
+
+def partners(spot, core, count):
+    even, odd = orders(count)
+    return [spot ^ jnp.where(core % 2 == 0, a, b) for a, b in zip(even, odd)]
 
 
 def round_up(value, unit):
@@ -159,17 +158,16 @@
     zero = jnp.zeros((8, lanes), F32)
 
     height = dense_rows(part, channels)
-    for base, arrived in ((own_base, own), (other_base, other)):
+    for core, base, arrived in ((here, own_base, own), (1 - here, other_base, other)):
         if ways == 1:
             place = pl.ds(pl.multiple_of(base, columns), own_rows * columns)
             field[place, lanes - LANES :] = jnp.zeros((own_rows * columns, LANES), F32)
             field[place, :channels] = arrived[0][...].astype(F32)
             continue
         held = [(block, at) for block in arrived for at in range(0, block.shape[0], height)]
-        for (block, at), d in zip(held, distances(shards)):
-            here_part = base + partner(spot, d, shards) * part
+        for (block, at), q in zip(held, partners(spot, core, shards)):
             for i, first, values in unpack_part(block, at, part, channels):
-                place = pl.multiple_of(here_part + first, 8)
+                place = pl.multiple_of(base + q * part + first, 8)
                 field[pl.ds(place, values.shape[0]), i * LANES : (i + 1) * LANES] = values
 
     def sum_row(i, carry):
@@ -201,8 +199,8 @@
     scale, shift = group_scale(total, square, entries, group_width, channels)
     first_row = here * own_rows
     activate(hidden, targets, scale, shift, rows, columns, first_row, 0, own_rows + 2)
-    for i, d in enumerate(distances(shards)):
-        start = partner(spot, d, shards) * part
+    for i, q in enumerate(partners(spot, here, shards)):
+        start = q * part
         base = field[pl.ds(pl.multiple_of(own_base + start, 8), part), :]
         if i < sooner:
             convolve_part(targets, kernels.at[1], start, columns, base, outs[i])
@@ -213,8 +211,8 @@
 def finish_kernel(columns, shards, sooner, keep, middle, edge, pair, kernels, *outs):
     part = keep.shape[0] // (shards - sooner)
     spot = lax.axis_index("shard")
-    for i, d in enumerate(distances(shards)[sooner:]):
-        start = partner(spot, d, shards) * part
+    for i, q in enumerate(partners(spot, lax.axis_index("halo"), shards)[sooner:]):
+        start = q * part
         base = keep[i * part : (i + 1) * part, :]
         convolve_part((middle, edge, pair), kernels.at[1], start, columns, base, outs[i])
 
@@ -345,9 +343,6 @@
 
 def leave(values, target):
     pixels, channels = values.shape
-    if target.shape == values.shape:
-        target[...] = values.astype(BF16)
-        return
     spare = round_up(channels, LANES) - channels
     values = jnp.concatenate([values, jnp.zeros((pixels, spare), F32)], axis=1)
     pack_part(values, target, 0, channels)
@@ -391,29 +386,39 @@
     )
     lane = lax.broadcasted_iota(jnp.int32, (1, LANES), 1)
     sharing = LANES // HEAD_DIM
+    chosen = [(lane >= j * HEAD_DIM) & (lane < (j + 1) * HEAD_DIM) for j in range(sharing)]
     for first in range(0, pixels, pack):
         places = [slice(f * pixels + first, f * pixels + first + pack) for f in range(frames)]
+
+        def gather(at):
+            return jnp.concatenate([projected[p, at : at + LANES] for p in places])
+
+        heads = [(h * HEAD_DIM // LANES * LANES, h % sharing) for h in range(channels // HEAD_DIM)]
+        scores = [
+            lax.dot_general(
+                gather(at) * chosen[j].astype(BF16),
+                gather(lanes + at),
+                (((1,), (1,)), ((), ())),
+                preferred_element_type=F32,
+            )
+            for at, j in heads
+        ]
+        scores = [jnp.where(same, score, float(jnp.finfo(F32).min)) for score in scores]
+        tops = [jnp.max(score, axis=1, keepdims=True) for score in scores]
+        powers = [
+            jnp.exp((score - top) * HEAD_DIM ** (-0.5)) for score, top in zip(scores, tops)
+        ]
+        totals = [1.0 / jnp.sum(power, axis=1, keepdims=True) for power in powers]
+        weights = [(power * total).astype(BF16) for power, total in zip(powers, totals)]
+        results = [
+            jnp.dot(weight, gather(2 * lanes + at), preferred_element_type=F32)
+            for weight, (at, _) in zip(weights, heads)
+        ]
         for at in range(0, channels, LANES):
-            query, key, value = [
-                jnp.concatenate([projected[p, i * lanes + at : i * lanes + at + LANES] for p in places])
-                for i in range(3)
-            ]
             mix = None
-            for j in range(min(sharing, (channels - at) // HEAD_DIM)):
-                chosen = (lane >= j * HEAD_DIM) & (lane < (j + 1) * HEAD_DIM)
-                scores = lax.dot_general(
-                    query * chosen.astype(BF16),
-                    key,
-                    (((1,), (1,)), ((), ())),
-                    preferred_element_type=F32,
-                )
-                scores = jnp.where(same, scores, float(jnp.finfo(F32).min))
-                top = jnp.max(scores, axis=1, keepdims=True)
-                powers = jnp.exp((scores - top) * HEAD_DIM ** (-0.5))
-                total = jnp.sum(powers, axis=1, keepdims=True)
-                weights = (powers * (1.0 / total)).astype(BF16)
-                head = jnp.dot(weights, value, preferred_element_type=F32)
-                mix = head if mix is None else jnp.where(chosen, head, mix)
+            for result, (spot, j) in zip(results, heads):
+                if spot == at:
+                    mix = result if mix is None else jnp.where(chosen[j], result, mix)
             mix = mix.astype(BF16)
             for f, p in enumerate(places):
                 mixed[p, at : at + LANES] = mix[f * pack : (f + 1) * pack]
@@ -426,7 +431,7 @@
         leave(done[f * pixels : (f + 1) * pixels, :], outs[f])
 
 
-def temporal(parts, weights, dense):
+def temporal(parts, weights):
     ways = len(parts)
     frames = lax.axis_size("shard")
     sooner = frames // 2
@@ -437,9 +442,7 @@
     tokens = frames * pixels
     inner = weights[3].shape[1]
     vmem = pl.BlockSpec(memory_space=pltpu.VMEM)
-    piece = jax.ShapeDtypeStruct(
-        (dense_rows(pixels, channels), LANES) if dense else (pixels, channels), BF16
-    )
+    piece = jax.ShapeDtypeStruct((dense_rows(pixels, channels), LANES), BF16)
     feed_flops = 6 * pixels * channels * inner
     params = pltpu.CompilerParams(vmem_limit_bytes=14 * 1024 * 1024)
     *first, rest = pl.pallas_call(
@@ -483,22 +486,22 @@
     return lax.ppermute(block, axis, [(i, (i + distance) % count) for i in range(count)])
 
 
-def exchange(parts, back=False, across=0):
-    shards, sections = lax.axis_size("shard"), lax.axis_size("section")
+def exchange(parts, across=0):
+    sizes = [lax.axis_size(axis) for axis in ("shard", "section", "halo")]
+    shards, sections, cores = sizes
     arrived = []
-    for part, d in zip(parts, distances(shards)):
-        target = [partner(z, d, shards) for z in range(shards)]
-        if back:
-            target = [target.index(z) for z in range(shards)]
-        if across:
+    for part, *distance in zip(parts, *orders(shards)):
+        if across or any(distance):
             route = [
-                (z * sections + s, target[z] * sections + (s + across) % sections)
+                (
+                    (z * sections + s) * cores + h,
+                    ((z ^ distance[h % 2]) * sections + (s + across) % sections) * cores + h,
+                )
                 for z in range(shards)
                 for s in range(sections)
+                for h in range(cores)
             ]
-            part = lax.ppermute(part, ("shard", "section"), route)
-        elif d:
-            part = lax.ppermute(part, "shard", list(enumerate(target)))
+            part = lax.ppermute(part, ("shard", "section", "halo"), route)
         arrived.append(part)
     return arrived
 
@@ -523,14 +526,31 @@
     )(*parts)
 
 
-def assemble(parts):
-    size, channels = parts[0].shape
-    spot = lax.axis_index("shard")
-    whole = jnp.zeros((len(parts) * size, channels), parts[0].dtype)
-    for part, d in zip(parts, distances(len(parts))):
-        place = partner(spot, d, len(parts)) * size
-        whole = lax.dynamic_update_slice_in_dim(whole, part, place, axis=0)
-    return whole
+def unpack_kernel(shards, *refs):
+    parts, (whole,) = refs[:-1], refs[-1:]
+    tokens, channels = whole.shape
+    pixels = tokens // shards
+    height = dense_rows(pixels, channels)
+    held = [(block, at) for block in parts for at in range(0, block.shape[0], height)]
+    places = partners(lax.axis_index("shard"), lax.axis_index("halo"), shards)
+    for (block, at), q in zip(held, places):
+        for i, first, values in unpack_part(block, at, pixels, channels):
+            place = pl.multiple_of(q * pixels + first, 16)
+            width = min(LANES, channels - i * LANES)
+            lanes = slice(i * LANES, i * LANES + width)
+            whole[pl.ds(place, values.shape[0]), lanes] = values[:, :width].astype(BF16)
+
+
+def unpack(parts, shards, tokens, channels):
+    vmem = pl.BlockSpec(memory_space=pltpu.VMEM)
+    return pl.pallas_call(
+        functools.partial(unpack_kernel, shards),
+        out_shape=jax.ShapeDtypeStruct((tokens, channels), BF16),
+        in_specs=[vmem] * len(parts),
+        out_specs=vmem,
+        compiler_params=pltpu.CompilerParams(vmem_limit_bytes=4 * 1024 * 1024),
+        name="unpack",
+    )(*parts)
 
 
 def embed_time(stamps, time_weight):
@@ -580,10 +600,10 @@
         )
         parts = exchange(parts)
         parts = [join(parts[: shards // 2]), *parts[shards // 2 :]]
-        parts = temporal(parts, temporal_weights, dense=not last)
-        parts = exchange(parts, back=True, across=0 if last else 1)
+        parts = temporal(parts, temporal_weights)
+        parts = exchange(parts, across=0 if last else 1)
         own = [join(parts[: shards // 2]), *parts[shards // 2 :]]
-    return assemble(parts).reshape(features.shape)
+    return unpack(own, shards, own_rows * columns, channels).reshape(features.shape)
 
 
 def solution(mesh):

time: 80.8 us -> 78.5 us (0.972)
  waiting for transfers between devices: 31.6 us -> 29.7 us
  local copies, waits for them, and re-layouts: 5.23 us -> 4.36 us
    ppermute x13, waiting for transfers between devices: 24.8 us -> 22.9 us  [exchange(): part = lax.ppermute(part, ('shard', 'section', 'halo'), route)]
    pallas_call x0 -> x1, Pallas kernels: none -> 0.87 us  [unpack(): pl.pallas_call(functools.partial(unpack_kernel, shards), out_shape=jax.Sh...]
    unnamed x18 -> x16, local copies, waits for them, and re-layouts: 5.09 us -> 4.35 us
  transfers between devices with their start and end apart: 18 -> 18, of which waited for: 15 -> 16; matrix products, arithmetic and copies ran while one was open for 1% -> 0% of each run, Pallas kernels for 6% -> 7%
where the time goes in v4:
time: 78.5 us; the launch traced here: 78.3 us
  waiting for transfers between devices  29.7 us (38%)
  Pallas kernels  22.7 us (29%)
  starting transfers between devices  21.1 us (27%)
  local copies, waits for them, and re-layouts  4.36 us (6%)
    ppermute x13, waiting for transfers between devices, exchange(): part = lax.ppermute(part, ('shard', 'section', 'halo'), route)  22.9 us
    ppermute x13, starting transfers between devices, exchange(): part = lax.ppermute(part, ('shard', 'section', 'halo'), route)  18.1 us
    pallas_call x2, Pallas kernels, spatial(): pl.pallas_call(functools.partial(spatial_kernel, rows, half, columns, cha...  8.37 us
    pallas_call x2, Pallas kernels, temporal(): pl.pallas_call(functools.partial(temporal_kernel, frames, ways, sooner),...  8.13 us
    ppermute x5, waiting for transfers between devices, send(): lax.ppermute(block, axis, [(i, (i + distance) % count) for i in range(cou...  6.86 us
    unnamed x16, local copies, waits for them, and re-layouts  4.35 us
    ppermute x5, starting transfers between devices, send(): lax.ppermute(block, axis, [(i, (i + distance) % count) for i in range(cou...  3.02 us
    pallas_call x2, Pallas kernels, temporal(): pl.pallas_call(functools.partial(feed_kernel, later), out_shape=[piece] *...  2.92 us
  transfers between devices with their start and end apart: 18, of which 16 were waited for; matrix products, arithmetic and copies ran while one was open for 0% of the time, Pallas kernels for 7%

profile of v4, /device:TPU:0, one launch (start us, length us, event | category | flops | bytes accessed | tf_op | source)
XLA Modules:
  0.0 78.3 jit_solution(213648957800965365)
XLA Ops:
  0.0 2.9 %collective-permute-start = (bf16[512,320]{1,0:T(8,128)(2,1)}, bf16[512,320]{1,0:T(8,128)(2,1)S(1)}, u32[]{:S(2)}, u32[]{:S(2)}) collective-permute-start(bf16[512,320]{1,0:T(8,128)(2,1)} %bitcast.28), channel_id=1, source_target_pairs={{0,2},{2,0},{1,3},{3,1},{4,6},{6,4},{5,7},{7,5},{8,10},{10,8},{9,1... | collective-permute-start | bytes 983048 | tf_op jit(solution)/shard_map/ppermute | solution.py:486
  2.9 1.6 %copy-done.3 = bf16[1,3,3,320,320]{4,3,2,1,0:T(8,128)(2,1)S(1)} copy-done((bf16[1,3,3,320,320]{4,3,2,1,0:T(8,128)(2,1)S(1)}, bf16[1,3,3,320,320]{4,3,2,1,0:T(8,128)(2,1)}, u32[]{:S(2)}) %copy-start.3) | copy-done | bytes 1843224
  4.6 1.6 %copy-done.4 = bf16[1,3,3,320,320]{4,3,2,1,0:T(8,128)(2,1)S(1)} copy-done((bf16[1,3,3,320,320]{4,3,2,1,0:T(8,128)(2,1)S(1)}, bf16[1,3,3,320,320]{4,3,2,1,0:T(8,128)(2,1)}, u32[]{:S(2)}) %copy-start.4) | copy-done | bytes 1843224
  6.2 1.1 %copy-done.5 = bf16[1,320,960]{2,1,0:T(8,128)(2,1)S(1)} copy-done((bf16[1,320,960]{2,1,0:T(8,128)(2,1)S(1)}, bf16[1,320,960]{2,1,0:T(8,128)(2,1)}, u32[]{:S(2)}) %copy-start.5) | copy-done | bytes 614424
  7.3 0.7 prepare.1
  8.0 4.2 %collective-permute-done.refs_0_ = bf16[512,320]{1,0:T(8,128)(2,1)S(1)} collective-permute-done((bf16[512,320]{1,0:T(8,128)(2,1)}, bf16[512,320]{1,0:T(8,128)(2,1)S(1)}, u32[]{:S(2)}, u32[]{:S(2)}) %collective-permute-start) | collective-permute-done | bytes 327712 | tf_op jit(solution)/shard_map/ppermute | solution.py:486
  12.3 0.1 multiply_cosine_fusion
  12.4 0.2 fusion
  12.6 1.4 %collective-permute-done.1.refs_1_ = bf16[512,320]{1,0:T(8,128)(2,1)S(1)} collective-permute-done((bf16[512,320]{1,0:T(8,128)(2,1)S(1)}, bf16[512,320]{1,0:T(8,128)(2,1)S(1)}, u32[]{:S(2)}, u32[]{:S(2)}) %collective-permute-start.1) | collective-permute-done | bytes 327712 | tf_op jit(solution)/shard_map/ppermute | solution.py:486
  14.0 4.1 %spatial.2 = (bf16[320,128]{1,0:T(8,128)(2,1)S(1)}, bf16[320,128]{1,0:T(8,128)(2,1)S(1)}, f32[256,384]{1,0:T(8,128)S(1)}, bf16[640,256]{1,0:T(8,128)(2,1)S(1)}, ...) custom-call(bf16[512,320]{1,0:T(8,128)(2,1)S(1)} %collective-permute-done.refs_0_, ...), custom_call_target="tpu_custom_call" | custom-call | flops 3221225472 | bytes 6000000 | tf_op jit(solution)/shard_map/spatial/pallas_call | solution.py:236
  18.1 2.9 %collective-permute-start.2 = (bf16[320,128]{1,0:T(8,128)(2,1)S(1)}, bf16[320,128]{1,0:T(8,128)(2,1)S(1)}, u32[]{:S(2)}, u32[]{:S(2)}) collective-permute-start(bf16[320,128]{1,0:T(8,128)(2,1)S(1)} %get-tuple-element.40), channel_id=1, source_target_pairs={{0,8},{1,5},{2,10},{3,7},{4,12},{5,1},{6,14},{7,3},{8,0},{9,13},{1... | collective-permute-start | bytes 245768 | tf_op jit(solution)/shard_map/ppermute | solution.py:504
  21.0 1.4 %collective-permute-start.3 = (bf16[320,128]{1,0:T(8,128)(2,1)S(1)}, bf16[320,128]{1,0:T(8,128)(2,1)S(1)}, u32[]{:S(2)}, u32[]{:S(2)}) collective-permute-start(bf16[320,128]{1,0:T(8,128)(2,1)S(1)} %get-tuple-element.41), channel_id=1, source_target_pairs={{0,12},{1,9},{2,14},{3,11},{4,8},{5,13},{6,10},{7,15},{8,4},{9,1},... | collective-permute-start | bytes 245768 | tf_op jit(solution)/shard_map/ppermute | solution.py:504
  22.3 0.8 %finish.2 = (bf16[320,128]{1,0:T(8,128)(2,1)S(1)}, bf16[320,128]{1,0:T(8,128)(2,1)S(1)}) custom-call(f32[256,384]{1,0:T(8,128)S(1)} %get-tuple-element.42.keep, bf16[640,256]{1,0:T(8,128)(2,1)S(1)} %get-tuple-element.43.middle, bf16[640,128]{1,0:T(8,128)(2,1)S(1)} %get-tuple-element.44.edge, bf16[640,128]{1,0:T(8,128)(2,1)S(1)} %get-tuple-element.45.pair, ...), custom_call_target="tpu_custom_call" | custom-call | flops 536870912 | bytes 3000000 | tf_op jit(solution)/shard_map/finish/pallas_call | solution.py:267
  23.2 0.3 collective-permute-start.4
  23.5 0.2 collective-permute-done.2.refs_0_
  23.7 3.7 %collective-permute-done.3.refs_1_ = bf16[320,128]{1,0:T(8,128)(2,1)S(1)} collective-permute-done((bf16[320,128]{1,0:T(8,128)(2,1)S(1)}, bf16[320,128]{1,0:T(8,128)(2,1)S(1)}, u32[]{:S(2)}, u32[]{:S(2)}) %collective-permute-start.3) | collective-permute-done | bytes 81952 | tf_op jit(solution)/shard_map/ppermute | solution.py:504
  27.4 1.7 %collective-permute-done.4.refs_1_ = bf16[320,128]{1,0:T(8,128)(2,1)S(1)} collective-permute-done((bf16[320,128]{1,0:T(8,128)(2,1)S(1)}, bf16[320,128]{1,0:T(8,128)(2,1)S(1)}, u32[]{:S(2)}, u32[]{:S(2)}) %collective-permute-start.4) | collective-permute-done | bytes 81952 | tf_op jit(solution)/shard_map/ppermute | solution.py:504
  29.1 4.1 %temporal.2 = (bf16[320,128]{1,0:T(8,128)(2,1)S(1)}, bf16[320,128]{1,0:T(8,128)(2,1)S(1)}, bf16[256,320]{1,0:T(8,128)(2,1)S(1)}) custom-call(bf16[640,128]{1,0:T(8,128)(2,1)S(1)} %join.4.refs_0_, bf16[320,128]{1,0:T(8,128)(2,1)S(1)} %collective-permute-done.4.refs_1_, bf16[320,128]{1,0:T(8,128)(2,1)S(1)} %get-tuple-element.47.refs_2_, ...), custom_call_target="tpu_custom_call" | custom-call | flops 1132462080 | bytes 4000000 | tf_op jit(solution)/shard_map/temporal/pallas_call | solution.py:448
  33.2 3.9 %collective-permute-start.5 = (bf16[320,128]{1,0:T(8,128)(2,1)S(1)}, bf16[320,128]{1,0:T(8,128)(2,1)S(1)}, u32[]{:S(2)}, u32[]{:S(2)}) collective-permute-start(bf16[320,128]{1,0:T(8,128)(2,1)S(1)} %get-tuple-element.49), channel_id=1, source_target_pairs={{0,10},{1,7},{2,8},{3,5},{4,14},{5,3},{6,12},{7,1},{8,2},{9,15},{1... | collective-permute-start | bytes 245768 | tf_op jit(solution)/shard_map/ppermute | solution.py:504
  37.0 0.4 collective-permute-start.6
  37.4 1.5 %feed.2 = (bf16[320,128]{1,0:T(8,128)(2,1)S(1)}, bf16[320,128]{1,0:T(8,128)(2,1)S(1)}) custom-call(bf16[256,320]{1,0:T(8,128)(2,1)S(1)} %get-tuple-element.51.refs_0_, bf16[320,2560]{1,0:T(8,128)(2,1)S(1)} %bitcast.16, bf16[320,1280]{1,0:T(8,128)(2,1)S(1)} %bitcast.20), custom_call_target="tpu_custom_call" | custom-call | flops 629145600 | bytes 3000000 | tf_op jit(solution)/shard_map/feed/pallas_call | solution.py:467
  38.9 1.3 %collective-permute-start.7 = (bf16[320,128]{1,0:T(8,128)(2,1)S(1)}, bf16[320,128]{1,0:T(8,128)(2,1)S(1)}, u32[]{:S(2)}, u32[]{:S(2)}) collective-permute-start(bf16[320,128]{1,0:T(8,128)(2,1)S(1)} %get-tuple-element.52), channel_id=1, source_target_pairs={{0,6},{1,15},{2,4},{3,13},{4,2},{5,11},{6,0},{7,9},{8,14},{9,7},{1... | collective-permute-start | bytes 245768 | tf_op jit(solution)/shard_map/ppermute | solution.py:504
  40.2 0.4 collective-permute-start.8
  40.7 0.9 %collective-permute-done.5.refs_0_ = bf16[320,128]{1,0:T(8,128)(2,1)S(1)} collective-permute-done((bf16[320,128]{1,0:T(8,128)(2,1)S(1)}, bf16[320,128]{1,0:T(8,128)(2,1)S(1)}, u32[]{:S(2)}, u32[]{:S(2)}) %collective-permute-start.5) | collective-permute-done | bytes 81952 | tf_op jit(solution)/shard_map/ppermute | solution.py:504
  41.5 3.6 %collective-permute-done.6.refs_1_ = bf16[320,128]{1,0:T(8,128)(2,1)S(1)} collective-permute-done((bf16[320,128]{1,0:T(8,128)(2,1)S(1)}, bf16[320,128]{1,0:T(8,128)(2,1)S(1)}, u32[]{:S(2)}, u32[]{:S(2)}) %collective-permute-start.6) | collective-permute-done | bytes 81952 | tf_op jit(solution)/shard_map/ppermute | solution.py:504
  45.1 0.1 collective-permute-start.9
  45.2 0.7 collective-permute-done.7.refs_1_
  45.9 0.9 %collective-permute-done.8.refs_2_ = bf16[320,128]{1,0:T(8,128)(2,1)S(1)} collective-permute-done((bf16[320,128]{1,0:T(8,128)(2,1)S(1)}, bf16[320,128]{1,0:T(8,128)(2,1)S(1)}, u32[]{:S(2)}, u32[]{:S(2)}) %collective-permute-start.8) | collective-permute-done | bytes 81952 | tf_op jit(solution)/shard_map/ppermute | solution.py:504
  46.8 0.0 collective-permute-start.11
  46.8 0.3 collective-permute-done.10.refs_4_
  47.2 0.9 %collective-permute-done.11.refs_5_ = bf16[320,128]{1,0:T(8,128)(2,1)S(1)} collective-permute-done((bf16[320,128]{1,0:T(8,128)(2,1)S(1)}, bf16[320,128]{1,0:T(8,128)(2,1)S(1)}, u32[]{:S(2)}, u32[]{:S(2)}) %collective-permute-start.11) | collective-permute-done | bytes 81952 | tf_op jit(solution)/shard_map/ppermute | solution.py:486
  48.1 0.0 collective-permute-done.9.refs_3_
  48.1 4.3 %spatial.3 = (bf16[320,128]{1,0:T(8,128)(2,1)S(1)}, bf16[320,128]{1,0:T(8,128)(2,1)S(1)}, f32[256,384]{1,0:T(8,128)S(1)}, bf16[640,256]{1,0:T(8,128)(2,1)S(1)}, ...) custom-call(bf16[640,128]{1,0:T(8,128)(2,1)S(1)} %join.5.refs_0_, ...), custom_call_target="tpu_custom_call" | custom-call | flops 3221225472 | bytes 6000000 | tf_op jit(solution)/shard_map/spatial/pallas_call | solution.py:236
  52.4 2.2 %collective-permute-start.12 = (bf16[320,128]{1,0:T(8,128)(2,1)S(1)}, bf16[320,128]{1,0:T(8,128)(2,1)S(1)}, u32[]{:S(2)}, u32[]{:S(2)}) collective-permute-start(bf16[320,128]{1,0:T(8,128)(2,1)S(1)} %get-tuple-element.54), channel_id=1, source_target_pairs={{0,8},{1,5},{2,10},{3,7},{4,12},{5,1},{6,14},{7,3},{8,0},{9,13},{1... | collective-permute-start | bytes 245768 | tf_op jit(solution)/shard_map/ppermute | solution.py:504
  54.6 0.4 collective-permute-start.13
  55.0 0.8 %finish.3 = (bf16[320,128]{1,0:T(8,128)(2,1)S(1)}, bf16[320,128]{1,0:T(8,128)(2,1)S(1)}) custom-call(f32[256,384]{1,0:T(8,128)S(1)} %get-tuple-element.56.keep, bf16[640,256]{1,0:T(8,128)(2,1)S(1)} %get-tuple-element.57.middle, bf16[640,128]{1,0:T(8,128)(2,1)S(1)} %get-tuple-element.58.edge, bf16[640,128]{1,0:T(8,128)(2,1)S(1)} %get-tuple-element.59.pair, ...), custom_call_target="tpu_custom_call" | custom-call | flops 536870912 | bytes 3000000 | tf_op jit(solution)/shard_map/finish/pallas_call | solution.py:267
  55.9 1.0 %collective-permute-start.14 = (bf16[320,128]{1,0:T(8,128)(2,1)S(1)}, bf16[320,128]{1,0:T(8,128)(2,1)S(1)}, u32[]{:S(2)}, u32[]{:S(2)}) collective-permute-start(bf16[320,128]{1,0:T(8,128)(2,1)S(1)} %get-tuple-element.60), channel_id=1, source_target_pairs={{0,4},{1,13},{2,6},{3,15},{4,0},{5,9},{6,2},{7,11},{8,12},{9,5},{1... | collective-permute-start | bytes 245768 | tf_op jit(solution)/shard_map/ppermute | solution.py:504
  56.8 5.0 %collective-permute-done.12.refs_0_ = bf16[320,128]{1,0:T(8,128)(2,1)S(1)} collective-permute-done((bf16[320,128]{1,0:T(8,128)(2,1)S(1)}, bf16[320,128]{1,0:T(8,128)(2,1)S(1)}, u32[]{:S(2)}, u32[]{:S(2)}) %collective-permute-start.12) | collective-permute-done | bytes 81952 | tf_op jit(solution)/shard_map/ppermute | solution.py:504
  61.8 0.6 collective-permute-done.14.refs_1_
  62.5 4.1 %temporal.3 = (bf16[320,128]{1,0:T(8,128)(2,1)S(1)}, bf16[320,128]{1,0:T(8,128)(2,1)S(1)}, bf16[256,320]{1,0:T(8,128)(2,1)S(1)}) custom-call(bf16[640,128]{1,0:T(8,128)(2,1)S(1)} %join.6.refs_0_, bf16[320,128]{1,0:T(8,128)(2,1)S(1)} %collective-permute-done.14.refs_1_, bf16[320,128]{1,0:T(8,128)(2,1)S(1)} %get-tuple-element.61.refs_2_, ...), custom_call_target="tpu_custom_call" | custom-call | flops 1132462080 | bytes 4000000 | tf_op jit(solution)/shard_map/temporal/pallas_call | solution.py:448
  66.5 2.8 %collective-permute-start.15 = (bf16[320,128]{1,0:T(8,128)(2,1)S(1)}, bf16[320,128]{1,0:T(8,128)(2,1)S(1)}, u32[]{:S(2)}, u32[]{:S(2)}) collective-permute-start(bf16[320,128]{1,0:T(8,128)(2,1)S(1)} %get-tuple-element.62), channel_id=1, source_target_pairs={{0,8},{1,5},{2,10},{3,7},{4,12},{5,1},{6,14},{7,3},{8,0},{9,13},{1... | collective-permute-start | bytes 245768 | tf_op jit(solution)/shard_map/ppermute | solution.py:504
  69.4 0.9 %collective-permute-start.16 = (bf16[320,128]{1,0:T(8,128)(2,1)S(1)}, bf16[320,128]{1,0:T(8,128)(2,1)S(1)}, u32[]{:S(2)}, u32[]{:S(2)}) collective-permute-start(bf16[320,128]{1,0:T(8,128)(2,1)S(1)} %get-tuple-element.63), channel_id=1, source_target_pairs={{0,12},{1,9},{2,14},{3,11},{4,8},{5,13},{6,10},{7,15},{8,4},{9,1},... | collective-permute-start | bytes 245768 | tf_op jit(solution)/shard_map/ppermute | solution.py:504
  70.3 1.5 %feed.3 = (bf16[320,128]{1,0:T(8,128)(2,1)S(1)}, bf16[320,128]{1,0:T(8,128)(2,1)S(1)}) custom-call(bf16[256,320]{1,0:T(8,128)(2,1)S(1)} %get-tuple-element.64.refs_0_, bf16[320,2560]{1,0:T(8,128)(2,1)S(1)} %bitcast.18, bf16[320,1280]{1,0:T(8,128)(2,1)S(1)} %bitcast.22), custom_call_target="tpu_custom_call" | custom-call | flops 629145600 | bytes 3000000 | tf_op jit(solution)/shard_map/feed/pallas_call | solution.py:467
  71.8 0.1 collective-permute-start.17
  71.8 2.6 %collective-permute-done.15.refs_0_ = bf16[320,128]{1,0:T(8,128)(2,1)S(1)} collective-permute-done((bf16[320,128]{1,0:T(8,128)(2,1)S(1)}, bf16[320,128]{1,0:T(8,128)(2,1)S(1)}, u32[]{:S(2)}, u32[]{:S(2)}) %collective-permute-start.15) | collective-permute-done | bytes 81952 | tf_op jit(solution)/shard_map/ppermute | solution.py:504
  74.4 1.9 %collective-permute-done.16.refs_1_ = bf16[320,128]{1,0:T(8,128)(2,1)S(1)} collective-permute-done((bf16[320,128]{1,0:T(8,128)(2,1)S(1)}, bf16[320,128]{1,0:T(8,128)(2,1)S(1)}, u32[]{:S(2)}, u32[]{:S(2)}) %collective-permute-start.16) | collective-permute-done | bytes 81952 | tf_op jit(solution)/shard_map/ppermute | solution.py:504
  76.3 1.1 %collective-permute-done.17.refs_1_ = bf16[320,128]{1,0:T(8,128)(2,1)S(1)} collective-permute-done((bf16[320,128]{1,0:T(8,128)(2,1)S(1)}, bf16[320,128]{1,0:T(8,128)(2,1)S(1)}, u32[]{:S(2)}, u32[]{:S(2)}) %collective-permute-start.17) | collective-permute-done | bytes 81952 | tf_op jit(solution)/shard_map/ppermute | solution.py:504
  77.4 0.9 %unpack.1 = bf16[512,320]{1,0:T(8,128)(2,1)} custom-call(bf16[640,128]{1,0:T(8,128)(2,1)S(1)} %join.7.refs_0_, bf16[320,128]{1,0:T(8,128)(2,1)S(1)} %collective-permute-done.17.refs_1_, bf16[320,128]{1,0:T(8,128)(2,1)S(1)} %get-tuple-element.66.refs_2_), custom_call_target="tpu_custom_call" | custom-call | tf_op jit(solution)/shard_map/unpack/pallas_call | solution.py:546
  (23 shorter events, 0.1 us)
Async XLA Ops:
  0.0 12.4 %copy-start = (bf16[1,320,320]{2,1,0:T(8,128)(2,1)S(1)}, bf16[1,320,320]{2,1,0:T(8,128)(2,1)}, u32[]{:S(2)}) copy-start(bf16[1,320,320]{2,1,0:T(8,128)(2,1)} %param.13) | copy-start | bytes 614404
  0.0 12.3 %collective-permute-start = (bf16[512,320]{1,0:T(8,128)(2,1)}, bf16[512,320]{1,0:T(8,128)(2,1)S(1)}, u32[]{:S(2)}, u32[]{:S(2)}) collective-permute-start(bf16[512,320]{1,0:T(8,128)(2,1)} %bitcast.28), channel_id=1, source_target_pairs={{0,2},{2,0},{1,3},{3,1},{4,6},{6,4},{5,7},{7,5},{8,10},{10,8},{9,1... | collective-permute-start | bytes 983048 | tf_op jit(solution)/shard_map/ppermute | solution.py:486
  2.9 1.6 %copy-start.3 = (bf16[1,3,3,320,320]{4,3,2,1,0:T(8,128)(2,1)S(1)}, bf16[1,3,3,320,320]{4,3,2,1,0:T(8,128)(2,1)}, u32[]{:S(2)}) copy-start(bf16[1,3,3,320,320]{4,3,2,1,0:T(8,128)(2,1)} %param.11) | copy-start | bytes 5529604
  4.6 1.6 %copy-start.4 = (bf16[1,3,3,320,320]{4,3,2,1,0:T(8,128)(2,1)S(1)}, bf16[1,3,3,320,320]{4,3,2,1,0:T(8,128)(2,1)}, u32[]{:S(2)}) copy-start(bf16[1,3,3,320,320]{4,3,2,1,0:T(8,128)(2,1)} %param.12) | copy-start | bytes 5529604
  6.2 1.1 %copy-start.5 = (bf16[1,320,960]{2,1,0:T(8,128)(2,1)S(1)}, bf16[1,320,960]{2,1,0:T(8,128)(2,1)}, u32[]{:S(2)}) copy-start(bf16[1,320,960]{2,1,0:T(8,128)(2,1)} %param.14) | copy-start | bytes 1843204
  7.3 0.8 copy-start.7
  12.3 1.7 %collective-permute-start.1 = (bf16[512,320]{1,0:T(8,128)(2,1)S(1)}, bf16[512,320]{1,0:T(8,128)(2,1)S(1)}, u32[]{:S(2)}, u32[]{:S(2)}) collective-permute-start(bf16[512,320]{1,0:T(8,128)(2,1)S(1)} %collective-permute-done.refs_0_), channel_id=1, source_target_pairs={{0,1},{1,0},{2,3},{3,2},{4,5},{5,4},{6,7},{7,6},{8,9},{9,8},{10,11... | collective-permute-start | bytes 983048 | tf_op jit(solution)/shard_map/ppermute | solution.py:486
  18.1 5.6 %collective-permute-start.2 = (bf16[320,128]{1,0:T(8,128)(2,1)S(1)}, bf16[320,128]{1,0:T(8,128)(2,1)S(1)}, u32[]{:S(2)}, u32[]{:S(2)}) collective-permute-start(bf16[320,128]{1,0:T(8,128)(2,1)S(1)} %get-tuple-element.40), channel_id=1, source_target_pairs={{0,8},{1,5},{2,10},{3,7},{4,12},{5,1},{6,14},{7,3},{8,0},{9,13},{1... | collective-permute-start | bytes 245768 | tf_op jit(solution)/shard_map/ppermute | solution.py:504
  21.0 6.4 %collective-permute-start.3 = (bf16[320,128]{1,0:T(8,128)(2,1)S(1)}, bf16[320,128]{1,0:T(8,128)(2,1)S(1)}, u32[]{:S(2)}, u32[]{:S(2)}) collective-permute-start(bf16[320,128]{1,0:T(8,128)(2,1)S(1)} %get-tuple-element.41), channel_id=1, source_target_pairs={{0,12},{1,9},{2,14},{3,11},{4,8},{5,13},{6,10},{7,15},{8,4},{9,1},... | collective-permute-start | bytes 245768 | tf_op jit(solution)/shard_map/ppermute | solution.py:504
  22.3 6.7 %copy-start.1 = (bf16[1,320,2560]{2,1,0:T(8,128)(2,1)S(1)}, bf16[1,320,2560]{2,1,0:T(8,128)(2,1)}, u32[]{:S(2)}) copy-start(bf16[1,320,2560]{2,1,0:T(8,128)(2,1)} %param.16) | copy-start | bytes 4915204
  22.3 6.7 %copy-start.2 = (bf16[1,1280,320]{1,2,0:T(8,128)(2,1)S(1)}, bf16[1,1280,320]{1,2,0:T(8,128)(2,1)}, u32[]{:S(2)}) copy-start(bf16[1,1280,320]{1,2,0:T(8,128)(2,1)} %param.17) | copy-start | bytes 2457604
  22.3 6.7 %copy-start.6 = (bf16[1,320,320]{2,1,0:T(8,128)(2,1)S(1)}, bf16[1,320,320]{2,1,0:T(8,128)(2,1)}, u32[]{:S(2)}) copy-start(bf16[1,320,320]{2,1,0:T(8,128)(2,1)} %param.15) | copy-start | bytes 614404
  23.2 5.9 %collective-permute-start.4 = (bf16[320,128]{1,0:T(8,128)(2,1)S(1)}, bf16[320,128]{1,0:T(8,128)(2,1)S(1)}, u32[]{:S(2)}, u32[]{:S(2)}) collective-permute-start(bf16[320,128]{1,0:T(8,128)(2,1)S(1)} %get-tuple-element.46), channel_id=1, source_target_pairs={{0,4},{1,13},{2,6},{3,15},{4,0},{5,9},{6,2},{7,11},{8,12},{9,5},{1... | collective-permute-start | bytes 245768 | tf_op jit(solution)/shard_map/ppermute | solution.py:504
  33.2 8.4 %collective-permute-start.5 = (bf16[320,128]{1,0:T(8,128)(2,1)S(1)}, bf16[320,128]{1,0:T(8,128)(2,1)S(1)}, u32[]{:S(2)}, u32[]{:S(2)}) collective-permute-start(bf16[320,128]{1,0:T(8,128)(2,1)S(1)} %get-tuple-element.49), channel_id=1, source_target_pairs={{0,10},{1,7},{2,8},{3,5},{4,14},{5,3},{6,12},{7,1},{8,2},{9,15},{1... | collective-permute-start | bytes 245768 | tf_op jit(solution)/shard_map/ppermute | solution.py:504
  37.0 8.1 %collective-permute-start.6 = (bf16[320,128]{1,0:T(8,128)(2,1)S(1)}, bf16[320,128]{1,0:T(8,128)(2,1)S(1)}, u32[]{:S(2)}, u32[]{:S(2)}) collective-permute-start(bf16[320,128]{1,0:T(8,128)(2,1)S(1)} %get-tuple-element.50), channel_id=1, source_target_pairs={{0,14},{1,11},{2,12},{3,9},{4,10},{5,15},{6,8},{7,13},{8,6},{9,3},... | collective-permute-start | bytes 245768 | tf_op jit(solution)/shard_map/ppermute | solution.py:504
  38.9 7.0 %collective-permute-start.7 = (bf16[320,128]{1,0:T(8,128)(2,1)S(1)}, bf16[320,128]{1,0:T(8,128)(2,1)S(1)}, u32[]{:S(2)}, u32[]{:S(2)}) collective-permute-start(bf16[320,128]{1,0:T(8,128)(2,1)S(1)} %get-tuple-element.52), channel_id=1, source_target_pairs={{0,6},{1,15},{2,4},{3,13},{4,2},{5,11},{6,0},{7,9},{8,14},{9,7},{1... | collective-permute-start | bytes 245768 | tf_op jit(solution)/shard_map/ppermute | solution.py:504
  40.2 6.6 %collective-permute-start.8 = (bf16[320,128]{1,0:T(8,128)(2,1)S(1)}, bf16[320,128]{1,0:T(8,128)(2,1)S(1)}, u32[]{:S(2)}, u32[]{:S(2)}) collective-permute-start(bf16[320,128]{1,0:T(8,128)(2,1)S(1)} %get-tuple-element.53), channel_id=1, source_target_pairs={{0,2},{1,3},{2,0},{3,1},{4,6},{5,7},{6,4},{7,5},{8,10},{9,11},{10,... | collective-permute-start | bytes 245768 | tf_op jit(solution)/shard_map/ppermute | solution.py:504
  45.1 3.0 %collective-permute-start.9 = (bf16[640,128]{1,0:T(8,128)(2,1)S(1)}, bf16[640,128]{1,0:T(8,128)(2,1)S(1)}, u32[]{:S(2)}, u32[]{:S(2)}) collective-permute-start(bf16[640,128]{1,0:T(8,128)(2,1)S(1)} %join.5.refs_0_), channel_id=1, source_target_pairs={{0,1},{1,0},{2,3},{3,2},{4,5},{5,4},{6,7},{7,6},{8,9},{9,8},{10,11... | collective-permute-start | bytes 491528 | tf_op jit(solution)/shard_map/ppermute | solution.py:486
  45.9 1.3 %collective-permute-start.10 = (bf16[320,128]{1,0:T(8,128)(2,1)S(1)}, bf16[320,128]{1,0:T(8,128)(2,1)S(1)}, u32[]{:S(2)}, u32[]{:S(2)}) collective-permute-start(bf16[320,128]{1,0:T(8,128)(2,1)S(1)} %collective-permute-done.7.refs_1_), channel_id=1, source_target_pairs={{0,1},{1,0},{2,3},{3,2},{4,5},{5,4},{6,7},{7,6},{8,9},{9,8},{10,11... | collective-permute-start | bytes 245768 | tf_op jit(solution)/shard_map/ppermute | solution.py:486
  46.8 1.3 %collective-permute-start.11 = (bf16[320,128]{1,0:T(8,128)(2,1)S(1)}, bf16[320,128]{1,0:T(8,128)(2,1)S(1)}, u32[]{:S(2)}, u32[]{:S(2)}) collective-permute-start(bf16[320,128]{1,0:T(8,128)(2,1)S(1)} %collective-permute-done.8.refs_2_), channel_id=1, source_target_pairs={{0,1},{1,0},{2,3},{3,2},{4,5},{5,4},{6,7},{7,6},{8,9},{9,8},{10,11... | collective-permute-start | bytes 245768 | tf_op jit(solution)/shard_map/ppermute | solution.py:486
  52.4 9.4 %collective-permute-start.12 = (bf16[320,128]{1,0:T(8,128)(2,1)S(1)}, bf16[320,128]{1,0:T(8,128)(2,1)S(1)}, u32[]{:S(2)}, u32[]{:S(2)}) collective-permute-start(bf16[320,128]{1,0:T(8,128)(2,1)S(1)} %get-tuple-element.54), channel_id=1, source_target_pairs={{0,8},{1,5},{2,10},{3,7},{4,12},{5,1},{6,14},{7,3},{8,0},{9,13},{1... | collective-permute-start | bytes 245768 | tf_op jit(solution)/shard_map/ppermute | solution.py:504
  54.6 7.2 %collective-permute-start.13 = (bf16[320,128]{1,0:T(8,128)(2,1)S(1)}, bf16[320,128]{1,0:T(8,128)(2,1)S(1)}, u32[]{:S(2)}, u32[]{:S(2)}) collective-permute-start(bf16[320,128]{1,0:T(8,128)(2,1)S(1)} %get-tuple-element.55), channel_id=1, source_target_pairs={{0,12},{1,9},{2,14},{3,11},{4,8},{5,13},{6,10},{7,15},{8,4},{9,1},... | collective-permute-start | bytes 245768 | tf_op jit(solution)/shard_map/ppermute | solution.py:504
  55.9 6.6 %collective-permute-start.14 = (bf16[320,128]{1,0:T(8,128)(2,1)S(1)}, bf16[320,128]{1,0:T(8,128)(2,1)S(1)}, u32[]{:S(2)}, u32[]{:S(2)}) collective-permute-start(bf16[320,128]{1,0:T(8,128)(2,1)S(1)} %get-tuple-element.60), channel_id=1, source_target_pairs={{0,4},{1,13},{2,6},{3,15},{4,0},{5,9},{6,2},{7,11},{8,12},{9,5},{1... | collective-permute-start | bytes 245768 | tf_op jit(solution)/shard_map/ppermute | solution.py:504
  66.5 7.9 %collective-permute-start.15 = (bf16[320,128]{1,0:T(8,128)(2,1)S(1)}, bf16[320,128]{1,0:T(8,128)(2,1)S(1)}, u32[]{:S(2)}, u32[]{:S(2)}) collective-permute-start(bf16[320,128]{1,0:T(8,128)(2,1)S(1)} %get-tuple-element.62), channel_id=1, source_target_pairs={{0,8},{1,5},{2,10},{3,7},{4,12},{5,1},{6,14},{7,3},{8,0},{9,13},{1... | collective-permute-start | bytes 245768 | tf_op jit(solution)/shard_map/ppermute | solution.py:504
  69.4 6.9 %collective-permute-start.16 = (bf16[320,128]{1,0:T(8,128)(2,1)S(1)}, bf16[320,128]{1,0:T(8,128)(2,1)S(1)}, u32[]{:S(2)}, u32[]{:S(2)}) collective-permute-start(bf16[320,128]{1,0:T(8,128)(2,1)S(1)} %get-tuple-element.63), channel_id=1, source_target_pairs={{0,12},{1,9},{2,14},{3,11},{4,8},{5,13},{6,10},{7,15},{8,4},{9,1},... | collective-permute-start | bytes 245768 | tf_op jit(solution)/shard_map/ppermute | solution.py:504
  71.8 5.7 %collective-permute-start.17 = (bf16[320,128]{1,0:T(8,128)(2,1)S(1)}, bf16[320,128]{1,0:T(8,128)(2,1)S(1)}, u32[]{:S(2)}, u32[]{:S(2)}) collective-permute-start(bf16[320,128]{1,0:T(8,128)(2,1)S(1)} %get-tuple-element.65), channel_id=1, source_target_pairs={{0,4},{1,13},{2,6},{3,15},{4,0},{5,9},{6,2},{7,11},{8,12},{9,5},{1... | collective-permute-start | bytes 245768 | tf_op jit(solution)/shard_map/ppermute | solution.py:504

commit v5 on v4

--- a/solution.py
+++ b/solution.py
@@ -17,17 +17,14 @@
 BF16 = jnp.bfloat16
 
 
-def orders(count):
-    far, near, low = list(range(count // 2, count)), [], count // 2
-    while low > 1:
-        near += range(low // 2, low)
-        low //= 2
-    return far + near + [0], near + far + [0]
-
-
-def partners(spot, core, count):
-    even, odd = orders(count)
-    return [spot ^ jnp.where(core % 2 == 0, a, b) for a, b in zip(even, odd)]
+def order_out(count):
+    return [d for d in reversed(range(count)) if d % 2] + [
+        d for d in reversed(range(count)) if d % 2 == 0
+    ]
+
+
+def order_back(count):
+    return order_out(count)
 
 
 def round_up(value, unit):
@@ -158,16 +155,16 @@
     zero = jnp.zeros((8, lanes), F32)
 
     height = dense_rows(part, channels)
-    for core, base, arrived in ((here, own_base, own), (1 - here, other_base, other)):
+    for base, arrived in ((own_base, own), (other_base, other)):
         if ways == 1:
             place = pl.ds(pl.multiple_of(base, columns), own_rows * columns)
             field[place, lanes - LANES :] = jnp.zeros((own_rows * columns, LANES), F32)
             field[place, :channels] = arrived[0][...].astype(F32)
             continue
         held = [(block, at) for block in arrived for at in range(0, block.shape[0], height)]
-        for (block, at), q in zip(held, partners(spot, core, shards)):
+        for (block, at), d in zip(held, order_back(shards)):
             for i, first, values in unpack_part(block, at, part, channels):
-                place = pl.multiple_of(base + q * part + first, 8)
+                place = pl.multiple_of(base + (spot ^ d) * part + first, 8)
                 field[pl.ds(place, values.shape[0]), i * LANES : (i + 1) * LANES] = values
 
     def sum_row(i, carry):
@@ -199,8 +196,8 @@
     scale, shift = group_scale(total, square, entries, group_width, channels)
     first_row = here * own_rows
     activate(hidden, targets, scale, shift, rows, columns, first_row, 0, own_rows + 2)
-    for i, q in enumerate(partners(spot, here, shards)):
-        start = q * part
+    for i, d in enumerate(order_out(shards)):
+        start = (spot ^ d) * part
         base = field[pl.ds(pl.multiple_of(own_base + start, 8), part), :]
         if i < sooner:
             convolve_part(targets, kernels.at[1], start, columns, base, outs[i])
@@ -211,8 +208,8 @@
 def finish_kernel(columns, shards, sooner, keep, middle, edge, pair, kernels, *outs):
     part = keep.shape[0] // (shards - sooner)
     spot = lax.axis_index("shard")
-    for i, q in enumerate(partners(spot, lax.axis_index("halo"), shards)[sooner:]):
-        start = q * part
+    for i, d in enumerate(order_out(shards)[sooner:]):
+        start = (spot ^ d) * part
         base = keep[i * part : (i + 1) * part, :]
         convolve_part((middle, edge, pair), kernels.at[1], start, columns, base, outs[i])
 
@@ -370,7 +367,8 @@
 
     height = dense_rows(pixels, channels)
     held = [(block, at) for block in parts for at in range(0, block.shape[0], height)]
-    for f, (block, at) in enumerate(held):
+    for (block, at), d in zip(held, order_out(frames)):
+        f = order_back(frames).index(d)
         for i, first, values in unpack_part(block, at, pixels, channels):
             rows = slice(f * pixels + first, f * pixels + first + values.shape[0])
             width = min(LANES, channels - i * LANES)
@@ -486,22 +484,19 @@
     return lax.ppermute(block, axis, [(i, (i + distance) % count) for i in range(count)])
 
 
-def exchange(parts, across=0):
-    sizes = [lax.axis_size(axis) for axis in ("shard", "section", "halo")]
-    shards, sections, cores = sizes
+def exchange(parts, order, across=0):
+    shards, sections = lax.axis_size("shard"), lax.axis_size("section")
     arrived = []
-    for part, *distance in zip(parts, *orders(shards)):
-        if across or any(distance):
+    for part, d in zip(parts, order):
+        if across:
             route = [
-                (
-                    (z * sections + s) * cores + h,
-                    ((z ^ distance[h % 2]) * sections + (s + across) % sections) * cores + h,
-                )
+                (z * sections + s, (z ^ d) * sections + (s + across) % sections)
                 for z in range(shards)
                 for s in range(sections)
-                for h in range(cores)
             ]
-            part = lax.ppermute(part, ("shard", "section", "halo"), route)
+            part = lax.ppermute(part, ("shard", "section"), route)
+        elif d:
+            part = lax.ppermute(part, "shard", [(z, z ^ d) for z in range(shards)])
         arrived.append(part)
     return arrived
 
@@ -532,10 +527,10 @@
     pixels = tokens // shards
     height = dense_rows(pixels, channels)
     held = [(block, at) for block in parts for at in range(0, block.shape[0], height)]
-    places = partners(lax.axis_index("shard"), lax.axis_index("halo"), shards)
-    for (block, at), q in zip(held, places):
+    spot = lax.axis_index("shard")
+    for (block, at), d in zip(held, order_back(shards)):
         for i, first, values in unpack_part(block, at, pixels, channels):
-            place = pl.multiple_of(q * pixels + first, 16)
+            place = pl.multiple_of((spot ^ d) * pixels + first, 16)
             width = min(LANES, channels - i * LANES)
             lanes = slice(i * LANES, i * LANES + width)
             whole[pl.ds(place, values.shape[0]), lanes] = values[:, :width].astype(BF16)
@@ -598,10 +593,10 @@
             half,
             shards,
         )
-        parts = exchange(parts)
+        parts = exchange(parts, order_out(shards))
         parts = [join(parts[: shards // 2]), *parts[shards // 2 :]]
         parts = temporal(parts, temporal_weights)
-        parts = exchange(parts, across=0 if last else 1)
+        parts = exchange(parts, order_back(shards), across=0 if last else 1)
         own = [join(parts[: shards // 2]), *parts[shards // 2 :]]
     return unpack(own, shards, own_rows * columns, channels).reshape(features.shape)
 

time: 78.5 us -> 76.2 us (0.971)
  waiting for transfers between devices: 29.7 us -> 24.9 us
  starting transfers between devices: 21.1 us -> 23.6 us
    ppermute x13, waiting for transfers between devices: 22.9 us -> 18.1 us  [the longest x9 14.3 us: exchange(): part = lax.ppermute(part, 'shard', [(z, z ^ d) for z in range(shards)])]
    ppermute x13, starting transfers between devices: 18.1 us -> 20.5 us  [the longest x9 13.7 us: exchange(): part = lax.ppermute(part, 'shard', [(z, z ^ d) for z in range(shards)])]
  transfers between devices with their start and end apart: 18 -> 18, of which waited for: 16 -> 15; matrix products, arithmetic and copies ran while one was open for 0% -> 0% of each run, Pallas kernels for 7% -> 7%
where the time goes in v5:
time: 76.2 us; the launch traced here: 76 us
  waiting for transfers between devices  24.9 us (33%)
  starting transfers between devices  23.6 us (31%)
  Pallas kernels  22.7 us (30%)
  local copies, waits for them, and re-layouts  4.36 us (6%)
    ppermute x9, waiting for transfers between devices, exchange(): part = lax.ppermute(part, 'shard', [(z, z ^ d) for z in range(shards)])  14.3 us
    ppermute x9, starting transfers between devices, exchange(): part = lax.ppermute(part, 'shard', [(z, z ^ d) for z in range(shards)])  13.7 us
    pallas_call x2, Pallas kernels, spatial(): pl.pallas_call(functools.partial(spatial_kernel, rows, half, columns, cha...  8.36 us
    pallas_call x2, Pallas kernels, temporal(): pl.pallas_call(functools.partial(temporal_kernel, frames, ways, sooner),...  8.13 us
    ppermute x4, starting transfers between devices, exchange(): part = lax.ppermute(part, ('shard', 'section'), route)  6.88 us
    ppermute x5, waiting for transfers between devices, send(): lax.ppermute(block, axis, [(i, (i + distance) % count) for i in range(cou...  6.86 us
    unnamed x16, local copies, waits for them, and re-layouts  4.35 us
    ppermute x4, waiting for transfers between devices, exchange(): part = lax.ppermute(part, ('shard', 'section'), route)  3.81 us
  transfers between devices with their start and end apart: 18, of which 15 were waited for; matrix products, arithmetic and copies ran while one was open for 0% of the time, Pallas kernels for 7%

profile of v5, /device:TPU:0, one launch (start us, length us, event | category | flops | bytes accessed | tf_op | source)
XLA Modules:
  0.0 76.0 jit_solution(3506729452278273619)
XLA Ops:
  0.0 2.9 %collective-permute-start = (bf16[512,320]{1,0:T(8,128)(2,1)}, bf16[512,320]{1,0:T(8,128)(2,1)S(1)}, u32[]{:S(2)}, u32[]{:S(2)}) collective-permute-start(bf16[512,320]{1,0:T(8,128)(2,1)} %bitcast.28), channel_id=1, source_target_pairs={{0,2},{2,0},{1,3},{3,1},{4,6},{6,4},{5,7},{7,5},{8,10},{10,8},{9,1... | collective-permute-start | bytes 983048 | tf_op jit(solution)/shard_map/ppermute | solution.py:484
  2.9 1.6 %copy-done.3 = bf16[1,3,3,320,320]{4,3,2,1,0:T(8,128)(2,1)S(1)} copy-done((bf16[1,3,3,320,320]{4,3,2,1,0:T(8,128)(2,1)S(1)}, bf16[1,3,3,320,320]{4,3,2,1,0:T(8,128)(2,1)}, u32[]{:S(2)}) %copy-start.3) | copy-done | bytes 1843224
  4.6 1.6 %copy-done.4 = bf16[1,3,3,320,320]{4,3,2,1,0:T(8,128)(2,1)S(1)} copy-done((bf16[1,3,3,320,320]{4,3,2,1,0:T(8,128)(2,1)S(1)}, bf16[1,3,3,320,320]{4,3,2,1,0:T(8,128)(2,1)}, u32[]{:S(2)}) %copy-start.4) | copy-done | bytes 1843224
  6.2 1.1 %copy-done.5 = bf16[1,320,960]{2,1,0:T(8,128)(2,1)S(1)} copy-done((bf16[1,320,960]{2,1,0:T(8,128)(2,1)S(1)}, bf16[1,320,960]{2,1,0:T(8,128)(2,1)}, u32[]{:S(2)}) %copy-start.5) | copy-done | bytes 614424
  7.3 0.7 prepare.1
  8.0 4.2 %collective-permute-done.refs_0_ = bf16[512,320]{1,0:T(8,128)(2,1)S(1)} collective-permute-done((bf16[512,320]{1,0:T(8,128)(2,1)}, bf16[512,320]{1,0:T(8,128)(2,1)S(1)}, u32[]{:S(2)}, u32[]{:S(2)}) %collective-permute-start) | collective-permute-done | bytes 327712 | tf_op jit(solution)/shard_map/ppermute | solution.py:484
  12.3 0.0 collective-permute-start.1
  12.3 0.1 multiply_cosine_fusion
  12.4 0.2 fusion
  12.6 1.4 %collective-permute-done.1.refs_1_ = bf16[512,320]{1,0:T(8,128)(2,1)S(1)} collective-permute-done((bf16[512,320]{1,0:T(8,128)(2,1)S(1)}, bf16[512,320]{1,0:T(8,128)(2,1)S(1)}, u32[]{:S(2)}, u32[]{:S(2)}) %collective-permute-start.1) | collective-permute-done | bytes 327712 | tf_op jit(solution)/shard_map/ppermute | solution.py:484
  14.0 4.1 %spatial.2 = (bf16[320,128]{1,0:T(8,128)(2,1)S(1)}, bf16[320,128]{1,0:T(8,128)(2,1)S(1)}, f32[256,384]{1,0:T(8,128)S(1)}, bf16[640,256]{1,0:T(8,128)(2,1)S(1)}, ...) custom-call(bf16[512,320]{1,0:T(8,128)(2,1)S(1)} %collective-permute-done.refs_0_, ...), custom_call_target="tpu_custom_call" | custom-call | flops 3221225472 | bytes 6000000 | tf_op jit(solution)/shard_map/spatial/pallas_call | solution.py:233
  18.1 3.9 %collective-permute-start.2 = (bf16[320,128]{1,0:T(8,128)(2,1)S(1)}, bf16[320,128]{1,0:T(8,128)(2,1)S(1)}, u32[]{:S(2)}, u32[]{:S(2)}) collective-permute-start(bf16[320,128]{1,0:T(8,128)(2,1)S(1)} %get-tuple-element.40), channel_id=1, source_target_pairs={{0,12},{4,8},{8,4},{12,0},{1,13},{5,9},{9,5},{13,1},{2,14},{6,10},... | collective-permute-start | bytes 245768 | tf_op jit(solution)/shard_map/ppermute | solution.py:499
  22.0 0.0 collective-permute-start.3
  22.0 0.8 %finish.2 = (bf16[320,128]{1,0:T(8,128)(2,1)S(1)}, bf16[320,128]{1,0:T(8,128)(2,1)S(1)}) custom-call(f32[256,384]{1,0:T(8,128)S(1)} %get-tuple-element.42.keep, bf16[640,256]{1,0:T(8,128)(2,1)S(1)} %get-tuple-element.43.middle, bf16[640,128]{1,0:T(8,128)(2,1)S(1)} %get-tuple-element.44.edge, bf16[640,128]{1,0:T(8,128)(2,1)S(1)} %get-tuple-element.45.pair, ...), custom_call_target="tpu_custom_call" | custom-call | flops 536870912 | bytes 3000000 | tf_op jit(solution)/shard_map/finish/pallas_call | solution.py:264
  22.8 0.7 collective-permute-start.4
  23.5 1.7 %collective-permute-done.2.refs_0_ = bf16[320,128]{1,0:T(8,128)(2,1)S(1)} collective-permute-done((bf16[320,128]{1,0:T(8,128)(2,1)S(1)}, bf16[320,128]{1,0:T(8,128)(2,1)S(1)}, u32[]{:S(2)}, u32[]{:S(2)}) %collective-permute-start.2) | collective-permute-done | bytes 81952 | tf_op jit(solution)/shard_map/ppermute | solution.py:499
  25.3 2.4 %collective-permute-done.3.refs_1_ = bf16[320,128]{1,0:T(8,128)(2,1)S(1)} collective-permute-done((bf16[320,128]{1,0:T(8,128)(2,1)S(1)}, bf16[320,128]{1,0:T(8,128)(2,1)S(1)}, u32[]{:S(2)}, u32[]{:S(2)}) %collective-permute-start.3) | collective-permute-done | bytes 81952 | tf_op jit(solution)/shard_map/ppermute | solution.py:499
  27.7 2.3 %collective-permute-done.4.refs_1_ = bf16[320,128]{1,0:T(8,128)(2,1)S(1)} collective-permute-done((bf16[320,128]{1,0:T(8,128)(2,1)S(1)}, bf16[320,128]{1,0:T(8,128)(2,1)S(1)}, u32[]{:S(2)}, u32[]{:S(2)}) %collective-permute-start.4) | collective-permute-done | bytes 81952 | tf_op jit(solution)/shard_map/ppermute | solution.py:499
  30.0 4.1 %temporal.2 = (bf16[320,128]{1,0:T(8,128)(2,1)S(1)}, bf16[320,128]{1,0:T(8,128)(2,1)S(1)}, bf16[256,320]{1,0:T(8,128)(2,1)S(1)}) custom-call(bf16[640,128]{1,0:T(8,128)(2,1)S(1)} %join.4.refs_0_, bf16[320,128]{1,0:T(8,128)(2,1)S(1)} %collective-permute-done.4.refs_1_, bf16[320,128]{1,0:T(8,128)(2,1)S(1)} %get-tuple-element.47.refs_2_, ...), custom_call_target="tpu_custom_call" | custom-call | flops 1132462080 | bytes 4000000 | tf_op jit(solution)/shard_map/temporal/pallas_call | solution.py:446
  34.1 2.9 %collective-permute-start.5 = (bf16[320,128]{1,0:T(8,128)(2,1)S(1)}, bf16[320,128]{1,0:T(8,128)(2,1)S(1)}, u32[]{:S(2)}, u32[]{:S(2)}) collective-permute-start(bf16[320,128]{1,0:T(8,128)(2,1)S(1)} %get-tuple-element.49), channel_id=1, source_target_pairs={{0,14},{2,12},{4,10},{6,8},{8,6},{10,4},{12,2},{14,0},{1,15},{3,13... | collective-permute-start | bytes 245768 | tf_op jit(solution)/shard_map/ppermute | solution.py:497
  37.0 0.0 collective-permute-start.6
  37.0 1.5 %feed.2 = (bf16[320,128]{1,0:T(8,128)(2,1)S(1)}, bf16[320,128]{1,0:T(8,128)(2,1)S(1)}) custom-call(bf16[256,320]{1,0:T(8,128)(2,1)S(1)} %get-tuple-element.51.refs_0_, bf16[320,2560]{1,0:T(8,128)(2,1)S(1)} %bitcast.16, bf16[320,1280]{1,0:T(8,128)(2,1)S(1)} %bitcast.20), custom_call_target="tpu_custom_call" | custom-call | flops 629145600 | bytes 3000000 | tf_op jit(solution)/shard_map/feed/pallas_call | solution.py:465
  38.4 3.4 %collective-permute-start.7 = (bf16[320,128]{1,0:T(8,128)(2,1)S(1)}, bf16[320,128]{1,0:T(8,128)(2,1)S(1)}, u32[]{:S(2)}, u32[]{:S(2)}) collective-permute-start(bf16[320,128]{1,0:T(8,128)(2,1)S(1)} %get-tuple-element.52), channel_id=1, source_target_pairs={{0,10},{2,8},{4,14},{6,12},{8,2},{10,0},{12,6},{14,4},{1,11},{3,9}... | collective-permute-start | bytes 245768 | tf_op jit(solution)/shard_map/ppermute | solution.py:497
  41.9 0.5 collective-permute-start.8
  42.4 0.0 collective-permute-done.5.refs_0_
  42.4 0.7 collective-permute-done.6.refs_1_
  43.1 0.1 collective-permute-start.9
  43.2 1.6 %collective-permute-done.7.refs_1_ = bf16[320,128]{1,0:T(8,128)(2,1)S(1)} collective-permute-done((bf16[320,128]{1,0:T(8,128)(2,1)S(1)}, bf16[320,128]{1,0:T(8,128)(2,1)S(1)}, u32[]{:S(2)}, u32[]{:S(2)}) %collective-permute-start.7) | collective-permute-done | bytes 81952 | tf_op jit(solution)/shard_map/ppermute | solution.py:497
  44.8 1.5 %collective-permute-done.8.refs_2_ = bf16[320,128]{1,0:T(8,128)(2,1)S(1)} collective-permute-done((bf16[320,128]{1,0:T(8,128)(2,1)S(1)}, bf16[320,128]{1,0:T(8,128)(2,1)S(1)}, u32[]{:S(2)}, u32[]{:S(2)}) %collective-permute-start.8) | collective-permute-done | bytes 81952 | tf_op jit(solution)/shard_map/ppermute | solution.py:497
  46.3 0.0 collective-permute-start.11
  46.3 0.0 collective-permute-done.10.refs_4_
  46.3 1.3 %collective-permute-done.11.refs_5_ = bf16[320,128]{1,0:T(8,128)(2,1)S(1)} collective-permute-done((bf16[320,128]{1,0:T(8,128)(2,1)S(1)}, bf16[320,128]{1,0:T(8,128)(2,1)S(1)}, u32[]{:S(2)}, u32[]{:S(2)}) %collective-permute-start.11) | collective-permute-done | bytes 81952 | tf_op jit(solution)/shard_map/ppermute | solution.py:484
  47.6 0.0 collective-permute-done.9.refs_3_
  47.6 4.3 %spatial.3 = (bf16[320,128]{1,0:T(8,128)(2,1)S(1)}, bf16[320,128]{1,0:T(8,128)(2,1)S(1)}, f32[256,384]{1,0:T(8,128)S(1)}, bf16[640,256]{1,0:T(8,128)(2,1)S(1)}, ...) custom-call(bf16[640,128]{1,0:T(8,128)(2,1)S(1)} %join.5.refs_0_, ...), custom_call_target="tpu_custom_call" | custom-call | flops 3221225472 | bytes 6000000 | tf_op jit(solution)/shard_map/spatial/pallas_call | solution.py:233
  51.9 2.0 %collective-permute-start.12 = (bf16[320,128]{1,0:T(8,128)(2,1)S(1)}, bf16[320,128]{1,0:T(8,128)(2,1)S(1)}, u32[]{:S(2)}, u32[]{:S(2)}) collective-permute-start(bf16[320,128]{1,0:T(8,128)(2,1)S(1)} %get-tuple-element.54), channel_id=1, source_target_pairs={{0,12},{4,8},{8,4},{12,0},{1,13},{5,9},{9,5},{13,1},{2,14},{6,10},... | collective-permute-start | bytes 245768 | tf_op jit(solution)/shard_map/ppermute | solution.py:499
  53.9 0.8 %finish.3 = (bf16[320,128]{1,0:T(8,128)(2,1)S(1)}, bf16[320,128]{1,0:T(8,128)(2,1)S(1)}) custom-call(f32[256,384]{1,0:T(8,128)S(1)} %get-tuple-element.56.keep, bf16[640,256]{1,0:T(8,128)(2,1)S(1)} %get-tuple-element.57.middle, bf16[640,128]{1,0:T(8,128)(2,1)S(1)} %get-tuple-element.58.edge, bf16[640,128]{1,0:T(8,128)(2,1)S(1)} %get-tuple-element.59.pair, ...), custom_call_target="tpu_custom_call" | custom-call | flops 536870912 | bytes 3000000 | tf_op jit(solution)/shard_map/finish/pallas_call | solution.py:264
  54.7 2.5 %collective-permute-start.14 = (bf16[320,128]{1,0:T(8,128)(2,1)S(1)}, bf16[320,128]{1,0:T(8,128)(2,1)S(1)}, u32[]{:S(2)}, u32[]{:S(2)}) collective-permute-start(bf16[320,128]{1,0:T(8,128)(2,1)S(1)} %get-tuple-element.60), channel_id=1, source_target_pairs={{0,8},{4,12},{8,0},{12,4},{1,9},{5,13},{9,1},{13,5},{2,10},{6,14},... | collective-permute-start | bytes 245768 | tf_op jit(solution)/shard_map/ppermute | solution.py:499
  57.2 1.9 %collective-permute-done.12.refs_0_ = bf16[320,128]{1,0:T(8,128)(2,1)S(1)} collective-permute-done((bf16[320,128]{1,0:T(8,128)(2,1)S(1)}, bf16[320,128]{1,0:T(8,128)(2,1)S(1)}, u32[]{:S(2)}, u32[]{:S(2)}) %collective-permute-start.12) | collective-permute-done | bytes 81952 | tf_op jit(solution)/shard_map/ppermute | solution.py:499
  59.1 2.2 %collective-permute-done.13.refs_1_ = bf16[320,128]{1,0:T(8,128)(2,1)S(1)} collective-permute-done((bf16[320,128]{1,0:T(8,128)(2,1)S(1)}, bf16[320,128]{1,0:T(8,128)(2,1)S(1)}, u32[]{:S(2)}, u32[]{:S(2)}) %collective-permute-start.13) | collective-permute-done | bytes 81952 | tf_op jit(solution)/shard_map/ppermute | solution.py:499
  61.3 0.8 %collective-permute-done.14.refs_1_ = bf16[320,128]{1,0:T(8,128)(2,1)S(1)} collective-permute-done((bf16[320,128]{1,0:T(8,128)(2,1)S(1)}, bf16[320,128]{1,0:T(8,128)(2,1)S(1)}, u32[]{:S(2)}, u32[]{:S(2)}) %collective-permute-start.14) | collective-permute-done | bytes 81952 | tf_op jit(solution)/shard_map/ppermute | solution.py:499
  62.1 4.1 %temporal.3 = (bf16[320,128]{1,0:T(8,128)(2,1)S(1)}, bf16[320,128]{1,0:T(8,128)(2,1)S(1)}, bf16[256,320]{1,0:T(8,128)(2,1)S(1)}) custom-call(bf16[640,128]{1,0:T(8,128)(2,1)S(1)} %join.6.refs_0_, bf16[320,128]{1,0:T(8,128)(2,1)S(1)} %collective-permute-done.14.refs_1_, bf16[320,128]{1,0:T(8,128)(2,1)S(1)} %get-tuple-element.61.refs_2_, ...), custom_call_target="tpu_custom_call" | custom-call | flops 1132462080 | bytes 4000000 | tf_op jit(solution)/shard_map/temporal/pallas_call | solution.py:446
  66.2 2.0 %collective-permute-start.15 = (bf16[320,128]{1,0:T(8,128)(2,1)S(1)}, bf16[320,128]{1,0:T(8,128)(2,1)S(1)}, u32[]{:S(2)}, u32[]{:S(2)}) collective-permute-start(bf16[320,128]{1,0:T(8,128)(2,1)S(1)} %get-tuple-element.62), channel_id=1, source_target_pairs={{0,12},{4,8},{8,4},{12,0},{1,13},{5,9},{9,5},{13,1},{2,14},{6,10},... | collective-permute-start | bytes 245768 | tf_op jit(solution)/shard_map/ppermute | solution.py:499
  68.2 1.5 %feed.3 = (bf16[320,128]{1,0:T(8,128)(2,1)S(1)}, bf16[320,128]{1,0:T(8,128)(2,1)S(1)}) custom-call(bf16[256,320]{1,0:T(8,128)(2,1)S(1)} %get-tuple-element.64.refs_0_, bf16[320,2560]{1,0:T(8,128)(2,1)S(1)} %bitcast.18, bf16[320,1280]{1,0:T(8,128)(2,1)S(1)} %bitcast.22), custom_call_target="tpu_custom_call" | custom-call | flops 629145600 | bytes 3000000 | tf_op jit(solution)/shard_map/feed/pallas_call | solution.py:465
  69.6 2.5 %collective-permute-start.17 = (bf16[320,128]{1,0:T(8,128)(2,1)S(1)}, bf16[320,128]{1,0:T(8,128)(2,1)S(1)}, u32[]{:S(2)}, u32[]{:S(2)}) collective-permute-start(bf16[320,128]{1,0:T(8,128)(2,1)S(1)} %get-tuple-element.65), channel_id=1, source_target_pairs={{0,8},{4,12},{8,0},{12,4},{1,9},{5,13},{9,1},{13,5},{2,10},{6,14},... | collective-permute-start | bytes 245768 | tf_op jit(solution)/shard_map/ppermute | solution.py:499
  72.2 0.5 collective-permute-done.15.refs_0_
  72.6 1.6 %collective-permute-done.16.refs_1_ = bf16[320,128]{1,0:T(8,128)(2,1)S(1)} collective-permute-done((bf16[320,128]{1,0:T(8,128)(2,1)S(1)}, bf16[320,128]{1,0:T(8,128)(2,1)S(1)}, u32[]{:S(2)}, u32[]{:S(2)}) %collective-permute-start.16) | collective-permute-done | bytes 81952 | tf_op jit(solution)/shard_map/ppermute | solution.py:499
  74.3 0.9 %collective-permute-done.17.refs_1_ = bf16[320,128]{1,0:T(8,128)(2,1)S(1)} collective-permute-done((bf16[320,128]{1,0:T(8,128)(2,1)S(1)}, bf16[320,128]{1,0:T(8,128)(2,1)S(1)}, u32[]{:S(2)}, u32[]{:S(2)}) %collective-permute-start.17) | collective-permute-done | bytes 81952 | tf_op jit(solution)/shard_map/ppermute | solution.py:499
  75.1 0.9 %unpack.1 = bf16[512,320]{1,0:T(8,128)(2,1)} custom-call(bf16[640,128]{1,0:T(8,128)(2,1)S(1)} %join.7.refs_0_, bf16[320,128]{1,0:T(8,128)(2,1)S(1)} %collective-permute-done.17.refs_1_, bf16[320,128]{1,0:T(8,128)(2,1)S(1)} %get-tuple-element.66.refs_2_), custom_call_target="tpu_custom_call" | custom-call | tf_op jit(solution)/shard_map/unpack/pallas_call | solution.py:541
  (23 shorter events, 0.1 us)
Async XLA Ops:
  0.0 12.4 %copy-start = (bf16[1,320,320]{2,1,0:T(8,128)(2,1)S(1)}, bf16[1,320,320]{2,1,0:T(8,128)(2,1)}, u32[]{:S(2)}) copy-start(bf16[1,320,320]{2,1,0:T(8,128)(2,1)} %param.13) | copy-start | bytes 614404
  0.0 12.3 %collective-permute-start = (bf16[512,320]{1,0:T(8,128)(2,1)}, bf16[512,320]{1,0:T(8,128)(2,1)S(1)}, u32[]{:S(2)}, u32[]{:S(2)}) collective-permute-start(bf16[512,320]{1,0:T(8,128)(2,1)} %bitcast.28), channel_id=1, source_target_pairs={{0,2},{2,0},{1,3},{3,1},{4,6},{6,4},{5,7},{7,5},{8,10},{10,8},{9,1... | collective-permute-start | bytes 983048 | tf_op jit(solution)/shard_map/ppermute | solution.py:484
  2.9 1.6 %copy-start.3 = (bf16[1,3,3,320,320]{4,3,2,1,0:T(8,128)(2,1)S(1)}, bf16[1,3,3,320,320]{4,3,2,1,0:T(8,128)(2,1)}, u32[]{:S(2)}) copy-start(bf16[1,3,3,320,320]{4,3,2,1,0:T(8,128)(2,1)} %param.11) | copy-start | bytes 5529604
  4.6 1.6 %copy-start.4 = (bf16[1,3,3,320,320]{4,3,2,1,0:T(8,128)(2,1)S(1)}, bf16[1,3,3,320,320]{4,3,2,1,0:T(8,128)(2,1)}, u32[]{:S(2)}) copy-start(bf16[1,3,3,320,320]{4,3,2,1,0:T(8,128)(2,1)} %param.12) | copy-start | bytes 5529604
  6.2 1.1 %copy-start.5 = (bf16[1,320,960]{2,1,0:T(8,128)(2,1)S(1)}, bf16[1,320,960]{2,1,0:T(8,128)(2,1)}, u32[]{:S(2)}) copy-start(bf16[1,320,960]{2,1,0:T(8,128)(2,1)} %param.14) | copy-start | bytes 1843204
  7.3 0.8 copy-start.7
  12.3 1.7 %collective-permute-start.1 = (bf16[512,320]{1,0:T(8,128)(2,1)S(1)}, bf16[512,320]{1,0:T(8,128)(2,1)S(1)}, u32[]{:S(2)}, u32[]{:S(2)}) collective-permute-start(bf16[512,320]{1,0:T(8,128)(2,1)S(1)} %collective-permute-done.refs_0_), channel_id=1, source_target_pairs={{0,1},{1,0},{2,3},{3,2},{4,5},{5,4},{6,7},{7,6},{8,9},{9,8},{10,11... | collective-permute-start | bytes 983048 | tf_op jit(solution)/shard_map/ppermute | solution.py:484
  18.1 7.2 %collective-permute-start.2 = (bf16[320,128]{1,0:T(8,128)(2,1)S(1)}, bf16[320,128]{1,0:T(8,128)(2,1)S(1)}, u32[]{:S(2)}, u32[]{:S(2)}) collective-permute-start(bf16[320,128]{1,0:T(8,128)(2,1)S(1)} %get-tuple-element.40), channel_id=1, source_target_pairs={{0,12},{4,8},{8,4},{12,0},{1,13},{5,9},{9,5},{13,1},{2,14},{6,10},... | collective-permute-start | bytes 245768 | tf_op jit(solution)/shard_map/ppermute | solution.py:499
  22.0 5.7 %collective-permute-start.3 = (bf16[320,128]{1,0:T(8,128)(2,1)S(1)}, bf16[320,128]{1,0:T(8,128)(2,1)S(1)}, u32[]{:S(2)}, u32[]{:S(2)}) collective-permute-start(bf16[320,128]{1,0:T(8,128)(2,1)S(1)} %get-tuple-element.41), channel_id=1, source_target_pairs={{0,4},{4,0},{8,12},{12,8},{1,5},{5,1},{9,13},{13,9},{2,6},{6,2},{1... | collective-permute-start | bytes 245768 | tf_op jit(solution)/shard_map/ppermute | solution.py:499
  22.0 8.0 %copy-start.1 = (bf16[1,320,2560]{2,1,0:T(8,128)(2,1)S(1)}, bf16[1,320,2560]{2,1,0:T(8,128)(2,1)}, u32[]{:S(2)}) copy-start(bf16[1,320,2560]{2,1,0:T(8,128)(2,1)} %param.16) | copy-start | bytes 4915204
  22.0 8.0 %copy-start.2 = (bf16[1,1280,320]{1,2,0:T(8,128)(2,1)S(1)}, bf16[1,1280,320]{1,2,0:T(8,128)(2,1)}, u32[]{:S(2)}) copy-start(bf16[1,1280,320]{1,2,0:T(8,128)(2,1)} %param.17) | copy-start | bytes 2457604
  22.0 8.0 %copy-start.6 = (bf16[1,320,320]{2,1,0:T(8,128)(2,1)S(1)}, bf16[1,320,320]{2,1,0:T(8,128)(2,1)}, u32[]{:S(2)}) copy-start(bf16[1,320,320]{2,1,0:T(8,128)(2,1)} %param.15) | copy-start | bytes 614404
  22.8 7.2 %collective-permute-start.4 = (bf16[320,128]{1,0:T(8,128)(2,1)S(1)}, bf16[320,128]{1,0:T(8,128)(2,1)S(1)}, u32[]{:S(2)}, u32[]{:S(2)}) collective-permute-start(bf16[320,128]{1,0:T(8,128)(2,1)S(1)} %get-tuple-element.46), channel_id=1, source_target_pairs={{0,8},{4,12},{8,0},{12,4},{1,9},{5,13},{9,1},{13,5},{2,10},{6,14},... | collective-permute-start | bytes 245768 | tf_op jit(solution)/shard_map/ppermute | solution.py:499
  34.1 8.3 %collective-permute-start.5 = (bf16[320,128]{1,0:T(8,128)(2,1)S(1)}, bf16[320,128]{1,0:T(8,128)(2,1)S(1)}, u32[]{:S(2)}, u32[]{:S(2)}) collective-permute-start(bf16[320,128]{1,0:T(8,128)(2,1)S(1)} %get-tuple-element.49), channel_id=1, source_target_pairs={{0,14},{2,12},{4,10},{6,8},{8,6},{10,4},{12,2},{14,0},{1,15},{3,13... | collective-permute-start | bytes 245768 | tf_op jit(solution)/shard_map/ppermute | solution.py:497
  37.0 6.2 %collective-permute-start.6 = (bf16[320,128]{1,0:T(8,128)(2,1)S(1)}, bf16[320,128]{1,0:T(8,128)(2,1)S(1)}, u32[]{:S(2)}, u32[]{:S(2)}) collective-permute-start(bf16[320,128]{1,0:T(8,128)(2,1)S(1)} %get-tuple-element.50), channel_id=1, source_target_pairs={{0,6},{2,4},{4,2},{6,0},{8,14},{10,12},{12,10},{14,8},{1,7},{3,5},... | collective-permute-start | bytes 245768 | tf_op jit(solution)/shard_map/ppermute | solution.py:497
  38.4 6.3 %collective-permute-start.7 = (bf16[320,128]{1,0:T(8,128)(2,1)S(1)}, bf16[320,128]{1,0:T(8,128)(2,1)S(1)}, u32[]{:S(2)}, u32[]{:S(2)}) collective-permute-start(bf16[320,128]{1,0:T(8,128)(2,1)S(1)} %get-tuple-element.52), channel_id=1, source_target_pairs={{0,10},{2,8},{4,14},{6,12},{8,2},{10,0},{12,6},{14,4},{1,11},{3,9}... | collective-permute-start | bytes 245768 | tf_op jit(solution)/shard_map/ppermute | solution.py:497
  41.9 4.4 %collective-permute-start.8 = (bf16[320,128]{1,0:T(8,128)(2,1)S(1)}, bf16[320,128]{1,0:T(8,128)(2,1)S(1)}, u32[]{:S(2)}, u32[]{:S(2)}) collective-permute-start(bf16[320,128]{1,0:T(8,128)(2,1)S(1)} %get-tuple-element.53), channel_id=1, source_target_pairs={{0,2},{2,0},{4,6},{6,4},{8,10},{10,8},{12,14},{14,12},{1,3},{3,1},... | collective-permute-start | bytes 245768 | tf_op jit(solution)/shard_map/ppermute | solution.py:497
  43.1 4.5 %collective-permute-start.9 = (bf16[640,128]{1,0:T(8,128)(2,1)S(1)}, bf16[640,128]{1,0:T(8,128)(2,1)S(1)}, u32[]{:S(2)}, u32[]{:S(2)}) collective-permute-start(bf16[640,128]{1,0:T(8,128)(2,1)S(1)} %join.5.refs_0_), channel_id=1, source_target_pairs={{0,1},{1,0},{2,3},{3,2},{4,5},{5,4},{6,7},{7,6},{8,9},{9,8},{10,11... | collective-permute-start | bytes 491528 | tf_op jit(solution)/shard_map/ppermute | solution.py:484
  44.8 1.5 %collective-permute-start.10 = (bf16[320,128]{1,0:T(8,128)(2,1)S(1)}, bf16[320,128]{1,0:T(8,128)(2,1)S(1)}, u32[]{:S(2)}, u32[]{:S(2)}) collective-permute-start(bf16[320,128]{1,0:T(8,128)(2,1)S(1)} %collective-permute-done.7.refs_1_), channel_id=1, source_target_pairs={{0,1},{1,0},{2,3},{3,2},{4,5},{5,4},{6,7},{7,6},{8,9},{9,8},{10,11... | collective-permute-start | bytes 245768 | tf_op jit(solution)/shard_map/ppermute | solution.py:484
  46.3 1.3 %collective-permute-start.11 = (bf16[320,128]{1,0:T(8,128)(2,1)S(1)}, bf16[320,128]{1,0:T(8,128)(2,1)S(1)}, u32[]{:S(2)}, u32[]{:S(2)}) collective-permute-start(bf16[320,128]{1,0:T(8,128)(2,1)S(1)} %collective-permute-done.8.refs_2_), channel_id=1, source_target_pairs={{0,1},{1,0},{2,3},{3,2},{4,5},{5,4},{6,7},{7,6},{8,9},{9,8},{10,11... | collective-permute-start | bytes 245768 | tf_op jit(solution)/shard_map/ppermute | solution.py:484
  51.9 7.3 %collective-permute-start.12 = (bf16[320,128]{1,0:T(8,128)(2,1)S(1)}, bf16[320,128]{1,0:T(8,128)(2,1)S(1)}, u32[]{:S(2)}, u32[]{:S(2)}) collective-permute-start(bf16[320,128]{1,0:T(8,128)(2,1)S(1)} %get-tuple-element.54), channel_id=1, source_target_pairs={{0,12},{4,8},{8,4},{12,0},{1,13},{5,9},{9,5},{13,1},{2,14},{6,10},... | collective-permute-start | bytes 245768 | tf_op jit(solution)/shard_map/ppermute | solution.py:499
  53.9 7.4 %collective-permute-start.13 = (bf16[320,128]{1,0:T(8,128)(2,1)S(1)}, bf16[320,128]{1,0:T(8,128)(2,1)S(1)}, u32[]{:S(2)}, u32[]{:S(2)}) collective-permute-start(bf16[320,128]{1,0:T(8,128)(2,1)S(1)} %get-tuple-element.55), channel_id=1, source_target_pairs={{0,4},{4,0},{8,12},{12,8},{1,5},{5,1},{9,13},{13,9},{2,6},{6,2},{1... | collective-permute-start | bytes 245768 | tf_op jit(solution)/shard_map/ppermute | solution.py:499
  54.7 7.4 %collective-permute-start.14 = (bf16[320,128]{1,0:T(8,128)(2,1)S(1)}, bf16[320,128]{1,0:T(8,128)(2,1)S(1)}, u32[]{:S(2)}, u32[]{:S(2)}) collective-permute-start(bf16[320,128]{1,0:T(8,128)(2,1)S(1)} %get-tuple-element.60), channel_id=1, source_target_pairs={{0,8},{4,12},{8,0},{12,4},{1,9},{5,13},{9,1},{13,5},{2,10},{6,14},... | collective-permute-start | bytes 245768 | tf_op jit(solution)/shard_map/ppermute | solution.py:499
  66.2 6.5 %collective-permute-start.15 = (bf16[320,128]{1,0:T(8,128)(2,1)S(1)}, bf16[320,128]{1,0:T(8,128)(2,1)S(1)}, u32[]{:S(2)}, u32[]{:S(2)}) collective-permute-start(bf16[320,128]{1,0:T(8,128)(2,1)S(1)} %get-tuple-element.62), channel_id=1, source_target_pairs={{0,12},{4,8},{8,4},{12,0},{1,13},{5,9},{9,5},{13,1},{2,14},{6,10},... | collective-permute-start | bytes 245768 | tf_op jit(solution)/shard_map/ppermute | solution.py:499
  68.2 6.1 %collective-permute-start.16 = (bf16[320,128]{1,0:T(8,128)(2,1)S(1)}, bf16[320,128]{1,0:T(8,128)(2,1)S(1)}, u32[]{:S(2)}, u32[]{:S(2)}) collective-permute-start(bf16[320,128]{1,0:T(8,128)(2,1)S(1)} %get-tuple-element.63), channel_id=1, source_target_pairs={{0,4},{4,0},{8,12},{12,8},{1,5},{5,1},{9,13},{13,9},{2,6},{6,2},{1... | collective-permute-start | bytes 245768 | tf_op jit(solution)/shard_map/ppermute | solution.py:499
  69.6 5.5 %collective-permute-start.17 = (bf16[320,128]{1,0:T(8,128)(2,1)S(1)}, bf16[320,128]{1,0:T(8,128)(2,1)S(1)}, u32[]{:S(2)}, u32[]{:S(2)}) collective-permute-start(bf16[320,128]{1,0:T(8,128)(2,1)S(1)} %get-tuple-element.65), channel_id=1, source_target_pairs={{0,8},{4,12},{8,0},{12,4},{1,9},{5,13},{9,1},{13,5},{2,10},{6,14},... | collective-permute-start | bytes 245768 | tf_op jit(solution)/shard_map/ppermute | solution.py:499

commit v6 on v5

--- a/solution.py
+++ b/solution.py
@@ -138,7 +138,8 @@
     target[WIDE // LANES * pixels :, :] = both.astype(BF16)
 
 
-def spatial_kernel(rows, half, columns, channels, group_width, step, ways, shards, sooner, *refs):
+def spatial_kernel(rows, half, columns, channels, group_width, step, ways, order, sooner, *refs):
+    shards = len(order)
     own, other = refs[:ways], refs[ways : 2 * ways]
     kernels, embeds = refs[2 * ways : 2 * ways + 2]
     outs = refs[2 * ways + 2 : 2 * ways + 2 + sooner]
@@ -156,15 +157,10 @@
 
     height = dense_rows(part, channels)
     for base, arrived in ((own_base, own), (other_base, other)):
-        if ways == 1:
-            place = pl.ds(pl.multiple_of(base, columns), own_rows * columns)
-            field[place, lanes - LANES :] = jnp.zeros((own_rows * columns, LANES), F32)
-            field[place, :channels] = arrived[0][...].astype(F32)
-            continue
         held = [(block, at) for block in arrived for at in range(0, block.shape[0], height)]
-        for (block, at), d in zip(held, order_back(shards)):
+        for (block, at), d in zip(held, order):
             for i, first, values in unpack_part(block, at, part, channels):
-                place = pl.multiple_of(base + (spot ^ d) * part + first, 8)
+                place = pl.multiple_of(base + (d if step == 0 else spot ^ d) * part + first, 8)
                 field[pl.ds(place, values.shape[0]), i * LANES : (i + 1) * LANES] = values
 
     def sum_row(i, carry):
@@ -240,7 +236,7 @@
             channels // GROUPS,
             step,
             ways,
-            shards,
+            order_back(shards) if step else list(range(shards)),
             sooner,
         ),
         out_shape=[piece] * sooner
@@ -521,6 +517,37 @@
     )(*parts)
 
 
+def pack_kernel(shards, field, *outs):
+    tokens, channels = field.shape
+    pixels, full = tokens // shards, channels // LANES
+    height = dense_rows(pixels, channels)
+    for q in range(shards):
+        out = outs[q * len(outs) // shards]
+        at = q * height % out.shape[0]
+        for i in range(full):
+            block = field[q * pixels : (q + 1) * pixels, i * LANES : (i + 1) * LANES]
+            out[at + i * pixels : at + (i + 1) * pixels, :] = block
+        if channels % LANES:
+            halves = [
+                field[q * pixels + j : q * pixels + j + pixels // 2, full * LANES :]
+                for j in (0, pixels // 2)
+            ]
+            out[at + full * pixels : at + height, :] = jnp.concatenate(halves, axis=1)
+
+
+def pack(field, shards, ways):
+    rows = dense_rows(*field.shape) // ways
+    vmem = pl.BlockSpec(memory_space=pltpu.VMEM)
+    return pl.pallas_call(
+        functools.partial(pack_kernel, shards),
+        out_shape=[jax.ShapeDtypeStruct((rows, LANES), BF16)] * ways,
+        in_specs=[vmem],
+        out_specs=[vmem] * ways,
+        compiler_params=pltpu.CompilerParams(vmem_limit_bytes=4 * 1024 * 1024),
+        name="pack",
+    )(field)
+
+
 def unpack_kernel(shards, *refs):
     parts, (whole,) = refs[:-1], refs[-1:]
     tokens, channels = whole.shape
@@ -573,12 +600,13 @@
     rows = own_rows * half
     shards = lax.axis_size("shard")
 
-    moved = send(features.reshape(own_rows * columns, channels), "section", 1)
+    start = pack(features.reshape(own_rows * columns, channels), shards, 2)
+    *early, moved = [send(block, "section", 1) for block in start]
     embeds = embed_time(timesteps[0], time_weight[0])
     spatial_weights, padded = prepare(conv_first[0], conv_second[0], qkv_weight[0])
 
     moved, spatial_weights, padded = lax.optimization_barrier((moved, spatial_weights, padded))
-    own = [moved]
+    own = [*early, moved]
     temporal_weights = (padded, attn_out[0], geglu_in[0], geglu_out[0].T)
     for denoise_step in range(STEPS):
         last = denoise_step == STEPS - 1

time: 76.2 us -> 75.6 us (level)
  waiting for transfers between devices: 24.9 us -> 21.9 us
  local copies, waits for them, and re-layouts: 4.36 us -> 5.39 us
    ppermute x5 -> x7, waiting for transfers between devices: 6.86 us -> 3.94 us  [send(): lax.ppermute(block, axis, [(i, (i + distance) % count) for i in range(cou...]
    unnamed x16, local copies, waits for them, and re-layouts: 4.35 us -> 5.39 us
    ppermute x5 -> x7, starting transfers between devices: 3.02 us -> 3.67 us  [send(): lax.ppermute(block, axis, [(i, (i + distance) % count) for i in range(cou...]
  transfers between devices with their start and end apart: 18 -> 20, of which waited for: 15 -> 16; matrix products, arithmetic and copies ran while one was open for 0% -> 1% of each run, Pallas kernels for 7% -> 7%
where the time goes in v6:
time: 75.6 us; the launch traced here: 75.3 us
  starting transfers between devices  24.2 us (32%)
  Pallas kernels  22.8 us (30%)
  waiting for transfers between devices  21.9 us (29%)
  local copies, waits for them, and re-layouts  5.39 us (7%)
  other arithmetic  0.79 us (1%)
    ppermute x9, waiting for transfers between devices, exchange(): part = lax.ppermute(part, 'shard', [(z, z ^ d) for z in range(shards)])  14.1 us
    ppermute x9, starting transfers between devices, exchange(): part = lax.ppermute(part, 'shard', [(z, z ^ d) for z in range(shards)])  13.7 us
    pallas_call x2, Pallas kernels, spatial(): pl.pallas_call(functools.partial(spatial_kernel, rows, half, columns, cha...  8.37 us
    pallas_call x2, Pallas kernels, temporal(): pl.pallas_call(functools.partial(temporal_kernel, frames, ways, sooner),...  8.13 us
    ppermute x4, starting transfers between devices, exchange(): part = lax.ppermute(part, ('shard', 'section'), route)  6.88 us
    unnamed x16, local copies, waits for them, and re-layouts  5.39 us
    ppermute x7, waiting for transfers between devices, send(): lax.ppermute(block, axis, [(i, (i + distance) % count) for i in range(cou...  3.94 us
    ppermute x4, waiting for transfers between devices, exchange(): part = lax.ppermute(part, ('shard', 'section'), route)  3.81 us
  transfers between devices with their start and end apart: 20, of which 16 were waited for; matrix products, arithmetic and copies ran while one was open for 1% of the time, Pallas kernels for 7%

profile of v6, /device:TPU:0, one launch (start us, length us, event | category | flops | bytes accessed | tf_op | source)
XLA Modules:
  0.0 75.3 jit_solution(9085136788209451456)
XLA Ops:
  0.0 1.0 %copy-done.6 = bf16[1,1,8,64,320]{4,3,2,1,0:T(8,128)(2,1)S(1)} copy-done((bf16[1,1,8,64,320]{4,3,2,1,0:T(8,128)(2,1)S(1)}, bf16[1,1,8,64,320]{4,3,2,1,0:T(8,128)(2,1)}, u32[]{:S(2)}) %copy-start.6) | copy-done | bytes 327704
  1.0 0.1 pack.1
  1.1 3.0 %collective-permute-start = (bf16[640,128]{1,0:T(8,128)(2,1)S(1)}, bf16[640,128]{1,0:T(8,128)(2,1)S(1)}, u32[]{:S(2)}, u32[]{:S(2)}) collective-permute-start(bf16[640,128]{1,0:T(8,128)(2,1)S(1)} %get-tuple-element.38), channel_id=1, source_target_pairs={{0,2},{2,0},{1,3},{3,1},{4,6},{6,4},{5,7},{7,5},{8,10},{10,8},{9,1... | collective-permute-start | bytes 491528 | tf_op jit(solution)/shard_map/ppermute | solution.py:480
  4.1 0.1 collective-permute-start.1
  4.2 0.7 convert_bitcast_fusion
  4.9 1.6 %copy-done.3 = bf16[1,3,3,320,320]{4,3,2,1,0:T(8,128)(2,1)S(1)} copy-done((bf16[1,3,3,320,320]{4,3,2,1,0:T(8,128)(2,1)S(1)}, bf16[1,3,3,320,320]{4,3,2,1,0:T(8,128)(2,1)}, u32[]{:S(2)}) %copy-start.3) | copy-done | bytes 1843224
  6.5 1.6 %copy-done.4 = bf16[1,3,3,320,320]{4,3,2,1,0:T(8,128)(2,1)S(1)} copy-done((bf16[1,3,3,320,320]{4,3,2,1,0:T(8,128)(2,1)S(1)}, bf16[1,3,3,320,320]{4,3,2,1,0:T(8,128)(2,1)}, u32[]{:S(2)}) %copy-start.4) | copy-done | bytes 1843224
  8.1 1.1 %copy-done.5 = bf16[1,320,960]{2,1,0:T(8,128)(2,1)S(1)} copy-done((bf16[1,320,960]{2,1,0:T(8,128)(2,1)S(1)}, bf16[1,320,960]{2,1,0:T(8,128)(2,1)}, u32[]{:S(2)}) %copy-start.5) | copy-done | bytes 614424
  9.2 0.7 prepare.1
  10.0 0.1 multiply_cosine_fusion
  10.1 1.8 %collective-permute-done.1.refs_1_ = bf16[640,128]{1,0:T(8,128)(2,1)S(1)} collective-permute-done((bf16[640,128]{1,0:T(8,128)(2,1)S(1)}, bf16[640,128]{1,0:T(8,128)(2,1)S(1)}, u32[]{:S(2)}, u32[]{:S(2)}) %collective-permute-start.1) | collective-permute-done | bytes 163872 | tf_op jit(solution)/shard_map/ppermute | solution.py:480
  11.9 0.5 collective-permute-start.2
  12.4 0.2 fusion
  12.6 0.9 %collective-permute-done.2.refs_2_ = bf16[640,128]{1,0:T(8,128)(2,1)S(1)} collective-permute-done((bf16[640,128]{1,0:T(8,128)(2,1)S(1)}, bf16[640,128]{1,0:T(8,128)(2,1)S(1)}, u32[]{:S(2)}, u32[]{:S(2)}) %collective-permute-start.2) | collective-permute-done | bytes 163872 | tf_op jit(solution)/shard_map/ppermute | solution.py:480
  13.5 4.1 %spatial.2 = (bf16[320,128]{1,0:T(8,128)(2,1)S(1)}, bf16[320,128]{1,0:T(8,128)(2,1)S(1)}, f32[256,384]{1,0:T(8,128)S(1)}, bf16[640,256]{1,0:T(8,128)(2,1)S(1)}, ...) custom-call(bf16[640,128]{1,0:T(8,128)(2,1)S(1)} %collective-permute-done.refs_0_, ...), custom_call_target="tpu_custom_call" | custom-call | flops 3221225472 | bytes 6000000 | tf_op jit(solution)/shard_map/spatial/pallas_call | solution.py:229
  17.6 3.9 %collective-permute-start.4 = (bf16[320,128]{1,0:T(8,128)(2,1)S(1)}, bf16[320,128]{1,0:T(8,128)(2,1)S(1)}, u32[]{:S(2)}, u32[]{:S(2)}) collective-permute-start(bf16[320,128]{1,0:T(8,128)(2,1)S(1)} %get-tuple-element.44), channel_id=1, source_target_pairs={{0,12},{4,8},{8,4},{12,0},{1,13},{5,9},{9,5},{13,1},{2,14},{6,10},... | collective-permute-start | bytes 245768 | tf_op jit(solution)/shard_map/ppermute | solution.py:495
  21.5 0.8 %finish.2 = (bf16[320,128]{1,0:T(8,128)(2,1)S(1)}, bf16[320,128]{1,0:T(8,128)(2,1)S(1)}) custom-call(f32[256,384]{1,0:T(8,128)S(1)} %get-tuple-element.46.keep, bf16[640,256]{1,0:T(8,128)(2,1)S(1)} %get-tuple-element.47.middle, bf16[640,128]{1,0:T(8,128)(2,1)S(1)} %get-tuple-element.48.edge, bf16[640,128]{1,0:T(8,128)(2,1)S(1)} %get-tuple-element.49.pair, ...), custom_call_target="tpu_custom_call" | custom-call | flops 536870912 | bytes 3000000 | tf_op jit(solution)/shard_map/finish/pallas_call | solution.py:260
  22.3 0.7 collective-permute-start.6
  23.0 1.7 %collective-permute-done.4.refs_0_ = bf16[320,128]{1,0:T(8,128)(2,1)S(1)} collective-permute-done((bf16[320,128]{1,0:T(8,128)(2,1)S(1)}, bf16[320,128]{1,0:T(8,128)(2,1)S(1)}, u32[]{:S(2)}, u32[]{:S(2)}) %collective-permute-start.4) | collective-permute-done | bytes 81952 | tf_op jit(solution)/shard_map/ppermute | solution.py:495
  24.8 2.7 %collective-permute-done.5.refs_1_ = bf16[320,128]{1,0:T(8,128)(2,1)S(1)} collective-permute-done((bf16[320,128]{1,0:T(8,128)(2,1)S(1)}, bf16[320,128]{1,0:T(8,128)(2,1)S(1)}, u32[]{:S(2)}, u32[]{:S(2)}) %collective-permute-start.5) | collective-permute-done | bytes 81952 | tf_op jit(solution)/shard_map/ppermute | solution.py:495
  27.4 2.1 %collective-permute-done.6.refs_1_ = bf16[320,128]{1,0:T(8,128)(2,1)S(1)} collective-permute-done((bf16[320,128]{1,0:T(8,128)(2,1)S(1)}, bf16[320,128]{1,0:T(8,128)(2,1)S(1)}, u32[]{:S(2)}, u32[]{:S(2)}) %collective-permute-start.6) | collective-permute-done | bytes 81952 | tf_op jit(solution)/shard_map/ppermute | solution.py:495
  29.5 4.1 %temporal.2 = (bf16[320,128]{1,0:T(8,128)(2,1)S(1)}, bf16[320,128]{1,0:T(8,128)(2,1)S(1)}, bf16[256,320]{1,0:T(8,128)(2,1)S(1)}) custom-call(bf16[640,128]{1,0:T(8,128)(2,1)S(1)} %join.4.refs_0_, bf16[320,128]{1,0:T(8,128)(2,1)S(1)} %collective-permute-done.6.refs_1_, bf16[320,128]{1,0:T(8,128)(2,1)S(1)} %get-tuple-element.51.refs_2_, ...), custom_call_target="tpu_custom_call" | custom-call | flops 1132462080 | bytes 4000000 | tf_op jit(solution)/shard_map/temporal/pallas_call | solution.py:442
  33.6 1.9 %collective-permute-start.7 = (bf16[320,128]{1,0:T(8,128)(2,1)S(1)}, bf16[320,128]{1,0:T(8,128)(2,1)S(1)}, u32[]{:S(2)}, u32[]{:S(2)}) collective-permute-start(bf16[320,128]{1,0:T(8,128)(2,1)S(1)} %get-tuple-element.53), channel_id=1, source_target_pairs={{0,14},{2,12},{4,10},{6,8},{8,6},{10,4},{12,2},{14,0},{1,15},{3,13... | collective-permute-start | bytes 245768 | tf_op jit(solution)/shard_map/ppermute | solution.py:493
  35.4 0.7 collective-permute-start.8
  36.2 1.5 %feed.2 = (bf16[320,128]{1,0:T(8,128)(2,1)S(1)}, bf16[320,128]{1,0:T(8,128)(2,1)S(1)}) custom-call(bf16[256,320]{1,0:T(8,128)(2,1)S(1)} %get-tuple-element.55.refs_0_, bf16[320,2560]{1,0:T(8,128)(2,1)S(1)} %bitcast.16, bf16[320,1280]{1,0:T(8,128)(2,1)S(1)} %bitcast.20), custom_call_target="tpu_custom_call" | custom-call | flops 629145600 | bytes 3000000 | tf_op jit(solution)/shard_map/feed/pallas_call | solution.py:461
  37.6 3.7 %collective-permute-start.9 = (bf16[320,128]{1,0:T(8,128)(2,1)S(1)}, bf16[320,128]{1,0:T(8,128)(2,1)S(1)}, u32[]{:S(2)}, u32[]{:S(2)}) collective-permute-start(bf16[320,128]{1,0:T(8,128)(2,1)S(1)} %get-tuple-element.56), channel_id=1, source_target_pairs={{0,10},{2,8},{4,14},{6,12},{8,2},{10,0},{12,6},{14,4},{1,11},{3,9}... | collective-permute-start | bytes 245768 | tf_op jit(solution)/shard_map/ppermute | solution.py:493
  41.4 0.5 collective-permute-start.10
  41.9 0.6 collective-permute-done.8.refs_1_
  42.6 2.2 %collective-permute-done.9.refs_1_ = bf16[320,128]{1,0:T(8,128)(2,1)S(1)} collective-permute-done((bf16[320,128]{1,0:T(8,128)(2,1)S(1)}, bf16[320,128]{1,0:T(8,128)(2,1)S(1)}, u32[]{:S(2)}, u32[]{:S(2)}) %collective-permute-start.9) | collective-permute-done | bytes 81952 | tf_op jit(solution)/shard_map/ppermute | solution.py:493
  44.8 1.0 %collective-permute-done.10.refs_2_ = bf16[320,128]{1,0:T(8,128)(2,1)S(1)} collective-permute-done((bf16[320,128]{1,0:T(8,128)(2,1)S(1)}, bf16[320,128]{1,0:T(8,128)(2,1)S(1)}, u32[]{:S(2)}, u32[]{:S(2)}) %collective-permute-start.10) | collective-permute-done | bytes 81952 | tf_op jit(solution)/shard_map/ppermute | solution.py:493
  45.8 0.3 collective-permute-done.12.refs_4_
  46.1 1.0 %collective-permute-done.13.refs_5_ = bf16[320,128]{1,0:T(8,128)(2,1)S(1)} collective-permute-done((bf16[320,128]{1,0:T(8,128)(2,1)S(1)}, bf16[320,128]{1,0:T(8,128)(2,1)S(1)}, u32[]{:S(2)}, u32[]{:S(2)}) %collective-permute-start.13) | collective-permute-done | bytes 81952 | tf_op jit(solution)/shard_map/ppermute | solution.py:480
  47.1 4.3 %spatial.3 = (bf16[320,128]{1,0:T(8,128)(2,1)S(1)}, bf16[320,128]{1,0:T(8,128)(2,1)S(1)}, f32[256,384]{1,0:T(8,128)S(1)}, bf16[640,256]{1,0:T(8,128)(2,1)S(1)}, ...) custom-call(bf16[640,128]{1,0:T(8,128)(2,1)S(1)} %join.5.refs_0_, ...), custom_call_target="tpu_custom_call" | custom-call | flops 3221225472 | bytes 6000000 | tf_op jit(solution)/shard_map/spatial/pallas_call | solution.py:229
  51.4 1.3 %collective-permute-start.14 = (bf16[320,128]{1,0:T(8,128)(2,1)S(1)}, bf16[320,128]{1,0:T(8,128)(2,1)S(1)}, u32[]{:S(2)}, u32[]{:S(2)}) collective-permute-start(bf16[320,128]{1,0:T(8,128)(2,1)S(1)} %get-tuple-element.58), channel_id=1, source_target_pairs={{0,12},{4,8},{8,4},{12,0},{1,13},{5,9},{9,5},{13,1},{2,14},{6,10},... | collective-permute-start | bytes 245768 | tf_op jit(solution)/shard_map/ppermute | solution.py:495
  52.7 0.5 collective-permute-start.15
  53.2 0.8 %finish.3 = (bf16[320,128]{1,0:T(8,128)(2,1)S(1)}, bf16[320,128]{1,0:T(8,128)(2,1)S(1)}) custom-call(f32[256,384]{1,0:T(8,128)S(1)} %get-tuple-element.60.keep, bf16[640,256]{1,0:T(8,128)(2,1)S(1)} %get-tuple-element.61.middle, bf16[640,128]{1,0:T(8,128)(2,1)S(1)} %get-tuple-element.62.edge, bf16[640,128]{1,0:T(8,128)(2,1)S(1)} %get-tuple-element.63.pair, ...), custom_call_target="tpu_custom_call" | custom-call | flops 536870912 | bytes 3000000 | tf_op jit(solution)/shard_map/finish/pallas_call | solution.py:260
  54.0 2.7 %collective-permute-start.16 = (bf16[320,128]{1,0:T(8,128)(2,1)S(1)}, bf16[320,128]{1,0:T(8,128)(2,1)S(1)}, u32[]{:S(2)}, u32[]{:S(2)}) collective-permute-start(bf16[320,128]{1,0:T(8,128)(2,1)S(1)} %get-tuple-element.64), channel_id=1, source_target_pairs={{0,8},{4,12},{8,0},{12,4},{1,9},{5,13},{9,1},{13,5},{2,10},{6,14},... | collective-permute-start | bytes 245768 | tf_op jit(solution)/shard_map/ppermute | solution.py:495
  56.7 1.9 %collective-permute-done.14.refs_0_ = bf16[320,128]{1,0:T(8,128)(2,1)S(1)} collective-permute-done((bf16[320,128]{1,0:T(8,128)(2,1)S(1)}, bf16[320,128]{1,0:T(8,128)(2,1)S(1)}, u32[]{:S(2)}, u32[]{:S(2)}) %collective-permute-start.14) | collective-permute-done | bytes 81952 | tf_op jit(solution)/shard_map/ppermute | solution.py:495
  58.6 1.6 %collective-permute-done.15.refs_1_ = bf16[320,128]{1,0:T(8,128)(2,1)S(1)} collective-permute-done((bf16[320,128]{1,0:T(8,128)(2,1)S(1)}, bf16[320,128]{1,0:T(8,128)(2,1)S(1)}, u32[]{:S(2)}, u32[]{:S(2)}) %collective-permute-start.15) | collective-permute-done | bytes 81952 | tf_op jit(solution)/shard_map/ppermute | solution.py:495
  60.2 1.3 %collective-permute-done.16.refs_1_ = bf16[320,128]{1,0:T(8,128)(2,1)S(1)} collective-permute-done((bf16[320,128]{1,0:T(8,128)(2,1)S(1)}, bf16[320,128]{1,0:T(8,128)(2,1)S(1)}, u32[]{:S(2)}, u32[]{:S(2)}) %collective-permute-start.16) | collective-permute-done | bytes 81952 | tf_op jit(solution)/shard_map/ppermute | solution.py:495
  61.4 4.1 %temporal.3 = (bf16[320,128]{1,0:T(8,128)(2,1)S(1)}, bf16[320,128]{1,0:T(8,128)(2,1)S(1)}, bf16[256,320]{1,0:T(8,128)(2,1)S(1)}) custom-call(bf16[640,128]{1,0:T(8,128)(2,1)S(1)} %join.6.refs_0_, bf16[320,128]{1,0:T(8,128)(2,1)S(1)} %collective-permute-done.16.refs_1_, bf16[320,128]{1,0:T(8,128)(2,1)S(1)} %get-tuple-element.65.refs_2_, ...), custom_call_target="tpu_custom_call" | custom-call | flops 1132462080 | bytes 4000000 | tf_op jit(solution)/shard_map/temporal/pallas_call | solution.py:442
  65.5 2.1 %collective-permute-start.17 = (bf16[320,128]{1,0:T(8,128)(2,1)S(1)}, bf16[320,128]{1,0:T(8,128)(2,1)S(1)}, u32[]{:S(2)}, u32[]{:S(2)}) collective-permute-start(bf16[320,128]{1,0:T(8,128)(2,1)S(1)} %get-tuple-element.66), channel_id=1, source_target_pairs={{0,12},{4,8},{8,4},{12,0},{1,13},{5,9},{9,5},{13,1},{2,14},{6,10},... | collective-permute-start | bytes 245768 | tf_op jit(solution)/shard_map/ppermute | solution.py:495
  67.6 1.5 %feed.3 = (bf16[320,128]{1,0:T(8,128)(2,1)S(1)}, bf16[320,128]{1,0:T(8,128)(2,1)S(1)}) custom-call(bf16[256,320]{1,0:T(8,128)(2,1)S(1)} %get-tuple-element.68.refs_0_, bf16[320,2560]{1,0:T(8,128)(2,1)S(1)} %bitcast.18, bf16[320,1280]{1,0:T(8,128)(2,1)S(1)} %bitcast.22), custom_call_target="tpu_custom_call" | custom-call | flops 629145600 | bytes 3000000 | tf_op jit(solution)/shard_map/feed/pallas_call | solution.py:461
  69.1 2.4 %collective-permute-start.19 = (bf16[320,128]{1,0:T(8,128)(2,1)S(1)}, bf16[320,128]{1,0:T(8,128)(2,1)S(1)}, u32[]{:S(2)}, u32[]{:S(2)}) collective-permute-start(bf16[320,128]{1,0:T(8,128)(2,1)S(1)} %get-tuple-element.69), channel_id=1, source_target_pairs={{0,8},{4,12},{8,0},{12,4},{1,9},{5,13},{9,1},{13,5},{2,10},{6,14},... | collective-permute-start | bytes 245768 | tf_op jit(solution)/shard_map/ppermute | solution.py:495
  71.5 0.5 collective-permute-done.17.refs_0_
  72.0 1.5 %collective-permute-done.18.refs_1_ = bf16[320,128]{1,0:T(8,128)(2,1)S(1)} collective-permute-done((bf16[320,128]{1,0:T(8,128)(2,1)S(1)}, bf16[320,128]{1,0:T(8,128)(2,1)S(1)}, u32[]{:S(2)}, u32[]{:S(2)}) %collective-permute-start.18) | collective-permute-done | bytes 81952 | tf_op jit(solution)/shard_map/ppermute | solution.py:495
  73.5 0.9 %collective-permute-done.19.refs_1_ = bf16[320,128]{1,0:T(8,128)(2,1)S(1)} collective-permute-done((bf16[320,128]{1,0:T(8,128)(2,1)S(1)}, bf16[320,128]{1,0:T(8,128)(2,1)S(1)}, u32[]{:S(2)}, u32[]{:S(2)}) %collective-permute-start.19) | collective-permute-done | bytes 81952 | tf_op jit(solution)/shard_map/ppermute | solution.py:495
  74.5 0.9 %unpack.1 = bf16[512,320]{1,0:T(8,128)(2,1)} custom-call(bf16[640,128]{1,0:T(8,128)(2,1)S(1)} %join.7.refs_0_, bf16[320,128]{1,0:T(8,128)(2,1)S(1)} %collective-permute-done.19.refs_1_, bf16[320,128]{1,0:T(8,128)(2,1)S(1)} %get-tuple-element.70.refs_2_), custom_call_target="tpu_custom_call" | custom-call | tf_op jit(solution)/shard_map/unpack/pallas_call | solution.py:568
  (28 shorter events, 0.2 us)
Async XLA Ops:
  0.0 12.4 %copy-start = (bf16[1,320,320]{2,1,0:T(8,128)(2,1)S(1)}, bf16[1,320,320]{2,1,0:T(8,128)(2,1)}, u32[]{:S(2)}) copy-start(bf16[1,320,320]{2,1,0:T(8,128)(2,1)} %param.13) | copy-start | bytes 614404
  0.0 1.0 %copy-start.6 = (bf16[1,1,8,64,320]{4,3,2,1,0:T(8,128)(2,1)S(1)}, bf16[1,1,8,64,320]{4,3,2,1,0:T(8,128)(2,1)}, u32[]{:S(2)}) copy-start(bf16[1,1,8,64,320]{4,3,2,1,0:T(8,128)(2,1)} %param.9) | copy-start | bytes 983044
  1.1 10.7 %collective-permute-start = (bf16[640,128]{1,0:T(8,128)(2,1)S(1)}, bf16[640,128]{1,0:T(8,128)(2,1)S(1)}, u32[]{:S(2)}, u32[]{:S(2)}) collective-permute-start(bf16[640,128]{1,0:T(8,128)(2,1)S(1)} %get-tuple-element.38), channel_id=1, source_target_pairs={{0,2},{2,0},{1,3},{3,1},{4,6},{6,4},{5,7},{7,5},{8,10},{10,8},{9,1... | collective-permute-start | bytes 491528 | tf_op jit(solution)/shard_map/ppermute | solution.py:480
  4.1 7.7 %collective-permute-start.1 = (bf16[640,128]{1,0:T(8,128)(2,1)S(1)}, bf16[640,128]{1,0:T(8,128)(2,1)S(1)}, u32[]{:S(2)}, u32[]{:S(2)}) collective-permute-start(bf16[640,128]{1,0:T(8,128)(2,1)S(1)} %get-tuple-element.39), channel_id=1, source_target_pairs={{0,2},{2,0},{1,3},{3,1},{4,6},{6,4},{5,7},{7,5},{8,10},{10,8},{9,1... | collective-permute-start | bytes 491528 | tf_op jit(solution)/shard_map/ppermute | solution.py:480
  4.9 1.6 %copy-start.3 = (bf16[1,3,3,320,320]{4,3,2,1,0:T(8,128)(2,1)S(1)}, bf16[1,3,3,320,320]{4,3,2,1,0:T(8,128)(2,1)}, u32[]{:S(2)}) copy-start(bf16[1,3,3,320,320]{4,3,2,1,0:T(8,128)(2,1)} %param.11) | copy-start | bytes 5529604
  6.5 1.6 %copy-start.4 = (bf16[1,3,3,320,320]{4,3,2,1,0:T(8,128)(2,1)S(1)}, bf16[1,3,3,320,320]{4,3,2,1,0:T(8,128)(2,1)}, u32[]{:S(2)}) copy-start(bf16[1,3,3,320,320]{4,3,2,1,0:T(8,128)(2,1)} %param.12) | copy-start | bytes 5529604
  8.1 1.1 %copy-start.5 = (bf16[1,320,960]{2,1,0:T(8,128)(2,1)S(1)}, bf16[1,320,960]{2,1,0:T(8,128)(2,1)}, u32[]{:S(2)}) copy-start(bf16[1,320,960]{2,1,0:T(8,128)(2,1)} %param.14) | copy-start | bytes 1843204
  11.8 1.6 %collective-permute-start.3 = (bf16[640,128]{1,0:T(8,128)(2,1)S(1)}, bf16[640,128]{1,0:T(8,128)(2,1)S(1)}, u32[]{:S(2)}, u32[]{:S(2)}) collective-permute-start(bf16[640,128]{1,0:T(8,128)(2,1)S(1)} %collective-permute-done.1.refs_1_), channel_id=1, source_target_pairs={{0,1},{1,0},{2,3},{3,2},{4,5},{5,4},{6,7},{7,6},{8,9},{9,8},{10,11... | collective-permute-start | bytes 491528 | tf_op jit(solution)/shard_map/ppermute | solution.py:480
  11.9 1.6 %collective-permute-start.2 = (bf16[640,128]{1,0:T(8,128)(2,1)S(1)}, bf16[640,128]{1,0:T(8,128)(2,1)S(1)}, u32[]{:S(2)}, u32[]{:S(2)}) collective-permute-start(bf16[640,128]{1,0:T(8,128)(2,1)S(1)} %collective-permute-done.refs_0_), channel_id=1, source_target_pairs={{0,1},{1,0},{2,3},{3,2},{4,5},{5,4},{6,7},{7,6},{8,9},{9,8},{10,11... | collective-permute-start | bytes 491528 | tf_op jit(solution)/shard_map/ppermute | solution.py:480
  17.6 7.2 %collective-permute-start.4 = (bf16[320,128]{1,0:T(8,128)(2,1)S(1)}, bf16[320,128]{1,0:T(8,128)(2,1)S(1)}, u32[]{:S(2)}, u32[]{:S(2)}) collective-permute-start(bf16[320,128]{1,0:T(8,128)(2,1)S(1)} %get-tuple-element.44), channel_id=1, source_target_pairs={{0,12},{4,8},{8,4},{12,0},{1,13},{5,9},{9,5},{13,1},{2,14},{6,10},... | collective-permute-start | bytes 245768 | tf_op jit(solution)/shard_map/ppermute | solution.py:495
  21.5 5.9 %collective-permute-start.5 = (bf16[320,128]{1,0:T(8,128)(2,1)S(1)}, bf16[320,128]{1,0:T(8,128)(2,1)S(1)}, u32[]{:S(2)}, u32[]{:S(2)}) collective-permute-start(bf16[320,128]{1,0:T(8,128)(2,1)S(1)} %get-tuple-element.45), channel_id=1, source_target_pairs={{0,4},{4,0},{8,12},{12,8},{1,5},{5,1},{9,13},{13,9},{2,6},{6,2},{1... | collective-permute-start | bytes 245768 | tf_op jit(solution)/shard_map/ppermute | solution.py:495
  21.5 8.0 %copy-start.1 = (bf16[1,320,2560]{2,1,0:T(8,128)(2,1)S(1)}, bf16[1,320,2560]{2,1,0:T(8,128)(2,1)}, u32[]{:S(2)}) copy-start(bf16[1,320,2560]{2,1,0:T(8,128)(2,1)} %param.16) | copy-start | bytes 4915204
  21.5 8.0 %copy-start.2 = (bf16[1,1280,320]{1,2,0:T(8,128)(2,1)S(1)}, bf16[1,1280,320]{1,2,0:T(8,128)(2,1)}, u32[]{:S(2)}) copy-start(bf16[1,1280,320]{1,2,0:T(8,128)(2,1)} %param.17) | copy-start | bytes 2457604
  21.5 8.0 %copy-start.7 = (bf16[1,320,320]{2,1,0:T(8,128)(2,1)S(1)}, bf16[1,320,320]{2,1,0:T(8,128)(2,1)}, u32[]{:S(2)}) copy-start(bf16[1,320,320]{2,1,0:T(8,128)(2,1)} %param.15) | copy-start | bytes 614404
  22.3 7.2 %collective-permute-start.6 = (bf16[320,128]{1,0:T(8,128)(2,1)S(1)}, bf16[320,128]{1,0:T(8,128)(2,1)S(1)}, u32[]{:S(2)}, u32[]{:S(2)}) collective-permute-start(bf16[320,128]{1,0:T(8,128)(2,1)S(1)} %get-tuple-element.50), channel_id=1, source_target_pairs={{0,8},{4,12},{8,0},{12,4},{1,9},{5,13},{9,1},{13,5},{2,10},{6,14},... | collective-permute-start | bytes 245768 | tf_op jit(solution)/shard_map/ppermute | solution.py:495
  33.6 8.3 %collective-permute-start.7 = (bf16[320,128]{1,0:T(8,128)(2,1)S(1)}, bf16[320,128]{1,0:T(8,128)(2,1)S(1)}, u32[]{:S(2)}, u32[]{:S(2)}) collective-permute-start(bf16[320,128]{1,0:T(8,128)(2,1)S(1)} %get-tuple-element.53), channel_id=1, source_target_pairs={{0,14},{2,12},{4,10},{6,8},{8,6},{10,4},{12,2},{14,0},{1,15},{3,13... | collective-permute-start | bytes 245768 | tf_op jit(solution)/shard_map/ppermute | solution.py:493
  35.4 7.1 %collective-permute-start.8 = (bf16[320,128]{1,0:T(8,128)(2,1)S(1)}, bf16[320,128]{1,0:T(8,128)(2,1)S(1)}, u32[]{:S(2)}, u32[]{:S(2)}) collective-permute-start(bf16[320,128]{1,0:T(8,128)(2,1)S(1)} %get-tuple-element.54), channel_id=1, source_target_pairs={{0,6},{2,4},{4,2},{6,0},{8,14},{10,12},{12,10},{14,8},{1,7},{3,5},... | collective-permute-start | bytes 245768 | tf_op jit(solution)/shard_map/ppermute | solution.py:493
  37.6 7.2 %collective-permute-start.9 = (bf16[320,128]{1,0:T(8,128)(2,1)S(1)}, bf16[320,128]{1,0:T(8,128)(2,1)S(1)}, u32[]{:S(2)}, u32[]{:S(2)}) collective-permute-start(bf16[320,128]{1,0:T(8,128)(2,1)S(1)} %get-tuple-element.56), channel_id=1, source_target_pairs={{0,10},{2,8},{4,14},{6,12},{8,2},{10,0},{12,6},{14,4},{1,11},{3,9}... | collective-permute-start | bytes 245768 | tf_op jit(solution)/shard_map/ppermute | solution.py:493
  41.4 4.4 %collective-permute-start.10 = (bf16[320,128]{1,0:T(8,128)(2,1)S(1)}, bf16[320,128]{1,0:T(8,128)(2,1)S(1)}, u32[]{:S(2)}, u32[]{:S(2)}) collective-permute-start(bf16[320,128]{1,0:T(8,128)(2,1)S(1)} %get-tuple-element.57), channel_id=1, source_target_pairs={{0,2},{2,0},{4,6},{6,4},{8,10},{10,8},{12,14},{14,12},{1,3},{3,1},... | collective-permute-start | bytes 245768 | tf_op jit(solution)/shard_map/ppermute | solution.py:493
  42.6 4.5 %collective-permute-start.11 = (bf16[640,128]{1,0:T(8,128)(2,1)S(1)}, bf16[640,128]{1,0:T(8,128)(2,1)S(1)}, u32[]{:S(2)}, u32[]{:S(2)}) collective-permute-start(bf16[640,128]{1,0:T(8,128)(2,1)S(1)} %join.5.refs_0_), channel_id=1, source_target_pairs={{0,1},{1,0},{2,3},{3,2},{4,5},{5,4},{6,7},{7,6},{8,9},{9,8},{10,11... | collective-permute-start | bytes 491528 | tf_op jit(solution)/shard_map/ppermute | solution.py:480
  44.8 1.3 %collective-permute-start.12 = (bf16[320,128]{1,0:T(8,128)(2,1)S(1)}, bf16[320,128]{1,0:T(8,128)(2,1)S(1)}, u32[]{:S(2)}, u32[]{:S(2)}) collective-permute-start(bf16[320,128]{1,0:T(8,128)(2,1)S(1)} %collective-permute-done.9.refs_1_), channel_id=1, source_target_pairs={{0,1},{1,0},{2,3},{3,2},{4,5},{5,4},{6,7},{7,6},{8,9},{9,8},{10,11... | collective-permute-start | bytes 245768 | tf_op jit(solution)/shard_map/ppermute | solution.py:480
  45.8 1.3 %collective-permute-start.13 = (bf16[320,128]{1,0:T(8,128)(2,1)S(1)}, bf16[320,128]{1,0:T(8,128)(2,1)S(1)}, u32[]{:S(2)}, u32[]{:S(2)}) collective-permute-start(bf16[320,128]{1,0:T(8,128)(2,1)S(1)} %collective-permute-done.10.refs_2_), channel_id=1, source_target_pairs={{0,1},{1,0},{2,3},{3,2},{4,5},{5,4},{6,7},{7,6},{8,9},{9,8},{10,11... | collective-permute-start | bytes 245768 | tf_op jit(solution)/shard_map/ppermute | solution.py:480
  51.4 7.2 %collective-permute-start.14 = (bf16[320,128]{1,0:T(8,128)(2,1)S(1)}, bf16[320,128]{1,0:T(8,128)(2,1)S(1)}, u32[]{:S(2)}, u32[]{:S(2)}) collective-permute-start(bf16[320,128]{1,0:T(8,128)(2,1)S(1)} %get-tuple-element.58), channel_id=1, source_target_pairs={{0,12},{4,8},{8,4},{12,0},{1,13},{5,9},{9,5},{13,1},{2,14},{6,10},... | collective-permute-start | bytes 245768 | tf_op jit(solution)/shard_map/ppermute | solution.py:495
  52.7 7.5 %collective-permute-start.15 = (bf16[320,128]{1,0:T(8,128)(2,1)S(1)}, bf16[320,128]{1,0:T(8,128)(2,1)S(1)}, u32[]{:S(2)}, u32[]{:S(2)}) collective-permute-start(bf16[320,128]{1,0:T(8,128)(2,1)S(1)} %get-tuple-element.59), channel_id=1, source_target_pairs={{0,4},{4,0},{8,12},{12,8},{1,5},{5,1},{9,13},{13,9},{2,6},{6,2},{1... | collective-permute-start | bytes 245768 | tf_op jit(solution)/shard_map/ppermute | solution.py:495
  54.0 7.5 %collective-permute-start.16 = (bf16[320,128]{1,0:T(8,128)(2,1)S(1)}, bf16[320,128]{1,0:T(8,128)(2,1)S(1)}, u32[]{:S(2)}, u32[]{:S(2)}) collective-permute-start(bf16[320,128]{1,0:T(8,128)(2,1)S(1)} %get-tuple-element.64), channel_id=1, source_target_pairs={{0,8},{4,12},{8,0},{12,4},{1,9},{5,13},{9,1},{13,5},{2,10},{6,14},... | collective-permute-start | bytes 245768 | tf_op jit(solution)/shard_map/ppermute | solution.py:495
  65.5 6.5 %collective-permute-start.17 = (bf16[320,128]{1,0:T(8,128)(2,1)S(1)}, bf16[320,128]{1,0:T(8,128)(2,1)S(1)}, u32[]{:S(2)}, u32[]{:S(2)}) collective-permute-start(bf16[320,128]{1,0:T(8,128)(2,1)S(1)} %get-tuple-element.66), channel_id=1, source_target_pairs={{0,12},{4,8},{8,4},{12,0},{1,13},{5,9},{9,5},{13,1},{2,14},{6,10},... | collective-permute-start | bytes 245768 | tf_op jit(solution)/shard_map/ppermute | solution.py:495
  67.6 5.9 %collective-permute-start.18 = (bf16[320,128]{1,0:T(8,128)(2,1)S(1)}, bf16[320,128]{1,0:T(8,128)(2,1)S(1)}, u32[]{:S(2)}, u32[]{:S(2)}) collective-permute-start(bf16[320,128]{1,0:T(8,128)(2,1)S(1)} %get-tuple-element.67), channel_id=1, source_target_pairs={{0,4},{4,0},{8,12},{12,8},{1,5},{5,1},{9,13},{13,9},{2,6},{6,2},{1... | collective-permute-start | bytes 245768 | tf_op jit(solution)/shard_map/ppermute | solution.py:495
  69.1 5.4 %collective-permute-start.19 = (bf16[320,128]{1,0:T(8,128)(2,1)S(1)}, bf16[320,128]{1,0:T(8,128)(2,1)S(1)}, u32[]{:S(2)}, u32[]{:S(2)}) collective-permute-start(bf16[320,128]{1,0:T(8,128)(2,1)S(1)} %get-tuple-element.69), channel_id=1, source_target_pairs={{0,8},{4,12},{8,0},{12,4},{1,9},{5,13},{9,1},{13,5},{2,10},{6,14},... | collective-permute-start | bytes 245768 | tf_op jit(solution)/shard_map/ppermute | solution.py:495

commit v7 on v6

--- a/solution.py
+++ b/solution.py
@@ -17,14 +17,15 @@
 BF16 = jnp.bfloat16
 
 
-def order_out(count):
-    return [d for d in reversed(range(count)) if d % 2] + [
-        d for d in reversed(range(count)) if d % 2 == 0
-    ]
+def order_out(count, step):
+    falling = list(reversed(range(count)))
+    if step == 0:
+        return falling
+    return [d for d in falling if d % 2] + [d for d in falling if d % 2 == 0]
 
 
 def order_back(count):
-    return order_out(count)
+    return order_out(count, 1)
 
 
 def round_up(value, unit):
@@ -192,7 +193,7 @@
     scale, shift = group_scale(total, square, entries, group_width, channels)
     first_row = here * own_rows
     activate(hidden, targets, scale, shift, rows, columns, first_row, 0, own_rows + 2)
-    for i, d in enumerate(order_out(shards)):
+    for i, d in enumerate(order_out(shards, step)):
         start = (spot ^ d) * part
         base = field[pl.ds(pl.multiple_of(own_base + start, 8), part), :]
         if i < sooner:
@@ -201,10 +202,10 @@
             keep[(i - sooner) * part : (i - sooner + 1) * part, :] = base
 
 
-def finish_kernel(columns, shards, sooner, keep, middle, edge, pair, kernels, *outs):
+def finish_kernel(columns, shards, sooner, step, keep, middle, edge, pair, kernels, *outs):
     part = keep.shape[0] // (shards - sooner)
     spot = lax.axis_index("shard")
-    for i, d in enumerate(order_out(shards)[sooner:]):
+    for i, d in enumerate(order_out(shards, step)[sooner:]):
         start = (spot ^ d) * part
         base = keep[i * part : (i + 1) * part, :]
         convolve_part((middle, edge, pair), kernels.at[1], start, columns, base, outs[i])
@@ -258,7 +259,7 @@
         name="spatial",
     )(*own, *other, weights, embeds)
     second = pl.pallas_call(
-        functools.partial(finish_kernel, columns, shards, sooner),
+        functools.partial(finish_kernel, columns, shards, sooner, step),
         out_shape=[piece] * later,
         in_specs=[vmem] * 5,
         out_specs=[vmem] * later,
@@ -351,7 +352,7 @@
         leave(done[i * pixels : (i + 1) * pixels, :], outs[i])
 
 
-def temporal_kernel(frames, ways, sooner, *refs):
+def temporal_kernel(frames, ways, sooner, step, *refs):
     parts = refs[:ways]
     qkv, attn_out, geglu_in, geglu_out = refs[ways : ways + 4]
     outs = refs[ways + 4 : ways + 4 + sooner]
@@ -363,7 +364,7 @@
 
     height = dense_rows(pixels, channels)
     held = [(block, at) for block in parts for at in range(0, block.shape[0], height)]
-    for (block, at), d in zip(held, order_out(frames)):
+    for (block, at), d in zip(held, order_out(frames, step)):
         f = order_back(frames).index(d)
         for i, first, values in unpack_part(block, at, pixels, channels):
             rows = slice(f * pixels + first, f * pixels + first + values.shape[0])
@@ -403,10 +404,10 @@
             jnp.exp((score - top) * HEAD_DIM ** (-0.5)) for score, top in zip(scores, tops)
         ]
         totals = [1.0 / jnp.sum(power, axis=1, keepdims=True) for power in powers]
-        weights = [(power * total).astype(BF16) for power, total in zip(powers, totals)]
+        weights = [power.astype(BF16) for power in powers]
         results = [
-            jnp.dot(weight, gather(2 * lanes + at), preferred_element_type=F32)
-            for weight, (at, _) in zip(weights, heads)
+            jnp.dot(weight, gather(2 * lanes + at), preferred_element_type=F32) * total
+            for weight, total, (at, _) in zip(weights, totals, heads)
         ]
         for at in range(0, channels, LANES):
             mix = None
@@ -425,7 +426,7 @@
         leave(done[f * pixels : (f + 1) * pixels, :], outs[f])
 
 
-def temporal(parts, weights):
+def temporal(parts, weights, step):
     ways = len(parts)
     frames = lax.axis_size("shard")
     sooner = frames // 2
@@ -440,7 +441,7 @@
     feed_flops = 6 * pixels * channels * inner
     params = pltpu.CompilerParams(vmem_limit_bytes=14 * 1024 * 1024)
     *first, rest = pl.pallas_call(
-        functools.partial(temporal_kernel, frames, ways, sooner),
+        functools.partial(temporal_kernel, frames, ways, sooner, step),
         out_shape=[piece] * sooner + [jax.ShapeDtypeStruct((later * pixels, channels), BF16)],
         in_specs=[vmem] * (ways + 4),
         out_specs=[vmem] * (sooner + 1),
@@ -621,9 +622,9 @@
             half,
             shards,
         )
-        parts = exchange(parts, order_out(shards))
+        parts = exchange(parts, order_out(shards, denoise_step))
         parts = [join(parts[: shards // 2]), *parts[shards // 2 :]]
-        parts = temporal(parts, temporal_weights)
+        parts = temporal(parts, temporal_weights, denoise_step)
         parts = exchange(parts, order_back(shards), across=0 if last else 1)
         own = [join(parts[: shards // 2]), *parts[shards // 2 :]]
     return unpack(own, shards, own_rows * columns, channels).reshape(features.shape)

time: 75.6 us -> 75.1 us (level)
  transfers between devices with their start and end apart: 20 -> 20, of which waited for: 16 -> 15; matrix products, arithmetic and copies ran while one was open for 1% -> 1% of each run, Pallas kernels for 7% -> 7%
where the time goes in v7:
time: 75.1 us; the launch traced here: 74.9 us
  starting transfers between devices  24.2 us (32%)
  Pallas kernels  22.5 us (30%)
  waiting for transfers between devices  21.7 us (29%)
  local copies, waits for them, and re-layouts  5.39 us (7%)
  other arithmetic  0.79 us (1%)
    ppermute x9, waiting for transfers between devices, exchange(): part = lax.ppermute(part, 'shard', [(z, z ^ d) for z in range(shards)])  13.8 us
    ppermute x9, starting transfers between devices, exchange(): part = lax.ppermute(part, 'shard', [(z, z ^ d) for z in range(shards)])  13.7 us
    pallas_call x2, Pallas kernels, spatial(): pl.pallas_call(functools.partial(spatial_kernel, rows, half, columns, cha...  8.37 us
    pallas_call x2, Pallas kernels, temporal(): pl.pallas_call(functools.partial(temporal_kernel, frames, ways, sooner, s...  7.82 us
    ppermute x4, starting transfers between devices, exchange(): part = lax.ppermute(part, ('shard', 'section'), route)  6.88 us
    unnamed x16, local copies, waits for them, and re-layouts  5.39 us
    ppermute x7, waiting for transfers between devices, send(): lax.ppermute(block, axis, [(i, (i + distance) % count) for i in range(cou...  3.94 us
    ppermute x4, waiting for transfers between devices, exchange(): part = lax.ppermute(part, ('shard', 'section'), route)  3.92 us
  transfers between devices with their start and end apart: 20, of which 15 were waited for; matrix products, arithmetic and copies ran while one was open for 1% of the time, Pallas kernels for 7%

profile of v7, /device:TPU:0, one launch (start us, length us, event | category | flops | bytes accessed | tf_op | source)
XLA Modules:
  0.0 74.9 jit_solution(17629120645929995903)
XLA Ops:
  0.0 1.0 %copy-done.6 = bf16[1,1,8,64,320]{4,3,2,1,0:T(8,128)(2,1)S(1)} copy-done((bf16[1,1,8,64,320]{4,3,2,1,0:T(8,128)(2,1)S(1)}, bf16[1,1,8,64,320]{4,3,2,1,0:T(8,128)(2,1)}, u32[]{:S(2)}) %copy-start.6) | copy-done | bytes 327704
  1.0 0.1 pack.1
  1.1 3.0 %collective-permute-start = (bf16[640,128]{1,0:T(8,128)(2,1)S(1)}, bf16[640,128]{1,0:T(8,128)(2,1)S(1)}, u32[]{:S(2)}, u32[]{:S(2)}) collective-permute-start(bf16[640,128]{1,0:T(8,128)(2,1)S(1)} %get-tuple-element.38), channel_id=1, source_target_pairs={{0,2},{2,0},{1,3},{3,1},{4,6},{6,4},{5,7},{7,5},{8,10},{10,8},{9,1... | collective-permute-start | bytes 491528 | tf_op jit(solution)/shard_map/ppermute | solution.py:481
  4.1 0.1 collective-permute-start.1
  4.2 0.7 convert_bitcast_fusion
  4.9 1.6 %copy-done.3 = bf16[1,3,3,320,320]{4,3,2,1,0:T(8,128)(2,1)S(1)} copy-done((bf16[1,3,3,320,320]{4,3,2,1,0:T(8,128)(2,1)S(1)}, bf16[1,3,3,320,320]{4,3,2,1,0:T(8,128)(2,1)}, u32[]{:S(2)}) %copy-start.3) | copy-done | bytes 1843224
  6.5 1.6 %copy-done.4 = bf16[1,3,3,320,320]{4,3,2,1,0:T(8,128)(2,1)S(1)} copy-done((bf16[1,3,3,320,320]{4,3,2,1,0:T(8,128)(2,1)S(1)}, bf16[1,3,3,320,320]{4,3,2,1,0:T(8,128)(2,1)}, u32[]{:S(2)}) %copy-start.4) | copy-done | bytes 1843224
  8.1 1.1 %copy-done.5 = bf16[1,320,960]{2,1,0:T(8,128)(2,1)S(1)} copy-done((bf16[1,320,960]{2,1,0:T(8,128)(2,1)S(1)}, bf16[1,320,960]{2,1,0:T(8,128)(2,1)}, u32[]{:S(2)}) %copy-start.5) | copy-done | bytes 614424
  9.2 0.7 prepare.1
  10.0 0.1 multiply_cosine_fusion
  10.1 1.8 %collective-permute-done.1.refs_1_ = bf16[640,128]{1,0:T(8,128)(2,1)S(1)} collective-permute-done((bf16[640,128]{1,0:T(8,128)(2,1)S(1)}, bf16[640,128]{1,0:T(8,128)(2,1)S(1)}, u32[]{:S(2)}, u32[]{:S(2)}) %collective-permute-start.1) | collective-permute-done | bytes 163872 | tf_op jit(solution)/shard_map/ppermute | solution.py:481
  11.9 0.5 collective-permute-start.2
  12.4 0.2 fusion
  12.6 0.9 %collective-permute-done.2.refs_2_ = bf16[640,128]{1,0:T(8,128)(2,1)S(1)} collective-permute-done((bf16[640,128]{1,0:T(8,128)(2,1)S(1)}, bf16[640,128]{1,0:T(8,128)(2,1)S(1)}, u32[]{:S(2)}, u32[]{:S(2)}) %collective-permute-start.2) | collective-permute-done | bytes 163872 | tf_op jit(solution)/shard_map/ppermute | solution.py:481
  13.5 4.1 %spatial.2 = (bf16[320,128]{1,0:T(8,128)(2,1)S(1)}, bf16[320,128]{1,0:T(8,128)(2,1)S(1)}, f32[256,384]{1,0:T(8,128)S(1)}, bf16[640,256]{1,0:T(8,128)(2,1)S(1)}, ...) custom-call(bf16[640,128]{1,0:T(8,128)(2,1)S(1)} %collective-permute-done.refs_0_, ...), custom_call_target="tpu_custom_call" | custom-call | flops 3221225472 | bytes 6000000 | tf_op jit(solution)/shard_map/spatial/pallas_call | solution.py:230
  17.6 3.9 %collective-permute-start.4 = (bf16[320,128]{1,0:T(8,128)(2,1)S(1)}, bf16[320,128]{1,0:T(8,128)(2,1)S(1)}, u32[]{:S(2)}, u32[]{:S(2)}) collective-permute-start(bf16[320,128]{1,0:T(8,128)(2,1)S(1)} %get-tuple-element.44), channel_id=1, source_target_pairs={{0,12},{4,8},{8,4},{12,0},{1,13},{5,9},{9,5},{13,1},{2,14},{6,10},... | collective-permute-start | bytes 245768 | tf_op jit(solution)/shard_map/ppermute | solution.py:496
  21.5 0.8 %finish.2 = (bf16[320,128]{1,0:T(8,128)(2,1)S(1)}, bf16[320,128]{1,0:T(8,128)(2,1)S(1)}) custom-call(f32[256,384]{1,0:T(8,128)S(1)} %get-tuple-element.46.keep, bf16[640,256]{1,0:T(8,128)(2,1)S(1)} %get-tuple-element.47.middle, bf16[640,128]{1,0:T(8,128)(2,1)S(1)} %get-tuple-element.48.edge, bf16[640,128]{1,0:T(8,128)(2,1)S(1)} %get-tuple-element.49.pair, ...), custom_call_target="tpu_custom_call" | custom-call | flops 536870912 | bytes 3000000 | tf_op jit(solution)/shard_map/finish/pallas_call | solution.py:261
  22.3 0.7 collective-permute-start.6
  23.0 1.8 %collective-permute-done.4.refs_0_ = bf16[320,128]{1,0:T(8,128)(2,1)S(1)} collective-permute-done((bf16[320,128]{1,0:T(8,128)(2,1)S(1)}, bf16[320,128]{1,0:T(8,128)(2,1)S(1)}, u32[]{:S(2)}, u32[]{:S(2)}) %collective-permute-start.4) | collective-permute-done | bytes 81952 | tf_op jit(solution)/shard_map/ppermute | solution.py:496
  24.8 4.0 %collective-permute-done.5.refs_1_ = bf16[320,128]{1,0:T(8,128)(2,1)S(1)} collective-permute-done((bf16[320,128]{1,0:T(8,128)(2,1)S(1)}, bf16[320,128]{1,0:T(8,128)(2,1)S(1)}, u32[]{:S(2)}, u32[]{:S(2)}) %collective-permute-start.5) | collective-permute-done | bytes 81952 | tf_op jit(solution)/shard_map/ppermute | solution.py:496
  28.8 3.9 %temporal.2 = (bf16[320,128]{1,0:T(8,128)(2,1)S(1)}, bf16[320,128]{1,0:T(8,128)(2,1)S(1)}, bf16[256,320]{1,0:T(8,128)(2,1)S(1)}) custom-call(bf16[640,128]{1,0:T(8,128)(2,1)S(1)} %join.4.refs_0_, bf16[320,128]{1,0:T(8,128)(2,1)S(1)} %collective-permute-done.6.refs_1_, bf16[320,128]{1,0:T(8,128)(2,1)S(1)} %get-tuple-element.51.refs_2_, ...), custom_call_target="tpu_custom_call" | custom-call | flops 1132462080 | bytes 4000000 | tf_op jit(solution)/shard_map/temporal/pallas_call | solution.py:443
  32.8 3.5 %collective-permute-start.7 = (bf16[320,128]{1,0:T(8,128)(2,1)S(1)}, bf16[320,128]{1,0:T(8,128)(2,1)S(1)}, u32[]{:S(2)}, u32[]{:S(2)}) collective-permute-start(bf16[320,128]{1,0:T(8,128)(2,1)S(1)} %get-tuple-element.53), channel_id=1, source_target_pairs={{0,14},{2,12},{4,10},{6,8},{8,6},{10,4},{12,2},{14,0},{1,15},{3,13... | collective-permute-start | bytes 245768 | tf_op jit(solution)/shard_map/ppermute | solution.py:494
  36.2 1.5 %feed.2 = (bf16[320,128]{1,0:T(8,128)(2,1)S(1)}, bf16[320,128]{1,0:T(8,128)(2,1)S(1)}) custom-call(bf16[256,320]{1,0:T(8,128)(2,1)S(1)} %get-tuple-element.55.refs_0_, bf16[320,2560]{1,0:T(8,128)(2,1)S(1)} %bitcast.16, bf16[320,1280]{1,0:T(8,128)(2,1)S(1)} %bitcast.20), custom_call_target="tpu_custom_call" | custom-call | flops 629145600 | bytes 3000000 | tf_op jit(solution)/shard_map/feed/pallas_call | solution.py:462
  37.7 2.9 %collective-permute-start.9 = (bf16[320,128]{1,0:T(8,128)(2,1)S(1)}, bf16[320,128]{1,0:T(8,128)(2,1)S(1)}, u32[]{:S(2)}, u32[]{:S(2)}) collective-permute-start(bf16[320,128]{1,0:T(8,128)(2,1)S(1)} %get-tuple-element.56), channel_id=1, source_target_pairs={{0,10},{2,8},{4,14},{6,12},{8,2},{10,0},{12,6},{14,4},{1,11},{3,9}... | collective-permute-start | bytes 245768 | tf_op jit(solution)/shard_map/ppermute | solution.py:494
  40.6 0.5 collective-permute-start.10
  41.1 0.0 collective-permute-done.7.refs_0_
  41.1 1.4 %collective-permute-done.8.refs_1_ = bf16[320,128]{1,0:T(8,128)(2,1)S(1)} collective-permute-done((bf16[320,128]{1,0:T(8,128)(2,1)S(1)}, bf16[320,128]{1,0:T(8,128)(2,1)S(1)}, u32[]{:S(2)}, u32[]{:S(2)}) %collective-permute-start.8) | collective-permute-done | bytes 81952 | tf_op jit(solution)/shard_map/ppermute | solution.py:494
  42.5 0.1 collective-permute-start.11
  42.6 1.6 %collective-permute-done.9.refs_1_ = bf16[320,128]{1,0:T(8,128)(2,1)S(1)} collective-permute-done((bf16[320,128]{1,0:T(8,128)(2,1)S(1)}, bf16[320,128]{1,0:T(8,128)(2,1)S(1)}, u32[]{:S(2)}, u32[]{:S(2)}) %collective-permute-start.9) | collective-permute-done | bytes 81952 | tf_op jit(solution)/shard_map/ppermute | solution.py:494
  44.2 0.0 collective-permute-start.12
  44.3 0.9 %collective-permute-done.10.refs_2_ = bf16[320,128]{1,0:T(8,128)(2,1)S(1)} collective-permute-done((bf16[320,128]{1,0:T(8,128)(2,1)S(1)}, bf16[320,128]{1,0:T(8,128)(2,1)S(1)}, u32[]{:S(2)}, u32[]{:S(2)}) %collective-permute-start.10) | collective-permute-done | bytes 81952 | tf_op jit(solution)/shard_map/ppermute | solution.py:494
  45.1 0.4 collective-permute-done.12.refs_4_
  45.5 0.9 %collective-permute-done.13.refs_5_ = bf16[320,128]{1,0:T(8,128)(2,1)S(1)} collective-permute-done((bf16[320,128]{1,0:T(8,128)(2,1)S(1)}, bf16[320,128]{1,0:T(8,128)(2,1)S(1)}, u32[]{:S(2)}, u32[]{:S(2)}) %collective-permute-start.13) | collective-permute-done | bytes 81952 | tf_op jit(solution)/shard_map/ppermute | solution.py:481
  46.4 4.3 %spatial.3 = (bf16[320,128]{1,0:T(8,128)(2,1)S(1)}, bf16[320,128]{1,0:T(8,128)(2,1)S(1)}, f32[256,384]{1,0:T(8,128)S(1)}, bf16[640,256]{1,0:T(8,128)(2,1)S(1)}, ...) custom-call(bf16[640,128]{1,0:T(8,128)(2,1)S(1)} %join.5.refs_0_, ...), custom_call_target="tpu_custom_call" | custom-call | flops 3221225472 | bytes 6000000 | tf_op jit(solution)/shard_map/spatial/pallas_call | solution.py:230
  50.7 2.4 %collective-permute-start.14 = (bf16[320,128]{1,0:T(8,128)(2,1)S(1)}, bf16[320,128]{1,0:T(8,128)(2,1)S(1)}, u32[]{:S(2)}, u32[]{:S(2)}) collective-permute-start(bf16[320,128]{1,0:T(8,128)(2,1)S(1)} %get-tuple-element.58), channel_id=1, source_target_pairs={{0,12},{4,8},{8,4},{12,0},{1,13},{5,9},{9,5},{13,1},{2,14},{6,10},... | collective-permute-start | bytes 245768 | tf_op jit(solution)/shard_map/ppermute | solution.py:496
  53.1 0.8 %finish.3 = (bf16[320,128]{1,0:T(8,128)(2,1)S(1)}, bf16[320,128]{1,0:T(8,128)(2,1)S(1)}) custom-call(f32[256,384]{1,0:T(8,128)S(1)} %get-tuple-element.60.keep, bf16[640,256]{1,0:T(8,128)(2,1)S(1)} %get-tuple-element.61.middle, bf16[640,128]{1,0:T(8,128)(2,1)S(1)} %get-tuple-element.62.edge, bf16[640,128]{1,0:T(8,128)(2,1)S(1)} %get-tuple-element.63.pair, ...), custom_call_target="tpu_custom_call" | custom-call | flops 536870912 | bytes 3000000 | tf_op jit(solution)/shard_map/finish/pallas_call | solution.py:261
  54.0 2.1 %collective-permute-start.16 = (bf16[320,128]{1,0:T(8,128)(2,1)S(1)}, bf16[320,128]{1,0:T(8,128)(2,1)S(1)}, u32[]{:S(2)}, u32[]{:S(2)}) collective-permute-start(bf16[320,128]{1,0:T(8,128)(2,1)S(1)} %get-tuple-element.64), channel_id=1, source_target_pairs={{0,8},{4,12},{8,0},{12,4},{1,9},{5,13},{9,1},{13,5},{2,10},{6,14},... | collective-permute-start | bytes 245768 | tf_op jit(solution)/shard_map/ppermute | solution.py:496
  56.0 1.9 %collective-permute-done.14.refs_0_ = bf16[320,128]{1,0:T(8,128)(2,1)S(1)} collective-permute-done((bf16[320,128]{1,0:T(8,128)(2,1)S(1)}, bf16[320,128]{1,0:T(8,128)(2,1)S(1)}, u32[]{:S(2)}, u32[]{:S(2)}) %collective-permute-start.14) | collective-permute-done | bytes 81952 | tf_op jit(solution)/shard_map/ppermute | solution.py:496
  57.9 2.4 %collective-permute-done.15.refs_1_ = bf16[320,128]{1,0:T(8,128)(2,1)S(1)} collective-permute-done((bf16[320,128]{1,0:T(8,128)(2,1)S(1)}, bf16[320,128]{1,0:T(8,128)(2,1)S(1)}, u32[]{:S(2)}, u32[]{:S(2)}) %collective-permute-start.15) | collective-permute-done | bytes 81952 | tf_op jit(solution)/shard_map/ppermute | solution.py:496
  60.3 0.9 %collective-permute-done.16.refs_1_ = bf16[320,128]{1,0:T(8,128)(2,1)S(1)} collective-permute-done((bf16[320,128]{1,0:T(8,128)(2,1)S(1)}, bf16[320,128]{1,0:T(8,128)(2,1)S(1)}, u32[]{:S(2)}, u32[]{:S(2)}) %collective-permute-start.16) | collective-permute-done | bytes 81952 | tf_op jit(solution)/shard_map/ppermute | solution.py:496
  61.2 3.9 %temporal.3 = (bf16[320,128]{1,0:T(8,128)(2,1)S(1)}, bf16[320,128]{1,0:T(8,128)(2,1)S(1)}, bf16[256,320]{1,0:T(8,128)(2,1)S(1)}) custom-call(bf16[640,128]{1,0:T(8,128)(2,1)S(1)} %join.6.refs_0_, bf16[320,128]{1,0:T(8,128)(2,1)S(1)} %collective-permute-done.16.refs_1_, bf16[320,128]{1,0:T(8,128)(2,1)S(1)} %get-tuple-element.65.refs_2_, ...), custom_call_target="tpu_custom_call" | custom-call | flops 1132462080 | bytes 4000000 | tf_op jit(solution)/shard_map/temporal/pallas_call | solution.py:443
  65.1 1.9 %collective-permute-start.17 = (bf16[320,128]{1,0:T(8,128)(2,1)S(1)}, bf16[320,128]{1,0:T(8,128)(2,1)S(1)}, u32[]{:S(2)}, u32[]{:S(2)}) collective-permute-start(bf16[320,128]{1,0:T(8,128)(2,1)S(1)} %get-tuple-element.66), channel_id=1, source_target_pairs={{0,12},{4,8},{8,4},{12,0},{1,13},{5,9},{9,5},{13,1},{2,14},{6,10},... | collective-permute-start | bytes 245768 | tf_op jit(solution)/shard_map/ppermute | solution.py:496
  67.0 1.5 %feed.3 = (bf16[320,128]{1,0:T(8,128)(2,1)S(1)}, bf16[320,128]{1,0:T(8,128)(2,1)S(1)}) custom-call(bf16[256,320]{1,0:T(8,128)(2,1)S(1)} %get-tuple-element.68.refs_0_, bf16[320,2560]{1,0:T(8,128)(2,1)S(1)} %bitcast.18, bf16[320,1280]{1,0:T(8,128)(2,1)S(1)} %bitcast.22), custom_call_target="tpu_custom_call" | custom-call | flops 629145600 | bytes 3000000 | tf_op jit(solution)/shard_map/feed/pallas_call | solution.py:462
  68.5 2.6 %collective-permute-start.19 = (bf16[320,128]{1,0:T(8,128)(2,1)S(1)}, bf16[320,128]{1,0:T(8,128)(2,1)S(1)}, u32[]{:S(2)}, u32[]{:S(2)}) collective-permute-start(bf16[320,128]{1,0:T(8,128)(2,1)S(1)} %get-tuple-element.69), channel_id=1, source_target_pairs={{0,8},{4,12},{8,0},{12,4},{1,9},{5,13},{9,1},{13,5},{2,10},{6,14},... | collective-permute-start | bytes 245768 | tf_op jit(solution)/shard_map/ppermute | solution.py:496
  71.1 0.9 %collective-permute-done.17.refs_0_ = bf16[320,128]{1,0:T(8,128)(2,1)S(1)} collective-permute-done((bf16[320,128]{1,0:T(8,128)(2,1)S(1)}, bf16[320,128]{1,0:T(8,128)(2,1)S(1)}, u32[]{:S(2)}, u32[]{:S(2)}) %collective-permute-start.17) | collective-permute-done | bytes 81952 | tf_op jit(solution)/shard_map/ppermute | solution.py:496
  72.0 0.7 collective-permute-done.18.refs_1_
  72.7 1.3 %collective-permute-done.19.refs_1_ = bf16[320,128]{1,0:T(8,128)(2,1)S(1)} collective-permute-done((bf16[320,128]{1,0:T(8,128)(2,1)S(1)}, bf16[320,128]{1,0:T(8,128)(2,1)S(1)}, u32[]{:S(2)}, u32[]{:S(2)}) %collective-permute-start.19) | collective-permute-done | bytes 81952 | tf_op jit(solution)/shard_map/ppermute | solution.py:496
  74.0 0.9 %unpack.1 = bf16[512,320]{1,0:T(8,128)(2,1)} custom-call(bf16[640,128]{1,0:T(8,128)(2,1)S(1)} %join.7.refs_0_, bf16[320,128]{1,0:T(8,128)(2,1)S(1)} %collective-permute-done.19.refs_1_, bf16[320,128]{1,0:T(8,128)(2,1)S(1)} %get-tuple-element.70.refs_2_), custom_call_target="tpu_custom_call" | custom-call | tf_op jit(solution)/shard_map/unpack/pallas_call | solution.py:569
  (28 shorter events, 0.1 us)
Async XLA Ops:
  0.0 12.4 %copy-start = (bf16[1,320,320]{2,1,0:T(8,128)(2,1)S(1)}, bf16[1,320,320]{2,1,0:T(8,128)(2,1)}, u32[]{:S(2)}) copy-start(bf16[1,320,320]{2,1,0:T(8,128)(2,1)} %param.13) | copy-start | bytes 614404
  0.0 1.0 %copy-start.6 = (bf16[1,1,8,64,320]{4,3,2,1,0:T(8,128)(2,1)S(1)}, bf16[1,1,8,64,320]{4,3,2,1,0:T(8,128)(2,1)}, u32[]{:S(2)}) copy-start(bf16[1,1,8,64,320]{4,3,2,1,0:T(8,128)(2,1)} %param.9) | copy-start | bytes 983044
  1.1 10.7 %collective-permute-start = (bf16[640,128]{1,0:T(8,128)(2,1)S(1)}, bf16[640,128]{1,0:T(8,128)(2,1)S(1)}, u32[]{:S(2)}, u32[]{:S(2)}) collective-permute-start(bf16[640,128]{1,0:T(8,128)(2,1)S(1)} %get-tuple-element.38), channel_id=1, source_target_pairs={{0,2},{2,0},{1,3},{3,1},{4,6},{6,4},{5,7},{7,5},{8,10},{10,8},{9,1... | collective-permute-start | bytes 491528 | tf_op jit(solution)/shard_map/ppermute | solution.py:481
  4.1 7.7 %collective-permute-start.1 = (bf16[640,128]{1,0:T(8,128)(2,1)S(1)}, bf16[640,128]{1,0:T(8,128)(2,1)S(1)}, u32[]{:S(2)}, u32[]{:S(2)}) collective-permute-start(bf16[640,128]{1,0:T(8,128)(2,1)S(1)} %get-tuple-element.39), channel_id=1, source_target_pairs={{0,2},{2,0},{1,3},{3,1},{4,6},{6,4},{5,7},{7,5},{8,10},{10,8},{9,1... | collective-permute-start | bytes 491528 | tf_op jit(solution)/shard_map/ppermute | solution.py:481
  4.9 1.6 %copy-start.3 = (bf16[1,3,3,320,320]{4,3,2,1,0:T(8,128)(2,1)S(1)}, bf16[1,3,3,320,320]{4,3,2,1,0:T(8,128)(2,1)}, u32[]{:S(2)}) copy-start(bf16[1,3,3,320,320]{4,3,2,1,0:T(8,128)(2,1)} %param.11) | copy-start | bytes 5529604
  6.5 1.6 %copy-start.4 = (bf16[1,3,3,320,320]{4,3,2,1,0:T(8,128)(2,1)S(1)}, bf16[1,3,3,320,320]{4,3,2,1,0:T(8,128)(2,1)}, u32[]{:S(2)}) copy-start(bf16[1,3,3,320,320]{4,3,2,1,0:T(8,128)(2,1)} %param.12) | copy-start | bytes 5529604
  8.1 1.1 %copy-start.5 = (bf16[1,320,960]{2,1,0:T(8,128)(2,1)S(1)}, bf16[1,320,960]{2,1,0:T(8,128)(2,1)}, u32[]{:S(2)}) copy-start(bf16[1,320,960]{2,1,0:T(8,128)(2,1)} %param.14) | copy-start | bytes 1843204
  11.8 1.6 %collective-permute-start.3 = (bf16[640,128]{1,0:T(8,128)(2,1)S(1)}, bf16[640,128]{1,0:T(8,128)(2,1)S(1)}, u32[]{:S(2)}, u32[]{:S(2)}) collective-permute-start(bf16[640,128]{1,0:T(8,128)(2,1)S(1)} %collective-permute-done.1.refs_1_), channel_id=1, source_target_pairs={{0,1},{1,0},{2,3},{3,2},{4,5},{5,4},{6,7},{7,6},{8,9},{9,8},{10,11... | collective-permute-start | bytes 491528 | tf_op jit(solution)/shard_map/ppermute | solution.py:481
  11.9 1.6 %collective-permute-start.2 = (bf16[640,128]{1,0:T(8,128)(2,1)S(1)}, bf16[640,128]{1,0:T(8,128)(2,1)S(1)}, u32[]{:S(2)}, u32[]{:S(2)}) collective-permute-start(bf16[640,128]{1,0:T(8,128)(2,1)S(1)} %collective-permute-done.refs_0_), channel_id=1, source_target_pairs={{0,1},{1,0},{2,3},{3,2},{4,5},{5,4},{6,7},{7,6},{8,9},{9,8},{10,11... | collective-permute-start | bytes 491528 | tf_op jit(solution)/shard_map/ppermute | solution.py:481
  17.6 7.2 %collective-permute-start.4 = (bf16[320,128]{1,0:T(8,128)(2,1)S(1)}, bf16[320,128]{1,0:T(8,128)(2,1)S(1)}, u32[]{:S(2)}, u32[]{:S(2)}) collective-permute-start(bf16[320,128]{1,0:T(8,128)(2,1)S(1)} %get-tuple-element.44), channel_id=1, source_target_pairs={{0,12},{4,8},{8,4},{12,0},{1,13},{5,9},{9,5},{13,1},{2,14},{6,10},... | collective-permute-start | bytes 245768 | tf_op jit(solution)/shard_map/ppermute | solution.py:496
  21.5 7.3 %collective-permute-start.5 = (bf16[320,128]{1,0:T(8,128)(2,1)S(1)}, bf16[320,128]{1,0:T(8,128)(2,1)S(1)}, u32[]{:S(2)}, u32[]{:S(2)}) collective-permute-start(bf16[320,128]{1,0:T(8,128)(2,1)S(1)} %get-tuple-element.45), channel_id=1, source_target_pairs={{0,8},{4,12},{8,0},{12,4},{1,9},{5,13},{9,1},{13,5},{2,10},{6,14},... | collective-permute-start | bytes 245768 | tf_op jit(solution)/shard_map/ppermute | solution.py:496
  21.5 7.3 %copy-start.1 = (bf16[1,320,2560]{2,1,0:T(8,128)(2,1)S(1)}, bf16[1,320,2560]{2,1,0:T(8,128)(2,1)}, u32[]{:S(2)}) copy-start(bf16[1,320,2560]{2,1,0:T(8,128)(2,1)} %param.16) | copy-start | bytes 4915204
  21.5 7.3 %copy-start.2 = (bf16[1,1280,320]{1,2,0:T(8,128)(2,1)S(1)}, bf16[1,1280,320]{1,2,0:T(8,128)(2,1)}, u32[]{:S(2)}) copy-start(bf16[1,1280,320]{1,2,0:T(8,128)(2,1)} %param.17) | copy-start | bytes 2457604
  21.5 7.3 %copy-start.7 = (bf16[1,320,320]{2,1,0:T(8,128)(2,1)S(1)}, bf16[1,320,320]{2,1,0:T(8,128)(2,1)}, u32[]{:S(2)}) copy-start(bf16[1,320,320]{2,1,0:T(8,128)(2,1)} %param.15) | copy-start | bytes 614404
  22.3 6.5 %collective-permute-start.6 = (bf16[320,128]{1,0:T(8,128)(2,1)S(1)}, bf16[320,128]{1,0:T(8,128)(2,1)S(1)}, u32[]{:S(2)}, u32[]{:S(2)}) collective-permute-start(bf16[320,128]{1,0:T(8,128)(2,1)S(1)} %get-tuple-element.50), channel_id=1, source_target_pairs={{0,4},{4,0},{8,12},{12,8},{1,5},{5,1},{9,13},{13,9},{2,6},{6,2},{1... | collective-permute-start | bytes 245768 | tf_op jit(solution)/shard_map/ppermute | solution.py:496
  32.8 8.3 %collective-permute-start.7 = (bf16[320,128]{1,0:T(8,128)(2,1)S(1)}, bf16[320,128]{1,0:T(8,128)(2,1)S(1)}, u32[]{:S(2)}, u32[]{:S(2)}) collective-permute-start(bf16[320,128]{1,0:T(8,128)(2,1)S(1)} %get-tuple-element.53), channel_id=1, source_target_pairs={{0,14},{2,12},{4,10},{6,8},{8,6},{10,4},{12,2},{14,0},{1,15},{3,13... | collective-permute-start | bytes 245768 | tf_op jit(solution)/shard_map/ppermute | solution.py:494
  36.2 6.3 %collective-permute-start.8 = (bf16[320,128]{1,0:T(8,128)(2,1)S(1)}, bf16[320,128]{1,0:T(8,128)(2,1)S(1)}, u32[]{:S(2)}, u32[]{:S(2)}) collective-permute-start(bf16[320,128]{1,0:T(8,128)(2,1)S(1)} %get-tuple-element.54), channel_id=1, source_target_pairs={{0,6},{2,4},{4,2},{6,0},{8,14},{10,12},{12,10},{14,8},{1,7},{3,5},... | collective-permute-start | bytes 245768 | tf_op jit(solution)/shard_map/ppermute | solution.py:494
  37.7 6.5 %collective-permute-start.9 = (bf16[320,128]{1,0:T(8,128)(2,1)S(1)}, bf16[320,128]{1,0:T(8,128)(2,1)S(1)}, u32[]{:S(2)}, u32[]{:S(2)}) collective-permute-start(bf16[320,128]{1,0:T(8,128)(2,1)S(1)} %get-tuple-element.56), channel_id=1, source_target_pairs={{0,10},{2,8},{4,14},{6,12},{8,2},{10,0},{12,6},{14,4},{1,11},{3,9}... | collective-permute-start | bytes 245768 | tf_op jit(solution)/shard_map/ppermute | solution.py:494
  40.6 4.5 %collective-permute-start.10 = (bf16[320,128]{1,0:T(8,128)(2,1)S(1)}, bf16[320,128]{1,0:T(8,128)(2,1)S(1)}, u32[]{:S(2)}, u32[]{:S(2)}) collective-permute-start(bf16[320,128]{1,0:T(8,128)(2,1)S(1)} %get-tuple-element.57), channel_id=1, source_target_pairs={{0,2},{2,0},{4,6},{6,4},{8,10},{10,8},{12,14},{14,12},{1,3},{3,1},... | collective-permute-start | bytes 245768 | tf_op jit(solution)/shard_map/ppermute | solution.py:494
  42.5 3.9 %collective-permute-start.11 = (bf16[640,128]{1,0:T(8,128)(2,1)S(1)}, bf16[640,128]{1,0:T(8,128)(2,1)S(1)}, u32[]{:S(2)}, u32[]{:S(2)}) collective-permute-start(bf16[640,128]{1,0:T(8,128)(2,1)S(1)} %join.5.refs_0_), channel_id=1, source_target_pairs={{0,1},{1,0},{2,3},{3,2},{4,5},{5,4},{6,7},{7,6},{8,9},{9,8},{10,11... | collective-permute-start | bytes 491528 | tf_op jit(solution)/shard_map/ppermute | solution.py:481
  44.2 1.3 %collective-permute-start.12 = (bf16[320,128]{1,0:T(8,128)(2,1)S(1)}, bf16[320,128]{1,0:T(8,128)(2,1)S(1)}, u32[]{:S(2)}, u32[]{:S(2)}) collective-permute-start(bf16[320,128]{1,0:T(8,128)(2,1)S(1)} %collective-permute-done.9.refs_1_), channel_id=1, source_target_pairs={{0,1},{1,0},{2,3},{3,2},{4,5},{5,4},{6,7},{7,6},{8,9},{9,8},{10,11... | collective-permute-start | bytes 245768 | tf_op jit(solution)/shard_map/ppermute | solution.py:481
  45.1 1.3 %collective-permute-start.13 = (bf16[320,128]{1,0:T(8,128)(2,1)S(1)}, bf16[320,128]{1,0:T(8,128)(2,1)S(1)}, u32[]{:S(2)}, u32[]{:S(2)}) collective-permute-start(bf16[320,128]{1,0:T(8,128)(2,1)S(1)} %collective-permute-done.10.refs_2_), channel_id=1, source_target_pairs={{0,1},{1,0},{2,3},{3,2},{4,5},{5,4},{6,7},{7,6},{8,9},{9,8},{10,11... | collective-permute-start | bytes 245768 | tf_op jit(solution)/shard_map/ppermute | solution.py:481
  50.7 7.2 %collective-permute-start.14 = (bf16[320,128]{1,0:T(8,128)(2,1)S(1)}, bf16[320,128]{1,0:T(8,128)(2,1)S(1)}, u32[]{:S(2)}, u32[]{:S(2)}) collective-permute-start(bf16[320,128]{1,0:T(8,128)(2,1)S(1)} %get-tuple-element.58), channel_id=1, source_target_pairs={{0,12},{4,8},{8,4},{12,0},{1,13},{5,9},{9,5},{13,1},{2,14},{6,10},... | collective-permute-start | bytes 245768 | tf_op jit(solution)/shard_map/ppermute | solution.py:496
  53.1 7.2 %collective-permute-start.15 = (bf16[320,128]{1,0:T(8,128)(2,1)S(1)}, bf16[320,128]{1,0:T(8,128)(2,1)S(1)}, u32[]{:S(2)}, u32[]{:S(2)}) collective-permute-start(bf16[320,128]{1,0:T(8,128)(2,1)S(1)} %get-tuple-element.59), channel_id=1, source_target_pairs={{0,4},{4,0},{8,12},{12,8},{1,5},{5,1},{9,13},{13,9},{2,6},{6,2},{1... | collective-permute-start | bytes 245768 | tf_op jit(solution)/shard_map/ppermute | solution.py:496
  54.0 7.2 %collective-permute-start.16 = (bf16[320,128]{1,0:T(8,128)(2,1)S(1)}, bf16[320,128]{1,0:T(8,128)(2,1)S(1)}, u32[]{:S(2)}, u32[]{:S(2)}) collective-permute-start(bf16[320,128]{1,0:T(8,128)(2,1)S(1)} %get-tuple-element.64), channel_id=1, source_target_pairs={{0,8},{4,12},{8,0},{12,4},{1,9},{5,13},{9,1},{13,5},{2,10},{6,14},... | collective-permute-start | bytes 245768 | tf_op jit(solution)/shard_map/ppermute | solution.py:496
  65.1 6.9 %collective-permute-start.17 = (bf16[320,128]{1,0:T(8,128)(2,1)S(1)}, bf16[320,128]{1,0:T(8,128)(2,1)S(1)}, u32[]{:S(2)}, u32[]{:S(2)}) collective-permute-start(bf16[320,128]{1,0:T(8,128)(2,1)S(1)} %get-tuple-element.66), channel_id=1, source_target_pairs={{0,12},{4,8},{8,4},{12,0},{1,13},{5,9},{9,5},{13,1},{2,14},{6,10},... | collective-permute-start | bytes 245768 | tf_op jit(solution)/shard_map/ppermute | solution.py:496
  67.0 5.7 %collective-permute-start.18 = (bf16[320,128]{1,0:T(8,128)(2,1)S(1)}, bf16[320,128]{1,0:T(8,128)(2,1)S(1)}, u32[]{:S(2)}, u32[]{:S(2)}) collective-permute-start(bf16[320,128]{1,0:T(8,128)(2,1)S(1)} %get-tuple-element.67), channel_id=1, source_target_pairs={{0,4},{4,0},{8,12},{12,8},{1,5},{5,1},{9,13},{13,9},{2,6},{6,2},{1... | collective-permute-start | bytes 245768 | tf_op jit(solution)/shard_map/ppermute | solution.py:496
  68.5 5.5 %collective-permute-start.19 = (bf16[320,128]{1,0:T(8,128)(2,1)S(1)}, bf16[320,128]{1,0:T(8,128)(2,1)S(1)}, u32[]{:S(2)}, u32[]{:S(2)}) collective-permute-start(bf16[320,128]{1,0:T(8,128)(2,1)S(1)} %get-tuple-element.69), channel_id=1, source_target_pairs={{0,8},{4,12},{8,0},{12,4},{1,9},{5,13},{9,1},{13,5},{2,10},{6,14},... | collective-permute-start | bytes 245768 | tf_op jit(solution)/shard_map/ppermute | solution.py:496

commit v8 on v7

--- a/solution.py
+++ b/solution.py
@@ -401,7 +401,7 @@
         scores = [jnp.where(same, score, float(jnp.finfo(F32).min)) for score in scores]
         tops = [jnp.max(score, axis=1, keepdims=True) for score in scores]
         powers = [
-            jnp.exp((score - top) * HEAD_DIM ** (-0.5)) for score, top in zip(scores, tops)
+            jnp.exp2((score - top) * (HEAD_DIM ** (-0.5) / math.log(2.0))) for score, top in zip(scores, tops)
         ]
         totals = [1.0 / jnp.sum(power, axis=1, keepdims=True) for power in powers]
         weights = [power.astype(BF16) for power in powers]

time: 75.1 us -> 75 us (level)
  no operation moved by 1% of the time
where the time goes in v8:
time: 75 us; the launch traced here: 74.7 us
  starting transfers between devices  24.2 us (32%)
  Pallas kernels  22.3 us (30%)
  waiting for transfers between devices  21.7 us (29%)
  local copies, waits for them, and re-layouts  5.39 us (7%)
  other arithmetic  0.79 us (1%)
    ppermute x9, waiting for transfers between devices, exchange(): part = lax.ppermute(part, 'shard', [(z, z ^ d) for z in range(shards)])  13.8 us
    ppermute x9, starting transfers between devices, exchange(): part = lax.ppermute(part, 'shard', [(z, z ^ d) for z in range(shards)])  13.7 us
    pallas_call x2, Pallas kernels, spatial(): pl.pallas_call(functools.partial(spatial_kernel, rows, half, columns, cha...  8.37 us
    pallas_call x2, Pallas kernels, temporal(): pl.pallas_call(functools.partial(temporal_kernel, frames, ways, sooner, s...  7.68 us
    ppermute x4, starting transfers between devices, exchange(): part = lax.ppermute(part, ('shard', 'section'), route)  6.88 us
    unnamed x16, local copies, waits for them, and re-layouts  5.39 us
    ppermute x7, waiting for transfers between devices, send(): lax.ppermute(block, axis, [(i, (i + distance) % count) for i in range(cou...  3.94 us
    ppermute x4, waiting for transfers between devices, exchange(): part = lax.ppermute(part, ('shard', 'section'), route)  3.92 us
  transfers between devices with their start and end apart: 20, of which 15 were waited for; matrix products, arithmetic and copies ran while one was open for 1% of the time, Pallas kernels for 7%

profile of v8, /device:TPU:0, one launch (start us, length us, event | category | flops | bytes accessed | tf_op | source)
XLA Modules:
  0.0 74.7 jit_solution(14832817169405743982)
XLA Ops:
  0.0 1.0 %copy-done.6 = bf16[1,1,8,64,320]{4,3,2,1,0:T(8,128)(2,1)S(1)} copy-done((bf16[1,1,8,64,320]{4,3,2,1,0:T(8,128)(2,1)S(1)}, bf16[1,1,8,64,320]{4,3,2,1,0:T(8,128)(2,1)}, u32[]{:S(2)}) %copy-start.6) | copy-done | bytes 327704
  1.0 0.1 pack.1
  1.1 3.0 %collective-permute-start = (bf16[640,128]{1,0:T(8,128)(2,1)S(1)}, bf16[640,128]{1,0:T(8,128)(2,1)S(1)}, u32[]{:S(2)}, u32[]{:S(2)}) collective-permute-start(bf16[640,128]{1,0:T(8,128)(2,1)S(1)} %get-tuple-element.38), channel_id=1, source_target_pairs={{0,2},{2,0},{1,3},{3,1},{4,6},{6,4},{5,7},{7,5},{8,10},{10,8},{9,1... | collective-permute-start | bytes 491528 | tf_op jit(solution)/shard_map/ppermute | solution.py:481
  4.1 0.1 collective-permute-start.1
  4.2 0.7 convert_bitcast_fusion
  4.9 1.6 %copy-done.3 = bf16[1,3,3,320,320]{4,3,2,1,0:T(8,128)(2,1)S(1)} copy-done((bf16[1,3,3,320,320]{4,3,2,1,0:T(8,128)(2,1)S(1)}, bf16[1,3,3,320,320]{4,3,2,1,0:T(8,128)(2,1)}, u32[]{:S(2)}) %copy-start.3) | copy-done | bytes 1843224
  6.5 1.6 %copy-done.4 = bf16[1,3,3,320,320]{4,3,2,1,0:T(8,128)(2,1)S(1)} copy-done((bf16[1,3,3,320,320]{4,3,2,1,0:T(8,128)(2,1)S(1)}, bf16[1,3,3,320,320]{4,3,2,1,0:T(8,128)(2,1)}, u32[]{:S(2)}) %copy-start.4) | copy-done | bytes 1843224
  8.1 1.1 %copy-done.5 = bf16[1,320,960]{2,1,0:T(8,128)(2,1)S(1)} copy-done((bf16[1,320,960]{2,1,0:T(8,128)(2,1)S(1)}, bf16[1,320,960]{2,1,0:T(8,128)(2,1)}, u32[]{:S(2)}) %copy-start.5) | copy-done | bytes 614424
  9.2 0.7 prepare.1
  10.0 0.1 multiply_cosine_fusion
  10.1 1.8 %collective-permute-done.1.refs_1_ = bf16[640,128]{1,0:T(8,128)(2,1)S(1)} collective-permute-done((bf16[640,128]{1,0:T(8,128)(2,1)S(1)}, bf16[640,128]{1,0:T(8,128)(2,1)S(1)}, u32[]{:S(2)}, u32[]{:S(2)}) %collective-permute-start.1) | collective-permute-done | bytes 163872 | tf_op jit(solution)/shard_map/ppermute | solution.py:481
  11.8 0.0 collective-permute-done.refs_0_
  11.9 0.5 collective-permute-start.2
  12.4 0.2 fusion
  12.6 0.9 %collective-permute-done.2.refs_2_ = bf16[640,128]{1,0:T(8,128)(2,1)S(1)} collective-permute-done((bf16[640,128]{1,0:T(8,128)(2,1)S(1)}, bf16[640,128]{1,0:T(8,128)(2,1)S(1)}, u32[]{:S(2)}, u32[]{:S(2)}) %collective-permute-start.2) | collective-permute-done | bytes 163872 | tf_op jit(solution)/shard_map/ppermute | solution.py:481
  13.5 4.1 %spatial.2 = (bf16[320,128]{1,0:T(8,128)(2,1)S(1)}, bf16[320,128]{1,0:T(8,128)(2,1)S(1)}, f32[256,384]{1,0:T(8,128)S(1)}, bf16[640,256]{1,0:T(8,128)(2,1)S(1)}, ...) custom-call(bf16[640,128]{1,0:T(8,128)(2,1)S(1)} %collective-permute-done.refs_0_, ...), custom_call_target="tpu_custom_call" | custom-call | flops 3221225472 | bytes 6000000 | tf_op jit(solution)/shard_map/spatial/pallas_call | solution.py:230
  17.6 3.9 %collective-permute-start.4 = (bf16[320,128]{1,0:T(8,128)(2,1)S(1)}, bf16[320,128]{1,0:T(8,128)(2,1)S(1)}, u32[]{:S(2)}, u32[]{:S(2)}) collective-permute-start(bf16[320,128]{1,0:T(8,128)(2,1)S(1)} %get-tuple-element.44), channel_id=1, source_target_pairs={{0,12},{4,8},{8,4},{12,0},{1,13},{5,9},{9,5},{13,1},{2,14},{6,10},... | collective-permute-start | bytes 245768 | tf_op jit(solution)/shard_map/ppermute | solution.py:496
  21.5 0.0 collective-permute-start.5
  21.5 0.8 %finish.2 = (bf16[320,128]{1,0:T(8,128)(2,1)S(1)}, bf16[320,128]{1,0:T(8,128)(2,1)S(1)}) custom-call(f32[256,384]{1,0:T(8,128)S(1)} %get-tuple-element.46.keep, bf16[640,256]{1,0:T(8,128)(2,1)S(1)} %get-tuple-element.47.middle, bf16[640,128]{1,0:T(8,128)(2,1)S(1)} %get-tuple-element.48.edge, bf16[640,128]{1,0:T(8,128)(2,1)S(1)} %get-tuple-element.49.pair, ...), custom_call_target="tpu_custom_call" | custom-call | flops 536870912 | bytes 3000000 | tf_op jit(solution)/shard_map/finish/pallas_call | solution.py:261
  22.3 0.7 collective-permute-start.6
  23.0 1.8 %collective-permute-done.4.refs_0_ = bf16[320,128]{1,0:T(8,128)(2,1)S(1)} collective-permute-done((bf16[320,128]{1,0:T(8,128)(2,1)S(1)}, bf16[320,128]{1,0:T(8,128)(2,1)S(1)}, u32[]{:S(2)}, u32[]{:S(2)}) %collective-permute-start.4) | collective-permute-done | bytes 81952 | tf_op jit(solution)/shard_map/ppermute | solution.py:496
  24.8 4.0 %collective-permute-done.5.refs_1_ = bf16[320,128]{1,0:T(8,128)(2,1)S(1)} collective-permute-done((bf16[320,128]{1,0:T(8,128)(2,1)S(1)}, bf16[320,128]{1,0:T(8,128)(2,1)S(1)}, u32[]{:S(2)}, u32[]{:S(2)}) %collective-permute-start.5) | collective-permute-done | bytes 81952 | tf_op jit(solution)/shard_map/ppermute | solution.py:496
  28.8 3.8 %temporal.2 = (bf16[320,128]{1,0:T(8,128)(2,1)S(1)}, bf16[320,128]{1,0:T(8,128)(2,1)S(1)}, bf16[256,320]{1,0:T(8,128)(2,1)S(1)}) custom-call(bf16[640,128]{1,0:T(8,128)(2,1)S(1)} %join.4.refs_0_, bf16[320,128]{1,0:T(8,128)(2,1)S(1)} %collective-permute-done.6.refs_1_, bf16[320,128]{1,0:T(8,128)(2,1)S(1)} %get-tuple-element.51.refs_2_, ...), custom_call_target="tpu_custom_call" | custom-call | flops 1132462080 | bytes 4000000 | tf_op jit(solution)/shard_map/temporal/pallas_call | solution.py:443
  32.7 3.5 %collective-permute-start.7 = (bf16[320,128]{1,0:T(8,128)(2,1)S(1)}, bf16[320,128]{1,0:T(8,128)(2,1)S(1)}, u32[]{:S(2)}, u32[]{:S(2)}) collective-permute-start(bf16[320,128]{1,0:T(8,128)(2,1)S(1)} %get-tuple-element.53), channel_id=1, source_target_pairs={{0,14},{2,12},{4,10},{6,8},{8,6},{10,4},{12,2},{14,0},{1,15},{3,13... | collective-permute-start | bytes 245768 | tf_op jit(solution)/shard_map/ppermute | solution.py:494
  36.2 1.5 %feed.2 = (bf16[320,128]{1,0:T(8,128)(2,1)S(1)}, bf16[320,128]{1,0:T(8,128)(2,1)S(1)}) custom-call(bf16[256,320]{1,0:T(8,128)(2,1)S(1)} %get-tuple-element.55.refs_0_, bf16[320,2560]{1,0:T(8,128)(2,1)S(1)} %bitcast.16, bf16[320,1280]{1,0:T(8,128)(2,1)S(1)} %bitcast.20), custom_call_target="tpu_custom_call" | custom-call | flops 629145600 | bytes 3000000 | tf_op jit(solution)/shard_map/feed/pallas_call | solution.py:462
  37.6 2.9 %collective-permute-start.9 = (bf16[320,128]{1,0:T(8,128)(2,1)S(1)}, bf16[320,128]{1,0:T(8,128)(2,1)S(1)}, u32[]{:S(2)}, u32[]{:S(2)}) collective-permute-start(bf16[320,128]{1,0:T(8,128)(2,1)S(1)} %get-tuple-element.56), channel_id=1, source_target_pairs={{0,10},{2,8},{4,14},{6,12},{8,2},{10,0},{12,6},{14,4},{1,11},{3,9}... | collective-permute-start | bytes 245768 | tf_op jit(solution)/shard_map/ppermute | solution.py:494
  40.5 0.5 collective-permute-start.10
  41.0 1.4 %collective-permute-done.8.refs_1_ = bf16[320,128]{1,0:T(8,128)(2,1)S(1)} collective-permute-done((bf16[320,128]{1,0:T(8,128)(2,1)S(1)}, bf16[320,128]{1,0:T(8,128)(2,1)S(1)}, u32[]{:S(2)}, u32[]{:S(2)}) %collective-permute-start.8) | collective-permute-done | bytes 81952 | tf_op jit(solution)/shard_map/ppermute | solution.py:494
  42.5 0.1 collective-permute-start.11
  42.6 1.6 %collective-permute-done.9.refs_1_ = bf16[320,128]{1,0:T(8,128)(2,1)S(1)} collective-permute-done((bf16[320,128]{1,0:T(8,128)(2,1)S(1)}, bf16[320,128]{1,0:T(8,128)(2,1)S(1)}, u32[]{:S(2)}, u32[]{:S(2)}) %collective-permute-start.9) | collective-permute-done | bytes 81952 | tf_op jit(solution)/shard_map/ppermute | solution.py:494
  44.2 0.9 %collective-permute-done.10.refs_2_ = bf16[320,128]{1,0:T(8,128)(2,1)S(1)} collective-permute-done((bf16[320,128]{1,0:T(8,128)(2,1)S(1)}, bf16[320,128]{1,0:T(8,128)(2,1)S(1)}, u32[]{:S(2)}, u32[]{:S(2)}) %collective-permute-start.10) | collective-permute-done | bytes 81952 | tf_op jit(solution)/shard_map/ppermute | solution.py:494
  45.1 0.4 collective-permute-done.12.refs_4_
  45.5 0.9 %collective-permute-done.13.refs_5_ = bf16[320,128]{1,0:T(8,128)(2,1)S(1)} collective-permute-done((bf16[320,128]{1,0:T(8,128)(2,1)S(1)}, bf16[320,128]{1,0:T(8,128)(2,1)S(1)}, u32[]{:S(2)}, u32[]{:S(2)}) %collective-permute-start.13) | collective-permute-done | bytes 81952 | tf_op jit(solution)/shard_map/ppermute | solution.py:481
  46.3 4.3 %spatial.3 = (bf16[320,128]{1,0:T(8,128)(2,1)S(1)}, bf16[320,128]{1,0:T(8,128)(2,1)S(1)}, f32[256,384]{1,0:T(8,128)S(1)}, bf16[640,256]{1,0:T(8,128)(2,1)S(1)}, ...) custom-call(bf16[640,128]{1,0:T(8,128)(2,1)S(1)} %join.5.refs_0_, ...), custom_call_target="tpu_custom_call" | custom-call | flops 3221225472 | bytes 6000000 | tf_op jit(solution)/shard_map/spatial/pallas_call | solution.py:230
  50.6 2.4 %collective-permute-start.14 = (bf16[320,128]{1,0:T(8,128)(2,1)S(1)}, bf16[320,128]{1,0:T(8,128)(2,1)S(1)}, u32[]{:S(2)}, u32[]{:S(2)}) collective-permute-start(bf16[320,128]{1,0:T(8,128)(2,1)S(1)} %get-tuple-element.58), channel_id=1, source_target_pairs={{0,12},{4,8},{8,4},{12,0},{1,13},{5,9},{9,5},{13,1},{2,14},{6,10},... | collective-permute-start | bytes 245768 | tf_op jit(solution)/shard_map/ppermute | solution.py:496
  53.1 0.8 %finish.3 = (bf16[320,128]{1,0:T(8,128)(2,1)S(1)}, bf16[320,128]{1,0:T(8,128)(2,1)S(1)}) custom-call(f32[256,384]{1,0:T(8,128)S(1)} %get-tuple-element.60.keep, bf16[640,256]{1,0:T(8,128)(2,1)S(1)} %get-tuple-element.61.middle, bf16[640,128]{1,0:T(8,128)(2,1)S(1)} %get-tuple-element.62.edge, bf16[640,128]{1,0:T(8,128)(2,1)S(1)} %get-tuple-element.63.pair, ...), custom_call_target="tpu_custom_call" | custom-call | flops 536870912 | bytes 3000000 | tf_op jit(solution)/shard_map/finish/pallas_call | solution.py:261
  53.9 2.1 %collective-permute-start.16 = (bf16[320,128]{1,0:T(8,128)(2,1)S(1)}, bf16[320,128]{1,0:T(8,128)(2,1)S(1)}, u32[]{:S(2)}, u32[]{:S(2)}) collective-permute-start(bf16[320,128]{1,0:T(8,128)(2,1)S(1)} %get-tuple-element.64), channel_id=1, source_target_pairs={{0,8},{4,12},{8,0},{12,4},{1,9},{5,13},{9,1},{13,5},{2,10},{6,14},... | collective-permute-start | bytes 245768 | tf_op jit(solution)/shard_map/ppermute | solution.py:496
  56.0 1.9 %collective-permute-done.14.refs_0_ = bf16[320,128]{1,0:T(8,128)(2,1)S(1)} collective-permute-done((bf16[320,128]{1,0:T(8,128)(2,1)S(1)}, bf16[320,128]{1,0:T(8,128)(2,1)S(1)}, u32[]{:S(2)}, u32[]{:S(2)}) %collective-permute-start.14) | collective-permute-done | bytes 81952 | tf_op jit(solution)/shard_map/ppermute | solution.py:496
  57.9 2.4 %collective-permute-done.15.refs_1_ = bf16[320,128]{1,0:T(8,128)(2,1)S(1)} collective-permute-done((bf16[320,128]{1,0:T(8,128)(2,1)S(1)}, bf16[320,128]{1,0:T(8,128)(2,1)S(1)}, u32[]{:S(2)}, u32[]{:S(2)}) %collective-permute-start.15) | collective-permute-done | bytes 81952 | tf_op jit(solution)/shard_map/ppermute | solution.py:496
  60.2 0.9 %collective-permute-done.16.refs_1_ = bf16[320,128]{1,0:T(8,128)(2,1)S(1)} collective-permute-done((bf16[320,128]{1,0:T(8,128)(2,1)S(1)}, bf16[320,128]{1,0:T(8,128)(2,1)S(1)}, u32[]{:S(2)}, u32[]{:S(2)}) %collective-permute-start.16) | collective-permute-done | bytes 81952 | tf_op jit(solution)/shard_map/ppermute | solution.py:496
  61.1 3.8 %temporal.3 = (bf16[320,128]{1,0:T(8,128)(2,1)S(1)}, bf16[320,128]{1,0:T(8,128)(2,1)S(1)}, bf16[256,320]{1,0:T(8,128)(2,1)S(1)}) custom-call(bf16[640,128]{1,0:T(8,128)(2,1)S(1)} %join.6.refs_0_, bf16[320,128]{1,0:T(8,128)(2,1)S(1)} %collective-permute-done.16.refs_1_, bf16[320,128]{1,0:T(8,128)(2,1)S(1)} %get-tuple-element.65.refs_2_, ...), custom_call_target="tpu_custom_call" | custom-call | flops 1132462080 | bytes 4000000 | tf_op jit(solution)/shard_map/temporal/pallas_call | solution.py:443
  65.0 1.9 %collective-permute-start.17 = (bf16[320,128]{1,0:T(8,128)(2,1)S(1)}, bf16[320,128]{1,0:T(8,128)(2,1)S(1)}, u32[]{:S(2)}, u32[]{:S(2)}) collective-permute-start(bf16[320,128]{1,0:T(8,128)(2,1)S(1)} %get-tuple-element.66), channel_id=1, source_target_pairs={{0,12},{4,8},{8,4},{12,0},{1,13},{5,9},{9,5},{13,1},{2,14},{6,10},... | collective-permute-start | bytes 245768 | tf_op jit(solution)/shard_map/ppermute | solution.py:496
  66.9 1.5 %feed.3 = (bf16[320,128]{1,0:T(8,128)(2,1)S(1)}, bf16[320,128]{1,0:T(8,128)(2,1)S(1)}) custom-call(bf16[256,320]{1,0:T(8,128)(2,1)S(1)} %get-tuple-element.68.refs_0_, bf16[320,2560]{1,0:T(8,128)(2,1)S(1)} %bitcast.18, bf16[320,1280]{1,0:T(8,128)(2,1)S(1)} %bitcast.22), custom_call_target="tpu_custom_call" | custom-call | flops 629145600 | bytes 3000000 | tf_op jit(solution)/shard_map/feed/pallas_call | solution.py:462
  68.4 2.6 %collective-permute-start.19 = (bf16[320,128]{1,0:T(8,128)(2,1)S(1)}, bf16[320,128]{1,0:T(8,128)(2,1)S(1)}, u32[]{:S(2)}, u32[]{:S(2)}) collective-permute-start(bf16[320,128]{1,0:T(8,128)(2,1)S(1)} %get-tuple-element.69), channel_id=1, source_target_pairs={{0,8},{4,12},{8,0},{12,4},{1,9},{5,13},{9,1},{13,5},{2,10},{6,14},... | collective-permute-start | bytes 245768 | tf_op jit(solution)/shard_map/ppermute | solution.py:496
  71.0 0.9 %collective-permute-done.17.refs_0_ = bf16[320,128]{1,0:T(8,128)(2,1)S(1)} collective-permute-done((bf16[320,128]{1,0:T(8,128)(2,1)S(1)}, bf16[320,128]{1,0:T(8,128)(2,1)S(1)}, u32[]{:S(2)}, u32[]{:S(2)}) %collective-permute-start.17) | collective-permute-done | bytes 81952 | tf_op jit(solution)/shard_map/ppermute | solution.py:496
  71.9 0.7 collective-permute-done.18.refs_1_
  72.6 1.3 %collective-permute-done.19.refs_1_ = bf16[320,128]{1,0:T(8,128)(2,1)S(1)} collective-permute-done((bf16[320,128]{1,0:T(8,128)(2,1)S(1)}, bf16[320,128]{1,0:T(8,128)(2,1)S(1)}, u32[]{:S(2)}, u32[]{:S(2)}) %collective-permute-start.19) | collective-permute-done | bytes 81952 | tf_op jit(solution)/shard_map/ppermute | solution.py:496
  73.9 0.9 %unpack.1 = bf16[512,320]{1,0:T(8,128)(2,1)} custom-call(bf16[640,128]{1,0:T(8,128)(2,1)S(1)} %join.7.refs_0_, bf16[320,128]{1,0:T(8,128)(2,1)S(1)} %collective-permute-done.19.refs_1_, bf16[320,128]{1,0:T(8,128)(2,1)S(1)} %get-tuple-element.70.refs_2_), custom_call_target="tpu_custom_call" | custom-call | tf_op jit(solution)/shard_map/unpack/pallas_call | solution.py:569
  (28 shorter events, 0.1 us)
Async XLA Ops:
  0.0 12.4 %copy-start = (bf16[1,320,320]{2,1,0:T(8,128)(2,1)S(1)}, bf16[1,320,320]{2,1,0:T(8,128)(2,1)}, u32[]{:S(2)}) copy-start(bf16[1,320,320]{2,1,0:T(8,128)(2,1)} %param.13) | copy-start | bytes 614404
  0.0 1.0 %copy-start.6 = (bf16[1,1,8,64,320]{4,3,2,1,0:T(8,128)(2,1)S(1)}, bf16[1,1,8,64,320]{4,3,2,1,0:T(8,128)(2,1)}, u32[]{:S(2)}) copy-start(bf16[1,1,8,64,320]{4,3,2,1,0:T(8,128)(2,1)} %param.9) | copy-start | bytes 983044
  1.1 10.7 %collective-permute-start = (bf16[640,128]{1,0:T(8,128)(2,1)S(1)}, bf16[640,128]{1,0:T(8,128)(2,1)S(1)}, u32[]{:S(2)}, u32[]{:S(2)}) collective-permute-start(bf16[640,128]{1,0:T(8,128)(2,1)S(1)} %get-tuple-element.38), channel_id=1, source_target_pairs={{0,2},{2,0},{1,3},{3,1},{4,6},{6,4},{5,7},{7,5},{8,10},{10,8},{9,1... | collective-permute-start | bytes 491528 | tf_op jit(solution)/shard_map/ppermute | solution.py:481
  4.1 7.7 %collective-permute-start.1 = (bf16[640,128]{1,0:T(8,128)(2,1)S(1)}, bf16[640,128]{1,0:T(8,128)(2,1)S(1)}, u32[]{:S(2)}, u32[]{:S(2)}) collective-permute-start(bf16[640,128]{1,0:T(8,128)(2,1)S(1)} %get-tuple-element.39), channel_id=1, source_target_pairs={{0,2},{2,0},{1,3},{3,1},{4,6},{6,4},{5,7},{7,5},{8,10},{10,8},{9,1... | collective-permute-start | bytes 491528 | tf_op jit(solution)/shard_map/ppermute | solution.py:481
  4.9 1.6 %copy-start.3 = (bf16[1,3,3,320,320]{4,3,2,1,0:T(8,128)(2,1)S(1)}, bf16[1,3,3,320,320]{4,3,2,1,0:T(8,128)(2,1)}, u32[]{:S(2)}) copy-start(bf16[1,3,3,320,320]{4,3,2,1,0:T(8,128)(2,1)} %param.11) | copy-start | bytes 5529604
  6.5 1.6 %copy-start.4 = (bf16[1,3,3,320,320]{4,3,2,1,0:T(8,128)(2,1)S(1)}, bf16[1,3,3,320,320]{4,3,2,1,0:T(8,128)(2,1)}, u32[]{:S(2)}) copy-start(bf16[1,3,3,320,320]{4,3,2,1,0:T(8,128)(2,1)} %param.12) | copy-start | bytes 5529604
  8.1 1.1 %copy-start.5 = (bf16[1,320,960]{2,1,0:T(8,128)(2,1)S(1)}, bf16[1,320,960]{2,1,0:T(8,128)(2,1)}, u32[]{:S(2)}) copy-start(bf16[1,320,960]{2,1,0:T(8,128)(2,1)} %param.14) | copy-start | bytes 1843204
  11.8 1.6 %collective-permute-start.3 = (bf16[640,128]{1,0:T(8,128)(2,1)S(1)}, bf16[640,128]{1,0:T(8,128)(2,1)S(1)}, u32[]{:S(2)}, u32[]{:S(2)}) collective-permute-start(bf16[640,128]{1,0:T(8,128)(2,1)S(1)} %collective-permute-done.1.refs_1_), channel_id=1, source_target_pairs={{0,1},{1,0},{2,3},{3,2},{4,5},{5,4},{6,7},{7,6},{8,9},{9,8},{10,11... | collective-permute-start | bytes 491528 | tf_op jit(solution)/shard_map/ppermute | solution.py:481
  11.9 1.6 %collective-permute-start.2 = (bf16[640,128]{1,0:T(8,128)(2,1)S(1)}, bf16[640,128]{1,0:T(8,128)(2,1)S(1)}, u32[]{:S(2)}, u32[]{:S(2)}) collective-permute-start(bf16[640,128]{1,0:T(8,128)(2,1)S(1)} %collective-permute-done.refs_0_), channel_id=1, source_target_pairs={{0,1},{1,0},{2,3},{3,2},{4,5},{5,4},{6,7},{7,6},{8,9},{9,8},{10,11... | collective-permute-start | bytes 491528 | tf_op jit(solution)/shard_map/ppermute | solution.py:481
  17.6 7.2 %collective-permute-start.4 = (bf16[320,128]{1,0:T(8,128)(2,1)S(1)}, bf16[320,128]{1,0:T(8,128)(2,1)S(1)}, u32[]{:S(2)}, u32[]{:S(2)}) collective-permute-start(bf16[320,128]{1,0:T(8,128)(2,1)S(1)} %get-tuple-element.44), channel_id=1, source_target_pairs={{0,12},{4,8},{8,4},{12,0},{1,13},{5,9},{9,5},{13,1},{2,14},{6,10},... | collective-permute-start | bytes 245768 | tf_op jit(solution)/shard_map/ppermute | solution.py:496
  21.5 7.3 %collective-permute-start.5 = (bf16[320,128]{1,0:T(8,128)(2,1)S(1)}, bf16[320,128]{1,0:T(8,128)(2,1)S(1)}, u32[]{:S(2)}, u32[]{:S(2)}) collective-permute-start(bf16[320,128]{1,0:T(8,128)(2,1)S(1)} %get-tuple-element.45), channel_id=1, source_target_pairs={{0,8},{4,12},{8,0},{12,4},{1,9},{5,13},{9,1},{13,5},{2,10},{6,14},... | collective-permute-start | bytes 245768 | tf_op jit(solution)/shard_map/ppermute | solution.py:496
  21.5 7.3 %copy-start.1 = (bf16[1,320,2560]{2,1,0:T(8,128)(2,1)S(1)}, bf16[1,320,2560]{2,1,0:T(8,128)(2,1)}, u32[]{:S(2)}) copy-start(bf16[1,320,2560]{2,1,0:T(8,128)(2,1)} %param.16) | copy-start | bytes 4915204
  21.5 7.3 %copy-start.2 = (bf16[1,1280,320]{1,2,0:T(8,128)(2,1)S(1)}, bf16[1,1280,320]{1,2,0:T(8,128)(2,1)}, u32[]{:S(2)}) copy-start(bf16[1,1280,320]{1,2,0:T(8,128)(2,1)} %param.17) | copy-start | bytes 2457604
  21.5 7.3 %copy-start.7 = (bf16[1,320,320]{2,1,0:T(8,128)(2,1)S(1)}, bf16[1,320,320]{2,1,0:T(8,128)(2,1)}, u32[]{:S(2)}) copy-start(bf16[1,320,320]{2,1,0:T(8,128)(2,1)} %param.15) | copy-start | bytes 614404
  22.3 6.5 %collective-permute-start.6 = (bf16[320,128]{1,0:T(8,128)(2,1)S(1)}, bf16[320,128]{1,0:T(8,128)(2,1)S(1)}, u32[]{:S(2)}, u32[]{:S(2)}) collective-permute-start(bf16[320,128]{1,0:T(8,128)(2,1)S(1)} %get-tuple-element.50), channel_id=1, source_target_pairs={{0,4},{4,0},{8,12},{12,8},{1,5},{5,1},{9,13},{13,9},{2,6},{6,2},{1... | collective-permute-start | bytes 245768 | tf_op jit(solution)/shard_map/ppermute | solution.py:496
  32.7 8.3 %collective-permute-start.7 = (bf16[320,128]{1,0:T(8,128)(2,1)S(1)}, bf16[320,128]{1,0:T(8,128)(2,1)S(1)}, u32[]{:S(2)}, u32[]{:S(2)}) collective-permute-start(bf16[320,128]{1,0:T(8,128)(2,1)S(1)} %get-tuple-element.53), channel_id=1, source_target_pairs={{0,14},{2,12},{4,10},{6,8},{8,6},{10,4},{12,2},{14,0},{1,15},{3,13... | collective-permute-start | bytes 245768 | tf_op jit(solution)/shard_map/ppermute | solution.py:494
  36.2 6.3 %collective-permute-start.8 = (bf16[320,128]{1,0:T(8,128)(2,1)S(1)}, bf16[320,128]{1,0:T(8,128)(2,1)S(1)}, u32[]{:S(2)}, u32[]{:S(2)}) collective-permute-start(bf16[320,128]{1,0:T(8,128)(2,1)S(1)} %get-tuple-element.54), channel_id=1, source_target_pairs={{0,6},{2,4},{4,2},{6,0},{8,14},{10,12},{12,10},{14,8},{1,7},{3,5},... | collective-permute-start | bytes 245768 | tf_op jit(solution)/shard_map/ppermute | solution.py:494
  37.6 6.5 %collective-permute-start.9 = (bf16[320,128]{1,0:T(8,128)(2,1)S(1)}, bf16[320,128]{1,0:T(8,128)(2,1)S(1)}, u32[]{:S(2)}, u32[]{:S(2)}) collective-permute-start(bf16[320,128]{1,0:T(8,128)(2,1)S(1)} %get-tuple-element.56), channel_id=1, source_target_pairs={{0,10},{2,8},{4,14},{6,12},{8,2},{10,0},{12,6},{14,4},{1,11},{3,9}... | collective-permute-start | bytes 245768 | tf_op jit(solution)/shard_map/ppermute | solution.py:494
  40.5 4.5 %collective-permute-start.10 = (bf16[320,128]{1,0:T(8,128)(2,1)S(1)}, bf16[320,128]{1,0:T(8,128)(2,1)S(1)}, u32[]{:S(2)}, u32[]{:S(2)}) collective-permute-start(bf16[320,128]{1,0:T(8,128)(2,1)S(1)} %get-tuple-element.57), channel_id=1, source_target_pairs={{0,2},{2,0},{4,6},{6,4},{8,10},{10,8},{12,14},{14,12},{1,3},{3,1},... | collective-permute-start | bytes 245768 | tf_op jit(solution)/shard_map/ppermute | solution.py:494
  42.5 3.9 %collective-permute-start.11 = (bf16[640,128]{1,0:T(8,128)(2,1)S(1)}, bf16[640,128]{1,0:T(8,128)(2,1)S(1)}, u32[]{:S(2)}, u32[]{:S(2)}) collective-permute-start(bf16[640,128]{1,0:T(8,128)(2,1)S(1)} %join.5.refs_0_), channel_id=1, source_target_pairs={{0,1},{1,0},{2,3},{3,2},{4,5},{5,4},{6,7},{7,6},{8,9},{9,8},{10,11... | collective-permute-start | bytes 491528 | tf_op jit(solution)/shard_map/ppermute | solution.py:481
  44.2 1.3 %collective-permute-start.12 = (bf16[320,128]{1,0:T(8,128)(2,1)S(1)}, bf16[320,128]{1,0:T(8,128)(2,1)S(1)}, u32[]{:S(2)}, u32[]{:S(2)}) collective-permute-start(bf16[320,128]{1,0:T(8,128)(2,1)S(1)} %collective-permute-done.9.refs_1_), channel_id=1, source_target_pairs={{0,1},{1,0},{2,3},{3,2},{4,5},{5,4},{6,7},{7,6},{8,9},{9,8},{10,11... | collective-permute-start | bytes 245768 | tf_op jit(solution)/shard_map/ppermute | solution.py:481
  45.1 1.3 %collective-permute-start.13 = (bf16[320,128]{1,0:T(8,128)(2,1)S(1)}, bf16[320,128]{1,0:T(8,128)(2,1)S(1)}, u32[]{:S(2)}, u32[]{:S(2)}) collective-permute-start(bf16[320,128]{1,0:T(8,128)(2,1)S(1)} %collective-permute-done.10.refs_2_), channel_id=1, source_target_pairs={{0,1},{1,0},{2,3},{3,2},{4,5},{5,4},{6,7},{7,6},{8,9},{9,8},{10,11... | collective-permute-start | bytes 245768 | tf_op jit(solution)/shard_map/ppermute | solution.py:481
  50.6 7.2 %collective-permute-start.14 = (bf16[320,128]{1,0:T(8,128)(2,1)S(1)}, bf16[320,128]{1,0:T(8,128)(2,1)S(1)}, u32[]{:S(2)}, u32[]{:S(2)}) collective-permute-start(bf16[320,128]{1,0:T(8,128)(2,1)S(1)} %get-tuple-element.58), channel_id=1, source_target_pairs={{0,12},{4,8},{8,4},{12,0},{1,13},{5,9},{9,5},{13,1},{2,14},{6,10},... | collective-permute-start | bytes 245768 | tf_op jit(solution)/shard_map/ppermute | solution.py:496
  53.1 7.2 %collective-permute-start.15 = (bf16[320,128]{1,0:T(8,128)(2,1)S(1)}, bf16[320,128]{1,0:T(8,128)(2,1)S(1)}, u32[]{:S(2)}, u32[]{:S(2)}) collective-permute-start(bf16[320,128]{1,0:T(8,128)(2,1)S(1)} %get-tuple-element.59), channel_id=1, source_target_pairs={{0,4},{4,0},{8,12},{12,8},{1,5},{5,1},{9,13},{13,9},{2,6},{6,2},{1... | collective-permute-start | bytes 245768 | tf_op jit(solution)/shard_map/ppermute | solution.py:496
  53.9 7.2 %collective-permute-start.16 = (bf16[320,128]{1,0:T(8,128)(2,1)S(1)}, bf16[320,128]{1,0:T(8,128)(2,1)S(1)}, u32[]{:S(2)}, u32[]{:S(2)}) collective-permute-start(bf16[320,128]{1,0:T(8,128)(2,1)S(1)} %get-tuple-element.64), channel_id=1, source_target_pairs={{0,8},{4,12},{8,0},{12,4},{1,9},{5,13},{9,1},{13,5},{2,10},{6,14},... | collective-permute-start | bytes 245768 | tf_op jit(solution)/shard_map/ppermute | solution.py:496
  65.0 6.9 %collective-permute-start.17 = (bf16[320,128]{1,0:T(8,128)(2,1)S(1)}, bf16[320,128]{1,0:T(8,128)(2,1)S(1)}, u32[]{:S(2)}, u32[]{:S(2)}) collective-permute-start(bf16[320,128]{1,0:T(8,128)(2,1)S(1)} %get-tuple-element.66), channel_id=1, source_target_pairs={{0,12},{4,8},{8,4},{12,0},{1,13},{5,9},{9,5},{13,1},{2,14},{6,10},... | collective-permute-start | bytes 245768 | tf_op jit(solution)/shard_map/ppermute | solution.py:496
  66.9 5.7 %collective-permute-start.18 = (bf16[320,128]{1,0:T(8,128)(2,1)S(1)}, bf16[320,128]{1,0:T(8,128)(2,1)S(1)}, u32[]{:S(2)}, u32[]{:S(2)}) collective-permute-start(bf16[320,128]{1,0:T(8,128)(2,1)S(1)} %get-tuple-element.67), channel_id=1, source_target_pairs={{0,4},{4,0},{8,12},{12,8},{1,5},{5,1},{9,13},{13,9},{2,6},{6,2},{1... | collective-permute-start | bytes 245768 | tf_op jit(solution)/shard_map/ppermute | solution.py:496
  68.4 5.5 %collective-permute-start.19 = (bf16[320,128]{1,0:T(8,128)(2,1)S(1)}, bf16[320,128]{1,0:T(8,128)(2,1)S(1)}, u32[]{:S(2)}, u32[]{:S(2)}) collective-permute-start(bf16[320,128]{1,0:T(8,128)(2,1)S(1)} %get-tuple-element.69), channel_id=1, source_target_pairs={{0,8},{4,12},{8,0},{12,4},{1,9},{5,13},{9,1},{13,5},{2,10},{6,14},... | collective-permute-start | bytes 245768 | tf_op jit(solution)/shard_map/ppermute | solution.py:496
